TPU v7x, 512 devices: a whole 4x8x8 slice. The times are simulated.
512 devices in a mesh: row: 32 (over x_lo, y, core), col: 16 (over z, x_hi).
Axes of the slice: x: 4 (x_hi: 2, x_lo: 2; x = x_hi * 2 + x_lo), y: 8, z: 8, core: 2. Of those that a mesh axis runs over, the one named last changes fastest.
Arguments:
- biomass: bfloat16 [1024, 512, 256], P('row', 'col'), may hold values from 0 to 2
- block_stand: int32 [128, 64], P('row', 'col'), may hold values from 0 to 15
- stand_slot: int32 [32, 16, 16], P('row', 'col'), may hold values from 0 to 8
- tile_list: int32 [32, 16, 8], P('row', 'col'), may hold values from 0 to 63, as said below
- harvest_ops: bfloat16 [64, 256, 256], P('col')
- transition: bfloat16 [256, 256], replicated, may hold values from -0.5 to 0.5
- pattern: int32 [32, 32], replicated, may hold values 0 or 1
- fecundity: bfloat16 [256, 256], replicated, may hold values from -0.375 to 0.375
- radius: int32 [256], replicated, may hold values from 1 to 4, as said below
Outputs:
- final_biomass: bfloat16 [1024, 512, 256], P('row', 'col')
Inputs may be any that keep to these rules, and one draw needn't show every extreme that they name: `tile_list`: each tile lists 8 different prescriptions, held by 8 different indices of col: prescription p is held by index p // 4. `stand_slot`: slot 8 marks a stand left unharvested; a slot k below 8 names entry k of the tile's list. Some cohort has radius 4.
All inputs are finite; a program needn't handle non-finite values.
Results may differ from a plain program's by a relative error of at most 0.0073.
Values may be sent and summed in bfloat16 or wider, within the bound.
No kernel may reach another device: no remote copies, remote signals or barrier semaphores. Data moves between devices by JAX's collectives and lax.ppermute only.
A program may use at most 128 MiB of HBM per device.

v0:
```python
import math

import jax
import jax.numpy as jnp
from jax import lax
from jax.sharding import PartitionSpec as P

TB = 8
RMAX = 4
BX = 8
BY = 8
STEPS = 2


def padded_2(cells, sides, width):
    for axis, dim in sides:
        count = math.prod(lax.axis_size(name) for name in axis)
        ends = count - 1
        head = lax.slice_in_dim(cells, 0, width, axis=dim)
        tail = lax.slice_in_dim(cells, cells.shape[dim] - width, cells.shape[dim], axis=dim)
        cells = jnp.concatenate(
            [
                lax.ppermute(tail, axis, [(i, (i + 1) % count) for i in range(ends)]),
                cells,
                lax.ppermute(head, axis, [((i + 1) % count, i) for i in range(ends)]),
            ],
            axis=dim,
        )
    return cells


def kernel_weights(radius):
    offsets = jnp.arange(-RMAX, RMAX + 1).astype(jnp.float32)
    dist_sq = offsets[:, None] ** 2 + offsets[None, :] ** 2
    reach = (radius.astype(jnp.float32) ** 2)[:, None, None]
    values = jnp.exp(-dist_sq[None] / (2.0 * reach)) * (dist_sq[None] <= reach).astype(jnp.float32)
    return values / jnp.sum(values, axis=(1, 2), keepdims=True)


SPLIT = (("xl", 2), ("yh", 4), ("yl", 2), ("co", 2), ("zh", 4), ("zl", 2), ("xh", 2))
ROW = ("xl", "yh", "yl", "co")
COL = ("zh", "zl", "xh")
NEAR = ("xl", "yl", "co", "zl", "xh")


def fetch_operators(tile_list, harvest_ops):
    listed = tile_list[0, 0]
    count = listed.shape[0]
    held, cohorts, _ = harvest_ops.shape
    lists = lax.all_to_all(
        jnp.broadcast_to(listed[None, :, None], (32, count, 128)), NEAR, 0, 0, tiled=True
    )[:, :, 0]
    mine = (lax.axis_index("xl") * 2 + lax.axis_index("yl")) * 2 + lax.axis_index("co")
    strip = lax.dynamic_slice_in_dim(harvest_ops, mine * 32, 32, axis=1)
    strip = strip.reshape(held, 2, 16, 2, 128).transpose(1, 3, 0, 2, 4)
    spread = jnp.broadcast_to(strip[None], (4, 2, 2, held, 16, 128)).reshape(16, held, 16, 128)
    pieces = lax.all_to_all(spread, COL, 0, 0, tiled=True).reshape(16 * held, 16, 128)
    wanted = pieces[lists.reshape(-1)].reshape(32, count, 16, 128)
    parts = lax.all_to_all(wanted, NEAR, 0, 0, tiled=True)
    parts = parts.reshape(8, 2, 2, count, 16, 128).transpose(3, 0, 1, 4, 2, 5)
    return parts.reshape(count, cohorts, cohorts)


def local(
    biomass, block_stand, stand_slot, tile_list, harvest_ops, transition, pattern, fecundity, radius
):
    rows_here, cols_here, cohorts = biomass.shape
    count = tile_list.shape[-1]
    stands = stand_slot.shape[-1]
    kernel = kernel_weights(radius)
    block_mask = jnp.repeat(jnp.repeat(pattern, TB, 0), TB, 1).astype(jnp.float32)
    moves = (transition.astype(jnp.float32) * block_mask).astype(jnp.bfloat16)
    stand_hit = block_stand[:, :, None] == jnp.arange(stands)[None, None, :]
    block_slot = jnp.sum(jnp.where(stand_hit, stand_slot[0, 0][None, None, :], 0), axis=-1)
    cell_slot = jnp.repeat(jnp.repeat(block_slot, BX, 0), BY, 1)[:, :, None]
    operators = fetch_operators(tile_list, harvest_ops)
    width = 2 * RMAX + 1
    cohort_state = biomass
    for period in range(STEPS):
        padded = padded_2(cohort_state, ((ROW, 0), (COL, 1)), RMAX)
        seedfall = jnp.zeros((rows_here, cols_here, cohorts), jnp.float32)
        for row_off in range(width):
            for col_off in range(width):
                seedfall = seedfall + kernel[:, row_off, col_off] * padded[
                    row_off : row_off + rows_here, col_off : col_off + cols_here
                ].astype(jnp.float32)
        seed_bf = seedfall.astype(jnp.bfloat16)
        middle = (
            cohort_state.astype(jnp.float32)
            + jnp.dot(seed_bf, fecundity, preferred_element_type=jnp.float32)
        ).astype(jnp.bfloat16)
        shifted = jnp.dot(middle, moves, preferred_element_type=jnp.float32)
        grown_rows = (
            shifted * lax.rsqrt(1.0 + jnp.mean(shifted * shifted, axis=-1, keepdims=True))
        ).astype(jnp.bfloat16)
        result = jnp.where(cell_slot == count, grown_rows.astype(jnp.float32), 0.0)
        for slot in range(count):
            product = jnp.dot(grown_rows, operators[slot], preferred_element_type=jnp.float32)
            result = result + jnp.where(cell_slot == slot, product, 0.0)
        cohort_state = result.astype(jnp.bfloat16)
    return cohort_state


def solution(mesh):
    names = tuple(name for name, _ in SPLIT)
    sizes = tuple(size for _, size in SPLIT)
    fine = jax.sharding.Mesh(mesh.devices.reshape(sizes), names)
    placed = (
        P(ROW, COL, None),
        P(ROW, COL),
        P(ROW, COL, None),
        P(ROW, COL, None),
        P(COL, None, None),
        P(),
        P(),
        P(),
        P(),
    )
    return jax.shard_map(
        local, mesh=fine, in_specs=placed, out_specs=P(ROW, COL, None), check_vma=False
    )
```

profile of v0, /device:TPU:1, one launch (start us, length us, event | category | flops | bytes accessed | tf_op | source)
XLA Modules:
  0.0 161.0 jit_solution(9104235005514605658)
XLA Ops:
  0.0 1.4 broadcast_in_dim.192
  1.5 10.4 %all-to-all-start.1 = ((s32[32,8,128]{2,1,0:T(8,128)}), s32[32,8,128]{2,1,0:T(8,128)S(1)}, u32[]{:S(2)}, u32[]{:S(2)}) async-start(s32[32,8,128]{2,1,0:T(8,128)} %broadcast_in_dim.192), calls=%async_computation.1 | async-start | bytes 262144 | tf_op jit(solution)/shard_map/all_to_all | solution.py:50
  11.9 0.9 fusion.835
  12.8 2.2 %collective-permute-start.1 = (bf16[4,32,256]{2,1,0:T(8,128)(2,1)S(1)}, bf16[4,32,256]{2,1,0:T(8,128)(2,1)S(1)}, u32[]{:S(2)}, u32[]{:S(2)}) collective-permute-start(bf16[4,32,256]{2,1,0:T(8,128)(2,1)S(1)} %get-tuple-element.24), channel_id=1, source_target_pairs={{16,0},{32,16},{48,32},{64,48},{80,64},{96,80},{112,96},{128,112},... | collective-permute-start | bytes 196616 | tf_op jit(solution)/shard_map/ppermute | solution.py:25
  15.1 3.3 %collective-permute-start = (bf16[4,32,256]{2,1,0:T(8,128)(2,1)S(1)}, bf16[4,32,256]{2,1,0:T(8,128)(2,1)S(1)}, u32[]{:S(2)}, u32[]{:S(2)}) collective-permute-start(bf16[4,32,256]{2,1,0:T(8,128)(2,1)S(1)} %get-tuple-element.25), channel_id=1, source_target_pairs={{0,16},{16,32},{32,48},{48,64},{64,80},{80,96},{96,112},{112,128},... | collective-permute-start | bytes 196616 | tf_op jit(solution)/shard_map/ppermute | solution.py:23
  18.4 0.7 convert_multiply_fusion.2
  19.2 0.1 fusion.824
  19.8 0.7 fusion.837
  20.5 0.7 fusion.836
  21.2 0.2 select_reduce_fusion
  21.4 0.1 copy.85
  21.5 0.1 copy.112
  21.8 0.1 copy.106
  21.9 0.1 copy.103
  22.2 0.1 copy.94
  22.3 0.1 copy.90
  25.0 0.1 copy.87
  25.2 0.2 constant_dynamic-update-slice_fusion.3
  25.4 0.8 copy-done.8
  26.2 0.8 broadcast_in_dim.190
  27.1 10.2 %all-to-all-start = ((bf16[16,4,16,128]{3,2,1,0:T(8,128)(2,1)}), bf16[16,4,16,128]{3,2,1,0:T(8,128)(2,1)S(1)}, u32[]{:S(2)}, u32[]{:S(2)}) async-start(bf16[16,4,16,128]{3,2,1,0:T(8,128)(2,1)} %bitcast.89), calls=%async_computation | async-start | bytes 524288 | tf_op jit(solution)/shard_map/all_to_all | solution.py:57
  37.4 4.8 %collective-permute-start.2 = (bf16[40,4,256]{2,1,0:T(4,128)(2,1)S(1)}, bf16[40,4,256]{2,1,0:T(4,128)(2,1)S(1)}, u32[]{:S(2)}, u32[]{:S(2)}) collective-permute-start(bf16[40,4,256]{2,1,0:T(4,128)(2,1)S(1)} %get-tuple-element.17), channel_id=1, source_target_pairs={{0,1},{1,2},{2,3},{3,4},{4,5},{5,6},{6,7},{7,8},{8,9},{9,10},{10,1... | collective-permute-start | bytes 245768 | tf_op jit(solution)/shard_map/ppermute | solution.py:23
  42.2 1.3 collective-permute-start.3
  43.5 0.6 slice_reduce_fusion
  44.2 7.2 %all-to-all-done = bf16[16,4,16,128]{3,2,1,0:T(8,128)(2,1)S(1)} async-done(((bf16[16,4,16,128]{3,2,1,0:T(8,128)(2,1)}), bf16[16,4,16,128]{3,2,1,0:T(8,128)(2,1)S(1)}, u32[]{:S(2)}, u32[]{:S(2)}) %all-to-all-start) | async-done | bytes 262176 | tf_op jit(solution)/shard_map/all_to_all | solution.py:57
  51.4 1.8 %gather_fusion = bf16[256,16,128]{2,1,0:T(8,128)(2,1)} fusion(bf16[64,16,128]{2,1,0:T(8,128)(2,1)S(1)} %bitcast.193, s32[1024]{0:T(1024)S(1)} %pad_clamp_fusion), kind=kCustom, calls=%fused_computation | custom fusion | bytes 2098176 | tf_op jit(solution)/shard_map/gather | solution.py:58
  53.2 3.9 %all-to-all-start.2 = ((bf16[32,8,16,128]{3,2,1,0:T(8,128)(2,1)}), bf16[32,8,16,128]{3,2,1,0:T(8,128)(2,1)S(1)}, u32[]{:S(2)}, u32[]{:S(2)}) async-start(bf16[32,8,16,128]{3,2,1,0:T(8,128)(2,1)} %bitcast.93), calls=%async_computation.2 | async-start | bytes 2097152 | tf_op jit(solution)/shard_map/all_to_all | solution.py:59
  57.2 0.6 copy-done.50
  58.1 42.7 %multiply_reduce_fusion.1 = (f32[32,32]{1,0:T(8,128)S(1)}, f32[32,32,256]{2,1,0:T(8,128)S(1)}) fusion(bf16[256,256]{0,1:T(8,128)(2,1)S(1)} %copy.87, f32[256,32]{0,1:T(8,128)S(1)} %copy.88, bf16[32,32,256]{2,1,0:T(8,128)(2,1)S(1)} %copy-done.1, bf16[40,4,256]{2,1,0:T(4,128)(2,1)} %copy-done.51, bf16[40,4,256]{2,1,0:T(4,128)(2,1)} %copy-done.50, ...), kind=kOutput, calls=%fused_computation.167 | convolution fusion | flops 390265856 | bytes 7492608 | tf_op jit(solution)/shard_map/dot_general | solution.py:92
  100.8 0.2 multiply_convert_fusion.1
  101.0 0.3 fusion.832
  101.3 0.1 copy.93
  101.5 0.1 copy.114
  101.7 0.1 copy.111
  102.0 0.1 copy.108
  102.2 0.1 copy.105
  102.4 0.1 copy.102
  102.6 0.1 copy.99
  102.8 0.1 copy.96
  103.0 0.3 convolution_select_fusion.9
  103.4 0.3 convolution_select_fusion.10
  103.7 0.3 convolution_select_fusion.11
  104.0 0.3 convolution_select_fusion.12
  104.3 0.3 convolution_select_fusion.13
  104.6 0.3 convolution_select_fusion.14
  104.9 0.3 convolution_select_fusion.8
  105.2 0.9 fusion.19
  106.1 3.4 %collective-permute-start.4 = (bf16[4,32,256]{2,1,0:T(8,128)(2,1)S(1)}, bf16[4,32,256]{2,1,0:T(8,128)(2,1)S(1)}, u32[]{:S(2)}, u32[]{:S(2)}) collective-permute-start(bf16[4,32,256]{2,1,0:T(8,128)(2,1)S(1)} %get-tuple-element.19), channel_id=1, source_target_pairs={{0,16},{16,32},{32,48},{48,64},{64,80},{80,96},{96,112},{112,128},... | collective-permute-start | bytes 196616 | tf_op jit(solution)/shard_map/ppermute | solution.py:23
  109.6 1.9 %collective-permute-start.5 = (bf16[4,32,256]{2,1,0:T(8,128)(2,1)S(1)}, bf16[4,32,256]{2,1,0:T(8,128)(2,1)S(1)}, u32[]{:S(2)}, u32[]{:S(2)}) collective-permute-start(bf16[4,32,256]{2,1,0:T(8,128)(2,1)S(1)} %get-tuple-element.20), channel_id=1, source_target_pairs={{16,0},{32,16},{48,32},{64,48},{80,64},{96,80},{112,96},{128,112},... | collective-permute-start | bytes 196616 | tf_op jit(solution)/shard_map/ppermute | solution.py:25
  111.5 3.6 %collective-permute-done.5 = bf16[4,32,256]{2,1,0:T(8,128)(2,1)S(1)} collective-permute-done((bf16[4,32,256]{2,1,0:T(8,128)(2,1)S(1)}, bf16[4,32,256]{2,1,0:T(8,128)(2,1)S(1)}, u32[]{:S(2)}, u32[]{:S(2)}) %collective-permute-start.5) | collective-permute-done | bytes 65568 | tf_op jit(solution)/shard_map/ppermute | solution.py:25
  115.2 4.6 %collective-permute-start.6 = (bf16[40,4,256]{2,1,0:T(4,128)(2,1)S(1)}, bf16[40,4,256]{2,1,0:T(4,128)(2,1)S(1)}, u32[]{:S(2)}, u32[]{:S(2)}) collective-permute-start(bf16[40,4,256]{2,1,0:T(4,128)(2,1)S(1)} %get-tuple-element.15), channel_id=1, source_target_pairs={{0,1},{1,2},{2,3},{3,4},{4,5},{5,6},{6,7},{7,8},{8,9},{9,10},{10,1... | collective-permute-start | bytes 245768 | tf_op jit(solution)/shard_map/ppermute | solution.py:23
  119.9 1.6 %collective-permute-start.7 = (bf16[40,4,256]{2,1,0:T(4,128)(2,1)S(1)}, bf16[40,4,256]{2,1,0:T(4,128)(2,1)S(1)}, u32[]{:S(2)}, u32[]{:S(2)}) collective-permute-start(bf16[40,4,256]{2,1,0:T(4,128)(2,1)S(1)} %get-tuple-element.16), channel_id=1, source_target_pairs={{1,0},{2,1},{3,2},{4,3},{5,4},{6,5},{7,6},{8,7},{9,8},{10,9},{11,1... | collective-permute-start | bytes 245768 | tf_op jit(solution)/shard_map/ppermute | solution.py:25
  121.5 5.2 %collective-permute-done.7 = bf16[40,4,256]{2,1,0:T(4,128)(2,1)S(1)} collective-permute-done((bf16[40,4,256]{2,1,0:T(4,128)(2,1)S(1)}, bf16[40,4,256]{2,1,0:T(4,128)(2,1)S(1)}, u32[]{:S(2)}, u32[]{:S(2)}) %collective-permute-start.7) | collective-permute-done | bytes 81952 | tf_op jit(solution)/shard_map/ppermute | solution.py:25
  126.7 1.4 maximum_maximum_fusion
  128.1 27.6 %multiply_reduce_fusion = (f32[32,32]{1,0:T(8,128)S(1)}, f32[32,32,256]{2,1,0:T(8,128)}) fusion(bf16[256,256]{0,1:T(8,128)(2,1)S(1)} %copy-done.5, f32[256,32]{0,1:T(8,128)S(1)} %copy.88, bf16[32,32,256]{2,1,0:T(8,128)(2,1)S(1)} %fusion.19, bf16[4,32,256]{2,1,0:T(8,128)(2,1)S(1)} %collective-permute-done.5, ...), kind=kOutput, calls=%fused_computation.164 | convolution fusion | flops 335739904 | bytes 40358912 | tf_op jit(solution)/shard_map/dot_general | solution.py:92
  155.8 1.4 multiply_convert_fusion
  157.2 0.3 convolution_select_fusion.1
  157.5 0.3 convolution_select_fusion.2
  157.8 0.3 convolution_select_fusion.3
  158.1 0.3 convolution_select_fusion.4
  158.4 0.3 convolution_select_fusion.5
  158.7 0.3 convolution_select_fusion.6
  159.1 0.3 convolution_select_fusion
  159.4 1.6 fusion.18
  (180 shorter events, 4.3 us)
Async XLA Ops:
  0.0 24.9 %copy-start = (bf16[4,256,256]{2,1,0:T(8,128)(2,1)S(1)}, bf16[4,256,256]{2,1,0:T(8,128)(2,1)}, u32[]{:S(2)}) copy-start(bf16[4,256,256]{2,1,0:T(8,128)(2,1)} %param.13) | copy-start | bytes 1572868
  0.0 21.2 %copy-start.49 = (s32[1,1,16]{2,1,0:T(1,128)S(1)}, s32[1,1,16]{2,1,0:T(1,128)}, u32[]{:S(2)}) copy-start(s32[1,1,16]{2,1,0:T(1,128)} %param.11) | copy-start | bytes 196
  0.0 21.2 %copy-start.9 = (s32[4,4]{1,0:T(4,128)S(1)}, s32[4,4]{1,0:T(4,128)}, u32[]{:S(2)}) copy-start(s32[4,4]{1,0:T(4,128)} %param.10) | copy-start | bytes 196
  0.0 24.8 %copy-start.7 = (s32[32,32]{1,0:T(8,128)S(1)}, s32[32,32]{1,0:T(8,128)}, u32[]{:S(2)}) copy-start(s32[32,32]{1,0:T(8,128)} %param.15) | copy-start | bytes 12292
  0.0 25.0 %copy-start.3 = (bf16[256,256]{1,0:T(8,128)(2,1)S(1)}, bf16[256,256]{1,0:T(8,128)(2,1)}, u32[]{:S(2)}) copy-start(bf16[256,256]{1,0:T(8,128)(2,1)} %param.14) | copy-start | bytes 393220
  1.5 24.8 %all-to-all-start.1 = ((s32[32,8,128]{2,1,0:T(8,128)}), s32[32,8,128]{2,1,0:T(8,128)S(1)}, u32[]{:S(2)}, u32[]{:S(2)}) async-start(s32[32,8,128]{2,1,0:T(8,128)} %broadcast_in_dim.192), calls=%async_computation.1 | async-start | bytes 262144 | tf_op jit(solution)/shard_map/all_to_all | solution.py:50
  11.9 13.3 %copy-start.1 = (bf16[32,32,256]{2,1,0:T(8,128)(2,1)S(1)}, bf16[32,32,256]{2,1,0:T(8,128)(2,1)}, u32[]{:S(2)}) copy-start(bf16[32,32,256]{2,1,0:T(8,128)(2,1)} %param.9) | copy-start | bytes 1572868
  12.8 12.5 %collective-permute-start.1 = (bf16[4,32,256]{2,1,0:T(8,128)(2,1)S(1)}, bf16[4,32,256]{2,1,0:T(8,128)(2,1)S(1)}, u32[]{:S(2)}, u32[]{:S(2)}) collective-permute-start(bf16[4,32,256]{2,1,0:T(8,128)(2,1)S(1)} %get-tuple-element.24), channel_id=1, source_target_pairs={{16,0},{32,16},{48,32},{64,48},{80,64},{96,80},{112,96},{128,112},... | collective-permute-start | bytes 196616 | tf_op jit(solution)/shard_map/ppermute | solution.py:25
  15.1 10.1 %collective-permute-start = (bf16[4,32,256]{2,1,0:T(8,128)(2,1)S(1)}, bf16[4,32,256]{2,1,0:T(8,128)(2,1)S(1)}, u32[]{:S(2)}, u32[]{:S(2)}) collective-permute-start(bf16[4,32,256]{2,1,0:T(8,128)(2,1)S(1)} %get-tuple-element.25), channel_id=1, source_target_pairs={{0,16},{16,32},{32,48},{48,64},{64,80},{80,96},{96,112},{112,128},... | collective-permute-start | bytes 196616 | tf_op jit(solution)/shard_map/ppermute | solution.py:23
  19.5 38.3 %copy-start.10 = (f32[256,1,1]{0,2,1:T(1,128)}, f32[256,1,1]{0,2,1:T(1,128)S(1)}, u32[]{:S(2)}) copy-start(f32[256,1,1]{0,2,1:T(1,128)S(1)} %get-tuple-element.89) | copy-start | bytes 3076
  19.5 38.3 %copy-start.12 = (f32[256,1,1]{0,2,1:T(1,128)}, f32[256,1,1]{0,2,1:T(1,128)S(1)}, u32[]{:S(2)}) copy-start(f32[256,1,1]{0,2,1:T(1,128)S(1)} %get-tuple-element.90) | copy-start | bytes 3076
  19.5 38.3 %copy-start.14 = (f32[256,1,1]{0,2,1:T(1,128)}, f32[256,1,1]{0,2,1:T(1,128)S(1)}, u32[]{:S(2)}) copy-start(f32[256,1,1]{0,2,1:T(1,128)S(1)} %get-tuple-element.91) | copy-start | bytes 3076
  19.5 38.3 %copy-start.16 = (f32[256,1,1]{0,2,1:T(1,128)}, f32[256,1,1]{0,2,1:T(1,128)S(1)}, u32[]{:S(2)}) copy-start(f32[256,1,1]{0,2,1:T(1,128)S(1)} %get-tuple-element.92) | copy-start | bytes 3076
  19.5 38.3 %copy-start.18 = (f32[256,1,1]{0,2,1:T(1,128)}, f32[256,1,1]{0,2,1:T(1,128)S(1)}, u32[]{:S(2)}) copy-start(f32[256,1,1]{0,2,1:T(1,128)S(1)} %get-tuple-element.93) | copy-start | bytes 3076
  19.5 38.3 %copy-start.19 = (f32[256,1,1]{0,2,1:T(1,128)}, f32[256,1,1]{0,2,1:T(1,128)S(1)}, u32[]{:S(2)}) copy-start(f32[256,1,1]{0,2,1:T(1,128)S(1)} %get-tuple-element.94) | copy-start | bytes 3076
  19.5 38.3 %copy-start.20 = (f32[256,1,1]{0,2,1:T(1,128)}, f32[256,1,1]{0,2,1:T(1,128)S(1)}, u32[]{:S(2)}) copy-start(f32[256,1,1]{0,2,1:T(1,128)S(1)} %get-tuple-element.95) | copy-start | bytes 3076
  19.5 38.3 %copy-start.21 = (f32[256,1,1]{0,2,1:T(1,128)}, f32[256,1,1]{0,2,1:T(1,128)S(1)}, u32[]{:S(2)}) copy-start(f32[256,1,1]{0,2,1:T(1,128)S(1)} %get-tuple-element.96) | copy-start | bytes 3076
  19.6 38.3 %copy-start.22 = (f32[256,1,1]{0,2,1:T(1,128)}, f32[256,1,1]{0,2,1:T(1,128)S(1)}, u32[]{:S(2)}) copy-start(f32[256,1,1]{0,2,1:T(1,128)S(1)} %get-tuple-element.97) | copy-start | bytes 3076
  19.6 38.3 %copy-start.23 = (f32[256,1,1]{0,2,1:T(1,128)}, f32[256,1,1]{0,2,1:T(1,128)S(1)}, u32[]{:S(2)}) copy-start(f32[256,1,1]{0,2,1:T(1,128)S(1)} %get-tuple-element.98) | copy-start | bytes 3076
  19.6 38.3 %copy-start.24 = (f32[256,1,1]{0,2,1:T(1,128)}, f32[256,1,1]{0,2,1:T(1,128)S(1)}, u32[]{:S(2)}) copy-start(f32[256,1,1]{0,2,1:T(1,128)S(1)} %get-tuple-element.99) | copy-start | bytes 3076
  19.6 38.3 %copy-start.25 = (f32[256,1,1]{0,2,1:T(1,128)}, f32[256,1,1]{0,2,1:T(1,128)S(1)}, u32[]{:S(2)}) copy-start(f32[256,1,1]{0,2,1:T(1,128)S(1)} %get-tuple-element.100) | copy-start | bytes 3076
  19.6 38.3 %copy-start.26 = (f32[256,1,1]{0,2,1:T(1,128)}, f32[256,1,1]{0,2,1:T(1,128)S(1)}, u32[]{:S(2)}) copy-start(f32[256,1,1]{0,2,1:T(1,128)S(1)} %get-tuple-element.101) | copy-start | bytes 3076
  19.6 38.3 %copy-start.27 = (f32[256,1,1]{0,2,1:T(1,128)}, f32[256,1,1]{0,2,1:T(1,128)S(1)}, u32[]{:S(2)}) copy-start(f32[256,1,1]{0,2,1:T(1,128)S(1)} %get-tuple-element.64) | copy-start | bytes 3076
  19.6 38.3 %copy-start.28 = (f32[256,1,1]{0,2,1:T(1,128)}, f32[256,1,1]{0,2,1:T(1,128)S(1)}, u32[]{:S(2)}) copy-start(f32[256,1,1]{0,2,1:T(1,128)S(1)} %get-tuple-element.65) | copy-start | bytes 3076
  19.7 38.3 %copy-start.29 = (f32[256,1,1]{0,2,1:T(1,128)}, f32[256,1,1]{0,2,1:T(1,128)S(1)}, u32[]{:S(2)}) copy-start(f32[256,1,1]{0,2,1:T(1,128)S(1)} %get-tuple-element.66) | copy-start | bytes 3076
  19.7 38.3 %copy-start.30 = (f32[256,1,1]{0,2,1:T(1,128)}, f32[256,1,1]{0,2,1:T(1,128)S(1)}, u32[]{:S(2)}) copy-start(f32[256,1,1]{0,2,1:T(1,128)S(1)} %get-tuple-element.67) | copy-start | bytes 3076
  19.7 38.3 %copy-start.31 = (f32[256,1,1]{0,2,1:T(1,128)}, f32[256,1,1]{0,2,1:T(1,128)S(1)}, u32[]{:S(2)}) copy-start(f32[256,1,1]{0,2,1:T(1,128)S(1)} %get-tuple-element.68) | copy-start | bytes 3076
  19.7 38.3 %copy-start.32 = (f32[256,1,1]{0,2,1:T(1,128)}, f32[256,1,1]{0,2,1:T(1,128)S(1)}, u32[]{:S(2)}) copy-start(f32[256,1,1]{0,2,1:T(1,128)S(1)} %get-tuple-element.69) | copy-start | bytes 3076
  19.7 38.3 %copy-start.33 = (f32[256,1,1]{0,2,1:T(1,128)}, f32[256,1,1]{0,2,1:T(1,128)S(1)}, u32[]{:S(2)}) copy-start(f32[256,1,1]{0,2,1:T(1,128)S(1)} %get-tuple-element.70) | copy-start | bytes 3076
  19.7 38.3 %copy-start.34 = (f32[256,1,1]{0,2,1:T(1,128)}, f32[256,1,1]{0,2,1:T(1,128)S(1)}, u32[]{:S(2)}) copy-start(f32[256,1,1]{0,2,1:T(1,128)S(1)} %get-tuple-element.71) | copy-start | bytes 3076
  19.7 38.3 %copy-start.35 = (f32[256,1,1]{0,2,1:T(1,128)}, f32[256,1,1]{0,2,1:T(1,128)S(1)}, u32[]{:S(2)}) copy-start(f32[256,1,1]{0,2,1:T(1,128)S(1)} %get-tuple-element.72) | copy-start | bytes 3076
  19.7 38.3 %copy-start.36 = (f32[256,1,1]{0,2,1:T(1,128)}, f32[256,1,1]{0,2,1:T(1,128)S(1)}, u32[]{:S(2)}) copy-start(f32[256,1,1]{0,2,1:T(1,128)S(1)} %get-tuple-element.73) | copy-start | bytes 3076
  19.7 38.3 %copy-start.37 = (f32[256,1,1]{0,2,1:T(1,128)}, f32[256,1,1]{0,2,1:T(1,128)S(1)}, u32[]{:S(2)}) copy-start(f32[256,1,1]{0,2,1:T(1,128)S(1)} %get-tuple-element.74) | copy-start | bytes 3076
  19.7 38.3 %copy-start.38 = (f32[256,1,1]{0,2,1:T(1,128)}, f32[256,1,1]{0,2,1:T(1,128)S(1)}, u32[]{:S(2)}) copy-start(f32[256,1,1]{0,2,1:T(1,128)S(1)} %get-tuple-element.75) | copy-start | bytes 3076
  19.8 38.3 %copy-start.39 = (f32[256,1,1]{0,2,1:T(1,128)}, f32[256,1,1]{0,2,1:T(1,128)S(1)}, u32[]{:S(2)}) copy-start(f32[256,1,1]{0,2,1:T(1,128)S(1)} %get-tuple-element.76) | copy-start | bytes 3076
  19.8 38.3 %copy-start.40 = (f32[256,1,1]{0,2,1:T(1,128)}, f32[256,1,1]{0,2,1:T(1,128)S(1)}, u32[]{:S(2)}) copy-start(f32[256,1,1]{0,2,1:T(1,128)S(1)} %get-tuple-element.77) | copy-start | bytes 3076
  19.8 38.3 %copy-start.41 = (f32[256,1,1]{0,2,1:T(1,128)}, f32[256,1,1]{0,2,1:T(1,128)S(1)}, u32[]{:S(2)}) copy-start(f32[256,1,1]{0,2,1:T(1,128)S(1)} %get-tuple-element.78) | copy-start | bytes 3076
  19.8 38.3 %copy-start.42 = (f32[256,1,1]{0,2,1:T(1,128)}, f32[256,1,1]{0,2,1:T(1,128)S(1)}, u32[]{:S(2)}) copy-start(f32[256,1,1]{0,2,1:T(1,128)S(1)} %get-tuple-element.79) | copy-start | bytes 3076
  19.8 38.3 %copy-start.43 = (f32[256,1,1]{0,2,1:T(1,128)}, f32[256,1,1]{0,2,1:T(1,128)S(1)}, u32[]{:S(2)}) copy-start(f32[256,1,1]{0,2,1:T(1,128)S(1)} %get-tuple-element.80) | copy-start | bytes 3076
  19.8 38.3 %copy-start.44 = (f32[256,1,1]{0,2,1:T(1,128)}, f32[256,1,1]{0,2,1:T(1,128)S(1)}, u32[]{:S(2)}) copy-start(f32[256,1,1]{0,2,1:T(1,128)S(1)} %get-tuple-element.81) | copy-start | bytes 3076
  19.8 38.3 %copy-start.45 = (f32[256,1,1]{0,2,1:T(1,128)}, f32[256,1,1]{0,2,1:T(1,128)S(1)}, u32[]{:S(2)}) copy-start(f32[256,1,1]{0,2,1:T(1,128)S(1)} %get-tuple-element.82) | copy-start | bytes 3076
  20.5 37.6 %copy-start.46 = (f32[256,1,1]{0,2,1:T(1,128)}, f32[256,1,1]{0,2,1:T(1,128)S(1)}, u32[]{:S(2)}) copy-start(f32[256,1,1]{0,2,1:T(1,128)S(1)} %get-tuple-element.45) | copy-start | bytes 3076
  20.5 37.6 %copy-start.47 = (f32[256,1,1]{0,2,1:T(1,128)}, f32[256,1,1]{0,2,1:T(1,128)S(1)}, u32[]{:S(2)}) copy-start(f32[256,1,1]{0,2,1:T(1,128)S(1)} %get-tuple-element.46) | copy-start | bytes 3076
  20.5 37.6 %copy-start.48 = (f32[256,1,1]{0,2,1:T(1,128)}, f32[256,1,1]{0,2,1:T(1,128)S(1)}, u32[]{:S(2)}) copy-start(f32[256,1,1]{0,2,1:T(1,128)S(1)} %get-tuple-element.47) | copy-start | bytes 3076
  25.1 33.0 %copy-start.4 = (bf16[256,256]{0,1:T(8,128)(2,1)}, bf16[256,256]{0,1:T(8,128)(2,1)S(1)}, u32[]{:S(2)}) copy-start(bf16[256,256]{0,1:T(8,128)(2,1)S(1)} %copy.87) | copy-start | bytes 393220
  25.4 0.8 copy-start.8
  26.2 27.0 %copy-start.2 = (bf16[36,32,256]{2,1,0:T(8,128)(2,1)}, bf16[36,32,256]{2,1,0:T(8,128)(2,1)S(1)}, u32[]{:S(2)}) copy-start(bf16[36,32,256]{2,1,0:T(8,128)(2,1)S(1)} %get-tuple-element.109) | copy-start | bytes 1769476
  26.2 30.9 %copy-start.6 = (bf16[40,32,256]{2,1,0:T(8,128)(2,1)}, bf16[40,32,256]{2,1,0:T(8,128)(2,1)S(1)}, u32[]{:S(2)}) copy-start(bf16[40,32,256]{2,1,0:T(8,128)(2,1)S(1)} %get-tuple-element.110) | copy-start | bytes 1966084
  27.1 24.3 %all-to-all-start = ((bf16[16,4,16,128]{3,2,1,0:T(8,128)(2,1)}), bf16[16,4,16,128]{3,2,1,0:T(8,128)(2,1)S(1)}, u32[]{:S(2)}, u32[]{:S(2)}) async-start(bf16[16,4,16,128]{3,2,1,0:T(8,128)(2,1)} %bitcast.89), calls=%async_computation | async-start | bytes 524288 | tf_op jit(solution)/shard_map/all_to_all | solution.py:57
  37.4 19.7 %collective-permute-start.2 = (bf16[40,4,256]{2,1,0:T(4,128)(2,1)S(1)}, bf16[40,4,256]{2,1,0:T(4,128)(2,1)S(1)}, u32[]{:S(2)}, u32[]{:S(2)}) collective-permute-start(bf16[40,4,256]{2,1,0:T(4,128)(2,1)S(1)} %get-tuple-element.17), channel_id=1, source_target_pairs={{0,1},{1,2},{2,3},{3,4},{4,5},{5,6},{6,7},{7,8},{8,9},{9,10},{10,1... | collective-permute-start | bytes 245768 | tf_op jit(solution)/shard_map/ppermute | solution.py:23
  42.2 15.0 %collective-permute-start.3 = (bf16[40,4,256]{2,1,0:T(4,128)(2,1)S(1)}, bf16[40,4,256]{2,1,0:T(4,128)(2,1)S(1)}, u32[]{:S(2)}, u32[]{:S(2)}) collective-permute-start(bf16[40,4,256]{2,1,0:T(4,128)(2,1)S(1)} %get-tuple-element.18), channel_id=1, source_target_pairs={{1,0},{2,1},{3,2},{4,3},{5,4},{6,5},{7,6},{8,7},{9,8},{10,9},{11,1... | collective-permute-start | bytes 245768 | tf_op jit(solution)/shard_map/ppermute | solution.py:25
  53.2 47.8 %all-to-all-start.2 = ((bf16[32,8,16,128]{3,2,1,0:T(8,128)(2,1)}), bf16[32,8,16,128]{3,2,1,0:T(8,128)(2,1)S(1)}, u32[]{:S(2)}, u32[]{:S(2)}) async-start(bf16[32,8,16,128]{3,2,1,0:T(8,128)(2,1)} %bitcast.93), calls=%async_computation.2 | async-start | bytes 2097152 | tf_op jit(solution)/shard_map/all_to_all | solution.py:59
  57.1 0.6 copy-start.50
  57.1 0.6 copy-start.51
  106.1 5.3 %collective-permute-start.4 = (bf16[4,32,256]{2,1,0:T(8,128)(2,1)S(1)}, bf16[4,32,256]{2,1,0:T(8,128)(2,1)S(1)}, u32[]{:S(2)}, u32[]{:S(2)}) collective-permute-start(bf16[4,32,256]{2,1,0:T(8,128)(2,1)S(1)} %get-tuple-element.19), channel_id=1, source_target_pairs={{0,16},{16,32},{32,48},{48,64},{64,80},{80,96},{96,112},{112,128},... | collective-permute-start | bytes 196616 | tf_op jit(solution)/shard_map/ppermute | solution.py:23
  109.6 5.6 %collective-permute-start.5 = (bf16[4,32,256]{2,1,0:T(8,128)(2,1)S(1)}, bf16[4,32,256]{2,1,0:T(8,128)(2,1)S(1)}, u32[]{:S(2)}, u32[]{:S(2)}) collective-permute-start(bf16[4,32,256]{2,1,0:T(8,128)(2,1)S(1)} %get-tuple-element.20), channel_id=1, source_target_pairs={{16,0},{32,16},{48,32},{64,48},{80,64},{96,80},{112,96},{128,112},... | collective-permute-start | bytes 196616 | tf_op jit(solution)/shard_map/ppermute | solution.py:25
  115.2 6.3 %collective-permute-start.6 = (bf16[40,4,256]{2,1,0:T(4,128)(2,1)S(1)}, bf16[40,4,256]{2,1,0:T(4,128)(2,1)S(1)}, u32[]{:S(2)}, u32[]{:S(2)}) collective-permute-start(bf16[40,4,256]{2,1,0:T(4,128)(2,1)S(1)} %get-tuple-element.15), channel_id=1, source_target_pairs={{0,1},{1,2},{2,3},{3,4},{4,5},{5,6},{6,7},{7,8},{8,9},{9,10},{10,1... | collective-permute-start | bytes 245768 | tf_op jit(solution)/shard_map/ppermute | solution.py:23
  119.8 8.3 %copy-start.5 = (bf16[256,256]{0,1:T(8,128)(2,1)S(1)}, bf16[256,256]{0,1:T(8,128)(2,1)}, u32[]{:S(2)}) copy-start(bf16[256,256]{0,1:T(8,128)(2,1)} %copy-done.4) | copy-start | bytes 393220
  119.8 8.3 %copy-start.11 = (f32[256,1,1]{0,2,1:T(1,128)S(1)}, f32[256,1,1]{0,2,1:T(1,128)}, u32[]{:S(2)}) copy-start(f32[256,1,1]{0,2,1:T(1,128)} %copy-done.10) | copy-start | bytes 3076
  119.8 8.3 %copy-start.13 = (f32[256,1,1]{0,2,1:T(1,128)S(1)}, f32[256,1,1]{0,2,1:T(1,128)}, u32[]{:S(2)}) copy-start(f32[256,1,1]{0,2,1:T(1,128)} %copy-done.12) | copy-start | bytes 3076
  119.8 8.3 %copy-start.15 = (f32[256,1,1]{0,2,1:T(1,128)S(1)}, f32[256,1,1]{0,2,1:T(1,128)}, u32[]{:S(2)}) copy-start(f32[256,1,1]{0,2,1:T(1,128)} %copy-done.14) | copy-start | bytes 3076
  119.9 8.3 %copy-start.17 = (f32[256,1,1]{0,2,1:T(1,128)S(1)}, f32[256,1,1]{0,2,1:T(1,128)}, u32[]{:S(2)}) copy-start(f32[256,1,1]{0,2,1:T(1,128)} %copy-done.16) | copy-start | bytes 3076
  119.9 6.8 %collective-permute-start.7 = (bf16[40,4,256]{2,1,0:T(4,128)(2,1)S(1)}, bf16[40,4,256]{2,1,0:T(4,128)(2,1)S(1)}, u32[]{:S(2)}, u32[]{:S(2)}) collective-permute-start(bf16[40,4,256]{2,1,0:T(4,128)(2,1)S(1)} %get-tuple-element.16), channel_id=1, source_target_pairs={{1,0},{2,1},{3,2},{4,3},{5,4},{6,5},{7,6},{8,7},{9,8},{10,9},{11,1... | collective-permute-start | bytes 245768 | tf_op jit(solution)/shard_map/ppermute | solution.py:25
where the time goes:
time: 164 us; the launch traced here: 161 us
  matrix products  77 us (47%)
  starting transfers between devices  47.7 us (29%)
  waiting for transfers between devices  16 us (10%)
  local copies, waits for them, and re-layouts  14.5 us (9%)
  other arithmetic  4.36 us (3%)
    dot_general x2, matrix products, local(): shifted = jnp.dot(middle, moves, preferred_element_type=jnp.float32)  70.3 us
    ppermute x4, starting transfers between devices, padded_2(): lax.ppermute(tail, axis, [(i, (i + 1) % count) for i in range(ends)])  16.1 us
    all_to_all x1, starting transfers between devices, fetch_operators(): lax.all_to_all(jnp.broadcast_to(listed[None, :, None], (32, count, 128)),...  10.4 us
    all_to_all x1, starting transfers between devices, fetch_operators(): lax.all_to_all(spread, COL, 0, 0, tiled=True).reshape(16 * held, 16, 128)  10.2 us
    ppermute x4, waiting for transfers between devices, padded_2(): lax.ppermute(head, axis, [((i + 1) % count, i) for i in range(ends)])  8.81 us
    all_to_all x1, waiting for transfers between devices, fetch_operators(): lax.all_to_all(spread, COL, 0, 0, tiled=True).reshape(16 * held, 16, 128)  7.19 us
    ppermute x4, starting transfers between devices, padded_2(): lax.ppermute(head, axis, [((i + 1) % count, i) for i in range(ends)])  7.09 us
    dot_general x16, matrix products, local(): jnp.dot(grown_rows, operators[slot], preferred_element_type=jnp.float32)  6.78 us
  transfers between devices with their start and end apart: 11, of which 3 were waited for; matrix products, arithmetic and copies ran while one was open for 33% of the time, Pallas kernels for 0%

commit v1 on v0

v1 whole, which is shorter than its diff:
```python
import functools
import math

import jax
import jax.numpy as jnp
from jax import lax
from jax.experimental import pallas as pl
from jax.experimental.pallas import tpu as pltpu
from jax.sharding import PartitionSpec as P

TB = 8
RMAX = 4
BX = 8
BY = 8
STEPS = 2

SPLIT = (("xl", 2), ("yh", 4), ("yl", 2), ("co", 2), ("zh", 4), ("zl", 2), ("xh", 2))
ROW = ("xl", "yh", "yl", "co")
COL = ("zh", "zl", "xh")
NEAR = ("xl", "yl", "co", "zl", "xh")

DIST_SQ = (0, 1, 2, 4, 5, 8, 9, 10, 13, 16)
OFFSETS = (1, 4, 4, 4, 8, 4, 4, 8, 8, 4)

LEAD = 8


def shift_pairs(count):
    return [(i, i + 1) for i in range(count - 1)], [(i + 1, i) for i in range(count - 1)]


def halos(cells):
    count = math.prod(lax.axis_size(name) for name in ROW)
    down, up = shift_pairs(count)
    top = lax.ppermute(cells[-RMAX:], ROW, down)
    bottom = lax.ppermute(cells[:RMAX], ROW, up)
    count = math.prod(lax.axis_size(name) for name in COL)
    right, left = shift_pairs(count)
    tail = jnp.concatenate([top[:, -RMAX:], cells[:, -RMAX:], bottom[:, -RMAX:]], axis=0)
    head = jnp.concatenate([top[:, :RMAX], cells[:, :RMAX], bottom[:, :RMAX]], axis=0)
    return top, bottom, lax.ppermute(tail, COL, right), lax.ppermute(head, COL, left)


def class_weights(radius):
    dist = jnp.array(DIST_SQ, jnp.float32)[:, None]
    reach = (radius.astype(jnp.float32) ** 2)[None, :]
    values = jnp.exp(-dist / (2.0 * reach)) * (dist <= reach).astype(jnp.float32)
    total = jnp.sum(values * jnp.array(OFFSETS, jnp.float32)[:, None], axis=0, keepdims=True)
    return values / total


def fetch_operators(tile_list, harvest_ops):
    listed = tile_list[0, 0]
    count = listed.shape[0]
    held = harvest_ops.shape[0]
    lists = lax.all_to_all(
        jnp.broadcast_to(listed[None, :, None], (32, count, 128)), NEAR, 0, 0, tiled=True
    )[:, :, 0]
    mine = (lax.axis_index("xl") * 2 + lax.axis_index("yl")) * 2 + lax.axis_index("co")
    strip = lax.dynamic_slice_in_dim(harvest_ops, mine * 32, 32, axis=1)
    strip = strip.reshape(held, 2, 16, 2, 128).transpose(1, 3, 0, 2, 4)
    spread = jnp.broadcast_to(strip[None], (4, 2, 2, held, 16, 128)).reshape(16, held, 16, 128)
    pieces = lax.all_to_all(spread, COL, 0, 0, tiled=True).reshape(16 * held, 16, 128)
    wanted = pieces[lists.reshape(-1)].reshape(32, count, 16, 128)
    return lax.all_to_all(wanted, NEAR, 0, 0, tiled=True)


def grow(cells, top, bottom, left, right, weights, fecundity, moves, grown, padded, pairs, seeds):
    rows, cols, cohorts = cells.shape
    high = rows + 2 * RMAX
    f32 = jnp.float32

    for part, start in ((top, 0), (bottom, RMAX + rows)):
        for i in range(RMAX):
            padded[start + i, pl.ds(LEAD, cols), :] = part[i].astype(f32)

    def fill(x, carry):
        padded[RMAX + x, pl.ds(LEAD, cols), :] = cells[x].astype(f32)
        return carry

    lax.fori_loop(0, rows, fill, 0, unroll=4)

    def add_pairs(x, carry):
        padded[x, pl.ds(LEAD - RMAX, RMAX), :] = left[x].astype(f32)
        padded[x, pl.ds(LEAD + cols, RMAX), :] = right[x].astype(f32)
        for b in range(1, RMAX + 1):
            pairs[b - 1, x] = (
                padded[x, pl.ds(LEAD - b, cols), :] + padded[x, pl.ds(LEAD + b, cols), :]
            )
        return carry

    lax.fori_loop(0, high, add_pairs, 0, unroll=2)

    def row_sum(x, b):
        return padded[x, pl.ds(LEAD, cols), :] if b == 0 else pairs[b - 1, x]

    def both(x, a, b):
        return row_sum(x + a, b) + row_sum(x - a, b)

    def disperse(x):
        at = x + RMAX
        sums = (
            row_sum(at, 0),
            row_sum(at, 1) + both(at, 1, 0),
            both(at, 1, 1),
            row_sum(at, 2) + both(at, 2, 0),
            both(at, 2, 1) + both(at, 1, 2),
            both(at, 2, 2),
            row_sum(at, 3) + both(at, 3, 0),
            both(at, 1, 3) + both(at, 3, 1),
            both(at, 2, 3) + both(at, 3, 2),
            row_sum(at, 4) + both(at, 4, 0),
        )
        total = sums[0] * weights[0:1, :]
        for k in range(1, len(sums)):
            total = total + sums[k] * weights[k : k + 1, :]
        seeds[x] = total.astype(jnp.bfloat16)

    def chunk(i, carry):
        def one(j, inner):
            disperse(i * BX + j)
            return inner

        lax.fori_loop(0, BX, one, 0, unroll=2)
        span = pl.ds(pl.multiple_of(i * BX, BX), BX)
        arrived = jnp.dot(
            seeds[span].reshape(BX * cols, cohorts), fecundity[...], preferred_element_type=f32
        )
        here = cells[span].reshape(BX * cols, cohorts).astype(f32)
        middle = (here + arrived).astype(jnp.bfloat16)
        shifted = jnp.dot(middle, moves[...], preferred_element_type=f32)
        norm = lax.rsqrt(1.0 + jnp.mean(shifted * shifted, axis=-1, keepdims=True))
        grown[span] = (shifted * norm).astype(jnp.bfloat16).reshape(BX, cols, cohorts)
        return carry

    lax.fori_loop(0, rows // BX, chunk, 0)


def harvest(slots, grown, ops, out):
    rows, cols, cohorts = grown.shape
    count = ops.shape[0]
    wide = 2 * BY
    for i in range(rows // BX):
        for j in range(cols // wide):
            block = grown[i * BX : (i + 1) * BX, j * wide : (j + 1) * wide, :]
            flat = block.reshape(BX * wide, cohorts)
            halves = []
            for h in range(2):
                slot = slots[i, 2 * j + h]
                product = jnp.dot(
                    flat, ops[jnp.minimum(slot, count - 1)], preferred_element_type=jnp.float32
                )
                product = jnp.where(slot == count, flat.astype(jnp.float32), product)
                halves.append(product.reshape(BX, wide, cohorts)[:, h * BY : (h + 1) * BY])
            out[i * BX : (i + 1) * BX, j * wide : (j + 1) * wide, :] = jnp.concatenate(
                halves, axis=1
            ).astype(jnp.bfloat16)


def assemble(parts, ops):
    count = ops.shape[0]

    def one(k, carry):
        for piece in range(parts.shape[0]):
            r, h = divmod(piece, 2)
            ops[k, r * 16 : (r + 1) * 16, h * 128 : (h + 1) * 128] = parts[piece, k]
        return carry

    lax.fori_loop(0, count, one, 0)


def first_kernel(cells, top, bottom, left, right, weights, fecundity, moves, grown, padded, pairs, seeds):
    grow(cells, top, bottom, left, right, weights, fecundity, moves, grown, padded, pairs, seeds)


def harvest_kernel(slots, grown, parts, out, ops):
    assemble(parts, ops)
    harvest(slots, grown, ops, out)


def last_kernel(
    slots, cells, top, bottom, left, right, weights, fecundity, moves, ops,
    out, grown, padded, pairs, seeds,
):
    grow(cells, top, bottom, left, right, weights, fecundity, moves, grown, padded, pairs, seeds)
    harvest(slots, grown, ops, out)


VMEM = pl.BlockSpec(memory_space=pltpu.VMEM)
SMEM = pl.BlockSpec(memory_space=pltpu.SMEM)
PARAMS = pltpu.CompilerParams(vmem_limit_bytes=32 * 1024 * 1024)


def scratch(rows, cols, cohorts):
    high = rows + 2 * RMAX
    return [
        pltpu.VMEM((high, cols + 2 * LEAD, cohorts), jnp.float32),
        pltpu.VMEM((RMAX, high, cols, cohorts), jnp.float32),
        pltpu.VMEM((rows, cols, cohorts), jnp.bfloat16),
    ]


def local(
    biomass, block_stand, stand_slot, tile_list, harvest_ops, transition, pattern, fecundity, radius
):
    shape = biomass.shape
    rows, cols, cohorts = shape
    count = tile_list.shape[-1]
    stands = stand_slot.shape[-1]
    state = jax.ShapeDtypeStruct(shape, jnp.bfloat16)
    operators = jax.ShapeDtypeStruct((count, cohorts, cohorts), jnp.bfloat16)

    weights = class_weights(radius)
    block_mask = jnp.repeat(jnp.repeat(pattern, TB, 0), TB, 1).astype(jnp.float32)
    moves = (transition.astype(jnp.float32) * block_mask).astype(jnp.bfloat16)
    stand_hit = block_stand[:, :, None] == jnp.arange(stands)[None, None, :]
    slots = jnp.sum(jnp.where(stand_hit, stand_slot[0, 0][None, None, :], 0), axis=-1)

    parts = fetch_operators(tile_list, harvest_ops)
    grown = pl.pallas_call(
        first_kernel,
        out_shape=state,
        in_specs=[VMEM] * 8,
        out_specs=VMEM,
        scratch_shapes=scratch(*shape),
        compiler_params=PARAMS,
        cost_estimate=pl.CostEstimate(flops=2**28, bytes_accessed=2**24, transcendentals=0),
    )(biomass, *halos(biomass), weights, fecundity, moves)
    cells, ops = pl.pallas_call(
        harvest_kernel,
        out_shape=(state, operators),
        in_specs=[SMEM, VMEM, VMEM],
        out_specs=(VMEM, VMEM),
        compiler_params=PARAMS,
        cost_estimate=pl.CostEstimate(flops=2**28, bytes_accessed=2**22, transcendentals=0),
    )(slots, grown, parts)
    return pl.pallas_call(
        last_kernel,
        out_shape=state,
        in_specs=[SMEM] + [VMEM] * 9,
        out_specs=VMEM,
        scratch_shapes=[pltpu.VMEM(shape, jnp.bfloat16)] + scratch(*shape),
        compiler_params=PARAMS,
        cost_estimate=pl.CostEstimate(flops=2**29, bytes_accessed=2**24, transcendentals=0),
    )(slots, cells, *halos(cells), weights, fecundity, moves, ops)


def solution(mesh):
    names = tuple(name for name, _ in SPLIT)
    sizes = tuple(size for _, size in SPLIT)
    fine = jax.sharding.Mesh(mesh.devices.reshape(sizes), names)
    placed = (
        P(ROW, COL, None),
        P(ROW, COL),
        P(ROW, COL, None),
        P(ROW, COL, None),
        P(COL, None, None),
        P(),
        P(),
        P(),
        P(),
    )
    return jax.shard_map(
        local, mesh=fine, in_specs=placed, out_specs=P(ROW, COL, None), check_vma=False
    )
```

time: 164 us -> 106 us (0.65)
  the two profiles are of different devices: /device:TPU:1 before, /device:TPU:6 now
where the time goes in v1:
time: 106 us; the launch traced here: 105 us
  starting transfers between devices  55.7 us (53%)
  waiting for transfers between devices  28 us (26%)
  Pallas kernels  12 us (11%)
  local copies, waits for them, and re-layouts  8.17 us (8%)
    all_to_all x1, starting transfers between devices, fetch_operators(): lax.all_to_all(spread, COL, 0, 0, tiled=True).reshape(16 * held, 16, 128)  12.4 us
    ppermute x2, starting transfers between devices, halos(): lax.ppermute(tail, COL, right)  10.5 us
    all_to_all x1, starting transfers between devices, fetch_operators(): lax.all_to_all(jnp.broadcast_to(listed[None, :, None], (32, count, 128)),...  9.47 us
    ppermute x2, starting transfers between devices, halos(): bottom = lax.ppermute(cells[:RMAX], ROW, up)  8.63 us
    all_to_all x1, waiting for transfers between devices, fetch_operators(): lax.all_to_all(spread, COL, 0, 0, tiled=True).reshape(16 * held, 16, 128)  8.57 us
    ppermute x2, waiting for transfers between devices, halos(): lax.ppermute(tail, COL, right)  6.94 us
    ppermute x2, waiting for transfers between devices, halos(): lax.ppermute(head, COL, left)  6.77 us
    pallas_call x1, Pallas kernels, local(): pl.pallas_call(last_kernel, out_shape=state, in_specs=[SMEM] + [VMEM] * 9...  6.29 us
  transfers between devices with their start and end apart: 11, of which 4 were waited for; matrix products, arithmetic and copies ran while one was open for 5% of the time, Pallas kernels for 4%

profile of v1, /device:TPU:6, one launch (start us, length us, event | category | flops | bytes accessed | tf_op | source)
XLA Modules:
  0.0 105.0 jit_solution(9194104936503872891)
XLA Ops:
  0.0 0.0 copy-start
  0.0 0.0 copy-start.7
  0.0 0.7 copy-done.7
  0.7 0.7 broadcast_in_dim.47
  1.4 9.5 %all-to-all-start.1 = ((s32[32,8,128]{2,1,0:T(8,128)}), s32[32,8,128]{2,1,0:T(8,128)S(1)}, u32[]{:S(2)}, u32[]{:S(2)}) async-start(s32[32,8,128]{2,1,0:T(8,128)} %broadcast_in_dim.47), calls=%async_computation.1 | async-start | bytes 262144 | tf_op jit(solution)/shard_map/all_to_all | solution.py:56
  10.9 0.9 fusion.5
  11.8 3.6 %collective-permute-start.1 = (bf16[4,32,256]{2,1,0:T(8,128)(2,1)S(1)}, bf16[4,32,256]{2,1,0:T(8,128)(2,1)S(1)}, u32[]{:S(2)}, u32[]{:S(2)}) collective-permute-start(bf16[4,32,256]{2,1,0:T(8,128)(2,1)S(1)} %get-tuple-element.15), channel_id=1, source_target_pairs={{16,0},{32,16},{48,32},{64,48},{80,64},{96,80},{112,96},{128,112},... | collective-permute-start | bytes 196616 | tf_op jit(solution)/shard_map/ppermute | solution.py:36
  15.4 0.0 copy-start.4
  15.4 1.9 %collective-permute-start = (bf16[4,32,256]{2,1,0:T(8,128)(2,1)S(1)}, bf16[4,32,256]{2,1,0:T(8,128)(2,1)S(1)}, u32[]{:S(2)}, u32[]{:S(2)}) collective-permute-start(bf16[4,32,256]{2,1,0:T(8,128)(2,1)S(1)} %get-tuple-element.16), channel_id=1, source_target_pairs={{0,16},{16,32},{32,48},{48,64},{64,80},{80,96},{96,112},{112,128},... | collective-permute-start | bytes 196616 | tf_op jit(solution)/shard_map/ppermute | solution.py:35
  17.4 0.0 copy-done.4
  17.4 0.0 copy-done
  17.5 0.0 all-to-all-done.1
  17.5 0.8 broadcast_in_dim.45
  18.2 12.4 %all-to-all-start = ((bf16[16,4,16,128]{3,2,1,0:T(8,128)(2,1)}), bf16[16,4,16,128]{3,2,1,0:T(8,128)(2,1)S(1)}, u32[]{:S(2)}, u32[]{:S(2)}) async-start(bf16[16,4,16,128]{3,2,1,0:T(8,128)(2,1)} %bitcast.4), calls=%async_computation | async-start | bytes 524288 | tf_op jit(solution)/shard_map/all_to_all | solution.py:63
  30.6 0.1 copy.21
  30.7 0.6 slice_reduce_fusion
  31.3 0.1 reshape_squeeze.3
  31.4 8.6 %all-to-all-done = bf16[16,4,16,128]{3,2,1,0:T(8,128)(2,1)S(1)} async-done(((bf16[16,4,16,128]{3,2,1,0:T(8,128)(2,1)}), bf16[16,4,16,128]{3,2,1,0:T(8,128)(2,1)S(1)}, u32[]{:S(2)}, u32[]{:S(2)}) %all-to-all-start) | async-done | bytes 262176 | tf_op jit(solution)/shard_map/all_to_all | solution.py:63
  40.0 1.8 %gather_fusion = bf16[256,16,128]{2,1,0:T(8,128)(2,1)} fusion(bf16[64,16,128]{2,1,0:T(8,128)(2,1)S(1)} %bitcast.11, s32[1024]{0:T(1024)S(1)} %pad_clamp_fusion), kind=kCustom, calls=%fused_computation | custom fusion | bytes 2098176 | tf_op jit(solution)/shard_map/gather | solution.py:64
  41.8 5.9 %all-to-all-start.2 = ((bf16[32,8,16,128]{3,2,1,0:T(8,128)(2,1)}), bf16[32,8,16,128]{3,2,1,0:T(8,128)(2,1)S(1)}, u32[]{:S(2)}, u32[]{:S(2)}) async-start(bf16[32,8,16,128]{3,2,1,0:T(8,128)(2,1)} %bitcast.8), calls=%async_computation.2 | async-start | bytes 2097152 | tf_op jit(solution)/shard_map/all_to_all | solution.py:65
  47.7 0.0 copy-start.1
  47.8 0.0 copy-start.6
  47.8 0.1 copy.22
  47.9 0.6 copy-done.6
  48.5 0.0 copy-start.9
  48.5 0.6 copy-done.9
  49.2 0.0 copy-done.10
  49.2 0.0 copy-done.11
  49.2 0.1 multiply_reduce_fusion
  49.3 0.0 copy-done.1
  49.3 0.0 copy-start.3
  49.3 0.1 fusion.4
  49.4 0.8 copy-done.3
  50.2 0.1 fusion.1.weights
  50.3 0.0 collective-permute-done.1.bottom
  50.4 0.0 collective-permute-done.top
  50.4 0.0 copy-start.2
  50.4 0.1 pad_maximum_fusion
  50.5 4.3 %collective-permute-start.2 = (bf16[40,4,256]{2,1,0:T(4,128)(2,1)S(1)}, bf16[40,4,256]{2,1,0:T(4,128)(2,1)S(1)}, u32[]{:S(2)}, u32[]{:S(2)}) collective-permute-start(bf16[40,4,256]{2,1,0:T(4,128)(2,1)S(1)} %pad_maximum_fusion), channel_id=1, source_target_pairs={{0,1},{1,2},{2,3},{3,4},{4,5},{5,6},{6,7},{7,8},{8,9},{9,10},{10,1... | collective-permute-start | bytes 245768 | tf_op jit(solution)/shard_map/ppermute | solution.py:41
  54.7 0.0 copy-start.5
  54.8 0.1 pad_maximum_fusion.1
  54.8 0.0 copy-start.8
  54.8 3.1 %collective-permute-start.3 = (bf16[40,4,256]{2,1,0:T(4,128)(2,1)S(1)}, bf16[40,4,256]{2,1,0:T(4,128)(2,1)S(1)}, u32[]{:S(2)}, u32[]{:S(2)}) collective-permute-start(bf16[40,4,256]{2,1,0:T(4,128)(2,1)S(1)} %pad_maximum_fusion.1), channel_id=1, source_target_pairs={{1,0},{2,1},{3,2},{4,3},{5,4},{6,5},{7,6},{8,7},{9,8},{10,9},{11,1... | collective-permute-start | bytes 245768 | tf_op jit(solution)/shard_map/ppermute | solution.py:41
  57.9 0.0 copy-done.5
  57.9 0.0 copy-done.8
  57.9 0.2 select_reduce_fusion.slots
  58.2 6.9 %collective-permute-done.2.left = bf16[40,4,256]{2,1,0:T(4,128)(2,1)S(1)} collective-permute-done((bf16[40,4,256]{2,1,0:T(4,128)(2,1)S(1)}, bf16[40,4,256]{2,1,0:T(4,128)(2,1)S(1)}, u32[]{:S(2)}, u32[]{:S(2)}) %collective-permute-start.2) | collective-permute-done | bytes 81952 | tf_op jit(solution)/shard_map/ppermute | solution.py:41
  65.1 0.0 collective-permute-done.3.right
  65.1 0.0 copy-done.2
  65.1 4.5 %shard_map.109.grown = bf16[32,32,256]{2,1,0:T(8,128)(2,1)S(1)} custom-call(bf16[32,32,256]{2,1,0:T(8,128)(2,1)S(1)} %copy-done.1, bf16[4,32,256]{2,1,0:T(8,128)(2,1)S(1)} %collective-permute-done.top, bf16[4,32,256]{2,1,0:T(8,128)(2,1)S(1)} %collective-permute-done.1.bottom, bf16[40,4,256]{2,1,0:T(4,128)(2,1)S(1)} %collective-permute-done.2.left, ...), custom_call_target="tpu_custom_call" | custom-call | flops 268435456 | bytes 16777216 | tf_op jit(solution)/shard_map/pallas_call | solution.py:220
  69.5 0.0 all-to-all-done.2.parts
  69.5 1.2 %shard_map.110 = (bf16[32,32,256]{2,1,0:T(8,128)(2,1)S(1)}, bf16[8,256,256]{2,1,0:T(8,128)(2,1)S(1)}) custom-call(s32[4,4]{1,0:T(4,128)S(1)} %select_reduce_fusion.slots, bf16[32,32,256]{2,1,0:T(8,128)(2,1)S(1)} %shard_map.109.grown, bf16[32,8,16,128]{3,2,1,0:T(8,128)(2,1)S(1)} %all-to-all-done.2.parts), custom_call_target="tpu_custom_call" | custom-call | flops 268435456 | bytes 4194304 | tf_op jit(solution)/shard_map/pallas_call | solution.py:229
  70.8 5.0 %collective-permute-start.5 = (bf16[4,32,256]{2,1,0:T(8,128)(2,1)S(1)}, bf16[4,32,256]{2,1,0:T(8,128)(2,1)S(1)}, u32[]{:S(2)}, u32[]{:S(2)}) collective-permute-start(bf16[4,32,256]{2,1,0:T(8,128)(2,1)S(1)} %get-tuple-element.11), channel_id=1, source_target_pairs={{16,0},{32,16},{48,32},{64,48},{80,64},{96,80},{112,96},{128,112},... | collective-permute-start | bytes 196616 | tf_op jit(solution)/shard_map/ppermute | solution.py:36
  75.9 0.1 fusion.2
  75.9 1.9 %collective-permute-start.4 = (bf16[4,32,256]{2,1,0:T(8,128)(2,1)S(1)}, bf16[4,32,256]{2,1,0:T(8,128)(2,1)S(1)}, u32[]{:S(2)}, u32[]{:S(2)}) collective-permute-start(bf16[4,32,256]{2,1,0:T(8,128)(2,1)S(1)} %get-tuple-element.12), channel_id=1, source_target_pairs={{0,16},{16,32},{32,48},{48,64},{64,80},{80,96},{96,112},{112,128},... | collective-permute-start | bytes 196616 | tf_op jit(solution)/shard_map/ppermute | solution.py:35
  77.8 0.0 collective-permute-done.5.bottom
  77.9 5.7 %collective-permute-done.4.top = bf16[4,32,256]{2,1,0:T(8,128)(2,1)S(1)} collective-permute-done((bf16[4,32,256]{2,1,0:T(8,128)(2,1)S(1)}, bf16[4,32,256]{2,1,0:T(8,128)(2,1)S(1)}, u32[]{:S(2)}, u32[]{:S(2)}) %collective-permute-start.4) | collective-permute-done | bytes 65568 | tf_op jit(solution)/shard_map/ppermute | solution.py:35
  83.6 0.1 pad_maximum_fusion.2
  83.7 6.2 %collective-permute-start.6 = (bf16[40,4,256]{2,1,0:T(4,128)(2,1)S(1)}, bf16[40,4,256]{2,1,0:T(4,128)(2,1)S(1)}, u32[]{:S(2)}, u32[]{:S(2)}) collective-permute-start(bf16[40,4,256]{2,1,0:T(4,128)(2,1)S(1)} %pad_maximum_fusion.2), channel_id=1, source_target_pairs={{0,1},{1,2},{2,3},{3,4},{4,5},{5,6},{6,7},{7,8},{8,9},{9,10},{10,1... | collective-permute-start | bytes 245768 | tf_op jit(solution)/shard_map/ppermute | solution.py:41
  89.9 0.1 pad_maximum_fusion.3
  90.0 1.9 %collective-permute-start.7 = (bf16[40,4,256]{2,1,0:T(4,128)(2,1)S(1)}, bf16[40,4,256]{2,1,0:T(4,128)(2,1)S(1)}, u32[]{:S(2)}, u32[]{:S(2)}) collective-permute-start(bf16[40,4,256]{2,1,0:T(4,128)(2,1)S(1)} %pad_maximum_fusion.3), channel_id=1, source_target_pairs={{1,0},{2,1},{3,2},{4,3},{5,4},{6,5},{7,6},{8,7},{9,8},{10,9},{11,1... | collective-permute-start | bytes 245768 | tf_op jit(solution)/shard_map/ppermute | solution.py:41
  91.9 0.0 collective-permute-done.6.left
  91.9 6.8 %collective-permute-done.7.right = bf16[40,4,256]{2,1,0:T(4,128)(2,1)S(1)} collective-permute-done((bf16[40,4,256]{2,1,0:T(4,128)(2,1)S(1)}, bf16[40,4,256]{2,1,0:T(4,128)(2,1)S(1)}, u32[]{:S(2)}, u32[]{:S(2)}) %collective-permute-start.7) | collective-permute-done | bytes 81952 | tf_op jit(solution)/shard_map/ppermute | solution.py:41
  98.7 6.3 %shard_map.111 = bf16[32,32,256]{2,1,0:T(8,128)(2,1)} custom-call(s32[4,4]{1,0:T(4,128)S(1)} %select_reduce_fusion.slots, bf16[32,32,256]{2,1,0:T(8,128)(2,1)S(1)} %get-tuple-element.7.cells, bf16[4,32,256]{2,1,0:T(8,128)(2,1)S(1)} %collective-permute-done.4.top, bf16[4,32,256]{2,1,0:T(8,128)(2,1)S(1)} %collective-permute-done.5.bottom, ...), custom_call_target="tpu_custom_call" | custom-call | flops 536870912 | bytes 16777216 | tf_op jit(solution)/shard_map/pallas_call | solution.py:237
  (17 shorter events, 0.2 us)
Async XLA Ops:
  0.0 17.4 %copy-start = (bf16[4,256,256]{2,1,0:T(8,128)(2,1)S(1)}, bf16[4,256,256]{2,1,0:T(8,128)(2,1)}, u32[]{:S(2)}) copy-start(bf16[4,256,256]{2,1,0:T(8,128)(2,1)} %param.15) | copy-start | bytes 1572868
  0.0 0.7 copy-start.7
  1.4 16.0 %all-to-all-start.1 = ((s32[32,8,128]{2,1,0:T(8,128)}), s32[32,8,128]{2,1,0:T(8,128)S(1)}, u32[]{:S(2)}, u32[]{:S(2)}) async-start(s32[32,8,128]{2,1,0:T(8,128)} %broadcast_in_dim.47), calls=%async_computation.1 | async-start | bytes 262144 | tf_op jit(solution)/shard_map/all_to_all | solution.py:56
  11.8 38.5 %collective-permute-start.1 = (bf16[4,32,256]{2,1,0:T(8,128)(2,1)S(1)}, bf16[4,32,256]{2,1,0:T(8,128)(2,1)S(1)}, u32[]{:S(2)}, u32[]{:S(2)}) collective-permute-start(bf16[4,32,256]{2,1,0:T(8,128)(2,1)S(1)} %get-tuple-element.15), channel_id=1, source_target_pairs={{16,0},{32,16},{48,32},{64,48},{80,64},{96,80},{112,96},{128,112},... | collective-permute-start | bytes 196616 | tf_op jit(solution)/shard_map/ppermute | solution.py:36
  15.4 2.0 %copy-start.4 = (s32[32,32]{1,0:T(8,128)S(1)}, s32[32,32]{1,0:T(8,128)}, u32[]{:S(2)}) copy-start(s32[32,32]{1,0:T(8,128)} %param.17) | copy-start | bytes 12292
  15.4 34.9 %collective-permute-start = (bf16[4,32,256]{2,1,0:T(8,128)(2,1)S(1)}, bf16[4,32,256]{2,1,0:T(8,128)(2,1)S(1)}, u32[]{:S(2)}, u32[]{:S(2)}) collective-permute-start(bf16[4,32,256]{2,1,0:T(8,128)(2,1)S(1)} %get-tuple-element.16), channel_id=1, source_target_pairs={{0,16},{16,32},{32,48},{48,64},{64,80},{80,96},{96,112},{112,128},... | collective-permute-start | bytes 196616 | tf_op jit(solution)/shard_map/ppermute | solution.py:35
  18.2 21.8 %all-to-all-start = ((bf16[16,4,16,128]{3,2,1,0:T(8,128)(2,1)}), bf16[16,4,16,128]{3,2,1,0:T(8,128)(2,1)S(1)}, u32[]{:S(2)}, u32[]{:S(2)}) async-start(bf16[16,4,16,128]{3,2,1,0:T(8,128)(2,1)} %bitcast.4), calls=%async_computation | async-start | bytes 524288 | tf_op jit(solution)/shard_map/all_to_all | solution.py:63
  41.8 27.7 %all-to-all-start.2 = ((bf16[32,8,16,128]{3,2,1,0:T(8,128)(2,1)}), bf16[32,8,16,128]{3,2,1,0:T(8,128)(2,1)S(1)}, u32[]{:S(2)}, u32[]{:S(2)}) async-start(bf16[32,8,16,128]{3,2,1,0:T(8,128)(2,1)} %bitcast.8), calls=%async_computation.2 | async-start | bytes 2097152 | tf_op jit(solution)/shard_map/all_to_all | solution.py:65
  47.7 1.6 %copy-start.1 = (bf16[32,32,256]{2,1,0:T(8,128)(2,1)S(1)}, bf16[32,32,256]{2,1,0:T(8,128)(2,1)}, u32[]{:S(2)}) copy-start(bf16[32,32,256]{2,1,0:T(8,128)(2,1)} %cells.1) | copy-start | bytes 1572868
  47.8 0.7 copy-start.6
  48.5 0.7 copy-start.9
  48.5 0.7 copy-start.10
  48.5 0.7 copy-start.11
  49.3 0.9 copy-start.3
  50.4 14.7 %copy-start.2 = (bf16[256,256]{1,0:T(8,128)(2,1)S(1)}, bf16[256,256]{1,0:T(8,128)(2,1)}, u32[]{:S(2)}) copy-start(bf16[256,256]{1,0:T(8,128)(2,1)} %fecundity.3) | copy-start | bytes 393220
  50.5 14.6 %collective-permute-start.2 = (bf16[40,4,256]{2,1,0:T(4,128)(2,1)S(1)}, bf16[40,4,256]{2,1,0:T(4,128)(2,1)S(1)}, u32[]{:S(2)}, u32[]{:S(2)}) collective-permute-start(bf16[40,4,256]{2,1,0:T(4,128)(2,1)S(1)} %pad_maximum_fusion), channel_id=1, source_target_pairs={{0,1},{1,2},{2,3},{3,4},{4,5},{5,6},{6,7},{7,8},{8,9},{9,10},{10,1... | collective-permute-start | bytes 245768 | tf_op jit(solution)/shard_map/ppermute | solution.py:41
  54.7 3.2 %copy-start.5 = (s32[4,4]{1,0:T(4,128)S(1)}, s32[4,4]{1,0:T(4,128)}, u32[]{:S(2)}) copy-start(s32[4,4]{1,0:T(4,128)} %param.12) | copy-start | bytes 196
  54.8 3.1 %copy-start.8 = (s32[1,1,16]{2,1,0:T(1,128)S(1)}, s32[1,1,16]{2,1,0:T(1,128)}, u32[]{:S(2)}) copy-start(s32[1,1,16]{2,1,0:T(1,128)} %param.13) | copy-start | bytes 196
  54.8 10.2 %collective-permute-start.3 = (bf16[40,4,256]{2,1,0:T(4,128)(2,1)S(1)}, bf16[40,4,256]{2,1,0:T(4,128)(2,1)S(1)}, u32[]{:S(2)}, u32[]{:S(2)}) collective-permute-start(bf16[40,4,256]{2,1,0:T(4,128)(2,1)S(1)} %pad_maximum_fusion.1), channel_id=1, source_target_pairs={{1,0},{2,1},{3,2},{4,3},{5,4},{6,5},{7,6},{8,7},{9,8},{10,9},{11,1... | collective-permute-start | bytes 245768 | tf_op jit(solution)/shard_map/ppermute | solution.py:41
  70.8 7.0 %collective-permute-start.5 = (bf16[4,32,256]{2,1,0:T(8,128)(2,1)S(1)}, bf16[4,32,256]{2,1,0:T(8,128)(2,1)S(1)}, u32[]{:S(2)}, u32[]{:S(2)}) collective-permute-start(bf16[4,32,256]{2,1,0:T(8,128)(2,1)S(1)} %get-tuple-element.11), channel_id=1, source_target_pairs={{16,0},{32,16},{48,32},{64,48},{80,64},{96,80},{112,96},{128,112},... | collective-permute-start | bytes 196616 | tf_op jit(solution)/shard_map/ppermute | solution.py:36
  75.9 7.7 %collective-permute-start.4 = (bf16[4,32,256]{2,1,0:T(8,128)(2,1)S(1)}, bf16[4,32,256]{2,1,0:T(8,128)(2,1)S(1)}, u32[]{:S(2)}, u32[]{:S(2)}) collective-permute-start(bf16[4,32,256]{2,1,0:T(8,128)(2,1)S(1)} %get-tuple-element.12), channel_id=1, source_target_pairs={{0,16},{16,32},{32,48},{48,64},{64,80},{80,96},{96,112},{112,128},... | collective-permute-start | bytes 196616 | tf_op jit(solution)/shard_map/ppermute | solution.py:35
  83.7 8.2 %collective-permute-start.6 = (bf16[40,4,256]{2,1,0:T(4,128)(2,1)S(1)}, bf16[40,4,256]{2,1,0:T(4,128)(2,1)S(1)}, u32[]{:S(2)}, u32[]{:S(2)}) collective-permute-start(bf16[40,4,256]{2,1,0:T(4,128)(2,1)S(1)} %pad_maximum_fusion.2), channel_id=1, source_target_pairs={{0,1},{1,2},{2,3},{3,4},{4,5},{5,6},{6,7},{7,8},{8,9},{9,10},{10,1... | collective-permute-start | bytes 245768 | tf_op jit(solution)/shard_map/ppermute | solution.py:41
  90.0 8.7 %collective-permute-start.7 = (bf16[40,4,256]{2,1,0:T(4,128)(2,1)S(1)}, bf16[40,4,256]{2,1,0:T(4,128)(2,1)S(1)}, u32[]{:S(2)}, u32[]{:S(2)}) collective-permute-start(bf16[40,4,256]{2,1,0:T(4,128)(2,1)S(1)} %pad_maximum_fusion.3), channel_id=1, source_target_pairs={{1,0},{2,1},{3,2},{4,3},{5,4},{6,5},{7,6},{8,7},{9,8},{10,9},{11,1... | collective-permute-start | bytes 245768 | tf_op jit(solution)/shard_map/ppermute | solution.py:41

commit v2 on v1

v2 whole, which is shorter than its diff:
```python
import functools
import math

import jax
import jax.numpy as jnp
from jax import lax
from jax.experimental import pallas as pl
from jax.experimental.pallas import tpu as pltpu
from jax.sharding import PartitionSpec as P

TB = 8
RMAX = 4
BX = 8
BY = 8
STEPS = 2

SPLIT = (("xl", 2), ("yh", 4), ("yl", 2), ("co", 2), ("zh", 4), ("zl", 2), ("xh", 2))
ROW = ("xl", "yh", "yl", "co")
COL = ("zh", "zl", "xh")
NEAR = ("xl", "yl", "co", "zl", "xh")

DIST_SQ = (0, 1, 2, 4, 5, 8, 9, 10, 13, 16)
OFFSETS = (1, 4, 4, 4, 8, 4, 4, 8, 8, 4)

VMEM = pl.BlockSpec(memory_space=pltpu.VMEM)
SMEM = pl.BlockSpec(memory_space=pltpu.SMEM)
ANY = pl.BlockSpec(memory_space=pl.ANY)
PARAMS = pltpu.CompilerParams(vmem_limit_bytes=32 * 1024 * 1024)

LEAD = 8


def shift_pairs(count):
    return [(i, i + 1) for i in range(count - 1)], [(i + 1, i) for i in range(count - 1)]


def swap_rows(first, last):
    down, up = shift_pairs(math.prod(lax.axis_size(name) for name in ROW))
    return lax.ppermute(last, ROW, down), lax.ppermute(first, ROW, up)


def swap_columns(head, tail):
    right, left = shift_pairs(math.prod(lax.axis_size(name) for name in COL))
    return lax.ppermute(tail, COL, right), lax.ppermute(head, COL, left)


def class_weights(radius):
    dist = jnp.array(DIST_SQ, jnp.float32)[:, None]
    reach = (radius.astype(jnp.float32) ** 2)[None, :]
    values = jnp.exp(-dist / (2.0 * reach)) * (dist <= reach).astype(jnp.float32)
    total = jnp.sum(values * jnp.array(OFFSETS, jnp.float32)[:, None], axis=0, keepdims=True)
    return values / total


def edges_kernel(cells, lists, first, last, head, tail):
    del lists
    rows, cols, _ = cells.shape
    first[...] = cells[pl.ds(0, RMAX)]
    last[...] = cells[pl.ds(rows - RMAX, RMAX)]

    def one(x, carry):
        row = cells[x].astype(jnp.float32)
        head[x] = row[:RMAX].astype(jnp.bfloat16)
        tail[x] = row[cols - RMAX :].astype(jnp.bfloat16)
        return carry

    lax.fori_loop(0, rows, one, 0, unroll=4)


def gather_kernel(lists, pieces, top, bottom, own_head, own_tail, wanted, head, tail):
    members, count = wanted.shape[:2]
    rows, cols = own_head.shape[0], top.shape[1]

    def one(m, carry):
        found = [pieces[lists[m, 0, k]] for k in range(count)]
        for k in range(count):
            wanted[m, k] = found[k]
        return carry

    lax.fori_loop(0, members, one, 0, unroll=4)
    head[pl.ds(RMAX, rows)] = own_head[...]
    tail[pl.ds(RMAX, rows)] = own_tail[...]
    for part, start in ((top, 0), (bottom, RMAX + rows)):
        for i in range(RMAX):
            row = part[i].astype(jnp.float32)
            head[start + i] = row[:RMAX].astype(jnp.bfloat16)
            tail[start + i] = row[cols - RMAX :].astype(jnp.bfloat16)


def fetch(tile_list, harvest_ops, cells):
    rows, cols, cohorts = cells.shape
    count = tile_list.shape[-1]
    held = harvest_ops.shape[0]
    row_part = jax.ShapeDtypeStruct((RMAX, cols, cohorts), jnp.bfloat16)
    col_part = jax.ShapeDtypeStruct((rows, RMAX, cohorts), jnp.bfloat16)
    col_whole = jax.ShapeDtypeStruct((rows + 2 * RMAX, RMAX, cohorts), jnp.bfloat16)
    lists = lax.all_to_all(
        jnp.broadcast_to(jnp.pad(tile_list, ((0, 0), (0, 0), (0, 128 - count))), (32, 1, 128)),
        NEAR, 0, 0, tiled=True,
    )
    first, last, own_head, own_tail = pl.pallas_call(
        edges_kernel,
        out_shape=(row_part, row_part, col_part, col_part),
        in_specs=[VMEM, ANY],
        out_specs=(VMEM,) * 4,
        compiler_params=PARAMS,
        cost_estimate=pl.CostEstimate(flops=0, bytes_accessed=2**20, transcendentals=0),
    )(cells, lists)
    top, bottom = swap_rows(first, last)
    mine = (lax.axis_index("xl") * 2 + lax.axis_index("yl")) * 2 + lax.axis_index("co")
    strip = lax.dynamic_slice_in_dim(harvest_ops, mine * 32, 32, axis=1)
    strip = strip.reshape(held, 2, 16, 2, 128).transpose(1, 3, 0, 2, 4)
    spread = jnp.broadcast_to(strip[None], (4, 2, 2, held, 16, 128)).reshape(16, held, 16, 128)
    pieces = lax.all_to_all(spread, COL, 0, 0, tiled=True).reshape(16 * held, 16, 128)
    wanted, head, tail = pl.pallas_call(
        gather_kernel,
        out_shape=(
            jax.ShapeDtypeStruct((32, count, 16, 128), jnp.bfloat16), col_whole, col_whole
        ),
        in_specs=[SMEM] + [VMEM] * 5,
        out_specs=(VMEM,) * 3,
        compiler_params=PARAMS,
        cost_estimate=pl.CostEstimate(flops=0, bytes_accessed=2**21, transcendentals=0),
    )(lists, pieces, top, bottom, own_head, own_tail)
    parts = lax.all_to_all(wanted, NEAR, 0, 0, tiled=True)
    return parts, (top, bottom) + swap_columns(head, tail)


def fill_rows(cells, top, bottom, padded):
    rows, cols, _ = cells.shape
    for part, start in ((top, 0), (bottom, RMAX + rows)):
        for i in range(RMAX):
            padded[start + i, pl.ds(LEAD, cols), :] = part[i].astype(jnp.float32)

    def fill(x, carry):
        padded[RMAX + x, pl.ds(LEAD, cols), :] = cells[x].astype(jnp.float32)
        return carry

    lax.fori_loop(0, rows, fill, 0, unroll=4)


def fill_sides(left, right, padded, pairs):
    high, cols, cohorts = pairs.shape[1:]

    def one(x, carry):
        if left is None:
            before = after = jnp.zeros((RMAX, cohorts), jnp.float32)
        else:
            before, after = left[x].astype(jnp.float32), right[x].astype(jnp.float32)
        padded[x, pl.ds(LEAD - RMAX, RMAX), :] = before
        padded[x, pl.ds(LEAD + cols, RMAX), :] = after
        for b in range(1, RMAX + 1):
            pairs[b - 1, x] = (
                padded[x, pl.ds(LEAD - b, cols), :] + padded[x, pl.ds(LEAD + b, cols), :]
            )
        return carry

    lax.fori_loop(0, high, one, 0, unroll=2)


def weigh(x, row_sum, weights):
    at = x + RMAX

    def both(a, b):
        low, high = row_sum(at - a, b), row_sum(at + a, b)
        return None if low is None else low + high

    sums = (
        (row_sum(at, 0),),
        (row_sum(at, 1), both(1, 0)),
        (both(1, 1),),
        (row_sum(at, 2), both(2, 0)),
        (both(2, 1), both(1, 2)),
        (both(2, 2),),
        (row_sum(at, 3), both(3, 0)),
        (both(1, 3), both(3, 1)),
        (both(2, 3), both(3, 2)),
        (row_sum(at, 4), both(4, 0)),
    )
    total = None
    for k, terms in enumerate(sums):
        terms = [term for term in terms if term is not None]
        if terms:
            value = functools.reduce(lambda p, q: p + q, terms) * weights[k : k + 1, :]
            total = value if total is None else total + value
    return total


def establish(seeds, here, fecundity, moves):
    arrived = jnp.dot(seeds, fecundity[...], preferred_element_type=jnp.float32)
    middle = (here + arrived).astype(jnp.bfloat16)
    shifted = jnp.dot(middle, moves[...], preferred_element_type=jnp.float32)
    norm = lax.rsqrt(1.0 + jnp.mean(shifted * shifted, axis=-1, keepdims=True))
    return (shifted * norm).astype(jnp.bfloat16)


def remove(flat, slot, ops):
    count = ops.shape[0]
    product = jnp.dot(flat, ops[jnp.minimum(slot, count - 1)], preferred_element_type=jnp.float32)
    return jnp.where(slot == count, flat.astype(jnp.float32), product)


def remove_pair(flat, slots, ops):
    halves = []
    for h, slot in enumerate(slots):
        product = remove(flat, slot, ops).reshape(BX, 2 * BY, flat.shape[-1])
        halves.append(product[:, h * BY : (h + 1) * BY])
    return jnp.concatenate(halves, axis=1)


def assemble(parts, ops):
    count = ops.shape[0]

    def one(k, carry):
        for piece in range(parts.shape[0]):
            r, h = divmod(piece, 2)
            ops[k, r * 16 : (r + 1) * 16, h * 128 : (h + 1) * 128] = parts[piece, k]
        return carry

    lax.fori_loop(0, count, one, 0)


def first_kernel(cells, top, bottom, left, right, weights, fecundity, moves, grown, padded, pairs, seeds):
    rows, cols, cohorts = cells.shape
    fill_rows(cells, top, bottom, padded)
    fill_sides(left, right, padded, pairs)

    def row_sum(x, b):
        return padded[x, pl.ds(LEAD, cols), :] if b == 0 else pairs[b - 1, x]

    def one(x, carry):
        seeds[x] = weigh(x, row_sum, weights).astype(jnp.bfloat16)
        return carry

    lax.fori_loop(0, rows, one, 0, unroll=2)
    for i in range(rows // BX):
        span = pl.ds(i * BX, BX)
        here = cells[span].reshape(BX * cols, cohorts).astype(jnp.float32)
        result = establish(seeds[span].reshape(BX * cols, cohorts), here, fecundity, moves)
        grown[span] = result.reshape(BX, cols, cohorts)


def harvest_kernel(slots, grown, parts, out, ops, first, last, head, tail):
    assemble(parts, ops)
    rows, cols, cohorts = grown.shape
    wide = 2 * BY
    for i in range(rows // BX):
        span = pl.ds(i * BX, BX)
        done = []
        for j in range(cols // wide):
            flat = grown[span, pl.ds(j * wide, wide), :].reshape(BX * wide, cohorts)
            done.append(remove_pair(flat, (slots[i, 2 * j], slots[i, 2 * j + 1]), ops))
        whole = jnp.concatenate(done, axis=1)
        out[span] = whole.astype(jnp.bfloat16)
        head[span] = whole[:, :RMAX].astype(jnp.bfloat16)
        tail[span] = whole[:, cols - RMAX :].astype(jnp.bfloat16)
        if i == 0:
            first[...] = whole[:RMAX].astype(jnp.bfloat16)
        if i == rows // BX - 1:
            last[...] = whole[BX - RMAX :].astype(jnp.bfloat16)


def middle_kernel(
    slots, cells, top, bottom, weights, fecundity, moves, ops, inner, partial, padded, pairs, seeds
):
    rows, cols, cohorts = cells.shape
    fill_rows(cells, top, bottom, padded)
    fill_sides(None, None, padded, pairs)

    def row_sum(x, b):
        return padded[x, pl.ds(LEAD, cols), :] if b == 0 else pairs[b - 1, x]

    def one(x, carry):
        total = weigh(x, row_sum, weights)
        partial[x] = jnp.concatenate([total[:BY], total[cols - BY :]], axis=0)
        seeds[x] = total[BY : cols - BY].astype(jnp.bfloat16)
        return carry

    lax.fori_loop(0, rows, one, 0, unroll=2)
    for i in range(0, rows // BX, 2):
        span = pl.ds(i * BX, 2 * BX)
        here = cells[span].astype(jnp.float32)[:, BY : cols - BY].reshape(-1, cohorts)
        grown = establish(seeds[span].reshape(-1, cohorts), here, fecundity, moves)
        half = grown.shape[0] // 2
        for k in range(2):
            done = remove_pair(
                grown[k * half : (k + 1) * half], (slots[i + k, 1], slots[i + k, 2]), ops
            )
            inner[pl.ds((i + k) * BX, BX)] = done.astype(jnp.bfloat16)


def last_kernel(
    slots, cells, left, right, weights, fecundity, moves, ops, inner, partial,
    out, sides, pairs, seeds,
):
    rows, cols, cohorts = cells.shape
    near = lax.broadcasted_iota(jnp.int32, (BY, cohorts), 0) < RMAX
    gap = jnp.zeros((RMAX, cohorts), jnp.float32)

    def place(x, carry):
        sides[x, pl.ds(BY - RMAX, RMAX), :] = left[x].astype(jnp.float32)
        sides[x, pl.ds(BY, RMAX), :] = gap
        sides[x, pl.ds(BY + RMAX, RMAX), :] = right[x].astype(jnp.float32)
        for b in range(1, RMAX + 1):
            pairs[b - 1, x] = jnp.where(
                near, sides[x, pl.ds(BY - b, BY), :], sides[x, pl.ds(RMAX + b, BY), :]
            )
        return carry

    lax.fori_loop(0, rows + 2 * RMAX, place, 0, unroll=4)

    def row_sum(x, b):
        return None if b == 0 else pairs[b - 1, x]

    def one(x, carry):
        extra = weigh(x, row_sum, weights)
        both = jnp.concatenate([jnp.where(near, extra, 0.0), jnp.where(near, 0.0, extra)], axis=0)
        seeds[x] = (partial[x] + both).astype(jnp.bfloat16)
        return carry

    lax.fori_loop(0, rows, one, 0, unroll=4)
    for i in range(0, rows // BX, 2):
        span = pl.ds(i * BX, 2 * BX)
        here = cells[span].astype(jnp.float32)
        here = jnp.concatenate([here[:, :BY], here[:, cols - BY :]], axis=1).reshape(-1, cohorts)
        grown = establish(seeds[span].reshape(-1, cohorts), here, fecundity, moves)
        half = grown.shape[0] // 2
        for k in range(2):
            done = remove_pair(
                grown[k * half : (k + 1) * half], (slots[i + k, 0], slots[i + k, 3]), ops
            )
            at = pl.ds((i + k) * BX, BX)
            whole = jnp.concatenate(
                [done[:, :BY], inner[at].astype(jnp.float32), done[:, BY:]], axis=1
            )
            out[at] = whole.astype(jnp.bfloat16)


def scratch(rows, cols, cohorts, seeded=None):
    high = rows + 2 * RMAX
    return [
        pltpu.VMEM((high, cols + 2 * LEAD, cohorts), jnp.float32),
        pltpu.VMEM((RMAX, high, cols, cohorts), jnp.float32),
        pltpu.VMEM((rows, seeded or cols, cohorts), jnp.bfloat16),
    ]


def local(
    biomass, block_stand, stand_slot, tile_list, harvest_ops, transition, pattern, fecundity, radius
):
    shape = biomass.shape
    rows, cols, cohorts = shape
    count = tile_list.shape[-1]
    stands = stand_slot.shape[-1]
    state = jax.ShapeDtypeStruct(shape, jnp.bfloat16)
    operators = jax.ShapeDtypeStruct((count, cohorts, cohorts), jnp.bfloat16)

    weights = class_weights(radius)
    block_mask = jnp.repeat(jnp.repeat(pattern, TB, 0), TB, 1).astype(jnp.float32)
    moves = (transition.astype(jnp.float32) * block_mask).astype(jnp.bfloat16)
    stand_hit = block_stand[:, :, None] == jnp.arange(stands)[None, None, :]
    slots = jnp.sum(jnp.where(stand_hit, stand_slot[0, 0][None, None, :], 0), axis=-1)

    parts, around = fetch(tile_list, harvest_ops, biomass)
    grown = pl.pallas_call(
        first_kernel,
        out_shape=state,
        in_specs=[VMEM] * 8,
        out_specs=VMEM,
        scratch_shapes=scratch(*shape),
        compiler_params=PARAMS,
        cost_estimate=pl.CostEstimate(flops=2**28, bytes_accessed=2**24, transcendentals=0),
    )(biomass, *around, weights, fecundity, moves)
    row_part = jax.ShapeDtypeStruct((RMAX, cols, cohorts), jnp.bfloat16)
    col_part = jax.ShapeDtypeStruct((rows, RMAX, cohorts), jnp.bfloat16)
    cells, ops, first, last, head, tail = pl.pallas_call(
        harvest_kernel,
        out_shape=(state, operators, row_part, row_part, col_part, col_part),
        in_specs=[SMEM, VMEM, VMEM],
        out_specs=(VMEM,) * 6,
        compiler_params=PARAMS,
        cost_estimate=pl.CostEstimate(flops=2**28, bytes_accessed=2**22, transcendentals=0),
    )(slots, grown, parts)
    top, bottom = swap_rows(first, last)
    head = jnp.concatenate([top[:, :RMAX], head, bottom[:, :RMAX]], axis=0)
    tail = jnp.concatenate([top[:, -RMAX:], tail, bottom[:, -RMAX:]], axis=0)
    left, right = swap_columns(head, tail)
    high = rows + 2 * RMAX
    outer = 2 * BY
    inner, partial = pl.pallas_call(
        middle_kernel,
        out_shape=(
            jax.ShapeDtypeStruct((rows, cols - outer, cohorts), jnp.bfloat16),
            jax.ShapeDtypeStruct((rows, outer, cohorts), jnp.float32),
        ),
        in_specs=[SMEM] + [VMEM] * 7,
        out_specs=(VMEM, VMEM),
        scratch_shapes=scratch(rows, cols, cohorts, cols - outer),
        compiler_params=PARAMS,
        cost_estimate=pl.CostEstimate(flops=2**28, bytes_accessed=2**24, transcendentals=0),
    )(slots, cells, top, bottom, weights, fecundity, moves, ops)
    return pl.pallas_call(
        last_kernel,
        out_shape=state,
        in_specs=[SMEM] + [VMEM] * 9,
        out_specs=VMEM,
        scratch_shapes=[
            pltpu.VMEM((high, outer, cohorts), jnp.float32),
            pltpu.VMEM((RMAX, high, BY, cohorts), jnp.float32),
            pltpu.VMEM((rows, outer, cohorts), jnp.bfloat16),
        ],
        compiler_params=PARAMS,
        cost_estimate=pl.CostEstimate(flops=2**28, bytes_accessed=2**22, transcendentals=0),
    )(slots, cells, left, right, weights, fecundity, moves, ops, inner, partial)


def solution(mesh):
    names = tuple(name for name, _ in SPLIT)
    sizes = tuple(size for _, size in SPLIT)
    fine = jax.sharding.Mesh(mesh.devices.reshape(sizes), names)
    placed = (
        P(ROW, COL, None),
        P(ROW, COL),
        P(ROW, COL, None),
        P(ROW, COL, None),
        P(COL, None, None),
        P(),
        P(),
        P(),
        P(),
    )
    return jax.shard_map(
        local, mesh=fine, in_specs=placed, out_specs=P(ROW, COL, None), check_vma=False
    )
```

time: 106 us -> 95.9 us (0.905)
  the two profiles are of different devices: /device:TPU:6 before, /device:TPU:89 now
where the time goes in v2:
time: 95.9 us; the launch traced here: 95.3 us
  starting transfers between devices  53.4 us (56%)
  waiting for transfers between devices  23.1 us (24%)
  Pallas kernels  14.3 us (15%)
  local copies, waits for them, and re-layouts  3.63 us (4%)
    ppermute x4, starting transfers between devices, swap_columns(): return (lax.ppermute(tail, COL, right), lax.ppermute(head, COL, left))  15.5 us
    ppermute x4, starting transfers between devices, swap_rows(): return (lax.ppermute(last, ROW, down), lax.ppermute(first, ROW, up))  13.4 us
    all_to_all x1, starting transfers between devices, fetch(): lax.all_to_all(spread, COL, 0, 0, tiled=True).reshape(16 * held, 16, 128)  10.9 us
    ppermute x4, waiting for transfers between devices, swap_rows(): return (lax.ppermute(last, ROW, down), lax.ppermute(first, ROW, up))  9.99 us
    ppermute x4, waiting for transfers between devices, swap_columns(): return (lax.ppermute(tail, COL, right), lax.ppermute(head, COL, left))  8.88 us
    all_to_all x1, starting transfers between devices, fetch(): lax.all_to_all(jnp.broadcast_to(jnp.pad(tile_list, ((0, 0), (0, 0), (0, 1...  7.13 us
    all_to_all x1, starting transfers between devices, fetch(): parts = lax.all_to_all(wanted, NEAR, 0, 0, tiled=True)  6.4 us
    pallas_call x1, Pallas kernels, local(): pl.pallas_call(middle_kernel, out_shape=(jax.ShapeDtypeStruct((rows, cols...  4.36 us
  transfers between devices with their start and end apart: 11, of which 5 were waited for; matrix products, arithmetic and copies ran while one was open for 1% of the time, Pallas kernels for 8%

profile of v2, /device:TPU:89, one launch (start us, length us, event | category | flops | bytes accessed | tf_op | source)
XLA Modules:
  0.0 95.3 jit_solution(16917790301157989023)
XLA Ops:
  0.0 0.0 copy-start
  0.0 0.7 pad_bitcast_fusion
  0.7 0.6 broadcast_in_dim.43
  1.3 7.1 %all-to-all-start = ((s32[32,1,128]{2,1,0:T(1,128)}), s32[32,1,128]{2,1,0:T(1,128)S(1)}, u32[]{:S(2)}, u32[]{:S(2)}) async-start(s32[32,1,128]{2,1,0:T(1,128)} %broadcast_in_dim.43), calls=%async_computation | async-start | bytes 32768 | tf_op jit(solution)/shard_map/all_to_all | solution.py:97
  8.5 0.0 copy-done
  8.5 0.0 copy-start.1
  8.6 4.2 %all-to-all-done.lists = s32[32,1,128]{2,1,0:T(1,128)S(1)} async-done(((s32[32,1,128]{2,1,0:T(1,128)}), s32[32,1,128]{2,1,0:T(1,128)S(1)}, u32[]{:S(2)}, u32[]{:S(2)}) %all-to-all-start) | async-done | bytes 16416 | tf_op jit(solution)/shard_map/all_to_all | solution.py:97
  12.8 0.8 broadcast_in_dim.44
  13.5 10.9 %all-to-all-start.1 = ((bf16[16,4,16,128]{3,2,1,0:T(8,128)(2,1)}), bf16[16,4,16,128]{3,2,1,0:T(8,128)(2,1)S(1)}, u32[]{:S(2)}, u32[]{:S(2)}) async-start(bf16[16,4,16,128]{3,2,1,0:T(8,128)(2,1)} %bitcast.3), calls=%async_computation.1 | async-start | bytes 524288 | tf_op jit(solution)/shard_map/all_to_all | solution.py:114
  24.4 0.0 copy-done.1
  24.5 0.1 shard_map.109
  24.5 5.6 %collective-permute-start = (bf16[4,32,256]{2,1,0:T(8,128)(2,1)S(1)}, bf16[4,32,256]{2,1,0:T(8,128)(2,1)S(1)}, u32[]{:S(2)}, u32[]{:S(2)}) collective-permute-start(bf16[4,32,256]{2,1,0:T(8,128)(2,1)S(1)} %get-tuple-element.20), channel_id=1, source_target_pairs={{0,16},{16,32},{32,48},{48,64},{64,80},{80,96},{96,112},{112,128},... | collective-permute-start | bytes 196616 | tf_op jit(solution)/shard_map/ppermute | solution.py:39
  30.2 1.9 %collective-permute-start.1 = (bf16[4,32,256]{2,1,0:T(8,128)(2,1)S(1)}, bf16[4,32,256]{2,1,0:T(8,128)(2,1)S(1)}, u32[]{:S(2)}, u32[]{:S(2)}) collective-permute-start(bf16[4,32,256]{2,1,0:T(8,128)(2,1)S(1)} %get-tuple-element.21), channel_id=1, source_target_pairs={{16,0},{32,16},{48,32},{64,48},{80,64},{96,80},{112,96},{128,112},... | collective-permute-start | bytes 196616 | tf_op jit(solution)/shard_map/ppermute | solution.py:39
  32.1 0.0 collective-permute-done.top
  32.1 5.2 %collective-permute-done.1.bottom = bf16[4,32,256]{2,1,0:T(8,128)(2,1)S(1)} collective-permute-done((bf16[4,32,256]{2,1,0:T(8,128)(2,1)S(1)}, bf16[4,32,256]{2,1,0:T(8,128)(2,1)S(1)}, u32[]{:S(2)}, u32[]{:S(2)}) %collective-permute-start.1) | collective-permute-done | bytes 65568 | tf_op jit(solution)/shard_map/ppermute | solution.py:39
  37.2 0.0 all-to-all-done.1
  37.2 2.1 %shard_map.110 = (bf16[32,8,16,128]{3,2,1,0:T(8,128)(2,1)}, bf16[40,4,256]{2,1,0:T(4,128)(2,1)S(1)}, bf16[40,4,256]{2,1,0:T(4,128)(2,1)S(1)}) custom-call(s32[32,1,128]{2,1,0:T(1,128)S(1)} %all-to-all-done.lists, bf16[64,16,128]{2,1,0:T(8,128)(2,1)S(1)} %bitcast.10, bf16[4,32,256]{2,1,0:T(8,128)(2,1)S(1)} %collective-permute-done.top, ...), custom_call_target="tpu_custom_call" | custom-call | bytes 2097152 | tf_op jit(solution)/shard_map/pallas_call | solution.py:115
  39.4 0.0 copy-start.4
  39.4 6.4 %all-to-all-start.2 = ((bf16[32,8,16,128]{3,2,1,0:T(8,128)(2,1)}), bf16[32,8,16,128]{3,2,1,0:T(8,128)(2,1)S(1)}, u32[]{:S(2)}, u32[]{:S(2)}) async-start(bf16[32,8,16,128]{3,2,1,0:T(8,128)(2,1)} %get-tuple-element.26), calls=%async_computation.2 | async-start | bytes 2097152 | tf_op jit(solution)/shard_map/all_to_all | solution.py:125
  45.8 0.0 copy-done.4
  45.8 0.1 copy.19
  45.9 0.0 copy-start.6
  46.0 0.0 copy-start.3
  46.0 0.1 copy.20
  46.1 0.5 copy-done.6
  46.6 0.0 copy-start.8
  46.6 0.0 copy-start.9
  46.6 0.0 copy-start.10
  46.6 0.6 copy-done.8
  47.3 0.0 copy-done.9
  47.3 0.0 copy-done.10
  47.3 0.1 multiply_reduce_fusion
  47.4 0.1 fusion.1.weights
  47.5 0.0 copy-done.3
  47.5 0.0 copy-start.2
  47.6 0.0 copy-start.5
  47.6 4.7 %collective-permute-start.2 = (bf16[40,4,256]{2,1,0:T(4,128)(2,1)S(1)}, bf16[40,4,256]{2,1,0:T(4,128)(2,1)S(1)}, u32[]{:S(2)}, u32[]{:S(2)}) collective-permute-start(bf16[40,4,256]{2,1,0:T(4,128)(2,1)S(1)} %get-tuple-element.24), channel_id=1, source_target_pairs={{0,1},{1,2},{2,3},{3,4},{4,5},{5,6},{6,7},{7,8},{8,9},{9,10},{10,1... | collective-permute-start | bytes 245768 | tf_op jit(solution)/shard_map/ppermute | solution.py:44
  52.3 0.0 copy-start.7
  52.3 3.1 %collective-permute-start.3 = (bf16[40,4,256]{2,1,0:T(4,128)(2,1)S(1)}, bf16[40,4,256]{2,1,0:T(4,128)(2,1)S(1)}, u32[]{:S(2)}, u32[]{:S(2)}) collective-permute-start(bf16[40,4,256]{2,1,0:T(4,128)(2,1)S(1)} %get-tuple-element.25), channel_id=1, source_target_pairs={{1,0},{2,1},{3,2},{4,3},{5,4},{6,5},{7,6},{8,7},{9,8},{10,9},{11,1... | collective-permute-start | bytes 245768 | tf_op jit(solution)/shard_map/ppermute | solution.py:44
  55.4 0.0 copy-done.5
  55.4 0.0 copy-done.7
  55.4 0.2 select_reduce_fusion.slots
  55.7 6.8 %collective-permute-done.2.left = bf16[40,4,256]{2,1,0:T(4,128)(2,1)S(1)} collective-permute-done((bf16[40,4,256]{2,1,0:T(4,128)(2,1)S(1)}, bf16[40,4,256]{2,1,0:T(4,128)(2,1)S(1)}, u32[]{:S(2)}, u32[]{:S(2)}) %collective-permute-start.2) | collective-permute-done | bytes 81952 | tf_op jit(solution)/shard_map/ppermute | solution.py:44
  62.4 2.1 %collective-permute-done.3.right = bf16[40,4,256]{2,1,0:T(4,128)(2,1)S(1)} collective-permute-done((bf16[40,4,256]{2,1,0:T(4,128)(2,1)S(1)}, bf16[40,4,256]{2,1,0:T(4,128)(2,1)S(1)}, u32[]{:S(2)}, u32[]{:S(2)}) %collective-permute-start.3) | collective-permute-done | bytes 81952 | tf_op jit(solution)/shard_map/ppermute | solution.py:44
  64.5 0.0 copy-done.2
  64.5 3.4 %shard_map.111.grown = bf16[32,32,256]{2,1,0:T(8,128)(2,1)S(1)} custom-call(bf16[32,32,256]{2,1,0:T(8,128)(2,1)S(1)} %copy-done.1, bf16[4,32,256]{2,1,0:T(8,128)(2,1)S(1)} %collective-permute-done.top, bf16[4,32,256]{2,1,0:T(8,128)(2,1)S(1)} %collective-permute-done.1.bottom, bf16[40,4,256]{2,1,0:T(4,128)(2,1)S(1)} %collective-permute-done.2.left, ...), custom_call_target="tpu_custom_call" | custom-call | flops 268435456 | bytes 16777216 | tf_op jit(solution)/shard_map/pallas_call | solution.py:365
  68.0 0.0 all-to-all-done.2.parts
  68.0 1.2 %shard_map.112 = (bf16[32,32,256]{2,1,0:T(8,128)(2,1)S(1)}, bf16[8,256,256]{2,1,0:T(8,128)(2,1)S(1)}, bf16[4,32,256]{2,1,0:T(8,128)(2,1)S(1)}, bf16[4,32,256]{2,...) custom-call(s32[4,4]{1,0:T(4,128)S(1)} %select_reduce_fusion.slots, ...), custom_call_target="tpu_custom_call" | custom-call | flops 268435456 | bytes 4194304 | tf_op jit(solution)/shard_map/pallas_call | solution.py:376
  69.2 4.0 %collective-permute-start.4 = (bf16[4,32,256]{2,1,0:T(8,128)(2,1)S(1)}, bf16[4,32,256]{2,1,0:T(8,128)(2,1)S(1)}, u32[]{:S(2)}, u32[]{:S(2)}) collective-permute-start(bf16[4,32,256]{2,1,0:T(8,128)(2,1)S(1)} %get-tuple-element.28), channel_id=1, source_target_pairs={{0,16},{16,32},{32,48},{48,64},{64,80},{80,96},{96,112},{112,128},... | collective-permute-start | bytes 196616 | tf_op jit(solution)/shard_map/ppermute | solution.py:39
  73.2 1.9 %collective-permute-start.5 = (bf16[4,32,256]{2,1,0:T(8,128)(2,1)S(1)}, bf16[4,32,256]{2,1,0:T(8,128)(2,1)S(1)}, u32[]{:S(2)}, u32[]{:S(2)}) collective-permute-start(bf16[4,32,256]{2,1,0:T(8,128)(2,1)S(1)} %get-tuple-element.30), channel_id=1, source_target_pairs={{16,0},{32,16},{48,32},{64,48},{80,64},{96,80},{112,96},{128,112},... | collective-permute-start | bytes 196616 | tf_op jit(solution)/shard_map/ppermute | solution.py:39
  75.2 0.0 collective-permute-done.4.top
  75.2 4.8 %collective-permute-done.5.bottom = bf16[4,32,256]{2,1,0:T(8,128)(2,1)S(1)} collective-permute-done((bf16[4,32,256]{2,1,0:T(8,128)(2,1)S(1)}, bf16[4,32,256]{2,1,0:T(8,128)(2,1)S(1)}, u32[]{:S(2)}, u32[]{:S(2)}) %collective-permute-start.5) | collective-permute-done | bytes 65568 | tf_op jit(solution)/shard_map/ppermute | solution.py:39
  80.0 0.1 pad_maximum_fusion
  80.1 2.1 %collective-permute-start.6 = (bf16[40,4,256]{2,1,0:T(4,128)(2,1)S(1)}, bf16[40,4,256]{2,1,0:T(4,128)(2,1)S(1)}, u32[]{:S(2)}, u32[]{:S(2)}) collective-permute-start(bf16[40,4,256]{2,1,0:T(4,128)(2,1)S(1)} %pad_maximum_fusion), channel_id=1, source_target_pairs={{0,1},{1,2},{2,3},{3,4},{4,5},{5,6},{6,7},{7,8},{8,9},{9,10},{10,1... | collective-permute-start | bytes 245768 | tf_op jit(solution)/shard_map/ppermute | solution.py:44
  82.2 0.1 pad_maximum_fusion.1
  82.3 5.6 %collective-permute-start.7 = (bf16[40,4,256]{2,1,0:T(4,128)(2,1)S(1)}, bf16[40,4,256]{2,1,0:T(4,128)(2,1)S(1)}, u32[]{:S(2)}, u32[]{:S(2)}) collective-permute-start(bf16[40,4,256]{2,1,0:T(4,128)(2,1)S(1)} %pad_maximum_fusion.1), channel_id=1, source_target_pairs={{1,0},{2,1},{3,2},{4,3},{5,4},{6,5},{7,6},{8,7},{9,8},{10,9},{11,1... | collective-permute-start | bytes 245768 | tf_op jit(solution)/shard_map/ppermute | solution.py:44
  87.9 4.4 %shard_map.113 = (bf16[32,16,256]{2,1,0:T(8,128)(2,1)S(1)}, f32[32,16,256]{2,1,0:T(8,128)S(1)}) custom-call(s32[4,4]{1,0:T(4,128)S(1)} %select_reduce_fusion.slots, bf16[32,32,256]{2,1,0:T(8,128)(2,1)S(1)} %get-tuple-element.27.cells, bf16[4,32,256]{2,1,0:T(8,128)(2,1)S(1)} %collective-permute-done.4.top, ...), custom_call_target="tpu_custom_call" | custom-call | flops 268435456 | bytes 16777216 | tf_op jit(solution)/shard_map/pallas_call | solution.py:390
  92.2 0.0 collective-permute-done.6.left
  92.3 0.0 collective-permute-done.7.right
  92.3 3.0 %shard_map.114 = bf16[32,32,256]{2,1,0:T(8,128)(2,1)} custom-call(s32[4,4]{1,0:T(4,128)S(1)} %select_reduce_fusion.slots, bf16[32,32,256]{2,1,0:T(8,128)(2,1)S(1)} %get-tuple-element.27.cells, bf16[40,4,256]{2,1,0:T(4,128)(2,1)S(1)} %collective-permute-done.6.left, bf16[40,4,256]{2,1,0:T(4,128)(2,1)S(1)} %collective-permute-done.7.right, ...), custom_call_target="tpu_custom_call" | custom-call | flops 268435456 | bytes 4194304 | tf_op jit(solution)/shard_map/pallas_call | solution.py:402
  (10 shorter events, 0.1 us)
Async XLA Ops:
  0.0 8.5 %copy-start = (bf16[4,256,256]{2,1,0:T(8,128)(2,1)S(1)}, bf16[4,256,256]{2,1,0:T(8,128)(2,1)}, u32[]{:S(2)}) copy-start(bf16[4,256,256]{2,1,0:T(8,128)(2,1)} %param.15) | copy-start | bytes 1572868
  1.3 11.4 %all-to-all-start = ((s32[32,1,128]{2,1,0:T(1,128)}), s32[32,1,128]{2,1,0:T(1,128)S(1)}, u32[]{:S(2)}, u32[]{:S(2)}) async-start(s32[32,1,128]{2,1,0:T(1,128)} %broadcast_in_dim.43), calls=%async_computation | async-start | bytes 32768 | tf_op jit(solution)/shard_map/all_to_all | solution.py:97
  8.5 15.9 %copy-start.1 = (bf16[32,32,256]{2,1,0:T(8,128)(2,1)S(1)}, bf16[32,32,256]{2,1,0:T(8,128)(2,1)}, u32[]{:S(2)}) copy-start(bf16[32,32,256]{2,1,0:T(8,128)(2,1)} %cells.3) | copy-start | bytes 1572868
  13.5 23.7 %all-to-all-start.1 = ((bf16[16,4,16,128]{3,2,1,0:T(8,128)(2,1)}), bf16[16,4,16,128]{3,2,1,0:T(8,128)(2,1)S(1)}, u32[]{:S(2)}, u32[]{:S(2)}) async-start(bf16[16,4,16,128]{3,2,1,0:T(8,128)(2,1)} %bitcast.3), calls=%async_computation.1 | async-start | bytes 524288 | tf_op jit(solution)/shard_map/all_to_all | solution.py:114
  24.5 7.6 %collective-permute-start = (bf16[4,32,256]{2,1,0:T(8,128)(2,1)S(1)}, bf16[4,32,256]{2,1,0:T(8,128)(2,1)S(1)}, u32[]{:S(2)}, u32[]{:S(2)}) collective-permute-start(bf16[4,32,256]{2,1,0:T(8,128)(2,1)S(1)} %get-tuple-element.20), channel_id=1, source_target_pairs={{0,16},{16,32},{32,48},{48,64},{64,80},{80,96},{96,112},{112,128},... | collective-permute-start | bytes 196616 | tf_op jit(solution)/shard_map/ppermute | solution.py:39
  30.2 7.1 %collective-permute-start.1 = (bf16[4,32,256]{2,1,0:T(8,128)(2,1)S(1)}, bf16[4,32,256]{2,1,0:T(8,128)(2,1)S(1)}, u32[]{:S(2)}, u32[]{:S(2)}) collective-permute-start(bf16[4,32,256]{2,1,0:T(8,128)(2,1)S(1)} %get-tuple-element.21), channel_id=1, source_target_pairs={{16,0},{32,16},{48,32},{64,48},{80,64},{96,80},{112,96},{128,112},... | collective-permute-start | bytes 196616 | tf_op jit(solution)/shard_map/ppermute | solution.py:39
  39.4 6.4 %copy-start.4 = (s32[32,32]{1,0:T(8,128)S(1)}, s32[32,32]{1,0:T(8,128)}, u32[]{:S(2)}) copy-start(s32[32,32]{1,0:T(8,128)} %param.17) | copy-start | bytes 12292
  39.4 28.6 %all-to-all-start.2 = ((bf16[32,8,16,128]{3,2,1,0:T(8,128)(2,1)}), bf16[32,8,16,128]{3,2,1,0:T(8,128)(2,1)S(1)}, u32[]{:S(2)}, u32[]{:S(2)}) async-start(bf16[32,8,16,128]{3,2,1,0:T(8,128)(2,1)} %get-tuple-element.26), calls=%async_computation.2 | async-start | bytes 2097152 | tf_op jit(solution)/shard_map/all_to_all | solution.py:125
  45.9 0.7 copy-start.6
  46.0 1.5 %copy-start.3 = (bf16[256,256]{1,0:T(8,128)(2,1)S(1)}, bf16[256,256]{1,0:T(8,128)(2,1)}, u32[]{:S(2)}) copy-start(bf16[256,256]{1,0:T(8,128)(2,1)} %param.16) | copy-start | bytes 393220
  46.6 0.7 copy-start.8
  46.6 0.7 copy-start.9
  46.6 0.7 copy-start.10
  47.5 17.0 %copy-start.2 = (bf16[256,256]{1,0:T(8,128)(2,1)S(1)}, bf16[256,256]{1,0:T(8,128)(2,1)}, u32[]{:S(2)}) copy-start(bf16[256,256]{1,0:T(8,128)(2,1)} %fecundity.5) | copy-start | bytes 393220
  47.6 7.9 %copy-start.5 = (s32[4,4]{1,0:T(4,128)S(1)}, s32[4,4]{1,0:T(4,128)}, u32[]{:S(2)}) copy-start(s32[4,4]{1,0:T(4,128)} %param.12) | copy-start | bytes 196
  47.6 14.9 %collective-permute-start.2 = (bf16[40,4,256]{2,1,0:T(4,128)(2,1)S(1)}, bf16[40,4,256]{2,1,0:T(4,128)(2,1)S(1)}, u32[]{:S(2)}, u32[]{:S(2)}) collective-permute-start(bf16[40,4,256]{2,1,0:T(4,128)(2,1)S(1)} %get-tuple-element.24), channel_id=1, source_target_pairs={{0,1},{1,2},{2,3},{3,4},{4,5},{5,6},{6,7},{7,8},{8,9},{9,10},{10,1... | collective-permute-start | bytes 245768 | tf_op jit(solution)/shard_map/ppermute | solution.py:44
  52.3 3.1 %copy-start.7 = (s32[1,1,16]{2,1,0:T(1,128)S(1)}, s32[1,1,16]{2,1,0:T(1,128)}, u32[]{:S(2)}) copy-start(s32[1,1,16]{2,1,0:T(1,128)} %param.13) | copy-start | bytes 196
  52.3 12.2 %collective-permute-start.3 = (bf16[40,4,256]{2,1,0:T(4,128)(2,1)S(1)}, bf16[40,4,256]{2,1,0:T(4,128)(2,1)S(1)}, u32[]{:S(2)}, u32[]{:S(2)}) collective-permute-start(bf16[40,4,256]{2,1,0:T(4,128)(2,1)S(1)} %get-tuple-element.25), channel_id=1, source_target_pairs={{1,0},{2,1},{3,2},{4,3},{5,4},{6,5},{7,6},{8,7},{9,8},{10,9},{11,1... | collective-permute-start | bytes 245768 | tf_op jit(solution)/shard_map/ppermute | solution.py:44
  69.2 5.9 %collective-permute-start.4 = (bf16[4,32,256]{2,1,0:T(8,128)(2,1)S(1)}, bf16[4,32,256]{2,1,0:T(8,128)(2,1)S(1)}, u32[]{:S(2)}, u32[]{:S(2)}) collective-permute-start(bf16[4,32,256]{2,1,0:T(8,128)(2,1)S(1)} %get-tuple-element.28), channel_id=1, source_target_pairs={{0,16},{16,32},{32,48},{48,64},{64,80},{80,96},{96,112},{112,128},... | collective-permute-start | bytes 196616 | tf_op jit(solution)/shard_map/ppermute | solution.py:39
  73.2 6.8 %collective-permute-start.5 = (bf16[4,32,256]{2,1,0:T(8,128)(2,1)S(1)}, bf16[4,32,256]{2,1,0:T(8,128)(2,1)S(1)}, u32[]{:S(2)}, u32[]{:S(2)}) collective-permute-start(bf16[4,32,256]{2,1,0:T(8,128)(2,1)S(1)} %get-tuple-element.30), channel_id=1, source_target_pairs={{16,0},{32,16},{48,32},{64,48},{80,64},{96,80},{112,96},{128,112},... | collective-permute-start | bytes 196616 | tf_op jit(solution)/shard_map/ppermute | solution.py:39
  80.1 12.1 %collective-permute-start.6 = (bf16[40,4,256]{2,1,0:T(4,128)(2,1)S(1)}, bf16[40,4,256]{2,1,0:T(4,128)(2,1)S(1)}, u32[]{:S(2)}, u32[]{:S(2)}) collective-permute-start(bf16[40,4,256]{2,1,0:T(4,128)(2,1)S(1)} %pad_maximum_fusion), channel_id=1, source_target_pairs={{0,1},{1,2},{2,3},{3,4},{4,5},{5,6},{6,7},{7,8},{8,9},{9,10},{10,1... | collective-permute-start | bytes 245768 | tf_op jit(solution)/shard_map/ppermute | solution.py:44
  82.3 10.0 %collective-permute-start.7 = (bf16[40,4,256]{2,1,0:T(4,128)(2,1)S(1)}, bf16[40,4,256]{2,1,0:T(4,128)(2,1)S(1)}, u32[]{:S(2)}, u32[]{:S(2)}) collective-permute-start(bf16[40,4,256]{2,1,0:T(4,128)(2,1)S(1)} %pad_maximum_fusion.1), channel_id=1, source_target_pairs={{1,0},{2,1},{3,2},{4,3},{5,4},{6,5},{7,6},{8,7},{9,8},{10,9},{11,1... | collective-permute-start | bytes 245768 | tf_op jit(solution)/shard_map/ppermute | solution.py:44

commit v3 on v2

--- a/solution.py
+++ b/solution.py
@@ -34,14 +34,13 @@
     return [(i, i + 1) for i in range(count - 1)], [(i + 1, i) for i in range(count - 1)]
 
 
-def swap_rows(first, last):
+def surround(first, last, head, tail):
     down, up = shift_pairs(math.prod(lax.axis_size(name) for name in ROW))
-    return lax.ppermute(last, ROW, down), lax.ppermute(first, ROW, up)
-
-
-def swap_columns(head, tail):
+    top, bottom = lax.ppermute(last, ROW, down), lax.ppermute(first, ROW, up)
+    head = jnp.concatenate([top[:, :RMAX], head, bottom[:, :RMAX]], axis=0)
+    tail = jnp.concatenate([top[:, -RMAX:], tail, bottom[:, -RMAX:]], axis=0)
     right, left = shift_pairs(math.prod(lax.axis_size(name) for name in COL))
-    return lax.ppermute(tail, COL, right), lax.ppermute(head, COL, left)
+    return top, bottom, lax.ppermute(tail, COL, right), lax.ppermute(head, COL, left)
 
 
 def class_weights(radius):
@@ -52,8 +51,7 @@
     return values / total
 
 
-def edges_kernel(cells, lists, first, last, head, tail):
-    del lists
+def edges_kernel(cells, first, last, head, tail):
     rows, cols, _ = cells.shape
     first[...] = cells[pl.ds(0, RMAX)]
     last[...] = cells[pl.ds(rows - RMAX, RMAX)]
@@ -67,9 +65,21 @@
     lax.fori_loop(0, rows, one, 0, unroll=4)
 
 
-def gather_kernel(lists, pieces, top, bottom, own_head, own_tail, wanted, head, tail):
+def spread_kernel(held, weights, moves, spread):
+    del weights, moves
+    mine = (lax.axis_index("xl") * 2 + lax.axis_index("yl")) * 2 + lax.axis_index("co")
+    for k in range(held.shape[0]):
+        for near in range(4):
+            low, half = divmod(near, 2)
+            at = pl.multiple_of(mine * 32 + low * 16, 16)
+            piece = held[k, pl.ds(at, 16), pl.ds(half * 128, 128)]
+            for far in range(4):
+                spread[far * 4 + near, k] = piece
+
+
+def gather_kernel(lists, pieces, left, wanted):
+    del left
     members, count = wanted.shape[:2]
-    rows, cols = own_head.shape[0], top.shape[1]
 
     def one(m, carry):
         found = [pieces[lists[m, 0, k]] for k in range(count)]
@@ -78,52 +88,46 @@
         return carry
 
     lax.fori_loop(0, members, one, 0, unroll=4)
-    head[pl.ds(RMAX, rows)] = own_head[...]
-    tail[pl.ds(RMAX, rows)] = own_tail[...]
-    for part, start in ((top, 0), (bottom, RMAX + rows)):
-        for i in range(RMAX):
-            row = part[i].astype(jnp.float32)
-            head[start + i] = row[:RMAX].astype(jnp.bfloat16)
-            tail[start + i] = row[cols - RMAX :].astype(jnp.bfloat16)
-
-
-def fetch(tile_list, harvest_ops, cells):
+
+
+def fetch(tile_list, harvest_ops, cells, weights, moves):
     rows, cols, cohorts = cells.shape
     count = tile_list.shape[-1]
     held = harvest_ops.shape[0]
     row_part = jax.ShapeDtypeStruct((RMAX, cols, cohorts), jnp.bfloat16)
     col_part = jax.ShapeDtypeStruct((rows, RMAX, cohorts), jnp.bfloat16)
-    col_whole = jax.ShapeDtypeStruct((rows + 2 * RMAX, RMAX, cohorts), jnp.bfloat16)
     lists = lax.all_to_all(
         jnp.broadcast_to(jnp.pad(tile_list, ((0, 0), (0, 0), (0, 128 - count))), (32, 1, 128)),
         NEAR, 0, 0, tiled=True,
     )
-    first, last, own_head, own_tail = pl.pallas_call(
+    first, last, head, tail = pl.pallas_call(
         edges_kernel,
         out_shape=(row_part, row_part, col_part, col_part),
-        in_specs=[VMEM, ANY],
+        in_specs=[VMEM],
         out_specs=(VMEM,) * 4,
         compiler_params=PARAMS,
         cost_estimate=pl.CostEstimate(flops=0, bytes_accessed=2**20, transcendentals=0),
-    )(cells, lists)
-    top, bottom = swap_rows(first, last)
-    mine = (lax.axis_index("xl") * 2 + lax.axis_index("yl")) * 2 + lax.axis_index("co")
-    strip = lax.dynamic_slice_in_dim(harvest_ops, mine * 32, 32, axis=1)
-    strip = strip.reshape(held, 2, 16, 2, 128).transpose(1, 3, 0, 2, 4)
-    spread = jnp.broadcast_to(strip[None], (4, 2, 2, held, 16, 128)).reshape(16, held, 16, 128)
+    )(cells)
+    top, bottom, left, right = surround(first, last, head, tail)
+    spread = pl.pallas_call(
+        spread_kernel,
+        out_shape=jax.ShapeDtypeStruct((16, held, 16, 128), jnp.bfloat16),
+        in_specs=[VMEM, ANY, ANY],
+        out_specs=VMEM,
+        compiler_params=PARAMS,
+        cost_estimate=pl.CostEstimate(flops=0, bytes_accessed=2**20, transcendentals=0),
+    )(harvest_ops, weights, moves)
     pieces = lax.all_to_all(spread, COL, 0, 0, tiled=True).reshape(16 * held, 16, 128)
-    wanted, head, tail = pl.pallas_call(
+    wanted = pl.pallas_call(
         gather_kernel,
-        out_shape=(
-            jax.ShapeDtypeStruct((32, count, 16, 128), jnp.bfloat16), col_whole, col_whole
-        ),
-        in_specs=[SMEM] + [VMEM] * 5,
-        out_specs=(VMEM,) * 3,
+        out_shape=jax.ShapeDtypeStruct((32, count, 16, 128), jnp.bfloat16),
+        in_specs=[SMEM, VMEM, ANY],
+        out_specs=VMEM,
         compiler_params=PARAMS,
         cost_estimate=pl.CostEstimate(flops=0, bytes_accessed=2**21, transcendentals=0),
-    )(lists, pieces, top, bottom, own_head, own_tail)
+    )(lists, pieces, left)
     parts = lax.all_to_all(wanted, NEAR, 0, 0, tiled=True)
-    return parts, (top, bottom) + swap_columns(head, tail)
+    return parts, (top, bottom, left, right)
 
 
 def fill_rows(cells, top, bottom, padded):
@@ -361,7 +365,7 @@
     stand_hit = block_stand[:, :, None] == jnp.arange(stands)[None, None, :]
     slots = jnp.sum(jnp.where(stand_hit, stand_slot[0, 0][None, None, :], 0), axis=-1)
 
-    parts, around = fetch(tile_list, harvest_ops, biomass)
+    parts, around = fetch(tile_list, harvest_ops, biomass, weights, moves)
     grown = pl.pallas_call(
         first_kernel,
         out_shape=state,
@@ -381,10 +385,7 @@
         compiler_params=PARAMS,
         cost_estimate=pl.CostEstimate(flops=2**28, bytes_accessed=2**22, transcendentals=0),
     )(slots, grown, parts)
-    top, bottom = swap_rows(first, last)
-    head = jnp.concatenate([top[:, :RMAX], head, bottom[:, :RMAX]], axis=0)
-    tail = jnp.concatenate([top[:, -RMAX:], tail, bottom[:, -RMAX:]], axis=0)
-    left, right = swap_columns(head, tail)
+    top, bottom, left, right = surround(first, last, head, tail)
     high = rows + 2 * RMAX
     outer = 2 * BY
     inner, partial = pl.pallas_call(

time: 95.9 us -> 99.6 us (1.039)
  starting transfers between devices: 53.4 us -> 54.9 us
    all_to_all x1, waiting for transfers between devices: 4.18 us -> 0.01 us  [fetch(): lax.all_to_all(jnp.broadcast_to(jnp.pad(tile_list, ((0, 0), (0, 0), (0, 1...]
    ppermute x8, waiting for transfers between devices: 18.9 us -> 22.8 us  [the longest x2 12 us: surround(): lax.ppermute(head, COL, left)]
    unnamed x22 -> x24, local copies, waits for them, and re-layouts: 1.25 us -> 2.48 us
    all_to_all x1, waiting for transfers between devices: 0.01 us -> 1.13 us  [fetch(): lax.all_to_all(spread, COL, 0, 0, tiled=True).reshape(16 * held, 16, 128)]
    pallas_call x1 -> x2, Pallas kernels: 2.14 us -> 2.87 us  [the longest x1 2.12 us: fetch(): pl.pallas_call(gather_kernel, out_shape=jax.ShapeDtypeStruct((32, count,...]
  transfers between devices with their start and end apart: 11 -> 11, of which waited for: 5 -> 4; matrix products, arithmetic and copies ran while one was open for 1% -> 1% of each run, Pallas kernels for 8% -> 9%
where the time goes in v3:
time: 99.6 us; the launch traced here: 98.9 us
  starting transfers between devices  54.9 us (55%)
  waiting for transfers between devices  23.9 us (24%)
  Pallas kernels  15 us (15%)
  local copies, waits for them, and re-layouts  4.01 us (4%)
    ppermute x2, waiting for transfers between devices, surround(): lax.ppermute(head, COL, left)  12 us
    ppermute x4, starting transfers between devices, surround(): top, bottom = (lax.ppermute(last, ROW, down), lax.ppermute(first, ROW, up))  11.9 us
    all_to_all x1, starting transfers between devices, fetch(): lax.all_to_all(spread, COL, 0, 0, tiled=True).reshape(16 * held, 16, 128)  11.8 us
    ppermute x2, starting transfers between devices, surround(): lax.ppermute(head, COL, left)  10.4 us
    all_to_all x1, starting transfers between devices, fetch(): parts = lax.all_to_all(wanted, NEAR, 0, 0, tiled=True)  7.16 us
    all_to_all x1, starting transfers between devices, fetch(): lax.all_to_all(jnp.broadcast_to(jnp.pad(tile_list, ((0, 0), (0, 0), (0, 1...  7.13 us
    ppermute x2, starting transfers between devices, surround(): lax.ppermute(tail, COL, right)  6.52 us
    ppermute x2, waiting for transfers between devices, surround(): lax.ppermute(tail, COL, right)  5.98 us
  transfers between devices with their start and end apart: 11, of which 4 were waited for; matrix products, arithmetic and copies ran while one was open for 1% of the time, Pallas kernels for 9%

profile of v3, /device:TPU:89, one launch (start us, length us, event | category | flops | bytes accessed | tf_op | source)
XLA Modules:
  0.0 98.9 jit_solution(7168535863427014924)
XLA Ops:
  0.0 0.7 pad_bitcast_fusion
  0.7 0.6 broadcast_in_dim.39
  1.3 7.1 %all-to-all-start = ((s32[32,1,128]{2,1,0:T(1,128)}), s32[32,1,128]{2,1,0:T(1,128)S(1)}, u32[]{:S(2)}, u32[]{:S(2)}) async-start(s32[32,1,128]{2,1,0:T(1,128)} %broadcast_in_dim.39), calls=%async_computation | async-start | bytes 32768 | tf_op jit(solution)/shard_map/all_to_all | solution.py:99
  8.4 0.0 copy-start
  8.4 1.0 %copy-done = bf16[32,32,256]{2,1,0:T(8,128)(2,1)S(1)} copy-done((bf16[32,32,256]{2,1,0:T(8,128)(2,1)S(1)}, bf16[32,32,256]{2,1,0:T(8,128)(2,1)}, u32[]{:S(2)}) %copy-start) | copy-done | bytes 524312
  9.5 0.0 copy-start.5
  9.5 0.1 shard_map.109
  9.5 0.0 copy-start.7
  9.5 3.9 %collective-permute-start = (bf16[4,32,256]{2,1,0:T(8,128)(2,1)S(1)}, bf16[4,32,256]{2,1,0:T(8,128)(2,1)S(1)}, u32[]{:S(2)}, u32[]{:S(2)}) collective-permute-start(bf16[4,32,256]{2,1,0:T(8,128)(2,1)S(1)} %get-tuple-element.17), channel_id=1, source_target_pairs={{0,16},{16,32},{32,48},{48,64},{64,80},{80,96},{96,112},{112,128},... | collective-permute-start | bytes 196616 | tf_op jit(solution)/shard_map/ppermute | solution.py:39
  13.4 1.9 %collective-permute-start.1 = (bf16[4,32,256]{2,1,0:T(8,128)(2,1)S(1)}, bf16[4,32,256]{2,1,0:T(8,128)(2,1)S(1)}, u32[]{:S(2)}, u32[]{:S(2)}) collective-permute-start(bf16[4,32,256]{2,1,0:T(8,128)(2,1)S(1)} %get-tuple-element.18), channel_id=1, source_target_pairs={{16,0},{32,16},{48,32},{64,48},{80,64},{96,80},{112,96},{128,112},... | collective-permute-start | bytes 196616 | tf_op jit(solution)/shard_map/ppermute | solution.py:39
  15.3 0.0 copy-done.7
  15.4 0.0 copy-done.5
  15.4 0.1 copy.16
  15.5 0.0 copy-start.4
  15.5 0.0 copy-start.3
  15.5 0.1 copy.17
  15.7 0.7 copy-done.4
  16.4 0.0 copy-start.9
  16.4 0.0 copy-start.10
  16.4 0.0 copy-start.11
  16.5 0.6 copy-done.9
  17.1 0.0 copy-done.10
  17.1 0.0 copy-done.11
  17.1 0.1 multiply_reduce_fusion
  17.2 0.1 fusion.1.weights
  17.3 0.0 copy-done.3
  17.3 0.8 shard_map.111
  18.1 0.0 all-to-all-done.lists
  18.1 11.8 %all-to-all-start.1 = ((bf16[16,4,16,128]{3,2,1,0:T(8,128)(2,1)}), bf16[16,4,16,128]{3,2,1,0:T(8,128)(2,1)S(1)}, u32[]{:S(2)}, u32[]{:S(2)}) async-start(bf16[16,4,16,128]{3,2,1,0:T(8,128)(2,1)} %shard_map.111), calls=%async_computation.1 | async-start | bytes 524288 | tf_op jit(solution)/shard_map/all_to_all | solution.py:120
  29.9 0.0 collective-permute-done.top
  29.9 0.0 collective-permute-done.1.bottom
  29.9 0.1 pad_maximum_fusion
  30.0 4.6 %collective-permute-start.2 = (bf16[40,4,256]{2,1,0:T(4,128)(2,1)S(1)}, bf16[40,4,256]{2,1,0:T(4,128)(2,1)S(1)}, u32[]{:S(2)}, u32[]{:S(2)}) collective-permute-start(bf16[40,4,256]{2,1,0:T(4,128)(2,1)S(1)} %pad_maximum_fusion), channel_id=1, source_target_pairs={{0,1},{1,2},{2,3},{3,4},{4,5},{5,6},{6,7},{7,8},{8,9},{9,10},{10,1... | collective-permute-start | bytes 245768 | tf_op jit(solution)/shard_map/ppermute | solution.py:43
  34.6 6.0 %collective-permute-done.2.left = bf16[40,4,256]{2,1,0:T(4,128)(2,1)S(1)} collective-permute-done((bf16[40,4,256]{2,1,0:T(4,128)(2,1)S(1)}, bf16[40,4,256]{2,1,0:T(4,128)(2,1)S(1)}, u32[]{:S(2)}, u32[]{:S(2)}) %collective-permute-start.2) | collective-permute-done | bytes 81952 | tf_op jit(solution)/shard_map/ppermute | solution.py:43
  40.6 1.1 %all-to-all-done.1 = bf16[16,4,16,128]{3,2,1,0:T(8,128)(2,1)S(1)} async-done(((bf16[16,4,16,128]{3,2,1,0:T(8,128)(2,1)}), bf16[16,4,16,128]{3,2,1,0:T(8,128)(2,1)S(1)}, u32[]{:S(2)}, u32[]{:S(2)}) %all-to-all-start.1) | async-done | bytes 262176 | tf_op jit(solution)/shard_map/all_to_all | solution.py:120
  41.7 2.1 %shard_map.112 = bf16[32,8,16,128]{3,2,1,0:T(8,128)(2,1)} custom-call(s32[32,1,128]{2,1,0:T(1,128)S(1)} %all-to-all-done.lists, bf16[64,16,128]{2,1,0:T(8,128)(2,1)S(1)} %bitcast.8, bf16[40,4,256]{2,1,0:T(4,128)(2,1)S(1)} %collective-permute-done.2.left), custom_call_target="tpu_custom_call" | custom-call | bytes 2097152 | tf_op jit(solution)/shard_map/pallas_call | solution.py:121
  43.8 0.0 copy-start.1
  43.8 7.2 %all-to-all-start.2 = ((bf16[32,8,16,128]{3,2,1,0:T(8,128)(2,1)}), bf16[32,8,16,128]{3,2,1,0:T(8,128)(2,1)S(1)}, u32[]{:S(2)}, u32[]{:S(2)}) async-start(bf16[32,8,16,128]{3,2,1,0:T(8,128)(2,1)} %shard_map.112), calls=%async_computation.2 | async-start | bytes 2097152 | tf_op jit(solution)/shard_map/all_to_all | solution.py:129
  51.0 0.0 copy-start.2
  51.0 0.0 copy-start.6
  51.0 0.1 pad_maximum_fusion.1
  51.1 0.0 copy-start.8
  51.1 4.6 %collective-permute-start.3 = (bf16[40,4,256]{2,1,0:T(4,128)(2,1)S(1)}, bf16[40,4,256]{2,1,0:T(4,128)(2,1)S(1)}, u32[]{:S(2)}, u32[]{:S(2)}) collective-permute-start(bf16[40,4,256]{2,1,0:T(4,128)(2,1)S(1)} %pad_maximum_fusion.1), channel_id=1, source_target_pairs={{1,0},{2,1},{3,2},{4,3},{5,4},{6,5},{7,6},{8,7},{9,8},{10,9},{11,1... | collective-permute-start | bytes 245768 | tf_op jit(solution)/shard_map/ppermute | solution.py:43
  55.7 0.0 copy-done.6
  55.7 0.0 copy-done.8
  55.7 0.2 select_reduce_fusion.slots
  55.9 12.0 %collective-permute-done.3.right = bf16[40,4,256]{2,1,0:T(4,128)(2,1)S(1)} collective-permute-done((bf16[40,4,256]{2,1,0:T(4,128)(2,1)S(1)}, bf16[40,4,256]{2,1,0:T(4,128)(2,1)S(1)}, u32[]{:S(2)}, u32[]{:S(2)}) %collective-permute-start.3) | collective-permute-done | bytes 81952 | tf_op jit(solution)/shard_map/ppermute | solution.py:43
  67.9 0.0 copy-done.1
  67.9 0.0 copy-done.2
  67.9 3.4 %shard_map.110.grown = bf16[32,32,256]{2,1,0:T(8,128)(2,1)S(1)} custom-call(bf16[32,32,256]{2,1,0:T(8,128)(2,1)S(1)} %copy-done.1, bf16[4,32,256]{2,1,0:T(8,128)(2,1)S(1)} %collective-permute-done.top, bf16[4,32,256]{2,1,0:T(8,128)(2,1)S(1)} %collective-permute-done.1.bottom, bf16[40,4,256]{2,1,0:T(4,128)(2,1)S(1)} %collective-permute-done.2.left, ...), custom_call_target="tpu_custom_call" | custom-call | flops 268435456 | bytes 16777216 | tf_op jit(solution)/shard_map/pallas_call | solution.py:369
  71.4 0.0 all-to-all-done.2.parts
  71.4 1.2 %shard_map.113 = (bf16[32,32,256]{2,1,0:T(8,128)(2,1)S(1)}, bf16[8,256,256]{2,1,0:T(8,128)(2,1)S(1)}, bf16[4,32,256]{2,1,0:T(8,128)(2,1)S(1)}, bf16[4,32,256]{2,...) custom-call(s32[4,4]{1,0:T(4,128)S(1)} %select_reduce_fusion.slots, ...), custom_call_target="tpu_custom_call" | custom-call | flops 268435456 | bytes 4194304 | tf_op jit(solution)/shard_map/pallas_call | solution.py:380
  72.6 4.2 %collective-permute-start.4 = (bf16[4,32,256]{2,1,0:T(8,128)(2,1)S(1)}, bf16[4,32,256]{2,1,0:T(8,128)(2,1)S(1)}, u32[]{:S(2)}, u32[]{:S(2)}) collective-permute-start(bf16[4,32,256]{2,1,0:T(8,128)(2,1)S(1)} %get-tuple-element.22), channel_id=1, source_target_pairs={{0,16},{16,32},{32,48},{48,64},{64,80},{80,96},{96,112},{112,128},... | collective-permute-start | bytes 196616 | tf_op jit(solution)/shard_map/ppermute | solution.py:39
  76.9 1.9 %collective-permute-start.5 = (bf16[4,32,256]{2,1,0:T(8,128)(2,1)S(1)}, bf16[4,32,256]{2,1,0:T(8,128)(2,1)S(1)}, u32[]{:S(2)}, u32[]{:S(2)}) collective-permute-start(bf16[4,32,256]{2,1,0:T(8,128)(2,1)S(1)} %get-tuple-element.24), channel_id=1, source_target_pairs={{16,0},{32,16},{48,32},{64,48},{80,64},{96,80},{112,96},{128,112},... | collective-permute-start | bytes 196616 | tf_op jit(solution)/shard_map/ppermute | solution.py:39
  78.8 0.0 collective-permute-done.4.top
  78.8 4.8 %collective-permute-done.5.bottom = bf16[4,32,256]{2,1,0:T(8,128)(2,1)S(1)} collective-permute-done((bf16[4,32,256]{2,1,0:T(8,128)(2,1)S(1)}, bf16[4,32,256]{2,1,0:T(8,128)(2,1)S(1)}, u32[]{:S(2)}, u32[]{:S(2)}) %collective-permute-start.5) | collective-permute-done | bytes 65568 | tf_op jit(solution)/shard_map/ppermute | solution.py:39
  83.7 0.1 pad_maximum_fusion.2
  83.8 1.9 %collective-permute-start.6 = (bf16[40,4,256]{2,1,0:T(4,128)(2,1)S(1)}, bf16[40,4,256]{2,1,0:T(4,128)(2,1)S(1)}, u32[]{:S(2)}, u32[]{:S(2)}) collective-permute-start(bf16[40,4,256]{2,1,0:T(4,128)(2,1)S(1)} %pad_maximum_fusion.2), channel_id=1, source_target_pairs={{0,1},{1,2},{2,3},{3,4},{4,5},{5,6},{6,7},{7,8},{8,9},{9,10},{10,1... | collective-permute-start | bytes 245768 | tf_op jit(solution)/shard_map/ppermute | solution.py:43
  85.7 0.1 pad_maximum_fusion.3
  85.8 5.8 %collective-permute-start.7 = (bf16[40,4,256]{2,1,0:T(4,128)(2,1)S(1)}, bf16[40,4,256]{2,1,0:T(4,128)(2,1)S(1)}, u32[]{:S(2)}, u32[]{:S(2)}) collective-permute-start(bf16[40,4,256]{2,1,0:T(4,128)(2,1)S(1)} %pad_maximum_fusion.3), channel_id=1, source_target_pairs={{1,0},{2,1},{3,2},{4,3},{5,4},{6,5},{7,6},{8,7},{9,8},{10,9},{11,1... | collective-permute-start | bytes 245768 | tf_op jit(solution)/shard_map/ppermute | solution.py:43
  91.5 4.4 %shard_map.114 = (bf16[32,16,256]{2,1,0:T(8,128)(2,1)S(1)}, f32[32,16,256]{2,1,0:T(8,128)S(1)}) custom-call(s32[4,4]{1,0:T(4,128)S(1)} %select_reduce_fusion.slots, bf16[32,32,256]{2,1,0:T(8,128)(2,1)S(1)} %get-tuple-element.21.cells, bf16[4,32,256]{2,1,0:T(8,128)(2,1)S(1)} %collective-permute-done.4.top, ...), custom_call_target="tpu_custom_call" | custom-call | flops 268435456 | bytes 16777216 | tf_op jit(solution)/shard_map/pallas_call | solution.py:391
  95.9 0.0 collective-permute-done.6.left
  95.9 0.0 collective-permute-done.7.right
  95.9 3.0 %shard_map.115 = bf16[32,32,256]{2,1,0:T(8,128)(2,1)} custom-call(s32[4,4]{1,0:T(4,128)S(1)} %select_reduce_fusion.slots, bf16[32,32,256]{2,1,0:T(8,128)(2,1)S(1)} %get-tuple-element.21.cells, bf16[40,4,256]{2,1,0:T(4,128)(2,1)S(1)} %collective-permute-done.6.left, bf16[40,4,256]{2,1,0:T(4,128)(2,1)S(1)} %collective-permute-done.7.right, ...), custom_call_target="tpu_custom_call" | custom-call | flops 268435456 | bytes 4194304 | tf_op jit(solution)/shard_map/pallas_call | solution.py:403
  (9 shorter events, 0.1 us)
Async XLA Ops:
  1.3 16.8 %all-to-all-start = ((s32[32,1,128]{2,1,0:T(1,128)}), s32[32,1,128]{2,1,0:T(1,128)S(1)}, u32[]{:S(2)}, u32[]{:S(2)}) async-start(s32[32,1,128]{2,1,0:T(1,128)} %broadcast_in_dim.39), calls=%async_computation | async-start | bytes 32768 | tf_op jit(solution)/shard_map/all_to_all | solution.py:99
  8.4 1.0 %copy-start = (bf16[32,32,256]{2,1,0:T(8,128)(2,1)S(1)}, bf16[32,32,256]{2,1,0:T(8,128)(2,1)}, u32[]{:S(2)}) copy-start(bf16[32,32,256]{2,1,0:T(8,128)(2,1)} %cells.3) | copy-start | bytes 1572868
  9.5 5.9 %copy-start.5 = (s32[32,32]{1,0:T(8,128)S(1)}, s32[32,32]{1,0:T(8,128)}, u32[]{:S(2)}) copy-start(s32[32,32]{1,0:T(8,128)} %param.17) | copy-start | bytes 12292
  9.5 5.8 %copy-start.7 = (s32[256]{0:T(256)S(1)}, s32[256]{0:T(256)}, u32[]{:S(2)}) copy-start(s32[256]{0:T(256)} %param.19) | copy-start | bytes 3076
  9.5 20.4 %collective-permute-start = (bf16[4,32,256]{2,1,0:T(8,128)(2,1)S(1)}, bf16[4,32,256]{2,1,0:T(8,128)(2,1)S(1)}, u32[]{:S(2)}, u32[]{:S(2)}) collective-permute-start(bf16[4,32,256]{2,1,0:T(8,128)(2,1)S(1)} %get-tuple-element.17), channel_id=1, source_target_pairs={{0,16},{16,32},{32,48},{48,64},{64,80},{80,96},{96,112},{112,128},... | collective-permute-start | bytes 196616 | tf_op jit(solution)/shard_map/ppermute | solution.py:39
  13.4 16.5 %collective-permute-start.1 = (bf16[4,32,256]{2,1,0:T(8,128)(2,1)S(1)}, bf16[4,32,256]{2,1,0:T(8,128)(2,1)S(1)}, u32[]{:S(2)}, u32[]{:S(2)}) collective-permute-start(bf16[4,32,256]{2,1,0:T(8,128)(2,1)S(1)} %get-tuple-element.18), channel_id=1, source_target_pairs={{16,0},{32,16},{48,32},{64,48},{80,64},{96,80},{112,96},{128,112},... | collective-permute-start | bytes 196616 | tf_op jit(solution)/shard_map/ppermute | solution.py:39
  15.5 0.9 copy-start.4
  15.5 1.8 %copy-start.3 = (bf16[4,256,256]{2,1,0:T(8,128)(2,1)S(1)}, bf16[4,256,256]{2,1,0:T(8,128)(2,1)}, u32[]{:S(2)}) copy-start(bf16[4,256,256]{2,1,0:T(8,128)(2,1)} %held.1) | copy-start | bytes 1572868
  16.4 0.7 copy-start.9
  16.4 0.7 copy-start.10
  16.4 0.7 copy-start.11
  18.1 23.7 %all-to-all-start.1 = ((bf16[16,4,16,128]{3,2,1,0:T(8,128)(2,1)}), bf16[16,4,16,128]{3,2,1,0:T(8,128)(2,1)S(1)}, u32[]{:S(2)}, u32[]{:S(2)}) async-start(bf16[16,4,16,128]{3,2,1,0:T(8,128)(2,1)} %shard_map.111), calls=%async_computation.1 | async-start | bytes 524288 | tf_op jit(solution)/shard_map/all_to_all | solution.py:120
  30.0 10.6 %collective-permute-start.2 = (bf16[40,4,256]{2,1,0:T(4,128)(2,1)S(1)}, bf16[40,4,256]{2,1,0:T(4,128)(2,1)S(1)}, u32[]{:S(2)}, u32[]{:S(2)}) collective-permute-start(bf16[40,4,256]{2,1,0:T(4,128)(2,1)S(1)} %pad_maximum_fusion), channel_id=1, source_target_pairs={{0,1},{1,2},{2,3},{3,4},{4,5},{5,6},{6,7},{7,8},{8,9},{9,10},{10,1... | collective-permute-start | bytes 245768 | tf_op jit(solution)/shard_map/ppermute | solution.py:43
  43.8 24.1 %copy-start.1 = (bf16[32,32,256]{2,1,0:T(8,128)(2,1)S(1)}, bf16[32,32,256]{2,1,0:T(8,128)(2,1)}, u32[]{:S(2)}) copy-start(bf16[32,32,256]{2,1,0:T(8,128)(2,1)} %cells.3) | copy-start | bytes 1572868
  43.8 27.5 %all-to-all-start.2 = ((bf16[32,8,16,128]{3,2,1,0:T(8,128)(2,1)}), bf16[32,8,16,128]{3,2,1,0:T(8,128)(2,1)S(1)}, u32[]{:S(2)}, u32[]{:S(2)}) async-start(bf16[32,8,16,128]{3,2,1,0:T(8,128)(2,1)} %shard_map.112), calls=%async_computation.2 | async-start | bytes 2097152 | tf_op jit(solution)/shard_map/all_to_all | solution.py:129
  51.0 16.9 %copy-start.2 = (bf16[256,256]{1,0:T(8,128)(2,1)S(1)}, bf16[256,256]{1,0:T(8,128)(2,1)}, u32[]{:S(2)}) copy-start(bf16[256,256]{1,0:T(8,128)(2,1)} %fecundity.5) | copy-start | bytes 393220
  51.0 4.7 %copy-start.6 = (s32[4,4]{1,0:T(4,128)S(1)}, s32[4,4]{1,0:T(4,128)}, u32[]{:S(2)}) copy-start(s32[4,4]{1,0:T(4,128)} %param.12) | copy-start | bytes 196
  51.1 4.6 %copy-start.8 = (s32[1,1,16]{2,1,0:T(1,128)S(1)}, s32[1,1,16]{2,1,0:T(1,128)}, u32[]{:S(2)}) copy-start(s32[1,1,16]{2,1,0:T(1,128)} %param.13) | copy-start | bytes 196
  51.1 16.8 %collective-permute-start.3 = (bf16[40,4,256]{2,1,0:T(4,128)(2,1)S(1)}, bf16[40,4,256]{2,1,0:T(4,128)(2,1)S(1)}, u32[]{:S(2)}, u32[]{:S(2)}) collective-permute-start(bf16[40,4,256]{2,1,0:T(4,128)(2,1)S(1)} %pad_maximum_fusion.1), channel_id=1, source_target_pairs={{1,0},{2,1},{3,2},{4,3},{5,4},{6,5},{7,6},{8,7},{9,8},{10,9},{11,1... | collective-permute-start | bytes 245768 | tf_op jit(solution)/shard_map/ppermute | solution.py:43
  72.6 6.2 %collective-permute-start.4 = (bf16[4,32,256]{2,1,0:T(8,128)(2,1)S(1)}, bf16[4,32,256]{2,1,0:T(8,128)(2,1)S(1)}, u32[]{:S(2)}, u32[]{:S(2)}) collective-permute-start(bf16[4,32,256]{2,1,0:T(8,128)(2,1)S(1)} %get-tuple-element.22), channel_id=1, source_target_pairs={{0,16},{16,32},{32,48},{48,64},{64,80},{80,96},{96,112},{112,128},... | collective-permute-start | bytes 196616 | tf_op jit(solution)/shard_map/ppermute | solution.py:39
  76.9 6.8 %collective-permute-start.5 = (bf16[4,32,256]{2,1,0:T(8,128)(2,1)S(1)}, bf16[4,32,256]{2,1,0:T(8,128)(2,1)S(1)}, u32[]{:S(2)}, u32[]{:S(2)}) collective-permute-start(bf16[4,32,256]{2,1,0:T(8,128)(2,1)S(1)} %get-tuple-element.24), channel_id=1, source_target_pairs={{16,0},{32,16},{48,32},{64,48},{80,64},{96,80},{112,96},{128,112},... | collective-permute-start | bytes 196616 | tf_op jit(solution)/shard_map/ppermute | solution.py:39
  83.8 12.1 %collective-permute-start.6 = (bf16[40,4,256]{2,1,0:T(4,128)(2,1)S(1)}, bf16[40,4,256]{2,1,0:T(4,128)(2,1)S(1)}, u32[]{:S(2)}, u32[]{:S(2)}) collective-permute-start(bf16[40,4,256]{2,1,0:T(4,128)(2,1)S(1)} %pad_maximum_fusion.2), channel_id=1, source_target_pairs={{0,1},{1,2},{2,3},{3,4},{4,5},{5,6},{6,7},{7,8},{8,9},{9,10},{10,1... | collective-permute-start | bytes 245768 | tf_op jit(solution)/shard_map/ppermute | solution.py:43
  85.8 10.1 %collective-permute-start.7 = (bf16[40,4,256]{2,1,0:T(4,128)(2,1)S(1)}, bf16[40,4,256]{2,1,0:T(4,128)(2,1)S(1)}, u32[]{:S(2)}, u32[]{:S(2)}) collective-permute-start(bf16[40,4,256]{2,1,0:T(4,128)(2,1)S(1)} %pad_maximum_fusion.3), channel_id=1, source_target_pairs={{1,0},{2,1},{3,2},{4,3},{5,4},{6,5},{7,6},{8,7},{9,8},{10,9},{11,1... | collective-permute-start | bytes 245768 | tf_op jit(solution)/shard_map/ppermute | solution.py:43

commit v4 on v3

--- a/solution.py
+++ b/solution.py
@@ -18,6 +18,7 @@
 ROW = ("xl", "yh", "yl", "co")
 COL = ("zh", "zl", "xh")
 NEAR = ("xl", "yl", "co", "zl", "xh")
+WIDE = ("xl", "yl", "co", "zh", "zl", "xh")
 
 DIST_SQ = (0, 1, 2, 4, 5, 8, 9, 10, 13, 16)
 OFFSETS = (1, 4, 4, 4, 8, 4, 4, 8, 8, 4)
@@ -65,41 +66,57 @@
     lax.fori_loop(0, rows, one, 0, unroll=4)
 
 
-def spread_kernel(held, weights, moves, spread):
-    del weights, moves
+def spread_kernel(listed, held, spread):
     mine = (lax.axis_index("xl") * 2 + lax.axis_index("yl")) * 2 + lax.axis_index("co")
-    for k in range(held.shape[0]):
+    lane = lax.broadcasted_iota(jnp.int32, (8, 128), 1)
+    names = jnp.zeros((8, 128), jnp.float32)
+    for k in range(listed.shape[-1]):
+        names = jnp.where(lane == k, listed[0, 0, k].astype(jnp.float32), names)
+    held_at, upper = mine // 2, lax.rem(mine, 2) == 1
+    for group in range(8):
         for near in range(4):
             low, half = divmod(near, 2)
-            at = pl.multiple_of(mine * 32 + low * 16, 16)
-            piece = held[k, pl.ds(at, 16), pl.ds(half * 128, 128)]
+            piece = held[
+                held_at, pl.ds(group * 32 + low * 16, 16), pl.ds(half * 128, 128)
+            ].astype(jnp.float32)
+            part = jnp.where(upper, piece[8:], piece[:8])
+            message = jnp.concatenate([part, names], axis=0).astype(jnp.bfloat16)
             for far in range(4):
-                spread[far * 4 + near, k] = piece
-
-
-def gather_kernel(lists, pieces, left, wanted):
-    del left
+                spread[(group * 4 + far) * 4 + near] = message
+
+
+def gather_kernel(lists, arrived, left, right, weights, moves, wanted):
+    del left, right, weights, moves
     members, count = wanted.shape[:2]
 
     def one(m, carry):
-        found = [pieces[lists[m, 0, k]] for k in range(count)]
+        found = []
+        for k in range(count):
+            name = lists[m, k]
+            at = lax.rem(name, 4) * 32 + name // 4
+            parts = [arrived[at + 16 * h].astype(jnp.float32)[:8] for h in range(2)]
+            found.append(jnp.concatenate(parts, axis=0).astype(jnp.bfloat16))
         for k in range(count):
             wanted[m, k] = found[k]
         return carry
 
-    lax.fori_loop(0, members, one, 0, unroll=4)
+    lax.fori_loop(0, members, one, 0, unroll=2)
 
 
 def fetch(tile_list, harvest_ops, cells, weights, moves):
     rows, cols, cohorts = cells.shape
     count = tile_list.shape[-1]
-    held = harvest_ops.shape[0]
     row_part = jax.ShapeDtypeStruct((RMAX, cols, cohorts), jnp.bfloat16)
     col_part = jax.ShapeDtypeStruct((rows, RMAX, cohorts), jnp.bfloat16)
-    lists = lax.all_to_all(
-        jnp.broadcast_to(jnp.pad(tile_list, ((0, 0), (0, 0), (0, 128 - count))), (32, 1, 128)),
-        NEAR, 0, 0, tiled=True,
-    )
+    spread = pl.pallas_call(
+        spread_kernel,
+        out_shape=jax.ShapeDtypeStruct((128, 16, 128), jnp.bfloat16),
+        in_specs=[SMEM, VMEM],
+        out_specs=VMEM,
+        compiler_params=PARAMS,
+        cost_estimate=pl.CostEstimate(flops=0, bytes_accessed=2**20, transcendentals=0),
+    )(tile_list, harvest_ops)
+    arrived = lax.all_to_all(spread, WIDE, 0, 0, tiled=True)
     first, last, head, tail = pl.pallas_call(
         edges_kernel,
         out_shape=(row_part, row_part, col_part, col_part),
@@ -109,23 +126,17 @@
         cost_estimate=pl.CostEstimate(flops=0, bytes_accessed=2**20, transcendentals=0),
     )(cells)
     top, bottom, left, right = surround(first, last, head, tail)
-    spread = pl.pallas_call(
-        spread_kernel,
-        out_shape=jax.ShapeDtypeStruct((16, held, 16, 128), jnp.bfloat16),
-        in_specs=[VMEM, ANY, ANY],
-        out_specs=VMEM,
-        compiler_params=PARAMS,
-        cost_estimate=pl.CostEstimate(flops=0, bytes_accessed=2**20, transcendentals=0),
-    )(harvest_ops, weights, moves)
-    pieces = lax.all_to_all(spread, COL, 0, 0, tiled=True).reshape(16 * held, 16, 128)
+    lists = lax.dynamic_index_in_dim(
+        arrived.reshape(8, 4, 4, 16, 128), lax.axis_index("zh"), axis=1, keepdims=False
+    )[:, :, 8, :count].astype(jnp.int32).reshape(32, count)
     wanted = pl.pallas_call(
         gather_kernel,
         out_shape=jax.ShapeDtypeStruct((32, count, 16, 128), jnp.bfloat16),
-        in_specs=[SMEM, VMEM, ANY],
+        in_specs=[SMEM, VMEM] + [ANY] * 4,
         out_specs=VMEM,
         compiler_params=PARAMS,
         cost_estimate=pl.CostEstimate(flops=0, bytes_accessed=2**21, transcendentals=0),
-    )(lists, pieces, left)
+    )(lists, arrived, left, right, weights, moves)
     parts = lax.all_to_all(wanted, NEAR, 0, 0, tiled=True)
     return parts, (top, bottom, left, right)
 

time: 99.6 us -> 97.3 us (0.977)
  the two profiles are of different devices: /device:TPU:89 before, /device:TPU:153 now
where the time goes in v4:
time: 97.3 us; the launch traced here: 96.7 us
  starting transfers between devices  52.4 us (54%)
  waiting for transfers between devices  22.3 us (23%)
  Pallas kernels  16.9 us (17%)
  local copies, waits for them, and re-layouts  4.08 us (4%)
    ppermute x4, starting transfers between devices, surround(): top, bottom = (lax.ppermute(last, ROW, down), lax.ppermute(first, ROW, up))  15.5 us
    all_to_all x1, starting transfers between devices, fetch(): arrived = lax.all_to_all(spread, WIDE, 0, 0, tiled=True)  13.8 us
    all_to_all x1, waiting for transfers between devices, fetch(): parts = lax.all_to_all(wanted, NEAR, 0, 0, tiled=True)  10.4 us
    ppermute x2, starting transfers between devices, surround(): lax.ppermute(head, COL, left)  8.77 us
    all_to_all x1, starting transfers between devices, fetch(): parts = lax.all_to_all(wanted, NEAR, 0, 0, tiled=True)  7.61 us
    ppermute x2, starting transfers between devices, surround(): lax.ppermute(tail, COL, right)  6.6 us
    all_to_all x1, waiting for transfers between devices, fetch(): arrived = lax.all_to_all(spread, WIDE, 0, 0, tiled=True)  5.89 us
    ppermute x4, waiting for transfers between devices, surround(): top, bottom = (lax.ppermute(last, ROW, down), lax.ppermute(first, ROW, up))  4.85 us
  transfers between devices with their start and end apart: 10, of which 4 were waited for; matrix products, arithmetic and copies ran while one was open for 1% of the time, Pallas kernels for 10%

profile of v4, /device:TPU:153, one launch (start us, length us, event | category | flops | bytes accessed | tf_op | source)
XLA Modules:
  0.0 96.7 jit_solution(2207891612052769042)
XLA Ops:
  0.0 0.0 copy-start
  0.0 1.0 %copy-done = bf16[32,32,256]{2,1,0:T(8,128)(2,1)S(1)} copy-done((bf16[32,32,256]{2,1,0:T(8,128)(2,1)S(1)}, bf16[32,32,256]{2,1,0:T(8,128)(2,1)}, u32[]{:S(2)}) %copy-start) | copy-done | bytes 524312
  1.0 0.0 copy-start.3
  1.0 0.1 shard_map.109
  1.1 0.0 copy-start.4
  1.1 5.1 %collective-permute-start = (bf16[4,32,256]{2,1,0:T(8,128)(2,1)S(1)}, bf16[4,32,256]{2,1,0:T(8,128)(2,1)S(1)}, u32[]{:S(2)}, u32[]{:S(2)}) collective-permute-start(bf16[4,32,256]{2,1,0:T(8,128)(2,1)S(1)} %get-tuple-element.17), channel_id=1, source_target_pairs={{0,16},{16,32},{32,48},{48,64},{64,80},{80,96},{96,112},{112,128},... | collective-permute-start | bytes 196616 | tf_op jit(solution)/shard_map/ppermute | solution.py:40
  6.2 1.9 %collective-permute-start.1 = (bf16[4,32,256]{2,1,0:T(8,128)(2,1)S(1)}, bf16[4,32,256]{2,1,0:T(8,128)(2,1)S(1)}, u32[]{:S(2)}, u32[]{:S(2)}) collective-permute-start(bf16[4,32,256]{2,1,0:T(8,128)(2,1)S(1)} %get-tuple-element.18), channel_id=1, source_target_pairs={{16,0},{32,16},{48,32},{64,48},{80,64},{96,80},{112,96},{128,112},... | collective-permute-start | bytes 196616 | tf_op jit(solution)/shard_map/ppermute | solution.py:40
  8.2 0.0 copy-done.3
  8.2 0.0 copy-done.4
  8.2 1.4 %shard_map.111 = bf16[128,16,128]{2,1,0:T(8,128)(2,1)} custom-call(s32[1,1,8]{2,1,0:T(1,128)S(1)} %copy-done.4, bf16[4,256,256]{2,1,0:T(8,128)(2,1)S(1)} %copy-done.3), custom_call_target="tpu_custom_call" | custom-call | bytes 1048576 | tf_op jit(solution)/shard_map/pallas_call | solution.py:111
  9.6 0.0 copy-start.6
  9.6 13.8 %all-to-all-start = ((bf16[128,16,128]{2,1,0:T(8,128)(2,1)}), bf16[128,16,128]{2,1,0:T(8,128)(2,1)S(1)}, u32[]{:S(2)}, u32[]{:S(2)}) async-start(bf16[128,16,128]{2,1,0:T(8,128)(2,1)} %shard_map.111), calls=%async_computation | async-start | bytes 1048576 | tf_op jit(solution)/shard_map/all_to_all | solution.py:119
  23.4 0.0 copy-done.6
  23.5 0.1 copy.18
  23.6 0.0 copy-start.5
  23.6 0.1 copy.19
  23.7 0.8 copy-done.5
  24.5 0.0 copy-start.8
  24.5 0.6 copy-done.8
  25.2 0.0 copy-start.10
  25.2 0.0 copy-start.11
  25.2 0.0 copy-start.12
  25.2 0.6 copy-done.10
  25.8 0.0 copy-done.11
  25.8 0.0 copy-done.12
  25.9 0.1 multiply_reduce_fusion
  26.0 0.1 fusion.1.weights
  26.0 0.0 collective-permute-done.top
  26.1 0.0 collective-permute-done.1.bottom
  26.1 0.1 pad_maximum_fusion
  26.2 4.6 %collective-permute-start.2 = (bf16[40,4,256]{2,1,0:T(4,128)(2,1)S(1)}, bf16[40,4,256]{2,1,0:T(4,128)(2,1)S(1)}, u32[]{:S(2)}, u32[]{:S(2)}) collective-permute-start(bf16[40,4,256]{2,1,0:T(4,128)(2,1)S(1)} %pad_maximum_fusion), channel_id=1, source_target_pairs={{0,1},{1,2},{2,3},{3,4},{4,5},{5,6},{6,7},{7,8},{8,9},{9,10},{10,1... | collective-permute-start | bytes 245768 | tf_op jit(solution)/shard_map/ppermute | solution.py:44
  30.8 0.1 pad_maximum_fusion.1
  30.9 3.1 %collective-permute-start.3 = (bf16[40,4,256]{2,1,0:T(4,128)(2,1)S(1)}, bf16[40,4,256]{2,1,0:T(4,128)(2,1)S(1)}, u32[]{:S(2)}, u32[]{:S(2)}) collective-permute-start(bf16[40,4,256]{2,1,0:T(4,128)(2,1)S(1)} %pad_maximum_fusion.1), channel_id=1, source_target_pairs={{1,0},{2,1},{3,2},{4,3},{5,4},{6,5},{7,6},{8,7},{9,8},{10,9},{11,1... | collective-permute-start | bytes 245768 | tf_op jit(solution)/shard_map/ppermute | solution.py:44
  33.9 5.9 %all-to-all-done.arrived = bf16[128,16,128]{2,1,0:T(8,128)(2,1)S(1)} async-done(((bf16[128,16,128]{2,1,0:T(8,128)(2,1)}), bf16[128,16,128]{2,1,0:T(8,128)(2,1)S(1)}, u32[]{:S(2)}, u32[]{:S(2)}) %all-to-all-start) | async-done | bytes 524320 | tf_op jit(solution)/shard_map/all_to_all | solution.py:119
  39.9 0.0 collective-permute-done.2.left
  39.9 1.2 %collective-permute-done.3.right = bf16[40,4,256]{2,1,0:T(4,128)(2,1)S(1)} collective-permute-done((bf16[40,4,256]{2,1,0:T(4,128)(2,1)S(1)}, bf16[40,4,256]{2,1,0:T(4,128)(2,1)S(1)}, u32[]{:S(2)}, u32[]{:S(2)}) %collective-permute-start.3) | collective-permute-done | bytes 81952 | tf_op jit(solution)/shard_map/ppermute | solution.py:44
  41.1 3.4 %shard_map.112 = bf16[32,8,16,128]{3,2,1,0:T(8,128)(2,1)} custom-call(s32[32,8]{1,0:T(8,128)S(1)} %bitcast.12, bf16[128,16,128]{2,1,0:T(8,128)(2,1)S(1)} %all-to-all-done.arrived, bf16[40,4,256]{2,1,0:T(4,128)(2,1)S(1)} %collective-permute-done.2.left, bf16[40,4,256]{2,1,0:T(4,128)(2,1)S(1)} %collective-permute-done.3.right, f32[10,256]{1,0:T(8,128)S(1)} %fusion.1.weights, ...), custom_call_target="tpu_custom_call" | custom-call | bytes 2097152 | tf_op jit(solution)/shard_map/pallas_call | solution.py:132
  44.4 0.0 copy-start.7
  44.4 0.0 copy-start.1
  44.4 0.0 copy-start.2
  44.5 7.6 %all-to-all-start.1 = ((bf16[32,8,16,128]{3,2,1,0:T(8,128)(2,1)}), bf16[32,8,16,128]{3,2,1,0:T(8,128)(2,1)S(1)}, u32[]{:S(2)}, u32[]{:S(2)}) async-start(bf16[32,8,16,128]{3,2,1,0:T(8,128)(2,1)} %shard_map.112), calls=%async_computation.1 | async-start | bytes 2097152 | tf_op jit(solution)/shard_map/all_to_all | solution.py:140
  52.1 0.0 copy-start.9
  52.1 0.0 copy-done.7
  52.1 0.6 copy-done.9
  52.7 0.2 select_reduce_fusion.slots
  52.9 0.0 copy-done.1
  52.9 0.0 copy-done.2
  53.0 3.4 %shard_map.110.grown = bf16[32,32,256]{2,1,0:T(8,128)(2,1)S(1)} custom-call(bf16[32,32,256]{2,1,0:T(8,128)(2,1)S(1)} %copy-done.1, bf16[4,32,256]{2,1,0:T(8,128)(2,1)S(1)} %collective-permute-done.top, bf16[4,32,256]{2,1,0:T(8,128)(2,1)S(1)} %collective-permute-done.1.bottom, bf16[40,4,256]{2,1,0:T(4,128)(2,1)S(1)} %collective-permute-done.2.left, ...), custom_call_target="tpu_custom_call" | custom-call | flops 268435456 | bytes 16777216 | tf_op jit(solution)/shard_map/pallas_call | solution.py:380
  56.4 10.4 %all-to-all-done.1.parts = bf16[32,8,16,128]{3,2,1,0:T(8,128)(2,1)S(1)} async-done(((bf16[32,8,16,128]{3,2,1,0:T(8,128)(2,1)}), bf16[32,8,16,128]{3,2,1,0:T(8,128)(2,1)S(1)}, u32[]{:S(2)}, u32[]{:S(2)}) %all-to-all-start.1) | async-done | bytes 1048608 | tf_op jit(solution)/shard_map/all_to_all | solution.py:140
  66.8 1.2 %shard_map.113 = (bf16[32,32,256]{2,1,0:T(8,128)(2,1)S(1)}, bf16[8,256,256]{2,1,0:T(8,128)(2,1)S(1)}, bf16[4,32,256]{2,1,0:T(8,128)(2,1)S(1)}, bf16[4,32,256]{2,...) custom-call(s32[4,4]{1,0:T(4,128)S(1)} %select_reduce_fusion.slots, ...), custom_call_target="tpu_custom_call" | custom-call | flops 268435456 | bytes 4194304 | tf_op jit(solution)/shard_map/pallas_call | solution.py:391
  68.0 6.6 %collective-permute-start.4 = (bf16[4,32,256]{2,1,0:T(8,128)(2,1)S(1)}, bf16[4,32,256]{2,1,0:T(8,128)(2,1)S(1)}, u32[]{:S(2)}, u32[]{:S(2)}) collective-permute-start(bf16[4,32,256]{2,1,0:T(8,128)(2,1)S(1)} %get-tuple-element.22), channel_id=1, source_target_pairs={{0,16},{16,32},{32,48},{48,64},{64,80},{80,96},{96,112},{112,128},... | collective-permute-start | bytes 196616 | tf_op jit(solution)/shard_map/ppermute | solution.py:40
  74.6 1.9 %collective-permute-start.5 = (bf16[4,32,256]{2,1,0:T(8,128)(2,1)S(1)}, bf16[4,32,256]{2,1,0:T(8,128)(2,1)S(1)}, u32[]{:S(2)}, u32[]{:S(2)}) collective-permute-start(bf16[4,32,256]{2,1,0:T(8,128)(2,1)S(1)} %get-tuple-element.24), channel_id=1, source_target_pairs={{16,0},{32,16},{48,32},{64,48},{80,64},{96,80},{112,96},{128,112},... | collective-permute-start | bytes 196616 | tf_op jit(solution)/shard_map/ppermute | solution.py:40
  76.5 0.0 collective-permute-done.4.top
  76.6 4.8 %collective-permute-done.5.bottom = bf16[4,32,256]{2,1,0:T(8,128)(2,1)S(1)} collective-permute-done((bf16[4,32,256]{2,1,0:T(8,128)(2,1)S(1)}, bf16[4,32,256]{2,1,0:T(8,128)(2,1)S(1)}, u32[]{:S(2)}, u32[]{:S(2)}) %collective-permute-start.5) | collective-permute-done | bytes 65568 | tf_op jit(solution)/shard_map/ppermute | solution.py:40
  81.4 0.1 pad_maximum_fusion.2
  81.5 2.0 %collective-permute-start.6 = (bf16[40,4,256]{2,1,0:T(4,128)(2,1)S(1)}, bf16[40,4,256]{2,1,0:T(4,128)(2,1)S(1)}, u32[]{:S(2)}, u32[]{:S(2)}) collective-permute-start(bf16[40,4,256]{2,1,0:T(4,128)(2,1)S(1)} %pad_maximum_fusion.2), channel_id=1, source_target_pairs={{0,1},{1,2},{2,3},{3,4},{4,5},{5,6},{6,7},{7,8},{8,9},{9,10},{10,1... | collective-permute-start | bytes 245768 | tf_op jit(solution)/shard_map/ppermute | solution.py:44
  83.5 0.1 pad_maximum_fusion.3
  83.6 5.7 %collective-permute-start.7 = (bf16[40,4,256]{2,1,0:T(4,128)(2,1)S(1)}, bf16[40,4,256]{2,1,0:T(4,128)(2,1)S(1)}, u32[]{:S(2)}, u32[]{:S(2)}) collective-permute-start(bf16[40,4,256]{2,1,0:T(4,128)(2,1)S(1)} %pad_maximum_fusion.3), channel_id=1, source_target_pairs={{1,0},{2,1},{3,2},{4,3},{5,4},{6,5},{7,6},{8,7},{9,8},{10,9},{11,1... | collective-permute-start | bytes 245768 | tf_op jit(solution)/shard_map/ppermute | solution.py:44
  89.3 4.4 %shard_map.114 = (bf16[32,16,256]{2,1,0:T(8,128)(2,1)S(1)}, f32[32,16,256]{2,1,0:T(8,128)S(1)}) custom-call(s32[4,4]{1,0:T(4,128)S(1)} %select_reduce_fusion.slots, bf16[32,32,256]{2,1,0:T(8,128)(2,1)S(1)} %get-tuple-element.21.cells, bf16[4,32,256]{2,1,0:T(8,128)(2,1)S(1)} %collective-permute-done.4.top, ...), custom_call_target="tpu_custom_call" | custom-call | flops 268435456 | bytes 16777216 | tf_op jit(solution)/shard_map/pallas_call | solution.py:402
  93.6 0.0 collective-permute-done.6.left
  93.6 0.0 collective-permute-done.7.right
  93.7 3.0 %shard_map.115 = bf16[32,32,256]{2,1,0:T(8,128)(2,1)} custom-call(s32[4,4]{1,0:T(4,128)S(1)} %select_reduce_fusion.slots, bf16[32,32,256]{2,1,0:T(8,128)(2,1)S(1)} %get-tuple-element.21.cells, bf16[40,4,256]{2,1,0:T(4,128)(2,1)S(1)} %collective-permute-done.6.left, bf16[40,4,256]{2,1,0:T(4,128)(2,1)S(1)} %collective-permute-done.7.right, ...), custom_call_target="tpu_custom_call" | custom-call | flops 268435456 | bytes 4194304 | tf_op jit(solution)/shard_map/pallas_call | solution.py:414
  (11 shorter events, 0.1 us)
Async XLA Ops:
  0.0 1.0 %copy-start = (bf16[32,32,256]{2,1,0:T(8,128)(2,1)S(1)}, bf16[32,32,256]{2,1,0:T(8,128)(2,1)}, u32[]{:S(2)}) copy-start(bf16[32,32,256]{2,1,0:T(8,128)(2,1)} %cells.3) | copy-start | bytes 1572868
  1.0 7.1 %copy-start.3 = (bf16[4,256,256]{2,1,0:T(8,128)(2,1)S(1)}, bf16[4,256,256]{2,1,0:T(8,128)(2,1)}, u32[]{:S(2)}) copy-start(bf16[4,256,256]{2,1,0:T(8,128)(2,1)} %held.1) | copy-start | bytes 1572868
  1.1 7.1 %copy-start.4 = (s32[1,1,8]{2,1,0:T(1,128)S(1)}, s32[1,1,8]{2,1,0:T(1,128)}, u32[]{:S(2)}) copy-start(s32[1,1,8]{2,1,0:T(1,128)} %listed.1) | copy-start | bytes 100
  1.1 24.9 %collective-permute-start = (bf16[4,32,256]{2,1,0:T(8,128)(2,1)S(1)}, bf16[4,32,256]{2,1,0:T(8,128)(2,1)S(1)}, u32[]{:S(2)}, u32[]{:S(2)}) collective-permute-start(bf16[4,32,256]{2,1,0:T(8,128)(2,1)S(1)} %get-tuple-element.17), channel_id=1, source_target_pairs={{0,16},{16,32},{32,48},{48,64},{64,80},{80,96},{96,112},{112,128},... | collective-permute-start | bytes 196616 | tf_op jit(solution)/shard_map/ppermute | solution.py:40
  6.2 19.8 %collective-permute-start.1 = (bf16[4,32,256]{2,1,0:T(8,128)(2,1)S(1)}, bf16[4,32,256]{2,1,0:T(8,128)(2,1)S(1)}, u32[]{:S(2)}, u32[]{:S(2)}) collective-permute-start(bf16[4,32,256]{2,1,0:T(8,128)(2,1)S(1)} %get-tuple-element.18), channel_id=1, source_target_pairs={{16,0},{32,16},{48,32},{64,48},{80,64},{96,80},{112,96},{128,112},... | collective-permute-start | bytes 196616 | tf_op jit(solution)/shard_map/ppermute | solution.py:40
  9.6 13.9 %copy-start.6 = (s32[32,32]{1,0:T(8,128)S(1)}, s32[32,32]{1,0:T(8,128)}, u32[]{:S(2)}) copy-start(s32[32,32]{1,0:T(8,128)} %param.17) | copy-start | bytes 12292
  9.6 30.2 %all-to-all-start = ((bf16[128,16,128]{2,1,0:T(8,128)(2,1)}), bf16[128,16,128]{2,1,0:T(8,128)(2,1)S(1)}, u32[]{:S(2)}, u32[]{:S(2)}) async-start(bf16[128,16,128]{2,1,0:T(8,128)(2,1)} %shard_map.111), calls=%async_computation | async-start | bytes 1048576 | tf_op jit(solution)/shard_map/all_to_all | solution.py:119
  23.6 0.9 copy-start.5
  24.5 0.7 copy-start.8
  25.2 0.7 copy-start.10
  25.2 0.7 copy-start.11
  25.2 0.7 copy-start.12
  26.2 13.7 %collective-permute-start.2 = (bf16[40,4,256]{2,1,0:T(4,128)(2,1)S(1)}, bf16[40,4,256]{2,1,0:T(4,128)(2,1)S(1)}, u32[]{:S(2)}, u32[]{:S(2)}) collective-permute-start(bf16[40,4,256]{2,1,0:T(4,128)(2,1)S(1)} %pad_maximum_fusion), channel_id=1, source_target_pairs={{0,1},{1,2},{2,3},{3,4},{4,5},{5,6},{6,7},{7,8},{8,9},{9,10},{10,1... | collective-permute-start | bytes 245768 | tf_op jit(solution)/shard_map/ppermute | solution.py:44
  30.9 10.2 %collective-permute-start.3 = (bf16[40,4,256]{2,1,0:T(4,128)(2,1)S(1)}, bf16[40,4,256]{2,1,0:T(4,128)(2,1)S(1)}, u32[]{:S(2)}, u32[]{:S(2)}) collective-permute-start(bf16[40,4,256]{2,1,0:T(4,128)(2,1)S(1)} %pad_maximum_fusion.1), channel_id=1, source_target_pairs={{1,0},{2,1},{3,2},{4,3},{5,4},{6,5},{7,6},{8,7},{9,8},{10,9},{11,1... | collective-permute-start | bytes 245768 | tf_op jit(solution)/shard_map/ppermute | solution.py:44
  44.4 7.6 %copy-start.7 = (s32[4,4]{1,0:T(4,128)S(1)}, s32[4,4]{1,0:T(4,128)}, u32[]{:S(2)}) copy-start(s32[4,4]{1,0:T(4,128)} %param.12) | copy-start | bytes 196
  44.4 8.5 %copy-start.1 = (bf16[32,32,256]{2,1,0:T(8,128)(2,1)S(1)}, bf16[32,32,256]{2,1,0:T(8,128)(2,1)}, u32[]{:S(2)}) copy-start(bf16[32,32,256]{2,1,0:T(8,128)(2,1)} %cells.3) | copy-start | bytes 1572868
  44.4 8.5 %copy-start.2 = (bf16[256,256]{1,0:T(8,128)(2,1)S(1)}, bf16[256,256]{1,0:T(8,128)(2,1)}, u32[]{:S(2)}) copy-start(bf16[256,256]{1,0:T(8,128)(2,1)} %fecundity.5) | copy-start | bytes 393220
  44.5 22.3 %all-to-all-start.1 = ((bf16[32,8,16,128]{3,2,1,0:T(8,128)(2,1)}), bf16[32,8,16,128]{3,2,1,0:T(8,128)(2,1)S(1)}, u32[]{:S(2)}, u32[]{:S(2)}) async-start(bf16[32,8,16,128]{3,2,1,0:T(8,128)(2,1)} %shard_map.112), calls=%async_computation.1 | async-start | bytes 2097152 | tf_op jit(solution)/shard_map/all_to_all | solution.py:140
  52.1 0.7 copy-start.9
  68.0 8.5 %collective-permute-start.4 = (bf16[4,32,256]{2,1,0:T(8,128)(2,1)S(1)}, bf16[4,32,256]{2,1,0:T(8,128)(2,1)S(1)}, u32[]{:S(2)}, u32[]{:S(2)}) collective-permute-start(bf16[4,32,256]{2,1,0:T(8,128)(2,1)S(1)} %get-tuple-element.22), channel_id=1, source_target_pairs={{0,16},{16,32},{32,48},{48,64},{64,80},{80,96},{96,112},{112,128},... | collective-permute-start | bytes 196616 | tf_op jit(solution)/shard_map/ppermute | solution.py:40
  74.6 6.8 %collective-permute-start.5 = (bf16[4,32,256]{2,1,0:T(8,128)(2,1)S(1)}, bf16[4,32,256]{2,1,0:T(8,128)(2,1)S(1)}, u32[]{:S(2)}, u32[]{:S(2)}) collective-permute-start(bf16[4,32,256]{2,1,0:T(8,128)(2,1)S(1)} %get-tuple-element.24), channel_id=1, source_target_pairs={{16,0},{32,16},{48,32},{64,48},{80,64},{96,80},{112,96},{128,112},... | collective-permute-start | bytes 196616 | tf_op jit(solution)/shard_map/ppermute | solution.py:40
  81.5 12.1 %collective-permute-start.6 = (bf16[40,4,256]{2,1,0:T(4,128)(2,1)S(1)}, bf16[40,4,256]{2,1,0:T(4,128)(2,1)S(1)}, u32[]{:S(2)}, u32[]{:S(2)}) collective-permute-start(bf16[40,4,256]{2,1,0:T(4,128)(2,1)S(1)} %pad_maximum_fusion.2), channel_id=1, source_target_pairs={{0,1},{1,2},{2,3},{3,4},{4,5},{5,6},{6,7},{7,8},{8,9},{9,10},{10,1... | collective-permute-start | bytes 245768 | tf_op jit(solution)/shard_map/ppermute | solution.py:44
  83.6 10.1 %collective-permute-start.7 = (bf16[40,4,256]{2,1,0:T(4,128)(2,1)S(1)}, bf16[40,4,256]{2,1,0:T(4,128)(2,1)S(1)}, u32[]{:S(2)}, u32[]{:S(2)}) collective-permute-start(bf16[40,4,256]{2,1,0:T(4,128)(2,1)S(1)} %pad_maximum_fusion.3), channel_id=1, source_target_pairs={{1,0},{2,1},{3,2},{4,3},{5,4},{6,5},{7,6},{8,7},{9,8},{10,9},{11,1... | collective-permute-start | bytes 245768 | tf_op jit(solution)/shard_map/ppermute | solution.py:44

commit v5 on v4

--- a/solution.py
+++ b/solution.py
@@ -35,13 +35,16 @@
     return [(i, i + 1) for i in range(count - 1)], [(i + 1, i) for i in range(count - 1)]
 
 
+def swap(head, tail, axis):
+    after, before = shift_pairs(math.prod(lax.axis_size(name) for name in axis))
+    return lax.ppermute(tail, axis, after), lax.ppermute(head, axis, before)
+
+
 def surround(first, last, head, tail):
-    down, up = shift_pairs(math.prod(lax.axis_size(name) for name in ROW))
-    top, bottom = lax.ppermute(last, ROW, down), lax.ppermute(first, ROW, up)
+    top, bottom = swap(first, last, ROW)
     head = jnp.concatenate([top[:, :RMAX], head, bottom[:, :RMAX]], axis=0)
     tail = jnp.concatenate([top[:, -RMAX:], tail, bottom[:, -RMAX:]], axis=0)
-    right, left = shift_pairs(math.prod(lax.axis_size(name) for name in COL))
-    return top, bottom, lax.ppermute(tail, COL, right), lax.ppermute(head, COL, left)
+    return (top, bottom) + swap(head, tail, COL)
 
 
 def class_weights(radius):
@@ -52,10 +55,9 @@
     return values / total
 
 
-def edges_kernel(cells, first, last, head, tail):
+def sides_kernel(cells, spread, head, tail):
+    del spread
     rows, cols, _ = cells.shape
-    first[...] = cells[pl.ds(0, RMAX)]
-    last[...] = cells[pl.ds(rows - RMAX, RMAX)]
 
     def one(x, carry):
         row = cells[x].astype(jnp.float32)
@@ -66,21 +68,28 @@
     lax.fori_loop(0, rows, one, 0, unroll=4)
 
 
+def rows_kernel(cells, left, right, first, last):
+    rows = cells.shape[0]
+    for out, start in ((first, 0), (last, rows - RMAX)):
+        for i in range(RMAX):
+            parts = [left[start + i], cells[start + i], right[start + i]]
+            whole = jnp.concatenate([part.astype(jnp.float32) for part in parts], axis=0)
+            out[i] = whole.astype(jnp.bfloat16)
+
+
 def spread_kernel(listed, held, spread):
     mine = (lax.axis_index("xl") * 2 + lax.axis_index("yl")) * 2 + lax.axis_index("co")
-    lane = lax.broadcasted_iota(jnp.int32, (8, 128), 1)
-    names = jnp.zeros((8, 128), jnp.float32)
+    lane = lax.broadcasted_iota(jnp.int32, (16, 128), 1)
+    names = jnp.zeros((16, 128), jnp.float32)
     for k in range(listed.shape[-1]):
-        names = jnp.where(lane == k, listed[0, 0, k].astype(jnp.float32), names)
-    held_at, upper = mine // 2, lax.rem(mine, 2) == 1
+        names = jnp.where(lax.rem(lane, 64) == k, listed[0, 0, k].astype(jnp.float32), names)
+    held_at, upper = mine // 2, lax.rem(mine, 2)
+    sent = lane // 64 == upper
     for group in range(8):
         for near in range(4):
             low, half = divmod(near, 2)
-            piece = held[
-                held_at, pl.ds(group * 32 + low * 16, 16), pl.ds(half * 128, 128)
-            ].astype(jnp.float32)
-            part = jnp.where(upper, piece[8:], piece[:8])
-            message = jnp.concatenate([part, names], axis=0).astype(jnp.bfloat16)
+            piece = held[held_at, pl.ds(group * 32 + low * 16, 16), pl.ds(half * 128, 128)]
+            message = jnp.where(sent, piece.astype(jnp.float32), names).astype(jnp.bfloat16)
             for far in range(4):
                 spread[(group * 4 + far) * 4 + near] = message
 
@@ -88,14 +97,14 @@
 def gather_kernel(lists, arrived, left, right, weights, moves, wanted):
     del left, right, weights, moves
     members, count = wanted.shape[:2]
+    lower = lax.broadcasted_iota(jnp.int32, (16, 128), 1) < 64
 
     def one(m, carry):
         found = []
         for k in range(count):
             name = lists[m, k]
             at = lax.rem(name, 4) * 32 + name // 4
-            parts = [arrived[at + 16 * h].astype(jnp.float32)[:8] for h in range(2)]
-            found.append(jnp.concatenate(parts, axis=0).astype(jnp.bfloat16))
+            found.append(jnp.where(lower, arrived[at], arrived[at + 16]))
         for k in range(count):
             wanted[m, k] = found[k]
         return carry
@@ -106,36 +115,48 @@
 def fetch(tile_list, harvest_ops, cells, weights, moves):
     rows, cols, cohorts = cells.shape
     count = tile_list.shape[-1]
-    row_part = jax.ShapeDtypeStruct((RMAX, cols, cohorts), jnp.bfloat16)
     col_part = jax.ShapeDtypeStruct((rows, RMAX, cohorts), jnp.bfloat16)
+    row_part = jax.ShapeDtypeStruct((RMAX, cols + 2 * RMAX, cohorts), jnp.bfloat16)
+    small = pl.CostEstimate(flops=0, bytes_accessed=2**20, transcendentals=0)
     spread = pl.pallas_call(
         spread_kernel,
         out_shape=jax.ShapeDtypeStruct((128, 16, 128), jnp.bfloat16),
         in_specs=[SMEM, VMEM],
         out_specs=VMEM,
         compiler_params=PARAMS,
-        cost_estimate=pl.CostEstimate(flops=0, bytes_accessed=2**20, transcendentals=0),
+        cost_estimate=small,
     )(tile_list, harvest_ops)
     arrived = lax.all_to_all(spread, WIDE, 0, 0, tiled=True)
-    first, last, head, tail = pl.pallas_call(
-        edges_kernel,
-        out_shape=(row_part, row_part, col_part, col_part),
-        in_specs=[VMEM],
-        out_specs=(VMEM,) * 4,
-        compiler_params=PARAMS,
-        cost_estimate=pl.CostEstimate(flops=0, bytes_accessed=2**20, transcendentals=0),
-    )(cells)
-    top, bottom, left, right = surround(first, last, head, tail)
-    lists = lax.dynamic_index_in_dim(
+    head, tail = pl.pallas_call(
+        sides_kernel,
+        out_shape=(col_part, col_part),
+        in_specs=[VMEM, ANY],
+        out_specs=(VMEM,) * 2,
+        compiler_params=PARAMS,
+        cost_estimate=small,
+    )(cells, spread)
+    left, right = swap(head, tail, COL)
+    first, last = pl.pallas_call(
+        rows_kernel,
+        out_shape=(row_part, row_part),
+        in_specs=[VMEM] * 3,
+        out_specs=(VMEM,) * 2,
+        compiler_params=PARAMS,
+        cost_estimate=small,
+    )(cells, left, right)
+    top, bottom = swap(first, last, ROW)
+    own = lax.dynamic_index_in_dim(
         arrived.reshape(8, 4, 4, 16, 128), lax.axis_index("zh"), axis=1, keepdims=False
-    )[:, :, 8, :count].astype(jnp.int32).reshape(32, count)
+    )[:, :, 0].astype(jnp.int32)
+    even = jnp.arange(8)[:, None, None] % 2 == 0
+    lists = jnp.where(even, own[:, :, 64 : 64 + count], own[:, :, :count]).reshape(32, count)
     wanted = pl.pallas_call(
         gather_kernel,
         out_shape=jax.ShapeDtypeStruct((32, count, 16, 128), jnp.bfloat16),
         in_specs=[SMEM, VMEM] + [ANY] * 4,
         out_specs=VMEM,
         compiler_params=PARAMS,
-        cost_estimate=pl.CostEstimate(flops=0, bytes_accessed=2**21, transcendentals=0),
+        cost_estimate=small,
     )(lists, arrived, left, right, weights, moves)
     parts = lax.all_to_all(wanted, NEAR, 0, 0, tiled=True)
     return parts, (top, bottom, left, right)
@@ -143,9 +164,11 @@
 
 def fill_rows(cells, top, bottom, padded):
     rows, cols, _ = cells.shape
+    wide = top.shape[1]
     for part, start in ((top, 0), (bottom, RMAX + rows)):
         for i in range(RMAX):
-            padded[start + i, pl.ds(LEAD, cols), :] = part[i].astype(jnp.float32)
+            at = pl.ds(LEAD - (wide - cols) // 2, wide)
+            padded[start + i, at, :] = part[i].astype(jnp.float32)
 
     def fill(x, carry):
         padded[RMAX + x, pl.ds(LEAD, cols), :] = cells[x].astype(jnp.float32)
@@ -154,16 +177,32 @@
     lax.fori_loop(0, rows, fill, 0, unroll=4)
 
 
-def fill_sides(left, right, padded, pairs):
-    high, cols, cohorts = pairs.shape[1:]
-
-    def one(x, carry):
-        if left is None:
-            before = after = jnp.zeros((RMAX, cohorts), jnp.float32)
-        else:
-            before, after = left[x].astype(jnp.float32), right[x].astype(jnp.float32)
-        padded[x, pl.ds(LEAD - RMAX, RMAX), :] = before
-        padded[x, pl.ds(LEAD + cols, RMAX), :] = after
+def fill_sides(left, right, padded):
+    def one(x, carry):
+        at = RMAX + x
+        cols = padded.shape[1] - 2 * LEAD
+        padded[at, pl.ds(LEAD - RMAX, RMAX), :] = left[x].astype(jnp.float32)
+        padded[at, pl.ds(LEAD + cols, RMAX), :] = right[x].astype(jnp.float32)
+        return carry
+
+    lax.fori_loop(0, left.shape[0], one, 0, unroll=4)
+
+
+def clear_sides(padded):
+    gap = jnp.zeros((RMAX, padded.shape[2]), jnp.float32)
+
+    def one(x, carry):
+        padded[x, pl.ds(LEAD - RMAX, RMAX), :] = gap
+        padded[x, pl.ds(padded.shape[1] - LEAD, RMAX), :] = gap
+        return carry
+
+    lax.fori_loop(0, padded.shape[0], one, 0, unroll=4)
+
+
+def add_pairs(padded, pairs):
+    high, cols, _ = pairs.shape[1:]
+
+    def one(x, carry):
         for b in range(1, RMAX + 1):
             pairs[b - 1, x] = (
                 padded[x, pl.ds(LEAD - b, cols), :] + padded[x, pl.ds(LEAD + b, cols), :]
@@ -238,7 +277,8 @@
 def first_kernel(cells, top, bottom, left, right, weights, fecundity, moves, grown, padded, pairs, seeds):
     rows, cols, cohorts = cells.shape
     fill_rows(cells, top, bottom, padded)
-    fill_sides(left, right, padded, pairs)
+    fill_sides(left, right, padded)
+    add_pairs(padded, pairs)
 
     def row_sum(x, b):
         return padded[x, pl.ds(LEAD, cols), :] if b == 0 else pairs[b - 1, x]
@@ -280,7 +320,8 @@
 ):
     rows, cols, cohorts = cells.shape
     fill_rows(cells, top, bottom, padded)
-    fill_sides(None, None, padded, pairs)
+    clear_sides(padded)
+    add_pairs(padded, pairs)
 
     def row_sum(x, b):
         return padded[x, pl.ds(LEAD, cols), :] if b == 0 else pairs[b - 1, x]

time: 97.3 us -> 89.8 us (0.923)
  the two profiles are of different devices: /device:TPU:153 before, /device:TPU:1 now
where the time goes in v5:
time: 89.8 us; the launch traced here: 89.2 us
  starting transfers between devices  45 us (50%)
  waiting for transfers between devices  22.9 us (26%)
  Pallas kernels  17 us (19%)
  local copies, waits for them, and re-layouts  3.33 us (4%)
    ppermute x8, starting transfers between devices, swap(): return (lax.ppermute(tail, axis, after), lax.ppermute(head, axis, before))  22 us
    all_to_all x1, starting transfers between devices, fetch(): arrived = lax.all_to_all(spread, WIDE, 0, 0, tiled=True)  16.8 us
    ppermute x8, waiting for transfers between devices, swap(): return (lax.ppermute(tail, axis, after), lax.ppermute(head, axis, before))  13.5 us
    all_to_all x1, waiting for transfers between devices, fetch(): arrived = lax.all_to_all(spread, WIDE, 0, 0, tiled=True)  9.4 us
    all_to_all x1, starting transfers between devices, fetch(): parts = lax.all_to_all(wanted, NEAR, 0, 0, tiled=True)  6.23 us
    pallas_call x1, Pallas kernels, local(): pl.pallas_call(middle_kernel, out_shape=(jax.ShapeDtypeStruct((rows, cols...  4.39 us
    pallas_call x1, Pallas kernels, local(): pl.pallas_call(first_kernel, out_shape=state, in_specs=[VMEM] * 8, out_sp...  3.41 us
    pallas_call x1, Pallas kernels, fetch(): pl.pallas_call(gather_kernel, out_shape=jax.ShapeDtypeStruct((32, count,...  3.39 us
  transfers between devices with their start and end apart: 10, of which 5 were waited for; matrix products, arithmetic and copies ran while one was open for 1% of the time, Pallas kernels for 9%

profile of v5, /device:TPU:1, one launch (start us, length us, event | category | flops | bytes accessed | tf_op | source)
XLA Modules:
  0.0 89.2 jit_solution(10456091874897420569)
XLA Ops:
  0.0 0.0 copy-start.2
  0.0 1.0 %copy-done.2 = bf16[4,256,256]{2,1,0:T(8,128)(2,1)S(1)} copy-done((bf16[4,256,256]{2,1,0:T(8,128)(2,1)S(1)}, bf16[4,256,256]{2,1,0:T(8,128)(2,1)}, u32[]{:S(2)}) %copy-start.2) | copy-done | bytes 524312
  1.0 0.0 copy-start.3
  1.0 0.7 copy-done.3
  1.7 1.4 %shard_map.109.spread = bf16[128,16,128]{2,1,0:T(8,128)(2,1)} custom-call(s32[1,1,8]{2,1,0:T(1,128)S(1)} %copy-done.3, bf16[4,256,256]{2,1,0:T(8,128)(2,1)S(1)} %copy-done.2), custom_call_target="tpu_custom_call" | custom-call | bytes 1048576 | tf_op jit(solution)/shard_map/pallas_call | solution.py:121
  3.1 0.0 copy-start
  3.1 16.8 %all-to-all-start = ((bf16[128,16,128]{2,1,0:T(8,128)(2,1)}), bf16[128,16,128]{2,1,0:T(8,128)(2,1)S(1)}, u32[]{:S(2)}, u32[]{:S(2)}) async-start(bf16[128,16,128]{2,1,0:T(8,128)(2,1)} %shard_map.109.spread), calls=%async_computation | async-start | bytes 1048576 | tf_op jit(solution)/shard_map/all_to_all | solution.py:129
  19.9 0.0 copy-done
  19.9 0.0 copy-start.5
  19.9 0.1 shard_map.110
  20.0 4.8 %collective-permute-start = (bf16[32,4,256]{2,1,0:T(4,128)(2,1)S(1)}, bf16[32,4,256]{2,1,0:T(4,128)(2,1)S(1)}, u32[]{:S(2)}, u32[]{:S(2)}) collective-permute-start(bf16[32,4,256]{2,1,0:T(4,128)(2,1)S(1)} %get-tuple-element.17), channel_id=1, source_target_pairs={{0,1},{1,2},{2,3},{3,4},{4,5},{5,6},{6,7},{7,8},{8,9},{9,10},{10,1... | collective-permute-start | bytes 196616 | tf_op jit(solution)/shard_map/ppermute | solution.py:40
  24.8 1.3 %collective-permute-start.1 = (bf16[32,4,256]{2,1,0:T(4,128)(2,1)S(1)}, bf16[32,4,256]{2,1,0:T(4,128)(2,1)S(1)}, u32[]{:S(2)}, u32[]{:S(2)}) collective-permute-start(bf16[32,4,256]{2,1,0:T(4,128)(2,1)S(1)} %get-tuple-element.18), channel_id=1, source_target_pairs={{1,0},{2,1},{3,2},{4,3},{5,4},{6,5},{7,6},{8,7},{9,8},{10,9},{11,1... | collective-permute-start | bytes 196616 | tf_op jit(solution)/shard_map/ppermute | solution.py:40
  26.1 0.0 copy-done.5
  26.1 0.1 copy.18
  26.2 0.0 copy-start.4
  26.2 0.1 copy.19
  26.3 0.0 copy-start.7
  26.4 0.7 copy-done.7
  27.0 0.0 copy-start.9
  27.0 0.0 copy-start.10
  27.0 0.0 copy-start.11
  27.0 0.6 copy-done.9
  27.7 0.0 copy-done.10
  27.7 0.0 copy-done.11
  27.7 0.1 multiply_reduce_fusion
  27.8 0.1 fusion.1.weights
  27.9 0.0 copy-done.4
  27.9 9.4 %all-to-all-done.arrived = bf16[128,16,128]{2,1,0:T(8,128)(2,1)S(1)} async-done(((bf16[128,16,128]{2,1,0:T(8,128)(2,1)}), bf16[128,16,128]{2,1,0:T(8,128)(2,1)S(1)}, u32[]{:S(2)}, u32[]{:S(2)}) %all-to-all-start) | async-done | bytes 524320 | tf_op jit(solution)/shard_map/all_to_all | solution.py:129
  37.4 0.1 slice_select_fusion
  37.5 0.0 collective-permute-done.left
  37.5 0.0 collective-permute-done.1.right
  37.5 3.4 %shard_map.113 = bf16[32,8,16,128]{3,2,1,0:T(8,128)(2,1)} custom-call(s32[32,8]{1,0:T(8,128)S(1)} %bitcast.13, bf16[128,16,128]{2,1,0:T(8,128)(2,1)S(1)} %all-to-all-done.arrived, bf16[32,4,256]{2,1,0:T(4,128)(2,1)S(1)} %collective-permute-done.left, bf16[32,4,256]{2,1,0:T(4,128)(2,1)S(1)} %collective-permute-done.1.right, f32[10,256]{1,0:T(8,128)S(1)} %fusion.1.weights, ...), custom_call_target="tpu_custom_call" | custom-call | bytes 1048576 | tf_op jit(solution)/shard_map/pallas_call | solution.py:153
  40.9 6.2 %all-to-all-start.1 = ((bf16[32,8,16,128]{3,2,1,0:T(8,128)(2,1)}), bf16[32,8,16,128]{3,2,1,0:T(8,128)(2,1)S(1)}, u32[]{:S(2)}, u32[]{:S(2)}) async-start(bf16[32,8,16,128]{3,2,1,0:T(8,128)(2,1)} %shard_map.113), calls=%async_computation.1 | async-start | bytes 2097152 | tf_op jit(solution)/shard_map/all_to_all | solution.py:161
  47.1 0.0 copy-start.1
  47.2 0.0 copy-start.6
  47.2 3.5 %collective-permute-start.2 = (bf16[4,40,256]{2,1,0:T(8,128)(2,1)S(1)}, bf16[4,40,256]{2,1,0:T(8,128)(2,1)S(1)}, u32[]{:S(2)}, u32[]{:S(2)}) collective-permute-start(bf16[4,40,256]{2,1,0:T(8,128)(2,1)S(1)} %get-tuple-element.19), channel_id=1, source_target_pairs={{0,16},{16,32},{32,48},{48,64},{64,80},{80,96},{96,112},{112,128},... | collective-permute-start | bytes 245768 | tf_op jit(solution)/shard_map/ppermute | solution.py:40
  50.8 0.0 copy-start.8
  50.8 1.9 %collective-permute-start.3 = (bf16[4,40,256]{2,1,0:T(8,128)(2,1)S(1)}, bf16[4,40,256]{2,1,0:T(8,128)(2,1)S(1)}, u32[]{:S(2)}, u32[]{:S(2)}) collective-permute-start(bf16[4,40,256]{2,1,0:T(8,128)(2,1)S(1)} %get-tuple-element.20), channel_id=1, source_target_pairs={{16,0},{32,16},{48,32},{64,48},{80,64},{96,80},{112,96},{128,112},... | collective-permute-start | bytes 245768 | tf_op jit(solution)/shard_map/ppermute | solution.py:40
  52.7 0.0 copy-done.6
  52.7 0.0 copy-done.8
  52.7 0.2 select_reduce_fusion.slots
  52.9 6.9 %collective-permute-done.2.top = bf16[4,40,256]{2,1,0:T(8,128)(2,1)S(1)} collective-permute-done((bf16[4,40,256]{2,1,0:T(8,128)(2,1)S(1)}, bf16[4,40,256]{2,1,0:T(8,128)(2,1)S(1)}, u32[]{:S(2)}, u32[]{:S(2)}) %collective-permute-start.2) | collective-permute-done | bytes 81952 | tf_op jit(solution)/shard_map/ppermute | solution.py:40
  59.9 2.1 %collective-permute-done.3.bottom = bf16[4,40,256]{2,1,0:T(8,128)(2,1)S(1)} collective-permute-done((bf16[4,40,256]{2,1,0:T(8,128)(2,1)S(1)}, bf16[4,40,256]{2,1,0:T(8,128)(2,1)S(1)}, u32[]{:S(2)}, u32[]{:S(2)}) %collective-permute-start.3) | collective-permute-done | bytes 81952 | tf_op jit(solution)/shard_map/ppermute | solution.py:40
  62.0 0.0 copy-done.1
  62.0 3.4 %shard_map.112.grown = bf16[32,32,256]{2,1,0:T(8,128)(2,1)S(1)} custom-call(bf16[32,32,256]{2,1,0:T(8,128)(2,1)S(1)} %copy-done, bf16[4,40,256]{2,1,0:T(8,128)(2,1)S(1)} %collective-permute-done.2.top, bf16[4,40,256]{2,1,0:T(8,128)(2,1)S(1)} %collective-permute-done.3.bottom, bf16[32,4,256]{2,1,0:T(4,128)(2,1)S(1)} %collective-permute-done.left, ...), custom_call_target="tpu_custom_call" | custom-call | flops 268435456 | bytes 16777216 | tf_op jit(solution)/shard_map/pallas_call | solution.py:421
  65.4 0.0 all-to-all-done.1.parts
  65.4 1.2 %shard_map.114 = (bf16[32,32,256]{2,1,0:T(8,128)(2,1)S(1)}, bf16[8,256,256]{2,1,0:T(8,128)(2,1)S(1)}, bf16[4,32,256]{2,1,0:T(8,128)(2,1)S(1)}, bf16[4,32,256]{2,...) custom-call(s32[4,4]{1,0:T(4,128)S(1)} %select_reduce_fusion.slots, ...), custom_call_target="tpu_custom_call" | custom-call | flops 268435456 | bytes 4194304 | tf_op jit(solution)/shard_map/pallas_call | solution.py:432
  66.7 2.3 %collective-permute-start.4 = (bf16[4,32,256]{2,1,0:T(8,128)(2,1)S(1)}, bf16[4,32,256]{2,1,0:T(8,128)(2,1)S(1)}, u32[]{:S(2)}, u32[]{:S(2)}) collective-permute-start(bf16[4,32,256]{2,1,0:T(8,128)(2,1)S(1)} %get-tuple-element.22), channel_id=1, source_target_pairs={{0,16},{16,32},{32,48},{48,64},{64,80},{80,96},{96,112},{112,128},... | collective-permute-start | bytes 196616 | tf_op jit(solution)/shard_map/ppermute | solution.py:40
  68.9 2.1 %collective-permute-start.5 = (bf16[4,32,256]{2,1,0:T(8,128)(2,1)S(1)}, bf16[4,32,256]{2,1,0:T(8,128)(2,1)S(1)}, u32[]{:S(2)}, u32[]{:S(2)}) collective-permute-start(bf16[4,32,256]{2,1,0:T(8,128)(2,1)S(1)} %get-tuple-element.24), channel_id=1, source_target_pairs={{16,0},{32,16},{48,32},{64,48},{80,64},{96,80},{112,96},{128,112},... | collective-permute-start | bytes 196616 | tf_op jit(solution)/shard_map/ppermute | solution.py:40
  71.0 0.0 collective-permute-done.4.top
  71.0 3.5 %collective-permute-done.5.bottom = bf16[4,32,256]{2,1,0:T(8,128)(2,1)S(1)} collective-permute-done((bf16[4,32,256]{2,1,0:T(8,128)(2,1)S(1)}, bf16[4,32,256]{2,1,0:T(8,128)(2,1)S(1)}, u32[]{:S(2)}, u32[]{:S(2)}) %collective-permute-start.5) | collective-permute-done | bytes 65568 | tf_op jit(solution)/shard_map/ppermute | solution.py:40
  74.5 0.1 pad_maximum_fusion
  74.6 4.8 %collective-permute-start.6 = (bf16[40,4,256]{2,1,0:T(4,128)(2,1)S(1)}, bf16[40,4,256]{2,1,0:T(4,128)(2,1)S(1)}, u32[]{:S(2)}, u32[]{:S(2)}) collective-permute-start(bf16[40,4,256]{2,1,0:T(4,128)(2,1)S(1)} %pad_maximum_fusion), channel_id=1, source_target_pairs={{0,1},{1,2},{2,3},{3,4},{4,5},{5,6},{6,7},{7,8},{8,9},{9,10},{10,1... | collective-permute-start | bytes 245768 | tf_op jit(solution)/shard_map/ppermute | solution.py:40
  79.4 0.1 pad_maximum_fusion.1
  79.5 1.3 %collective-permute-start.7 = (bf16[40,4,256]{2,1,0:T(4,128)(2,1)S(1)}, bf16[40,4,256]{2,1,0:T(4,128)(2,1)S(1)}, u32[]{:S(2)}, u32[]{:S(2)}) collective-permute-start(bf16[40,4,256]{2,1,0:T(4,128)(2,1)S(1)} %pad_maximum_fusion.1), channel_id=1, source_target_pairs={{1,0},{2,1},{3,2},{4,3},{5,4},{6,5},{7,6},{8,7},{9,8},{10,9},{11,1... | collective-permute-start | bytes 245768 | tf_op jit(solution)/shard_map/ppermute | solution.py:40
  80.8 4.4 %shard_map.115 = (bf16[32,16,256]{2,1,0:T(8,128)(2,1)S(1)}, f32[32,16,256]{2,1,0:T(8,128)S(1)}) custom-call(s32[4,4]{1,0:T(4,128)S(1)} %select_reduce_fusion.slots, bf16[32,32,256]{2,1,0:T(8,128)(2,1)S(1)} %get-tuple-element.21.cells, bf16[4,32,256]{2,1,0:T(8,128)(2,1)S(1)} %collective-permute-done.4.top, ...), custom_call_target="tpu_custom_call" | custom-call | flops 268435456 | bytes 16777216 | tf_op jit(solution)/shard_map/pallas_call | solution.py:443
  85.2 0.0 collective-permute-done.6.left
  85.2 1.0 %collective-permute-done.7.right = bf16[40,4,256]{2,1,0:T(4,128)(2,1)S(1)} collective-permute-done((bf16[40,4,256]{2,1,0:T(4,128)(2,1)S(1)}, bf16[40,4,256]{2,1,0:T(4,128)(2,1)S(1)}, u32[]{:S(2)}, u32[]{:S(2)}) %collective-permute-start.7) | collective-permute-done | bytes 81952 | tf_op jit(solution)/shard_map/ppermute | solution.py:40
  86.2 3.0 %shard_map.116 = bf16[32,32,256]{2,1,0:T(8,128)(2,1)} custom-call(s32[4,4]{1,0:T(4,128)S(1)} %select_reduce_fusion.slots, bf16[32,32,256]{2,1,0:T(8,128)(2,1)S(1)} %get-tuple-element.21.cells, bf16[40,4,256]{2,1,0:T(4,128)(2,1)S(1)} %collective-permute-done.6.left, bf16[40,4,256]{2,1,0:T(4,128)(2,1)S(1)} %collective-permute-done.7.right, ...), custom_call_target="tpu_custom_call" | custom-call | flops 268435456 | bytes 4194304 | tf_op jit(solution)/shard_map/pallas_call | solution.py:455
  (11 shorter events, 0.2 us)
Async XLA Ops:
  0.0 1.0 %copy-start.2 = (bf16[4,256,256]{2,1,0:T(8,128)(2,1)S(1)}, bf16[4,256,256]{2,1,0:T(8,128)(2,1)}, u32[]{:S(2)}) copy-start(bf16[4,256,256]{2,1,0:T(8,128)(2,1)} %held.1) | copy-start | bytes 1572868
  1.0 0.7 copy-start.3
  3.1 16.8 %copy-start = (bf16[32,32,256]{2,1,0:T(8,128)(2,1)S(1)}, bf16[32,32,256]{2,1,0:T(8,128)(2,1)}, u32[]{:S(2)}) copy-start(bf16[32,32,256]{2,1,0:T(8,128)(2,1)} %cells.5) | copy-start | bytes 1572868
  3.1 34.3 %all-to-all-start = ((bf16[128,16,128]{2,1,0:T(8,128)(2,1)}), bf16[128,16,128]{2,1,0:T(8,128)(2,1)S(1)}, u32[]{:S(2)}, u32[]{:S(2)}) async-start(bf16[128,16,128]{2,1,0:T(8,128)(2,1)} %shard_map.109.spread), calls=%async_computation | async-start | bytes 1048576 | tf_op jit(solution)/shard_map/all_to_all | solution.py:129
  19.9 6.2 %copy-start.5 = (s32[32,32]{1,0:T(8,128)S(1)}, s32[32,32]{1,0:T(8,128)}, u32[]{:S(2)}) copy-start(s32[32,32]{1,0:T(8,128)} %param.17) | copy-start | bytes 12292
  20.0 17.5 %collective-permute-start = (bf16[32,4,256]{2,1,0:T(4,128)(2,1)S(1)}, bf16[32,4,256]{2,1,0:T(4,128)(2,1)S(1)}, u32[]{:S(2)}, u32[]{:S(2)}) collective-permute-start(bf16[32,4,256]{2,1,0:T(4,128)(2,1)S(1)} %get-tuple-element.17), channel_id=1, source_target_pairs={{0,1},{1,2},{2,3},{3,4},{4,5},{5,6},{6,7},{7,8},{8,9},{9,10},{10,1... | collective-permute-start | bytes 196616 | tf_op jit(solution)/shard_map/ppermute | solution.py:40
  24.8 12.7 %collective-permute-start.1 = (bf16[32,4,256]{2,1,0:T(4,128)(2,1)S(1)}, bf16[32,4,256]{2,1,0:T(4,128)(2,1)S(1)}, u32[]{:S(2)}, u32[]{:S(2)}) collective-permute-start(bf16[32,4,256]{2,1,0:T(4,128)(2,1)S(1)} %get-tuple-element.18), channel_id=1, source_target_pairs={{1,0},{2,1},{3,2},{4,3},{5,4},{6,5},{7,6},{8,7},{9,8},{10,9},{11,1... | collective-permute-start | bytes 196616 | tf_op jit(solution)/shard_map/ppermute | solution.py:40
  26.2 1.7 %copy-start.4 = (bf16[256,256]{1,0:T(8,128)(2,1)S(1)}, bf16[256,256]{1,0:T(8,128)(2,1)}, u32[]{:S(2)}) copy-start(bf16[256,256]{1,0:T(8,128)(2,1)} %param.16) | copy-start | bytes 393220
  26.3 0.7 copy-start.7
  27.0 0.7 copy-start.9
  27.0 0.7 copy-start.10
  27.0 0.7 copy-start.11
  40.9 24.5 %all-to-all-start.1 = ((bf16[32,8,16,128]{3,2,1,0:T(8,128)(2,1)}), bf16[32,8,16,128]{3,2,1,0:T(8,128)(2,1)S(1)}, u32[]{:S(2)}, u32[]{:S(2)}) async-start(bf16[32,8,16,128]{3,2,1,0:T(8,128)(2,1)} %shard_map.113), calls=%async_computation.1 | async-start | bytes 2097152 | tf_op jit(solution)/shard_map/all_to_all | solution.py:161
  47.1 14.8 %copy-start.1 = (bf16[256,256]{1,0:T(8,128)(2,1)S(1)}, bf16[256,256]{1,0:T(8,128)(2,1)}, u32[]{:S(2)}) copy-start(bf16[256,256]{1,0:T(8,128)(2,1)} %fecundity.5) | copy-start | bytes 393220
  47.2 5.5 %copy-start.6 = (s32[4,4]{1,0:T(4,128)S(1)}, s32[4,4]{1,0:T(4,128)}, u32[]{:S(2)}) copy-start(s32[4,4]{1,0:T(4,128)} %param.12) | copy-start | bytes 196
  47.2 12.6 %collective-permute-start.2 = (bf16[4,40,256]{2,1,0:T(8,128)(2,1)S(1)}, bf16[4,40,256]{2,1,0:T(8,128)(2,1)S(1)}, u32[]{:S(2)}, u32[]{:S(2)}) collective-permute-start(bf16[4,40,256]{2,1,0:T(8,128)(2,1)S(1)} %get-tuple-element.19), channel_id=1, source_target_pairs={{0,16},{16,32},{32,48},{48,64},{64,80},{80,96},{96,112},{112,128},... | collective-permute-start | bytes 245768 | tf_op jit(solution)/shard_map/ppermute | solution.py:40
  50.8 2.0 %copy-start.8 = (s32[1,1,16]{2,1,0:T(1,128)S(1)}, s32[1,1,16]{2,1,0:T(1,128)}, u32[]{:S(2)}) copy-start(s32[1,1,16]{2,1,0:T(1,128)} %param.13) | copy-start | bytes 196
  50.8 11.2 %collective-permute-start.3 = (bf16[4,40,256]{2,1,0:T(8,128)(2,1)S(1)}, bf16[4,40,256]{2,1,0:T(8,128)(2,1)S(1)}, u32[]{:S(2)}, u32[]{:S(2)}) collective-permute-start(bf16[4,40,256]{2,1,0:T(8,128)(2,1)S(1)} %get-tuple-element.20), channel_id=1, source_target_pairs={{16,0},{32,16},{48,32},{64,48},{80,64},{96,80},{112,96},{128,112},... | collective-permute-start | bytes 245768 | tf_op jit(solution)/shard_map/ppermute | solution.py:40
  66.7 4.3 %collective-permute-start.4 = (bf16[4,32,256]{2,1,0:T(8,128)(2,1)S(1)}, bf16[4,32,256]{2,1,0:T(8,128)(2,1)S(1)}, u32[]{:S(2)}, u32[]{:S(2)}) collective-permute-start(bf16[4,32,256]{2,1,0:T(8,128)(2,1)S(1)} %get-tuple-element.22), channel_id=1, source_target_pairs={{0,16},{16,32},{32,48},{48,64},{64,80},{80,96},{96,112},{112,128},... | collective-permute-start | bytes 196616 | tf_op jit(solution)/shard_map/ppermute | solution.py:40
  68.9 5.6 %collective-permute-start.5 = (bf16[4,32,256]{2,1,0:T(8,128)(2,1)S(1)}, bf16[4,32,256]{2,1,0:T(8,128)(2,1)S(1)}, u32[]{:S(2)}, u32[]{:S(2)}) collective-permute-start(bf16[4,32,256]{2,1,0:T(8,128)(2,1)S(1)} %get-tuple-element.24), channel_id=1, source_target_pairs={{16,0},{32,16},{48,32},{64,48},{80,64},{96,80},{112,96},{128,112},... | collective-permute-start | bytes 196616 | tf_op jit(solution)/shard_map/ppermute | solution.py:40
  74.6 10.6 %collective-permute-start.6 = (bf16[40,4,256]{2,1,0:T(4,128)(2,1)S(1)}, bf16[40,4,256]{2,1,0:T(4,128)(2,1)S(1)}, u32[]{:S(2)}, u32[]{:S(2)}) collective-permute-start(bf16[40,4,256]{2,1,0:T(4,128)(2,1)S(1)} %pad_maximum_fusion), channel_id=1, source_target_pairs={{0,1},{1,2},{2,3},{3,4},{4,5},{5,6},{6,7},{7,8},{8,9},{9,10},{10,1... | collective-permute-start | bytes 245768 | tf_op jit(solution)/shard_map/ppermute | solution.py:40
  79.5 6.7 %collective-permute-start.7 = (bf16[40,4,256]{2,1,0:T(4,128)(2,1)S(1)}, bf16[40,4,256]{2,1,0:T(4,128)(2,1)S(1)}, u32[]{:S(2)}, u32[]{:S(2)}) collective-permute-start(bf16[40,4,256]{2,1,0:T(4,128)(2,1)S(1)} %pad_maximum_fusion.1), channel_id=1, source_target_pairs={{1,0},{2,1},{3,2},{4,3},{5,4},{6,5},{7,6},{8,7},{9,8},{10,9},{11,1... | collective-permute-start | bytes 245768 | tf_op jit(solution)/shard_map/ppermute | solution.py:40

commit v6 on v5

--- a/solution.py
+++ b/solution.py
@@ -26,6 +26,7 @@
 VMEM = pl.BlockSpec(memory_space=pltpu.VMEM)
 SMEM = pl.BlockSpec(memory_space=pltpu.SMEM)
 ANY = pl.BlockSpec(memory_space=pl.ANY)
+HBM = pl.BlockSpec(memory_space=pltpu.HBM)
 PARAMS = pltpu.CompilerParams(vmem_limit_bytes=32 * 1024 * 1024)
 
 LEAD = 8
@@ -38,13 +39,6 @@
 def swap(head, tail, axis):
     after, before = shift_pairs(math.prod(lax.axis_size(name) for name in axis))
     return lax.ppermute(tail, axis, after), lax.ppermute(head, axis, before)
-
-
-def surround(first, last, head, tail):
-    top, bottom = swap(first, last, ROW)
-    head = jnp.concatenate([top[:, :RMAX], head, bottom[:, :RMAX]], axis=0)
-    tail = jnp.concatenate([top[:, -RMAX:], tail, bottom[:, -RMAX:]], axis=0)
-    return (top, bottom) + swap(head, tail, COL)
 
 
 def class_weights(radius):
@@ -77,24 +71,29 @@
             out[i] = whole.astype(jnp.bfloat16)
 
 
-def spread_kernel(listed, held, spread):
+def spread_kernel(tile_list, harvest_ops, spread, listed, held, sems):
     mine = (lax.axis_index("xl") * 2 + lax.axis_index("yl")) * 2 + lax.axis_index("co")
+    list_copy = pltpu.make_async_copy(tile_list, listed, sems.at[0])
+    held_copy = pltpu.make_async_copy(harvest_ops.at[mine // 2], held, sems.at[1])
+    list_copy.start()
+    held_copy.start()
+    list_copy.wait()
     lane = lax.broadcasted_iota(jnp.int32, (16, 128), 1)
     names = jnp.zeros((16, 128), jnp.float32)
     for k in range(listed.shape[-1]):
         names = jnp.where(lax.rem(lane, 64) == k, listed[0, 0, k].astype(jnp.float32), names)
-    held_at, upper = mine // 2, lax.rem(mine, 2)
-    sent = lane // 64 == upper
+    sent = lane // 64 == lax.rem(mine, 2)
+    held_copy.wait()
     for group in range(8):
         for near in range(4):
             low, half = divmod(near, 2)
-            piece = held[held_at, pl.ds(group * 32 + low * 16, 16), pl.ds(half * 128, 128)]
+            piece = held[pl.ds(group * 32 + low * 16, 16), pl.ds(half * 128, 128)]
             message = jnp.where(sent, piece.astype(jnp.float32), names).astype(jnp.bfloat16)
             for far in range(4):
                 spread[(group * 4 + far) * 4 + near] = message
 
 
-def gather_kernel(lists, arrived, left, right, weights, moves, wanted):
+def gather_kernel(places, arrived, left, right, weights, moves, wanted):
     del left, right, weights, moves
     members, count = wanted.shape[:2]
     lower = lax.broadcasted_iota(jnp.int32, (16, 128), 1) < 64
@@ -102,8 +101,7 @@
     def one(m, carry):
         found = []
         for k in range(count):
-            name = lists[m, k]
-            at = lax.rem(name, 4) * 32 + name // 4
+            at = places[m, k]
             found.append(jnp.where(lower, arrived[at], arrived[at + 16]))
         for k in range(count):
             wanted[m, k] = found[k]
@@ -121,8 +119,13 @@
     spread = pl.pallas_call(
         spread_kernel,
         out_shape=jax.ShapeDtypeStruct((128, 16, 128), jnp.bfloat16),
-        in_specs=[SMEM, VMEM],
+        in_specs=[HBM, HBM],
         out_specs=VMEM,
+        scratch_shapes=[
+            pltpu.SMEM(tile_list.shape, jnp.int32),
+            pltpu.VMEM((cohorts, cohorts), jnp.bfloat16),
+            pltpu.SemaphoreType.DMA((2,)),
+        ],
         compiler_params=PARAMS,
         cost_estimate=small,
     )(tile_list, harvest_ops)
@@ -149,7 +152,8 @@
         arrived.reshape(8, 4, 4, 16, 128), lax.axis_index("zh"), axis=1, keepdims=False
     )[:, :, 0].astype(jnp.int32)
     even = jnp.arange(8)[:, None, None] % 2 == 0
-    lists = jnp.where(even, own[:, :, 64 : 64 + count], own[:, :, :count]).reshape(32, count)
+    lists = jnp.where(even, own[:, :, 64 : 64 + count], own[:, :, :count])
+    places = (lists % 4 * 32 + lists // 4).reshape(32, count)
     wanted = pl.pallas_call(
         gather_kernel,
         out_shape=jax.ShapeDtypeStruct((32, count, 16, 128), jnp.bfloat16),
@@ -157,7 +161,7 @@
         out_specs=VMEM,
         compiler_params=PARAMS,
         cost_estimate=small,
-    )(lists, arrived, left, right, weights, moves)
+    )(places, arrived, left, right, weights, moves)
     parts = lax.all_to_all(wanted, NEAR, 0, 0, tiled=True)
     return parts, (top, bottom, left, right)
 
@@ -295,7 +299,7 @@
         grown[span] = result.reshape(BX, cols, cohorts)
 
 
-def harvest_kernel(slots, grown, parts, out, ops, first, last, head, tail):
+def harvest_kernel(slots, grown, parts, out, ops, last, head, tail):
     assemble(parts, ops)
     rows, cols, cohorts = grown.shape
     wide = 2 * BY
@@ -309,44 +313,87 @@
         out[span] = whole.astype(jnp.bfloat16)
         head[span] = whole[:, :RMAX].astype(jnp.bfloat16)
         tail[span] = whole[:, cols - RMAX :].astype(jnp.bfloat16)
-        if i == 0:
-            first[...] = whole[:RMAX].astype(jnp.bfloat16)
         if i == rows // BX - 1:
             last[...] = whole[BX - RMAX :].astype(jnp.bfloat16)
 
 
-def middle_kernel(
-    slots, cells, top, bottom, weights, fecundity, moves, ops, inner, partial, padded, pairs, seeds
-):
-    rows, cols, cohorts = cells.shape
-    fill_rows(cells, top, bottom, padded)
+def clear_and_pair(padded, pairs):
     clear_sides(padded)
     add_pairs(padded, pairs)
 
+
+def split_row(total):
+    cols = total.shape[0]
+    outer = jnp.concatenate([total[:BY], total[cols - BY :]], axis=0)
+    return outer, total[BY : cols - BY].astype(jnp.bfloat16)
+
+
+def inner_rows_kernel(cells, weights, first, partial, seeds, padded, pairs):
+    rows, cols, _ = cells.shape
+    first[...] = cells[pl.ds(0, RMAX)]
+
+    def fill(x, carry):
+        padded[x, pl.ds(LEAD, cols), :] = cells[x].astype(jnp.float32)
+        return carry
+
+    lax.fori_loop(0, rows, fill, 0, unroll=4)
+    clear_and_pair(padded, pairs)
+
+    def row_sum(x, b):
+        return padded[x - RMAX, pl.ds(LEAD, cols), :] if b == 0 else pairs[b - 1, x - RMAX]
+
+    def one(i, carry):
+        partial[i], seeds[i] = split_row(weigh(i + RMAX, row_sum, weights))
+        return carry
+
+    lax.fori_loop(0, rows - 2 * RMAX, one, 0, unroll=2)
+
+
+def outer_rows_kernel(cells, top, bottom, own_head, weights, head, partial, seeds, padded, pairs):
+    rows, cols, _ = cells.shape
+    head[pl.ds(RMAX, rows)] = own_head[...]
+    for part, start in ((top, 0), (bottom, RMAX + rows)):
+        for i in range(RMAX):
+            head[start + i] = part[i].astype(jnp.float32)[:RMAX].astype(jnp.bfloat16)
+    for i in range(RMAX):
+        padded[i, pl.ds(LEAD, cols), :] = top[i].astype(jnp.float32)
+        padded[5 * RMAX + i, pl.ds(LEAD, cols), :] = bottom[i].astype(jnp.float32)
+    for i in range(2 * RMAX):
+        padded[RMAX + i, pl.ds(LEAD, cols), :] = cells[i].astype(jnp.float32)
+        padded[3 * RMAX + i, pl.ds(LEAD, cols), :] = cells[rows - 2 * RMAX + i].astype(jnp.float32)
+    clear_and_pair(padded, pairs)
+
     def row_sum(x, b):
         return padded[x, pl.ds(LEAD, cols), :] if b == 0 else pairs[b - 1, x]
 
-    def one(x, carry):
-        total = weigh(x, row_sum, weights)
-        partial[x] = jnp.concatenate([total[:BY], total[cols - BY :]], axis=0)
-        seeds[x] = total[BY : cols - BY].astype(jnp.bfloat16)
-        return carry
-
-    lax.fori_loop(0, rows, one, 0, unroll=2)
-    for i in range(0, rows // BX, 2):
-        span = pl.ds(i * BX, 2 * BX)
+    def one(i, carry):
+        for h in range(2):
+            total = weigh(i + 3 * RMAX * h, row_sum, weights)
+            partial[i + RMAX * h], seeds[i + RMAX * h] = split_row(total)
+        return carry
+
+    lax.fori_loop(0, RMAX, one, 0)
+
+
+def inner_blocks_kernel(slots, cells, seeds_in, seeds_out, fecundity, moves, ops, inner):
+    rows, cols, cohorts = cells.shape
+    half = rows // 2
+    for h in range(2):
+        span = pl.ds(h * half, half)
+        middle = seeds_in[pl.ds(h * (half - RMAX), half - RMAX)]
+        edge = seeds_out[pl.ds(h * RMAX, RMAX)]
+        seeds = jnp.concatenate([middle, edge] if h else [edge, middle], axis=0)
         here = cells[span].astype(jnp.float32)[:, BY : cols - BY].reshape(-1, cohorts)
-        grown = establish(seeds[span].reshape(-1, cohorts), here, fecundity, moves)
-        half = grown.shape[0] // 2
-        for k in range(2):
-            done = remove_pair(
-                grown[k * half : (k + 1) * half], (slots[i + k, 1], slots[i + k, 2]), ops
-            )
-            inner[pl.ds((i + k) * BX, BX)] = done.astype(jnp.bfloat16)
+        grown = establish(seeds.reshape(-1, cohorts), here, fecundity, moves)
+        size = 2 * BY * BX
+        for k in range(half // BX):
+            i = h * (half // BX) + k
+            done = remove_pair(grown[k * size : (k + 1) * size], (slots[i, 1], slots[i, 2]), ops)
+            inner[pl.ds(i * BX, BX)] = done.astype(jnp.bfloat16)
 
 
 def last_kernel(
-    slots, cells, left, right, weights, fecundity, moves, ops, inner, partial,
+    slots, cells, left, right, weights, fecundity, moves, ops, inner, partial_in, partial_out,
     out, sides, pairs, seeds,
 ):
     rows, cols, cohorts = cells.shape
@@ -368,13 +415,19 @@
     def row_sum(x, b):
         return None if b == 0 else pairs[b - 1, x]
 
-    def one(x, carry):
+    def add(x, partial):
         extra = weigh(x, row_sum, weights)
         both = jnp.concatenate([jnp.where(near, extra, 0.0), jnp.where(near, 0.0, extra)], axis=0)
-        seeds[x] = (partial[x] + both).astype(jnp.bfloat16)
-        return carry
-
-    lax.fori_loop(0, rows, one, 0, unroll=4)
+        seeds[x] = (partial + both).astype(jnp.bfloat16)
+
+    def one(i, carry):
+        add(i + RMAX, partial_in[i])
+        return carry
+
+    lax.fori_loop(0, rows - 2 * RMAX, one, 0, unroll=4)
+    for i in range(RMAX):
+        add(i, partial_out[i])
+        add(rows - RMAX + i, partial_out[RMAX + i])
     for i in range(0, rows // BX, 2):
         span = pl.ds(i * BX, 2 * BX)
         here = cells[span].astype(jnp.float32)
@@ -392,12 +445,12 @@
             out[at] = whole.astype(jnp.bfloat16)
 
 
-def scratch(rows, cols, cohorts, seeded=None):
+def scratch(rows, cols, cohorts):
     high = rows + 2 * RMAX
     return [
         pltpu.VMEM((high, cols + 2 * LEAD, cohorts), jnp.float32),
         pltpu.VMEM((RMAX, high, cols, cohorts), jnp.float32),
-        pltpu.VMEM((rows, seeded or cols, cohorts), jnp.bfloat16),
+        pltpu.VMEM((rows, cols, cohorts), jnp.bfloat16),
     ]
 
 
@@ -429,33 +482,64 @@
     )(biomass, *around, weights, fecundity, moves)
     row_part = jax.ShapeDtypeStruct((RMAX, cols, cohorts), jnp.bfloat16)
     col_part = jax.ShapeDtypeStruct((rows, RMAX, cohorts), jnp.bfloat16)
-    cells, ops, first, last, head, tail = pl.pallas_call(
+    cells, ops, last, own_head, tail = pl.pallas_call(
         harvest_kernel,
-        out_shape=(state, operators, row_part, row_part, col_part, col_part),
+        out_shape=(state, operators, row_part, col_part, col_part),
         in_specs=[SMEM, VMEM, VMEM],
-        out_specs=(VMEM,) * 6,
+        out_specs=(VMEM,) * 5,
         compiler_params=PARAMS,
         cost_estimate=pl.CostEstimate(flops=2**28, bytes_accessed=2**22, transcendentals=0),
     )(slots, grown, parts)
-    top, bottom, left, right = surround(first, last, head, tail)
     high = rows + 2 * RMAX
     outer = 2 * BY
-    inner, partial = pl.pallas_call(
-        middle_kernel,
-        out_shape=(
-            jax.ShapeDtypeStruct((rows, cols - outer, cohorts), jnp.bfloat16),
-            jax.ShapeDtypeStruct((rows, outer, cohorts), jnp.float32),
-        ),
-        in_specs=[SMEM] + [VMEM] * 7,
-        out_specs=(VMEM, VMEM),
-        scratch_shapes=scratch(rows, cols, cohorts, cols - outer),
-        compiler_params=PARAMS,
-        cost_estimate=pl.CostEstimate(flops=2**28, bytes_accessed=2**24, transcendentals=0),
-    )(slots, cells, top, bottom, weights, fecundity, moves, ops)
+    few = 2 * RMAX
+
+    def halves(count):
+        return (
+            jax.ShapeDtypeStruct((count, outer, cohorts), jnp.float32),
+            jax.ShapeDtypeStruct((count, cols - outer, cohorts), jnp.bfloat16),
+        )
+
+    def room(count):
+        return [
+            pltpu.VMEM((count, cols + 2 * LEAD, cohorts), jnp.float32),
+            pltpu.VMEM((RMAX, count, cols, cohorts), jnp.float32),
+        ]
+
+    work = pl.CostEstimate(flops=2**28, bytes_accessed=2**23, transcendentals=0)
+    first, partial_in, seeds_in = pl.pallas_call(
+        inner_rows_kernel,
+        out_shape=(row_part,) + halves(rows - few),
+        in_specs=[VMEM] * 2,
+        out_specs=(VMEM,) * 3,
+        scratch_shapes=room(rows),
+        compiler_params=PARAMS,
+        cost_estimate=work,
+    )(cells, weights)
+    top, bottom = swap(first, last, ROW)
+    tail = jnp.concatenate([top[:, -RMAX:], tail, bottom[:, -RMAX:]], axis=0)
+    head, partial_out, seeds_out = pl.pallas_call(
+        outer_rows_kernel,
+        out_shape=(jax.ShapeDtypeStruct((high, RMAX, cohorts), jnp.bfloat16),) + halves(few),
+        in_specs=[VMEM] * 5,
+        out_specs=(VMEM,) * 3,
+        scratch_shapes=room(3 * few),
+        compiler_params=PARAMS,
+        cost_estimate=work,
+    )(cells, top, bottom, own_head, weights)
+    left, right = swap(head, tail, COL)
+    inner = pl.pallas_call(
+        inner_blocks_kernel,
+        out_shape=jax.ShapeDtypeStruct((rows, cols - outer, cohorts), jnp.bfloat16),
+        in_specs=[SMEM] + [VMEM] * 6,
+        out_specs=VMEM,
+        compiler_params=PARAMS,
+        cost_estimate=work,
+    )(slots, cells, seeds_in, seeds_out, fecundity, moves, ops)
     return pl.pallas_call(
         last_kernel,
         out_shape=state,
-        in_specs=[SMEM] + [VMEM] * 9,
+        in_specs=[SMEM] + [VMEM] * 10,
         out_specs=VMEM,
         scratch_shapes=[
             pltpu.VMEM((high, outer, cohorts), jnp.float32),
@@ -464,7 +548,7 @@
         ],
         compiler_params=PARAMS,
         cost_estimate=pl.CostEstimate(flops=2**28, bytes_accessed=2**22, transcendentals=0),
-    )(slots, cells, left, right, weights, fecundity, moves, ops, inner, partial)
+    )(slots, cells, left, right, weights, fecundity, moves, ops, inner, partial_in, partial_out)
 
 
 def solution(mesh):

time: 89.8 us -> 91.7 us (1.021)
  the two profiles are of different devices: /device:TPU:1 before, /device:TPU:89 now
where the time goes in v6:
time: 91.7 us; the launch traced here: 91.1 us
  starting transfers between devices  49.5 us (54%)
  waiting for transfers between devices  21 us (23%)
  Pallas kernels  16.3 us (18%)
  local copies, waits for them, and re-layouts  3.33 us (4%)
    ppermute x8, starting transfers between devices, swap(): return (lax.ppermute(tail, axis, after), lax.ppermute(head, axis, before))  26.8 us
    all_to_all x1, starting transfers between devices, fetch(): arrived = lax.all_to_all(spread, WIDE, 0, 0, tiled=True)  15.3 us
    ppermute x8, waiting for transfers between devices, swap(): return (lax.ppermute(tail, axis, after), lax.ppermute(head, axis, before))  14.4 us
    all_to_all x1, starting transfers between devices, fetch(): parts = lax.all_to_all(wanted, NEAR, 0, 0, tiled=True)  7.4 us
    all_to_all x1, waiting for transfers between devices, fetch(): arrived = lax.all_to_all(spread, WIDE, 0, 0, tiled=True)  6.46 us
    pallas_call x1, Pallas kernels, local(): pl.pallas_call(first_kernel, out_shape=state, in_specs=[VMEM] * 8, out_sp...  3.41 us
    unnamed x24, local copies, waits for them, and re-layouts  3.08 us
    pallas_call x1, Pallas kernels, local(): pl.pallas_call(last_kernel, out_shape=state, in_specs=[SMEM] + [VMEM] * 1...  2.95 us
  transfers between devices with their start and end apart: 10, of which 5 were waited for; matrix products, arithmetic and copies ran while one was open for 1% of the time, Pallas kernels for 8%

profile of v6, /device:TPU:89, one launch (start us, length us, event | category | flops | bytes accessed | tf_op | source)
XLA Modules:
  0.0 91.1 jit_solution(17542787932389979022)
XLA Ops:
  0.0 0.0 copy-start.2
  0.0 1.0 %copy-done.2 = bf16[4,256,256]{2,1,0:T(8,128)(2,1)S(1)} copy-done((bf16[4,256,256]{2,1,0:T(8,128)(2,1)S(1)}, bf16[4,256,256]{2,1,0:T(8,128)(2,1)}, u32[]{:S(2)}) %copy-start.2) | copy-done | bytes 524312
  1.0 0.0 copy-start.3
  1.0 0.7 copy-done.3
  1.7 1.4 %shard_map.109.spread = bf16[128,16,128]{2,1,0:T(8,128)(2,1)} custom-call(s32[1,1,8]{2,1,0:T(1,128)S(1)} %copy-done.3, bf16[4,256,256]{2,1,0:T(8,128)(2,1)S(1)} %copy-done.2), custom_call_target="tpu_custom_call" | custom-call | bytes 1048576 | tf_op jit(solution)/shard_map/pallas_call | solution.py:119
  3.1 0.0 copy-start
  3.1 15.3 %all-to-all-start = ((bf16[128,16,128]{2,1,0:T(8,128)(2,1)}), bf16[128,16,128]{2,1,0:T(8,128)(2,1)S(1)}, u32[]{:S(2)}, u32[]{:S(2)}) async-start(bf16[128,16,128]{2,1,0:T(8,128)(2,1)} %shard_map.109.spread), calls=%async_computation | async-start | bytes 1048576 | tf_op jit(solution)/shard_map/all_to_all | solution.py:132
  18.4 0.0 copy-done
  18.4 0.0 copy-start.5
  18.5 0.1 shard_map.110
  18.5 4.6 %collective-permute-start = (bf16[32,4,256]{2,1,0:T(4,128)(2,1)S(1)}, bf16[32,4,256]{2,1,0:T(4,128)(2,1)S(1)}, u32[]{:S(2)}, u32[]{:S(2)}) collective-permute-start(bf16[32,4,256]{2,1,0:T(4,128)(2,1)S(1)} %get-tuple-element.20), channel_id=1, source_target_pairs={{0,1},{1,2},{2,3},{3,4},{4,5},{5,6},{6,7},{7,8},{8,9},{9,10},{10,1... | collective-permute-start | bytes 196616 | tf_op jit(solution)/shard_map/ppermute | solution.py:41
  23.1 3.1 %collective-permute-start.1 = (bf16[32,4,256]{2,1,0:T(4,128)(2,1)S(1)}, bf16[32,4,256]{2,1,0:T(4,128)(2,1)S(1)}, u32[]{:S(2)}, u32[]{:S(2)}) collective-permute-start(bf16[32,4,256]{2,1,0:T(4,128)(2,1)S(1)} %get-tuple-element.21), channel_id=1, source_target_pairs={{1,0},{2,1},{3,2},{4,3},{5,4},{6,5},{7,6},{8,7},{9,8},{10,9},{11,1... | collective-permute-start | bytes 196616 | tf_op jit(solution)/shard_map/ppermute | solution.py:41
  26.2 0.0 copy-done.5
  26.3 0.1 copy.18
  26.4 0.0 copy-start.4
  26.4 0.1 copy.19
  26.5 0.0 copy-start.7
  26.5 0.7 copy-done.7
  27.2 0.0 copy-start.9
  27.2 0.0 copy-start.10
  27.2 0.0 copy-start.11
  27.2 0.6 copy-done.9
  27.9 0.0 copy-done.10
  27.9 0.0 copy-done.11
  27.9 0.1 multiply_reduce_fusion
  28.0 0.1 fusion.5.weights
  28.1 0.0 copy-done.4
  28.1 6.5 %all-to-all-done.arrived = bf16[128,16,128]{2,1,0:T(8,128)(2,1)S(1)} async-done(((bf16[128,16,128]{2,1,0:T(8,128)(2,1)}), bf16[128,16,128]{2,1,0:T(8,128)(2,1)S(1)}, u32[]{:S(2)}, u32[]{:S(2)}) %all-to-all-start) | async-done | bytes 524320 | tf_op jit(solution)/shard_map/all_to_all | solution.py:132
  34.6 0.1 fusion.2
  34.7 0.0 collective-permute-done.left
  34.7 0.0 collective-permute-done.1.right
  34.8 2.3 %shard_map.113 = bf16[32,8,16,128]{3,2,1,0:T(8,128)(2,1)} custom-call(s32[32,8]{1,0:T(8,128)S(1)} %bitcast.13, bf16[128,16,128]{2,1,0:T(8,128)(2,1)S(1)} %all-to-all-done.arrived, bf16[32,4,256]{2,1,0:T(4,128)(2,1)S(1)} %collective-permute-done.left, bf16[32,4,256]{2,1,0:T(4,128)(2,1)S(1)} %collective-permute-done.1.right, f32[10,256]{1,0:T(8,128)S(1)} %fusion.5.weights, ...), custom_call_target="tpu_custom_call" | custom-call | bytes 1048576 | tf_op jit(solution)/shard_map/pallas_call | solution.py:157
  37.1 7.4 %all-to-all-start.1 = ((bf16[32,8,16,128]{3,2,1,0:T(8,128)(2,1)}), bf16[32,8,16,128]{3,2,1,0:T(8,128)(2,1)S(1)}, u32[]{:S(2)}, u32[]{:S(2)}) async-start(bf16[32,8,16,128]{3,2,1,0:T(8,128)(2,1)} %shard_map.113), calls=%async_computation.1 | async-start | bytes 2097152 | tf_op jit(solution)/shard_map/all_to_all | solution.py:165
  44.5 0.0 copy-start.1
  44.5 0.0 copy-start.6
  44.5 3.9 %collective-permute-start.2 = (bf16[4,40,256]{2,1,0:T(8,128)(2,1)S(1)}, bf16[4,40,256]{2,1,0:T(8,128)(2,1)S(1)}, u32[]{:S(2)}, u32[]{:S(2)}) collective-permute-start(bf16[4,40,256]{2,1,0:T(8,128)(2,1)S(1)} %get-tuple-element.22), channel_id=1, source_target_pairs={{0,16},{16,32},{32,48},{48,64},{64,80},{80,96},{96,112},{112,128},... | collective-permute-start | bytes 245768 | tf_op jit(solution)/shard_map/ppermute | solution.py:41
  48.4 0.0 copy-start.8
  48.4 1.9 %collective-permute-start.3 = (bf16[4,40,256]{2,1,0:T(8,128)(2,1)S(1)}, bf16[4,40,256]{2,1,0:T(8,128)(2,1)S(1)}, u32[]{:S(2)}, u32[]{:S(2)}) collective-permute-start(bf16[4,40,256]{2,1,0:T(8,128)(2,1)S(1)} %get-tuple-element.23), channel_id=1, source_target_pairs={{16,0},{32,16},{48,32},{64,48},{80,64},{96,80},{112,96},{128,112},... | collective-permute-start | bytes 245768 | tf_op jit(solution)/shard_map/ppermute | solution.py:41
  50.4 0.0 copy-done.6
  50.4 0.0 copy-done.8
  50.4 0.2 select_reduce_fusion.slots
  50.6 0.0 collective-permute-done.2.top
  50.6 5.1 %collective-permute-done.3.bottom = bf16[4,40,256]{2,1,0:T(8,128)(2,1)S(1)} collective-permute-done((bf16[4,40,256]{2,1,0:T(8,128)(2,1)S(1)}, bf16[4,40,256]{2,1,0:T(8,128)(2,1)S(1)}, u32[]{:S(2)}, u32[]{:S(2)}) %collective-permute-start.3) | collective-permute-done | bytes 81952 | tf_op jit(solution)/shard_map/ppermute | solution.py:41
  55.7 0.0 copy-done.1
  55.7 3.4 %shard_map.112.grown = bf16[32,32,256]{2,1,0:T(8,128)(2,1)S(1)} custom-call(bf16[32,32,256]{2,1,0:T(8,128)(2,1)S(1)} %copy-done, bf16[4,40,256]{2,1,0:T(8,128)(2,1)S(1)} %collective-permute-done.2.top, bf16[4,40,256]{2,1,0:T(8,128)(2,1)S(1)} %collective-permute-done.3.bottom, bf16[32,4,256]{2,1,0:T(4,128)(2,1)S(1)} %collective-permute-done.left, ...), custom_call_target="tpu_custom_call" | custom-call | flops 268435456 | bytes 16777216 | tf_op jit(solution)/shard_map/pallas_call | solution.py:474
  59.1 0.2 all-to-all-done.1.parts
  59.3 1.2 %shard_map.114 = (bf16[32,32,256]{2,1,0:T(8,128)(2,1)S(1)}, bf16[8,256,256]{2,1,0:T(8,128)(2,1)S(1)}, bf16[4,32,256]{2,1,0:T(8,128)(2,1)S(1)}, bf16[32,4,256]{2,1,0:T(4,128)(2,1)S(1)}, bf16[32,4,256]{2,1,0:T(4,128)(2,1)S(1)}) custom-call(s32[4,4]{1,0:T(4,128)S(1)} %select_reduce_fusion.slots, bf16[32,32,256]{2,1,0:T(8,128)(2,1)S(1)} %shard_map.112.grown, ...), custom_call_target="tpu_custom_call" | custom-call | flops 268435456 | bytes 4194304 | tf_op jit(solution)/shard_map/pallas_call | solution.py:485
  60.5 4.6 %collective-permute-start.4 = (bf16[4,32,256]{2,1,0:T(8,128)(2,1)S(1)}, bf16[4,32,256]{2,1,0:T(8,128)(2,1)S(1)}, u32[]{:S(2)}, u32[]{:S(2)}) collective-permute-start(bf16[4,32,256]{2,1,0:T(8,128)(2,1)S(1)} %get-tuple-element.25), channel_id=1, source_target_pairs={{0,16},{16,32},{32,48},{48,64},{64,80},{80,96},{96,112},{112,128},... | collective-permute-start | bytes 196616 | tf_op jit(solution)/shard_map/ppermute | solution.py:41
  65.1 2.2 %shard_map.115 = (bf16[4,32,256]{2,1,0:T(8,128)(2,1)S(1)}, f32[24,16,256]{2,1,0:T(8,128)S(1)}, bf16[24,16,256]{2,1,0:T(8,128)(2,1)S(1)}) custom-call(bf16[32,32,256]{2,1,0:T(8,128)(2,1)S(1)} %get-tuple-element.24.cells, f32[10,256]{1,0:T(8,128)S(1)} %fusion.5.weights), custom_call_target="tpu_custom_call" | custom-call | flops 268435456 | bytes 8388608 | tf_op jit(solution)/shard_map/pallas_call | solution.py:510
  67.3 2.0 %collective-permute-start.5 = (bf16[4,32,256]{2,1,0:T(8,128)(2,1)S(1)}, bf16[4,32,256]{2,1,0:T(8,128)(2,1)S(1)}, u32[]{:S(2)}, u32[]{:S(2)}) collective-permute-start(bf16[4,32,256]{2,1,0:T(8,128)(2,1)S(1)} %get-tuple-element.27), channel_id=1, source_target_pairs={{16,0},{32,16},{48,32},{64,48},{80,64},{96,80},{112,96},{128,112},... | collective-permute-start | bytes 196616 | tf_op jit(solution)/shard_map/ppermute | solution.py:41
  69.3 0.0 collective-permute-done.4.top
  69.3 4.8 %collective-permute-done.5.bottom = bf16[4,32,256]{2,1,0:T(8,128)(2,1)S(1)} collective-permute-done((bf16[4,32,256]{2,1,0:T(8,128)(2,1)S(1)}, bf16[4,32,256]{2,1,0:T(8,128)(2,1)S(1)}, u32[]{:S(2)}, u32[]{:S(2)}) %collective-permute-start.5) | collective-permute-done | bytes 65568 | tf_op jit(solution)/shard_map/ppermute | solution.py:41
  74.1 1.1 %shard_map.116 = (bf16[40,4,256]{2,1,0:T(4,128)(2,1)S(1)}, f32[8,16,256]{2,1,0:T(8,128)S(1)}, bf16[8,16,256]{2,1,0:T(8,128)(2,1)S(1)}) custom-call(bf16[32,32,256]{2,1,0:T(8,128)(2,1)S(1)} %get-tuple-element.24.cells, bf16[4,32,256]{2,1,0:T(8,128)(2,1)S(1)} %collective-permute-done.4.top, bf16[4,32,256]{2,1,0:T(8,128)(2,1)S(1)} %collective-permute-done.5.bottom, ...), custom_call_target="tpu_custom_call" | custom-call | flops 268435456 | bytes 8388608 | tf_op jit(solution)/shard_map/pallas_call | solution.py:521
  75.2 4.1 %collective-permute-start.7 = (bf16[40,4,256]{2,1,0:T(4,128)(2,1)S(1)}, bf16[40,4,256]{2,1,0:T(4,128)(2,1)S(1)}, u32[]{:S(2)}, u32[]{:S(2)}) collective-permute-start(bf16[40,4,256]{2,1,0:T(4,128)(2,1)S(1)} %get-tuple-element.29), channel_id=1, source_target_pairs={{1,0},{2,1},{3,2},{4,3},{5,4},{6,5},{7,6},{8,7},{9,8},{10,9},{11,1... | collective-permute-start | bytes 245768 | tf_op jit(solution)/shard_map/ppermute | solution.py:41
  79.4 0.1 pad_maximum_fusion
  79.5 2.6 %collective-permute-start.6 = (bf16[40,4,256]{2,1,0:T(4,128)(2,1)S(1)}, bf16[40,4,256]{2,1,0:T(4,128)(2,1)S(1)}, u32[]{:S(2)}, u32[]{:S(2)}) collective-permute-start(bf16[40,4,256]{2,1,0:T(4,128)(2,1)S(1)} %pad_maximum_fusion), channel_id=1, source_target_pairs={{0,1},{1,2},{2,3},{3,4},{4,5},{5,6},{6,7},{7,8},{8,9},{9,10},{10,1... | collective-permute-start | bytes 245768 | tf_op jit(solution)/shard_map/ppermute | solution.py:41
  82.1 1.6 %shard_map.117.inner = bf16[32,16,256]{2,1,0:T(8,128)(2,1)S(1)} custom-call(s32[4,4]{1,0:T(4,128)S(1)} %select_reduce_fusion.slots, bf16[32,32,256]{2,1,0:T(8,128)(2,1)S(1)} %get-tuple-element.24.cells, bf16[24,16,256]{2,1,0:T(8,128)(2,1)S(1)} %get-tuple-element.31.seeds_in, bf16[8,16,256]{2,1,0:T(8,128)(2,1)S(1)} %get-tuple-element.32.seeds_out, ...), custom_call_target="tpu_custom_call" | custom-call | flops 268435456 | bytes 8388608 | tf_op jit(solution)/shard_map/pallas_call | solution.py:531
  83.7 0.0 collective-permute-done.7.right
  83.7 4.5 %collective-permute-done.6.left = bf16[40,4,256]{2,1,0:T(4,128)(2,1)S(1)} collective-permute-done((bf16[40,4,256]{2,1,0:T(4,128)(2,1)S(1)}, bf16[40,4,256]{2,1,0:T(4,128)(2,1)S(1)}, u32[]{:S(2)}, u32[]{:S(2)}) %collective-permute-start.6) | collective-permute-done | bytes 81952 | tf_op jit(solution)/shard_map/ppermute | solution.py:41
  88.2 3.0 %shard_map.118 = bf16[32,32,256]{2,1,0:T(8,128)(2,1)} custom-call(s32[4,4]{1,0:T(4,128)S(1)} %select_reduce_fusion.slots, bf16[32,32,256]{2,1,0:T(8,128)(2,1)S(1)} %get-tuple-element.24.cells, bf16[40,4,256]{2,1,0:T(4,128)(2,1)S(1)} %collective-permute-done.6.left, bf16[40,4,256]{2,1,0:T(4,128)(2,1)S(1)} %collective-permute-done.7.right, ...), custom_call_target="tpu_custom_call" | custom-call | flops 268435456 | bytes 4194304 | tf_op jit(solution)/shard_map/pallas_call | solution.py:539
  (11 shorter events, 0.2 us)
Async XLA Ops:
  0.0 1.0 %copy-start.2 = (bf16[4,256,256]{2,1,0:T(8,128)(2,1)S(1)}, bf16[4,256,256]{2,1,0:T(8,128)(2,1)}, u32[]{:S(2)}) copy-start(bf16[4,256,256]{2,1,0:T(8,128)(2,1)} %harvest_ops.1) | copy-start | bytes 1572868
  1.0 0.7 copy-start.3
  3.1 15.3 %copy-start = (bf16[32,32,256]{2,1,0:T(8,128)(2,1)S(1)}, bf16[32,32,256]{2,1,0:T(8,128)(2,1)}, u32[]{:S(2)}) copy-start(bf16[32,32,256]{2,1,0:T(8,128)(2,1)} %cells.5) | copy-start | bytes 1572868
  3.1 31.5 %all-to-all-start = ((bf16[128,16,128]{2,1,0:T(8,128)(2,1)}), bf16[128,16,128]{2,1,0:T(8,128)(2,1)S(1)}, u32[]{:S(2)}, u32[]{:S(2)}) async-start(bf16[128,16,128]{2,1,0:T(8,128)(2,1)} %shard_map.109.spread), calls=%async_computation | async-start | bytes 1048576 | tf_op jit(solution)/shard_map/all_to_all | solution.py:132
  18.4 7.8 %copy-start.5 = (s32[32,32]{1,0:T(8,128)S(1)}, s32[32,32]{1,0:T(8,128)}, u32[]{:S(2)}) copy-start(s32[32,32]{1,0:T(8,128)} %param.17) | copy-start | bytes 12292
  18.5 16.2 %collective-permute-start = (bf16[32,4,256]{2,1,0:T(4,128)(2,1)S(1)}, bf16[32,4,256]{2,1,0:T(4,128)(2,1)S(1)}, u32[]{:S(2)}, u32[]{:S(2)}) collective-permute-start(bf16[32,4,256]{2,1,0:T(4,128)(2,1)S(1)} %get-tuple-element.20), channel_id=1, source_target_pairs={{0,1},{1,2},{2,3},{3,4},{4,5},{5,6},{6,7},{7,8},{8,9},{9,10},{10,1... | collective-permute-start | bytes 196616 | tf_op jit(solution)/shard_map/ppermute | solution.py:41
  23.1 11.6 %collective-permute-start.1 = (bf16[32,4,256]{2,1,0:T(4,128)(2,1)S(1)}, bf16[32,4,256]{2,1,0:T(4,128)(2,1)S(1)}, u32[]{:S(2)}, u32[]{:S(2)}) collective-permute-start(bf16[32,4,256]{2,1,0:T(4,128)(2,1)S(1)} %get-tuple-element.21), channel_id=1, source_target_pairs={{1,0},{2,1},{3,2},{4,3},{5,4},{6,5},{7,6},{8,7},{9,8},{10,9},{11,1... | collective-permute-start | bytes 196616 | tf_op jit(solution)/shard_map/ppermute | solution.py:41
  26.4 1.7 %copy-start.4 = (bf16[256,256]{1,0:T(8,128)(2,1)S(1)}, bf16[256,256]{1,0:T(8,128)(2,1)}, u32[]{:S(2)}) copy-start(bf16[256,256]{1,0:T(8,128)(2,1)} %param.16) | copy-start | bytes 393220
  26.5 0.7 copy-start.7
  27.2 0.7 copy-start.9
  27.2 0.7 copy-start.10
  27.2 0.7 copy-start.11
  37.1 22.2 %all-to-all-start.1 = ((bf16[32,8,16,128]{3,2,1,0:T(8,128)(2,1)}), bf16[32,8,16,128]{3,2,1,0:T(8,128)(2,1)S(1)}, u32[]{:S(2)}, u32[]{:S(2)}) async-start(bf16[32,8,16,128]{3,2,1,0:T(8,128)(2,1)} %shard_map.113), calls=%async_computation.1 | async-start | bytes 2097152 | tf_op jit(solution)/shard_map/all_to_all | solution.py:165
  44.5 11.2 %copy-start.1 = (bf16[256,256]{1,0:T(8,128)(2,1)S(1)}, bf16[256,256]{1,0:T(8,128)(2,1)}, u32[]{:S(2)}) copy-start(bf16[256,256]{1,0:T(8,128)(2,1)} %fecundity.5) | copy-start | bytes 393220
  44.5 5.8 %copy-start.6 = (s32[4,4]{1,0:T(4,128)S(1)}, s32[4,4]{1,0:T(4,128)}, u32[]{:S(2)}) copy-start(s32[4,4]{1,0:T(4,128)} %param.12) | copy-start | bytes 196
  44.5 6.1 %collective-permute-start.2 = (bf16[4,40,256]{2,1,0:T(8,128)(2,1)S(1)}, bf16[4,40,256]{2,1,0:T(8,128)(2,1)S(1)}, u32[]{:S(2)}, u32[]{:S(2)}) collective-permute-start(bf16[4,40,256]{2,1,0:T(8,128)(2,1)S(1)} %get-tuple-element.22), channel_id=1, source_target_pairs={{0,16},{16,32},{32,48},{48,64},{64,80},{80,96},{96,112},{112,128},... | collective-permute-start | bytes 245768 | tf_op jit(solution)/shard_map/ppermute | solution.py:41
  48.4 2.0 %copy-start.8 = (s32[1,1,16]{2,1,0:T(1,128)S(1)}, s32[1,1,16]{2,1,0:T(1,128)}, u32[]{:S(2)}) copy-start(s32[1,1,16]{2,1,0:T(1,128)} %param.13) | copy-start | bytes 196
  48.4 7.3 %collective-permute-start.3 = (bf16[4,40,256]{2,1,0:T(8,128)(2,1)S(1)}, bf16[4,40,256]{2,1,0:T(8,128)(2,1)S(1)}, u32[]{:S(2)}, u32[]{:S(2)}) collective-permute-start(bf16[4,40,256]{2,1,0:T(8,128)(2,1)S(1)} %get-tuple-element.23), channel_id=1, source_target_pairs={{16,0},{32,16},{48,32},{64,48},{80,64},{96,80},{112,96},{128,112},... | collective-permute-start | bytes 245768 | tf_op jit(solution)/shard_map/ppermute | solution.py:41
  60.5 8.8 %collective-permute-start.4 = (bf16[4,32,256]{2,1,0:T(8,128)(2,1)S(1)}, bf16[4,32,256]{2,1,0:T(8,128)(2,1)S(1)}, u32[]{:S(2)}, u32[]{:S(2)}) collective-permute-start(bf16[4,32,256]{2,1,0:T(8,128)(2,1)S(1)} %get-tuple-element.25), channel_id=1, source_target_pairs={{0,16},{16,32},{32,48},{48,64},{64,80},{80,96},{96,112},{112,128},... | collective-permute-start | bytes 196616 | tf_op jit(solution)/shard_map/ppermute | solution.py:41
  67.3 6.8 %collective-permute-start.5 = (bf16[4,32,256]{2,1,0:T(8,128)(2,1)S(1)}, bf16[4,32,256]{2,1,0:T(8,128)(2,1)S(1)}, u32[]{:S(2)}, u32[]{:S(2)}) collective-permute-start(bf16[4,32,256]{2,1,0:T(8,128)(2,1)S(1)} %get-tuple-element.27), channel_id=1, source_target_pairs={{16,0},{32,16},{48,32},{64,48},{80,64},{96,80},{112,96},{128,112},... | collective-permute-start | bytes 196616 | tf_op jit(solution)/shard_map/ppermute | solution.py:41
  75.2 8.5 %collective-permute-start.7 = (bf16[40,4,256]{2,1,0:T(4,128)(2,1)S(1)}, bf16[40,4,256]{2,1,0:T(4,128)(2,1)S(1)}, u32[]{:S(2)}, u32[]{:S(2)}) collective-permute-start(bf16[40,4,256]{2,1,0:T(4,128)(2,1)S(1)} %get-tuple-element.29), channel_id=1, source_target_pairs={{1,0},{2,1},{3,2},{4,3},{5,4},{6,5},{7,6},{8,7},{9,8},{10,9},{11,1... | collective-permute-start | bytes 245768 | tf_op jit(solution)/shard_map/ppermute | solution.py:41
  79.5 8.7 %collective-permute-start.6 = (bf16[40,4,256]{2,1,0:T(4,128)(2,1)S(1)}, bf16[40,4,256]{2,1,0:T(4,128)(2,1)S(1)}, u32[]{:S(2)}, u32[]{:S(2)}) collective-permute-start(bf16[40,4,256]{2,1,0:T(4,128)(2,1)S(1)} %pad_maximum_fusion), channel_id=1, source_target_pairs={{0,1},{1,2},{2,3},{3,4},{4,5},{5,6},{6,7},{7,8},{8,9},{9,10},{10,1... | collective-permute-start | bytes 245768 | tf_op jit(solution)/shard_map/ppermute | solution.py:41

commit v7 on v5

--- a/solution.py
+++ b/solution.py
@@ -27,6 +27,7 @@
 SMEM = pl.BlockSpec(memory_space=pltpu.SMEM)
 ANY = pl.BlockSpec(memory_space=pl.ANY)
 PARAMS = pltpu.CompilerParams(vmem_limit_bytes=32 * 1024 * 1024)
+WHOLE = pltpu.CompilerParams(vmem_limit_bytes=60 * 1024 * 1024)
 
 LEAD = 8
 
@@ -40,8 +41,14 @@
     return lax.ppermute(tail, axis, after), lax.ppermute(head, axis, before)
 
 
-def surround(first, last, head, tail):
-    top, bottom = swap(first, last, ROW)
+def surround(near, far, head, tail):
+    even = lax.axis_index("co") == 0
+    count = math.prod(lax.axis_size(name) for name in ROW)
+    pairs = [(i, i + 1) for i in range(1, count - 1, 2)]
+    far = lax.ppermute(far, ROW, pairs + [(j, i) for i, j in pairs])
+    near = lax.all_to_all(near, "co", 0, 0, tiled=True)
+    near = jnp.where(even, near[1], near[0])
+    top, bottom = jnp.where(even, far, near), jnp.where(even, near, far)
     head = jnp.concatenate([top[:, :RMAX], head, bottom[:, :RMAX]], axis=0)
     tail = jnp.concatenate([top[:, -RMAX:], tail, bottom[:, -RMAX:]], axis=0)
     return (top, bottom) + swap(head, tail, COL)
@@ -55,8 +62,8 @@
     return values / total
 
 
-def sides_kernel(cells, spread, head, tail):
-    del spread
+def sides_kernel(cells, token, head, tail):
+    del token
     rows, cols, _ = cells.shape
 
     def one(x, carry):
@@ -77,24 +84,30 @@
             out[i] = whole.astype(jnp.bfloat16)
 
 
-def spread_kernel(listed, held, spread):
+def spread_kernel(tile_list, harvest_ops, spread, token, listed, held, sems):
     mine = (lax.axis_index("xl") * 2 + lax.axis_index("yl")) * 2 + lax.axis_index("co")
+    list_copy = pltpu.make_async_copy(tile_list, listed, sems.at[0])
+    held_copy = pltpu.make_async_copy(harvest_ops.at[mine // 2], held, sems.at[1])
+    list_copy.start()
+    held_copy.start()
+    list_copy.wait()
     lane = lax.broadcasted_iota(jnp.int32, (16, 128), 1)
     names = jnp.zeros((16, 128), jnp.float32)
     for k in range(listed.shape[-1]):
         names = jnp.where(lax.rem(lane, 64) == k, listed[0, 0, k].astype(jnp.float32), names)
-    held_at, upper = mine // 2, lax.rem(mine, 2)
-    sent = lane // 64 == upper
+    sent = lane // 64 == lax.rem(mine, 2)
+    token[...] = jnp.zeros_like(token)
+    held_copy.wait()
     for group in range(8):
         for near in range(4):
             low, half = divmod(near, 2)
-            piece = held[held_at, pl.ds(group * 32 + low * 16, 16), pl.ds(half * 128, 128)]
+            piece = held[pl.ds(group * 32 + low * 16, 16), pl.ds(half * 128, 128)]
             message = jnp.where(sent, piece.astype(jnp.float32), names).astype(jnp.bfloat16)
             for far in range(4):
                 spread[(group * 4 + far) * 4 + near] = message
 
 
-def gather_kernel(lists, arrived, left, right, weights, moves, wanted):
+def gather_kernel(places, arrived, left, right, weights, moves, wanted):
     del left, right, weights, moves
     members, count = wanted.shape[:2]
     lower = lax.broadcasted_iota(jnp.int32, (16, 128), 1) < 64
@@ -102,8 +115,7 @@
     def one(m, carry):
         found = []
         for k in range(count):
-            name = lists[m, k]
-            at = lax.rem(name, 4) * 32 + name // 4
+            at = places[m, k]
             found.append(jnp.where(lower, arrived[at], arrived[at + 16]))
         for k in range(count):
             wanted[m, k] = found[k]
@@ -118,12 +130,20 @@
     col_part = jax.ShapeDtypeStruct((rows, RMAX, cohorts), jnp.bfloat16)
     row_part = jax.ShapeDtypeStruct((RMAX, cols + 2 * RMAX, cohorts), jnp.bfloat16)
     small = pl.CostEstimate(flops=0, bytes_accessed=2**20, transcendentals=0)
-    spread = pl.pallas_call(
+    spread, token = pl.pallas_call(
         spread_kernel,
-        out_shape=jax.ShapeDtypeStruct((128, 16, 128), jnp.bfloat16),
-        in_specs=[SMEM, VMEM],
-        out_specs=VMEM,
-        compiler_params=PARAMS,
+        out_shape=(
+            jax.ShapeDtypeStruct((128, 16, 128), jnp.bfloat16),
+            jax.ShapeDtypeStruct((8, 128), jnp.float32),
+        ),
+        in_specs=[ANY, ANY],
+        out_specs=(VMEM, VMEM),
+        scratch_shapes=[
+            pltpu.SMEM(tile_list.shape, jnp.int32),
+            pltpu.VMEM((cohorts, cohorts), jnp.bfloat16),
+            pltpu.SemaphoreType.DMA((2,)),
+        ],
+        compiler_params=WHOLE,
         cost_estimate=small,
     )(tile_list, harvest_ops)
     arrived = lax.all_to_all(spread, WIDE, 0, 0, tiled=True)
@@ -134,7 +154,7 @@
         out_specs=(VMEM,) * 2,
         compiler_params=PARAMS,
         cost_estimate=small,
-    )(cells, spread)
+    )(cells, token)
     left, right = swap(head, tail, COL)
     first, last = pl.pallas_call(
         rows_kernel,
@@ -149,7 +169,8 @@
         arrived.reshape(8, 4, 4, 16, 128), lax.axis_index("zh"), axis=1, keepdims=False
     )[:, :, 0].astype(jnp.int32)
     even = jnp.arange(8)[:, None, None] % 2 == 0
-    lists = jnp.where(even, own[:, :, 64 : 64 + count], own[:, :, :count]).reshape(32, count)
+    lists = jnp.where(even, own[:, :, 64 : 64 + count], own[:, :, :count])
+    places = (lists % 4 * 32 + lists // 4).reshape(32, count)
     wanted = pl.pallas_call(
         gather_kernel,
         out_shape=jax.ShapeDtypeStruct((32, count, 16, 128), jnp.bfloat16),
@@ -157,7 +178,7 @@
         out_specs=VMEM,
         compiler_params=PARAMS,
         cost_estimate=small,
-    )(lists, arrived, left, right, weights, moves)
+    )(places, arrived, left, right, weights, moves)
     parts = lax.all_to_all(wanted, NEAR, 0, 0, tiled=True)
     return parts, (top, bottom, left, right)
 
@@ -295,7 +316,7 @@
         grown[span] = result.reshape(BX, cols, cohorts)
 
 
-def harvest_kernel(slots, grown, parts, out, ops, first, last, head, tail):
+def harvest_kernel(slots, grown, parts, out, ops, near, far, head, tail):
     assemble(parts, ops)
     rows, cols, cohorts = grown.shape
     wide = 2 * BY
@@ -309,10 +330,12 @@
         out[span] = whole.astype(jnp.bfloat16)
         head[span] = whole[:, :RMAX].astype(jnp.bfloat16)
         tail[span] = whole[:, cols - RMAX :].astype(jnp.bfloat16)
-        if i == 0:
-            first[...] = whole[:RMAX].astype(jnp.bfloat16)
-        if i == rows // BX - 1:
-            last[...] = whole[BX - RMAX :].astype(jnp.bfloat16)
+    even = lax.axis_index("co") == 0
+    at = jnp.where(even, rows - RMAX, 0)
+    for i in range(RMAX):
+        near[0, i] = out[at + i]
+        near[1, i] = out[at + i]
+        far[i] = out[rows - RMAX - at + i]
 
 
 def middle_kernel(
@@ -428,16 +451,17 @@
         cost_estimate=pl.CostEstimate(flops=2**28, bytes_accessed=2**24, transcendentals=0),
     )(biomass, *around, weights, fecundity, moves)
     row_part = jax.ShapeDtypeStruct((RMAX, cols, cohorts), jnp.bfloat16)
+    row_pair = jax.ShapeDtypeStruct((2, RMAX, cols, cohorts), jnp.bfloat16)
     col_part = jax.ShapeDtypeStruct((rows, RMAX, cohorts), jnp.bfloat16)
-    cells, ops, first, last, head, tail = pl.pallas_call(
+    cells, ops, near, far, head, tail = pl.pallas_call(
         harvest_kernel,
-        out_shape=(state, operators, row_part, row_part, col_part, col_part),
+        out_shape=(state, operators, row_pair, row_part, col_part, col_part),
         in_specs=[SMEM, VMEM, VMEM],
         out_specs=(VMEM,) * 6,
         compiler_params=PARAMS,
         cost_estimate=pl.CostEstimate(flops=2**28, bytes_accessed=2**22, transcendentals=0),
     )(slots, grown, parts)
-    top, bottom, left, right = surround(first, last, head, tail)
+    top, bottom, left, right = surround(near, far, head, tail)
     high = rows + 2 * RMAX
     outer = 2 * BY
     inner, partial = pl.pallas_call(

time: 89.8 us -> 89.3 us (level)
  waiting for transfers between devices: 22.9 us -> 18.8 us
  blocking collectives: 0 us -> 3.5 us
  starting transfers between devices: 45 us -> 42.9 us
  local copies, waits for them, and re-layouts: 3.33 us -> 4.38 us
    ppermute x8 -> x6, starting transfers between devices: 22 us -> 17.6 us  [swap(): return (lax.ppermute(tail, axis, after), lax.ppermute(head, axis, before))]
    ppermute x8 -> x6, waiting for transfers between devices: 13.5 us -> 9.42 us  [swap(): return (lax.ppermute(tail, axis, after), lax.ppermute(head, axis, before))]
    all_to_all x0 -> x1, blocking collectives: none -> 3.5 us  [surround(): near = lax.all_to_all(near, 'co', 0, 0, tiled=True)]
    ppermute x0 -> x1, starting transfers between devices: none -> 2.26 us  [surround(): far = lax.ppermute(far, ROW, pairs + [(j, i) for i, j in pairs])]
    pallas_call x1, Pallas kernels: 3.39 us -> 2.3 us  [fetch(): pl.pallas_call(gather_kernel, out_shape=jax.ShapeDtypeStruct((32, count,...]
    unnamed x24 -> x34, local copies, waits for them, and re-layouts: 3.07 us -> 4.12 us
    pallas_call x2, Pallas kernels: 2.64 us -> 3.64 us  [the longest x1 1.89 us: local(): pl.pallas_call(harvest_kernel, out_shape=(state, operators, row_pair, row...]
  transfers between devices with their start and end apart: 10 -> 9, of which waited for: 5 -> 4; matrix products, arithmetic and copies ran while one was open for 1% -> 2% of each run, Pallas kernels for 9% -> 9%
where the time goes in v7:
time: 89.3 us; the launch traced here: 88.2 us
  starting transfers between devices  42.9 us (48%)
  waiting for transfers between devices  18.8 us (21%)
  Pallas kernels  16.9 us (19%)
  local copies, waits for them, and re-layouts  4.38 us (5%)
  blocking collectives  3.5 us (4%)
  other arithmetic  1.3 us (1%)
    ppermute x6, starting transfers between devices, swap(): return (lax.ppermute(tail, axis, after), lax.ppermute(head, axis, before))  17.6 us
    all_to_all x1, starting transfers between devices, fetch(): arrived = lax.all_to_all(spread, WIDE, 0, 0, tiled=True)  16.8 us
    ppermute x6, waiting for transfers between devices, swap(): return (lax.ppermute(tail, axis, after), lax.ppermute(head, axis, before))  9.42 us
    all_to_all x1, waiting for transfers between devices, fetch(): arrived = lax.all_to_all(spread, WIDE, 0, 0, tiled=True)  9.39 us
    all_to_all x1, starting transfers between devices, fetch(): parts = lax.all_to_all(wanted, NEAR, 0, 0, tiled=True)  6.24 us
    pallas_call x1, Pallas kernels, local(): pl.pallas_call(middle_kernel, out_shape=(jax.ShapeDtypeStruct((rows, cols...  4.39 us
    unnamed x34, local copies, waits for them, and re-layouts  4.12 us
    all_to_all x1, blocking collectives, surround(): near = lax.all_to_all(near, 'co', 0, 0, tiled=True)  3.5 us
  transfers between devices with their start and end apart: 9, of which 4 were waited for; matrix products, arithmetic and copies ran while one was open for 2% of the time, Pallas kernels for 9%

profile of v7, /device:TPU:1, one launch (start us, length us, event | category | flops | bytes accessed | tf_op | source)
XLA Modules:
  0.0 88.2 jit_solution(2109888670814662617)
XLA Ops:
  0.0 1.8 %shard_map.109 = (bf16[128,16,128]{2,1,0:T(8,128)(2,1)}, f32[8,128]{1,0:T(8,128)}) custom-call(s32[1,1,8]{2,1,0:T(1,128)} %tile_list.1, bf16[4,256,256]{2,1,0:T(8,128)(2,1)} %harvest_ops.1), custom_call_target="tpu_custom_call" | custom-call | bytes 1048576 | tf_op jit(solution)/shard_map/pallas_call | solution.py:133
  1.8 0.0 copy-start
  1.8 0.0 copy-start.8
  1.8 16.8 %all-to-all-start = ((bf16[128,16,128]{2,1,0:T(8,128)(2,1)}), bf16[128,16,128]{2,1,0:T(8,128)(2,1)S(1)}, u32[]{:S(2)}, u32[]{:S(2)}) async-start(bf16[128,16,128]{2,1,0:T(8,128)(2,1)} %get-tuple-element.24), calls=%async_computation | async-start | bytes 1048576 | tf_op jit(solution)/shard_map/all_to_all | solution.py:149
  18.6 0.0 copy-done
  18.6 0.0 copy-done.8
  18.6 0.0 copy-start.10
  18.6 0.1 shard_map.110
  18.7 4.8 %collective-permute-start = (bf16[32,4,256]{2,1,0:T(4,128)(2,1)S(1)}, bf16[32,4,256]{2,1,0:T(4,128)(2,1)S(1)}, u32[]{:S(2)}, u32[]{:S(2)}) collective-permute-start(bf16[32,4,256]{2,1,0:T(4,128)(2,1)S(1)} %get-tuple-element.20), channel_id=1, source_target_pairs={{0,1},{1,2},{2,3},{3,4},{4,5},{5,6},{6,7},{7,8},{8,9},{9,10},{10,1... | collective-permute-start | bytes 196616 | tf_op jit(solution)/shard_map/ppermute | solution.py:41
  23.5 1.3 %collective-permute-start.1 = (bf16[32,4,256]{2,1,0:T(4,128)(2,1)S(1)}, bf16[32,4,256]{2,1,0:T(4,128)(2,1)S(1)}, u32[]{:S(2)}, u32[]{:S(2)}) collective-permute-start(bf16[32,4,256]{2,1,0:T(4,128)(2,1)S(1)} %get-tuple-element.21), channel_id=1, source_target_pairs={{1,0},{2,1},{3,2},{4,3},{5,4},{6,5},{7,6},{8,7},{9,8},{10,9},{11,1... | collective-permute-start | bytes 196616 | tf_op jit(solution)/shard_map/ppermute | solution.py:41
  24.8 0.0 copy-done.10
  24.8 0.1 copy.18
  24.9 0.0 copy-start.9
  24.9 0.1 copy.19
  25.1 0.0 copy-start.12
  25.1 0.7 copy-done.12
  25.8 0.0 copy-start.15
  25.8 0.0 copy-start.16
  25.8 0.6 copy-done.14
  26.4 0.0 copy-done.15
  26.4 0.0 copy-done.16
  26.4 0.1 multiply_reduce_fusion
  26.5 0.1 fusion.6.weights
  26.6 0.0 copy-done.9
  26.7 9.4 %all-to-all-done.arrived = bf16[128,16,128]{2,1,0:T(8,128)(2,1)S(1)} async-done(((bf16[128,16,128]{2,1,0:T(8,128)(2,1)}), bf16[128,16,128]{2,1,0:T(8,128)(2,1)S(1)}, u32[]{:S(2)}, u32[]{:S(2)}) %all-to-all-start) | async-done | bytes 524320 | tf_op jit(solution)/shard_map/all_to_all | solution.py:149
  36.1 0.1 fusion.3
  36.2 0.0 collective-permute-done.left
  36.2 0.0 collective-permute-done.1.right
  36.2 2.3 %shard_map.113 = bf16[32,8,16,128]{3,2,1,0:T(8,128)(2,1)} custom-call(s32[32,8]{1,0:T(8,128)S(1)} %bitcast.19, bf16[128,16,128]{2,1,0:T(8,128)(2,1)S(1)} %all-to-all-done.arrived, bf16[32,4,256]{2,1,0:T(4,128)(2,1)S(1)} %collective-permute-done.left, bf16[32,4,256]{2,1,0:T(4,128)(2,1)S(1)} %collective-permute-done.1.right, f32[10,256]{1,0:T(8,128)S(1)} %fusion.6.weights, ...), custom_call_target="tpu_custom_call" | custom-call | bytes 1048576 | tf_op jit(solution)/shard_map/pallas_call | solution.py:174
  38.5 6.2 %all-to-all-start.1 = ((bf16[32,8,16,128]{3,2,1,0:T(8,128)(2,1)}), bf16[32,8,16,128]{3,2,1,0:T(8,128)(2,1)S(1)}, u32[]{:S(2)}, u32[]{:S(2)}) async-start(bf16[32,8,16,128]{3,2,1,0:T(8,128)(2,1)} %shard_map.113), calls=%async_computation.1 | async-start | bytes 2097152 | tf_op jit(solution)/shard_map/all_to_all | solution.py:182
  44.8 0.0 copy-start.1
  44.8 0.0 copy-start.11
  44.8 3.5 %collective-permute-start.2 = (bf16[4,40,256]{2,1,0:T(8,128)(2,1)S(1)}, bf16[4,40,256]{2,1,0:T(8,128)(2,1)S(1)}, u32[]{:S(2)}, u32[]{:S(2)}) collective-permute-start(bf16[4,40,256]{2,1,0:T(8,128)(2,1)S(1)} %get-tuple-element.22), channel_id=1, source_target_pairs={{0,16},{16,32},{32,48},{48,64},{64,80},{80,96},{96,112},{112,128},... | collective-permute-start | bytes 245768 | tf_op jit(solution)/shard_map/ppermute | solution.py:41
  48.4 0.0 copy-start.13
  48.4 1.9 %collective-permute-start.3 = (bf16[4,40,256]{2,1,0:T(8,128)(2,1)S(1)}, bf16[4,40,256]{2,1,0:T(8,128)(2,1)S(1)}, u32[]{:S(2)}, u32[]{:S(2)}) collective-permute-start(bf16[4,40,256]{2,1,0:T(8,128)(2,1)S(1)} %get-tuple-element.23), channel_id=1, source_target_pairs={{16,0},{32,16},{48,32},{64,48},{80,64},{96,80},{112,96},{128,112},... | collective-permute-start | bytes 245768 | tf_op jit(solution)/shard_map/ppermute | solution.py:41
  50.3 0.0 copy-done.11
  50.3 0.0 copy-done.13
  50.4 0.8 select_reduce_fusion.slots
  51.2 6.3 %collective-permute-done.2.top = bf16[4,40,256]{2,1,0:T(8,128)(2,1)S(1)} collective-permute-done((bf16[4,40,256]{2,1,0:T(8,128)(2,1)S(1)}, bf16[4,40,256]{2,1,0:T(8,128)(2,1)S(1)}, u32[]{:S(2)}, u32[]{:S(2)}) %collective-permute-start.2) | collective-permute-done | bytes 81952 | tf_op jit(solution)/shard_map/ppermute | solution.py:41
  57.5 2.1 %collective-permute-done.3.bottom = bf16[4,40,256]{2,1,0:T(8,128)(2,1)S(1)} collective-permute-done((bf16[4,40,256]{2,1,0:T(8,128)(2,1)S(1)}, bf16[4,40,256]{2,1,0:T(8,128)(2,1)S(1)}, u32[]{:S(2)}, u32[]{:S(2)}) %collective-permute-start.3) | collective-permute-done | bytes 81952 | tf_op jit(solution)/shard_map/ppermute | solution.py:41
  59.6 0.0 copy-done.1
  59.6 3.4 %shard_map.112.grown = bf16[32,32,256]{2,1,0:T(8,128)(2,1)S(1)} custom-call(bf16[32,32,256]{2,1,0:T(8,128)(2,1)S(1)} %copy-done, bf16[4,40,256]{2,1,0:T(8,128)(2,1)S(1)} %collective-permute-done.2.top, bf16[4,40,256]{2,1,0:T(8,128)(2,1)S(1)} %collective-permute-done.3.bottom, bf16[32,4,256]{2,1,0:T(4,128)(2,1)S(1)} %collective-permute-done.left, ...), custom_call_target="tpu_custom_call" | custom-call | flops 268435456 | bytes 16777216 | tf_op jit(solution)/shard_map/pallas_call | solution.py:444
  63.0 0.0 all-to-all-done.1.parts
  63.0 0.0 copy-start.6
  63.0 0.7 copy-done.6
  63.7 1.9 %shard_map.114 = (bf16[32,32,256]{2,1,0:T(8,128)(2,1)S(1)}, bf16[8,256,256]{2,1,0:T(8,128)(2,1)S(1)}, bf16[2,4,32,256]{3,2,1,0:T(8,128)(2,1)S(1)}, bf16[4,32,256...) custom-call(s32[4,4]{1,0:T(4,128)S(1)} %copy-done.6, ...), custom_call_target="tpu_custom_call" | custom-call | flops 268435456 | bytes 4194304 | tf_op jit(solution)/shard_map/pallas_call | solution.py:456
  65.6 0.6 copy-done.2
  66.2 0.6 copy-done.4
  66.9 2.3 %collective-permute-start.4 = (bf16[4,32,256]{2,1,0:T(8,128)(2,1)}, bf16[4,32,256]{2,1,0:T(8,128)(2,1)S(1)}, u32[]{:S(2)}, u32[]{:S(2)}) collective-permute-start(bf16[4,32,256]{2,1,0:T(8,128)(2,1)} %get-tuple-element.26), channel_id=1, source_target_pairs={{16,32},{48,64},{80,96},{112,128},{144,160},{176,192},{208,224},{2... | collective-permute-start | bytes 196616 | tf_op jit(solution)/shard_map/ppermute | solution.py:48
  69.1 3.5 %all_to_all.15 = bf16[2,4,32,256]{3,2,1,0:T(8,128)(2,1)S(1)} all-to-all(bf16[2,4,32,256]{3,2,1,0:T(8,128)(2,1)S(1)} %get-tuple-element.27), channel_id=1, replica_groups=mesh['xl'=2,'yh'=4,'yl'=2,'co'=2,'zh'=4,'zl'=2,'xh'=2] {'co'}, dimensions={0} | all-to-all | bytes 262144 | tf_op jit(solution)/shard_map/all_to_all | solution.py:49
  72.6 0.0 collective-permute-done.4
  72.7 0.0 copy-start.5
  72.7 0.8 copy-done.5
  73.5 0.1 pad_maximum_fusion
  73.6 4.8 %collective-permute-start.5 = (bf16[40,4,256]{2,1,0:T(4,128)(2,1)S(1)}, bf16[40,4,256]{2,1,0:T(4,128)(2,1)S(1)}, u32[]{:S(2)}, u32[]{:S(2)}) collective-permute-start(bf16[40,4,256]{2,1,0:T(4,128)(2,1)S(1)} %pad_maximum_fusion), channel_id=1, source_target_pairs={{0,1},{1,2},{2,3},{3,4},{4,5},{5,6},{6,7},{7,8},{8,9},{9,10},{10,1... | collective-permute-start | bytes 245768 | tf_op jit(solution)/shard_map/ppermute | solution.py:41
  78.4 0.0 copy-done.3
  78.4 0.1 pad_maximum_fusion.1
  78.4 0.0 copy-start.7
  78.4 1.3 %collective-permute-start.6 = (bf16[40,4,256]{2,1,0:T(4,128)(2,1)S(1)}, bf16[40,4,256]{2,1,0:T(4,128)(2,1)S(1)}, u32[]{:S(2)}, u32[]{:S(2)}) collective-permute-start(bf16[40,4,256]{2,1,0:T(4,128)(2,1)S(1)} %pad_maximum_fusion.1), channel_id=1, source_target_pairs={{1,0},{2,1},{3,2},{4,3},{5,4},{6,5},{7,6},{8,7},{9,8},{10,9},{11,1... | collective-permute-start | bytes 245768 | tf_op jit(solution)/shard_map/ppermute | solution.py:41
  79.7 0.0 copy-done.7
  79.8 4.4 %shard_map.115 = (bf16[32,16,256]{2,1,0:T(8,128)(2,1)S(1)}, f32[32,16,256]{2,1,0:T(8,128)S(1)}) custom-call(s32[4,4]{1,0:T(4,128)S(1)} %copy-done.7, bf16[32,32,256]{2,1,0:T(8,128)(2,1)S(1)} %get-tuple-element.25.cells, bf16[4,32,256]{2,1,0:T(8,128)(2,1)S(1)} %get-tuple-element.33.top, bf16[4,32,256]{2,1,0:T(8,128)(2,1)S(1)} %get-tuple-element.34.bottom, ...), custom_call_target="tpu_custom_call" | custom-call | flops 268435456 | bytes 16777216 | tf_op jit(solution)/shard_map/pallas_call | solution.py:467
  84.2 0.0 collective-permute-done.5.left
  84.2 1.0 %collective-permute-done.6.right = bf16[40,4,256]{2,1,0:T(4,128)(2,1)S(1)} collective-permute-done((bf16[40,4,256]{2,1,0:T(4,128)(2,1)S(1)}, bf16[40,4,256]{2,1,0:T(4,128)(2,1)S(1)}, u32[]{:S(2)}, u32[]{:S(2)}) %collective-permute-start.6) | collective-permute-done | bytes 81952 | tf_op jit(solution)/shard_map/ppermute | solution.py:41
  85.1 3.0 %shard_map.116 = bf16[32,32,256]{2,1,0:T(8,128)(2,1)} custom-call(s32[4,4]{1,0:T(4,128)S(1)} %copy-done.7, bf16[32,32,256]{2,1,0:T(8,128)(2,1)S(1)} %get-tuple-element.25.cells, bf16[40,4,256]{2,1,0:T(4,128)(2,1)S(1)} %collective-permute-done.5.left, bf16[40,4,256]{2,1,0:T(4,128)(2,1)S(1)} %collective-permute-done.6.right, f32[10,256]{1,0:T(8,128)S(1)} %fusion.6.weights, ...), custom_call_target="tpu_custom_call" | custom-call | flops 268435456 | bytes 4194304 | tf_op jit(solution)/shard_map/pallas_call | solution.py:479
  (15 shorter events, 0.2 us)
Async XLA Ops:
  1.8 16.8 %copy-start = (bf16[32,32,256]{2,1,0:T(8,128)(2,1)S(1)}, bf16[32,32,256]{2,1,0:T(8,128)(2,1)}, u32[]{:S(2)}) copy-start(bf16[32,32,256]{2,1,0:T(8,128)(2,1)} %cells.5) | copy-start | bytes 1572868
  1.8 16.8 %copy-start.8 = (f32[8,128]{1,0:T(8,128)S(1)}, f32[8,128]{1,0:T(8,128)}, u32[]{:S(2)}) copy-start(f32[8,128]{1,0:T(8,128)} %get-tuple-element.19.token) | copy-start | bytes 12292
  1.8 34.3 %all-to-all-start = ((bf16[128,16,128]{2,1,0:T(8,128)(2,1)}), bf16[128,16,128]{2,1,0:T(8,128)(2,1)S(1)}, u32[]{:S(2)}, u32[]{:S(2)}) async-start(bf16[128,16,128]{2,1,0:T(8,128)(2,1)} %get-tuple-element.24), calls=%async_computation | async-start | bytes 1048576 | tf_op jit(solution)/shard_map/all_to_all | solution.py:149
  18.6 6.2 %copy-start.10 = (s32[32,32]{1,0:T(8,128)S(1)}, s32[32,32]{1,0:T(8,128)}, u32[]{:S(2)}) copy-start(s32[32,32]{1,0:T(8,128)} %param.17) | copy-start | bytes 12292
  18.7 17.5 %collective-permute-start = (bf16[32,4,256]{2,1,0:T(4,128)(2,1)S(1)}, bf16[32,4,256]{2,1,0:T(4,128)(2,1)S(1)}, u32[]{:S(2)}, u32[]{:S(2)}) collective-permute-start(bf16[32,4,256]{2,1,0:T(4,128)(2,1)S(1)} %get-tuple-element.20), channel_id=1, source_target_pairs={{0,1},{1,2},{2,3},{3,4},{4,5},{5,6},{6,7},{7,8},{8,9},{9,10},{10,1... | collective-permute-start | bytes 196616 | tf_op jit(solution)/shard_map/ppermute | solution.py:41
  23.5 12.8 %collective-permute-start.1 = (bf16[32,4,256]{2,1,0:T(4,128)(2,1)S(1)}, bf16[32,4,256]{2,1,0:T(4,128)(2,1)S(1)}, u32[]{:S(2)}, u32[]{:S(2)}) collective-permute-start(bf16[32,4,256]{2,1,0:T(4,128)(2,1)S(1)} %get-tuple-element.21), channel_id=1, source_target_pairs={{1,0},{2,1},{3,2},{4,3},{5,4},{6,5},{7,6},{8,7},{9,8},{10,9},{11,1... | collective-permute-start | bytes 196616 | tf_op jit(solution)/shard_map/ppermute | solution.py:41
  24.9 1.7 %copy-start.9 = (bf16[256,256]{1,0:T(8,128)(2,1)S(1)}, bf16[256,256]{1,0:T(8,128)(2,1)}, u32[]{:S(2)}) copy-start(bf16[256,256]{1,0:T(8,128)(2,1)} %param.16) | copy-start | bytes 393220
  25.1 0.7 copy-start.12
  25.7 0.7 copy-start.14
  25.8 0.7 copy-start.15
  25.8 0.7 copy-start.16
  38.5 24.5 %all-to-all-start.1 = ((bf16[32,8,16,128]{3,2,1,0:T(8,128)(2,1)}), bf16[32,8,16,128]{3,2,1,0:T(8,128)(2,1)S(1)}, u32[]{:S(2)}, u32[]{:S(2)}) async-start(bf16[32,8,16,128]{3,2,1,0:T(8,128)(2,1)} %shard_map.113), calls=%async_computation.1 | async-start | bytes 2097152 | tf_op jit(solution)/shard_map/all_to_all | solution.py:182
  44.8 14.8 %copy-start.1 = (bf16[256,256]{1,0:T(8,128)(2,1)S(1)}, bf16[256,256]{1,0:T(8,128)(2,1)}, u32[]{:S(2)}) copy-start(bf16[256,256]{1,0:T(8,128)(2,1)} %fecundity.5) | copy-start | bytes 393220
  44.8 5.5 %copy-start.11 = (s32[4,4]{1,0:T(4,128)S(1)}, s32[4,4]{1,0:T(4,128)}, u32[]{:S(2)}) copy-start(s32[4,4]{1,0:T(4,128)} %param.12) | copy-start | bytes 196
  44.8 12.6 %collective-permute-start.2 = (bf16[4,40,256]{2,1,0:T(8,128)(2,1)S(1)}, bf16[4,40,256]{2,1,0:T(8,128)(2,1)S(1)}, u32[]{:S(2)}, u32[]{:S(2)}) collective-permute-start(bf16[4,40,256]{2,1,0:T(8,128)(2,1)S(1)} %get-tuple-element.22), channel_id=1, source_target_pairs={{0,16},{16,32},{32,48},{48,64},{64,80},{80,96},{96,112},{112,128},... | collective-permute-start | bytes 245768 | tf_op jit(solution)/shard_map/ppermute | solution.py:41
  48.4 2.0 %copy-start.13 = (s32[1,1,16]{2,1,0:T(1,128)S(1)}, s32[1,1,16]{2,1,0:T(1,128)}, u32[]{:S(2)}) copy-start(s32[1,1,16]{2,1,0:T(1,128)} %param.13) | copy-start | bytes 196
  48.4 11.2 %collective-permute-start.3 = (bf16[4,40,256]{2,1,0:T(8,128)(2,1)S(1)}, bf16[4,40,256]{2,1,0:T(8,128)(2,1)S(1)}, u32[]{:S(2)}, u32[]{:S(2)}) collective-permute-start(bf16[4,40,256]{2,1,0:T(8,128)(2,1)S(1)} %get-tuple-element.23), channel_id=1, source_target_pairs={{16,0},{32,16},{48,32},{64,48},{80,64},{96,80},{112,96},{128,112},... | collective-permute-start | bytes 245768 | tf_op jit(solution)/shard_map/ppermute | solution.py:41
  63.0 0.7 copy-start.6
  65.6 0.6 copy-start.2
  66.2 0.6 copy-start.4
  66.9 5.8 %collective-permute-start.4 = (bf16[4,32,256]{2,1,0:T(8,128)(2,1)}, bf16[4,32,256]{2,1,0:T(8,128)(2,1)S(1)}, u32[]{:S(2)}, u32[]{:S(2)}) collective-permute-start(bf16[4,32,256]{2,1,0:T(8,128)(2,1)} %get-tuple-element.26), channel_id=1, source_target_pairs={{16,32},{48,64},{80,96},{112,128},{144,160},{176,192},{208,224},{2... | collective-permute-start | bytes 196616 | tf_op jit(solution)/shard_map/ppermute | solution.py:48
  72.7 0.8 copy-start.5
  73.5 4.9 %copy-start.3 = (bf16[32,4,256]{2,1,0:T(4,128)(2,1)S(1)}, bf16[32,4,256]{2,1,0:T(4,128)(2,1)}, u32[]{:S(2)}) copy-start(bf16[32,4,256]{2,1,0:T(4,128)(2,1)} %copy-done.2) | copy-start | bytes 196612
  73.6 10.6 %collective-permute-start.5 = (bf16[40,4,256]{2,1,0:T(4,128)(2,1)S(1)}, bf16[40,4,256]{2,1,0:T(4,128)(2,1)S(1)}, u32[]{:S(2)}, u32[]{:S(2)}) collective-permute-start(bf16[40,4,256]{2,1,0:T(4,128)(2,1)S(1)} %pad_maximum_fusion), channel_id=1, source_target_pairs={{0,1},{1,2},{2,3},{3,4},{4,5},{5,6},{6,7},{7,8},{8,9},{9,10},{10,1... | collective-permute-start | bytes 245768 | tf_op jit(solution)/shard_map/ppermute | solution.py:41
  78.4 1.3 %copy-start.7 = (s32[4,4]{1,0:T(4,128)S(1)}, s32[4,4]{1,0:T(4,128)}, u32[]{:S(2)}) copy-start(s32[4,4]{1,0:T(4,128)} %select_reduce_fusion.slots) | copy-start | bytes 196
  78.4 6.7 %collective-permute-start.6 = (bf16[40,4,256]{2,1,0:T(4,128)(2,1)S(1)}, bf16[40,4,256]{2,1,0:T(4,128)(2,1)S(1)}, u32[]{:S(2)}, u32[]{:S(2)}) collective-permute-start(bf16[40,4,256]{2,1,0:T(4,128)(2,1)S(1)} %pad_maximum_fusion.1), channel_id=1, source_target_pairs={{1,0},{2,1},{3,2},{4,3},{5,4},{6,5},{7,6},{8,7},{9,8},{10,9},{11,1... | collective-permute-start | bytes 245768 | tf_op jit(solution)/shard_map/ppermute | solution.py:41

commit v8 on v7

--- a/solution.py
+++ b/solution.py
@@ -316,7 +316,7 @@
         grown[span] = result.reshape(BX, cols, cohorts)
 
 
-def harvest_kernel(slots, grown, parts, out, ops, near, far, head, tail):
+def harvest_kernel(slots, grown, parts, out, ops, near, far):
     assemble(parts, ops)
     rows, cols, cohorts = grown.shape
     wide = 2 * BY
@@ -328,8 +328,6 @@
             done.append(remove_pair(flat, (slots[i, 2 * j], slots[i, 2 * j + 1]), ops))
         whole = jnp.concatenate(done, axis=1)
         out[span] = whole.astype(jnp.bfloat16)
-        head[span] = whole[:, :RMAX].astype(jnp.bfloat16)
-        tail[span] = whole[:, cols - RMAX :].astype(jnp.bfloat16)
     even = lax.axis_index("co") == 0
     at = jnp.where(even, rows - RMAX, 0)
     for i in range(RMAX):
@@ -452,16 +450,15 @@
     )(biomass, *around, weights, fecundity, moves)
     row_part = jax.ShapeDtypeStruct((RMAX, cols, cohorts), jnp.bfloat16)
     row_pair = jax.ShapeDtypeStruct((2, RMAX, cols, cohorts), jnp.bfloat16)
-    col_part = jax.ShapeDtypeStruct((rows, RMAX, cohorts), jnp.bfloat16)
-    cells, ops, near, far, head, tail = pl.pallas_call(
+    cells, ops, near, far = pl.pallas_call(
         harvest_kernel,
-        out_shape=(state, operators, row_pair, row_part, col_part, col_part),
+        out_shape=(state, operators, row_pair, row_part),
         in_specs=[SMEM, VMEM, VMEM],
-        out_specs=(VMEM,) * 6,
+        out_specs=(VMEM,) * 4,
         compiler_params=PARAMS,
         cost_estimate=pl.CostEstimate(flops=2**28, bytes_accessed=2**22, transcendentals=0),
     )(slots, grown, parts)
-    top, bottom, left, right = surround(near, far, head, tail)
+    top, bottom, left, right = surround(near, far, cells[:, :RMAX], cells[:, -RMAX:])
     high = rows + 2 * RMAX
     outer = 2 * BY
     inner, partial = pl.pallas_call(

time: 89.3 us -> 90.4 us (1.012)
  the two profiles are of different devices: /device:TPU:1 before, /device:TPU:6 now
where the time goes in v8:
time: 90.4 us; the launch traced here: 89.8 us
  starting transfers between devices  56.5 us (62%)
  Pallas kernels  16.9 us (19%)
  waiting for transfers between devices  13.6 us (15%)
  local copies, waits for them, and re-layouts  1.7 us (2%)
    ppermute x6, starting transfers between devices, swap(): return (lax.ppermute(tail, axis, after), lax.ppermute(head, axis, before))  22.4 us
    all_to_all x1, starting transfers between devices, fetch(): arrived = lax.all_to_all(spread, WIDE, 0, 0, tiled=True)  16.1 us
    all_to_all x1, waiting for transfers between devices, fetch(): arrived = lax.all_to_all(spread, WIDE, 0, 0, tiled=True)  7.39 us
    ppermute x1, starting transfers between devices, surround(): far = lax.ppermute(far, ROW, pairs + [(j, i) for i, j in pairs])  6.99 us
    all_to_all x1, starting transfers between devices, fetch(): parts = lax.all_to_all(wanted, NEAR, 0, 0, tiled=True)  6.66 us
    all_to_all x1, starting transfers between devices, surround(): near = lax.all_to_all(near, 'co', 0, 0, tiled=True)  4.43 us
    pallas_call x1, Pallas kernels, local(): pl.pallas_call(middle_kernel, out_shape=(jax.ShapeDtypeStruct((rows, cols...  4.39 us
    pallas_call x1, Pallas kernels, local(): pl.pallas_call(first_kernel, out_shape=state, in_specs=[VMEM] * 8, out_sp...  3.4 us
  transfers between devices with their start and end apart: 10, of which 6 were waited for; matrix products, arithmetic and copies ran while one was open for 1% of the time, Pallas kernels for 9%

profile of v8, /device:TPU:6, one launch (start us, length us, event | category | flops | bytes accessed | tf_op | source)
XLA Modules:
  0.0 89.8 jit_solution(8317278593996233026)
XLA Ops:
  0.0 1.8 %shard_map.109 = (bf16[128,16,128]{2,1,0:T(8,128)(2,1)}, f32[8,128]{1,0:T(8,128)}) custom-call(s32[1,1,8]{2,1,0:T(1,128)} %tile_list.1, bf16[4,256,256]{2,1,0:T(8,128)(2,1)} %harvest_ops.1), custom_call_target="tpu_custom_call" | custom-call | bytes 1048576 | tf_op jit(solution)/shard_map/pallas_call | solution.py:133
  1.8 0.0 copy-start
  1.8 0.0 copy-start.2
  1.8 16.1 %all-to-all-start = ((bf16[128,16,128]{2,1,0:T(8,128)(2,1)}), bf16[128,16,128]{2,1,0:T(8,128)(2,1)S(1)}, u32[]{:S(2)}, u32[]{:S(2)}) async-start(bf16[128,16,128]{2,1,0:T(8,128)(2,1)} %get-tuple-element.22), calls=%async_computation | async-start | bytes 1048576 | tf_op jit(solution)/shard_map/all_to_all | solution.py:149
  17.9 0.0 copy-done
  17.9 0.0 copy-done.2
  17.9 0.0 copy-start.4
  17.9 0.1 shard_map.110
  18.0 4.3 %collective-permute-start = (bf16[32,4,256]{2,1,0:T(4,128)(2,1)S(1)}, bf16[32,4,256]{2,1,0:T(4,128)(2,1)S(1)}, u32[]{:S(2)}, u32[]{:S(2)}) collective-permute-start(bf16[32,4,256]{2,1,0:T(4,128)(2,1)S(1)} %get-tuple-element.18), channel_id=1, source_target_pairs={{0,1},{1,2},{2,3},{3,4},{4,5},{5,6},{6,7},{7,8},{8,9},{9,10},{10,1... | collective-permute-start | bytes 196616 | tf_op jit(solution)/shard_map/ppermute | solution.py:41
  22.2 3.1 %collective-permute-start.1 = (bf16[32,4,256]{2,1,0:T(4,128)(2,1)S(1)}, bf16[32,4,256]{2,1,0:T(4,128)(2,1)S(1)}, u32[]{:S(2)}, u32[]{:S(2)}) collective-permute-start(bf16[32,4,256]{2,1,0:T(4,128)(2,1)S(1)} %get-tuple-element.19), channel_id=1, source_target_pairs={{1,0},{2,1},{3,2},{4,3},{5,4},{6,5},{7,6},{8,7},{9,8},{10,9},{11,1... | collective-permute-start | bytes 196616 | tf_op jit(solution)/shard_map/ppermute | solution.py:41
  25.3 0.0 copy-done.4
  25.4 0.1 copy.18
  25.5 0.0 copy-start.3
  25.5 0.1 copy.19
  25.6 0.0 copy-start.6
  25.6 0.7 copy-done.6
  26.3 0.0 copy-start.8
  26.3 0.0 copy-start.9
  26.3 0.0 copy-start.10
  26.3 0.6 copy-done.8
  27.0 0.0 copy-done.9
  27.0 0.0 copy-done.10
  27.0 0.1 multiply_reduce_fusion
  27.1 0.1 fusion.6.weights
  27.2 0.0 copy-done.3
  27.2 7.4 %all-to-all-done.arrived = bf16[128,16,128]{2,1,0:T(8,128)(2,1)S(1)} async-done(((bf16[128,16,128]{2,1,0:T(8,128)(2,1)}), bf16[128,16,128]{2,1,0:T(8,128)(2,1)S(1)}, u32[]{:S(2)}, u32[]{:S(2)}) %all-to-all-start) | async-done | bytes 524320 | tf_op jit(solution)/shard_map/all_to_all | solution.py:149
  34.6 0.1 fusion.3
  34.8 0.0 collective-permute-done.left
  34.8 0.0 collective-permute-done.1.right
  34.8 2.3 %shard_map.113 = bf16[32,8,16,128]{3,2,1,0:T(8,128)(2,1)} custom-call(s32[32,8]{1,0:T(8,128)S(1)} %bitcast.19, bf16[128,16,128]{2,1,0:T(8,128)(2,1)S(1)} %all-to-all-done.arrived, bf16[32,4,256]{2,1,0:T(4,128)(2,1)S(1)} %collective-permute-done.left, bf16[32,4,256]{2,1,0:T(4,128)(2,1)S(1)} %collective-permute-done.1.right, f32[10,256]{1,0:T(8,128)S(1)} %fusion.6.weights, ...), custom_call_target="tpu_custom_call" | custom-call | bytes 1048576 | tf_op jit(solution)/shard_map/pallas_call | solution.py:174
  37.1 6.7 %all-to-all-start.1 = ((bf16[32,8,16,128]{3,2,1,0:T(8,128)(2,1)}), bf16[32,8,16,128]{3,2,1,0:T(8,128)(2,1)S(1)}, u32[]{:S(2)}, u32[]{:S(2)}) async-start(bf16[32,8,16,128]{3,2,1,0:T(8,128)(2,1)} %shard_map.113), calls=%async_computation.1 | async-start | bytes 2097152 | tf_op jit(solution)/shard_map/all_to_all | solution.py:182
  43.8 0.0 copy-start.1
  43.8 0.0 copy-start.5
  43.9 2.1 %collective-permute-start.2 = (bf16[4,40,256]{2,1,0:T(8,128)(2,1)S(1)}, bf16[4,40,256]{2,1,0:T(8,128)(2,1)S(1)}, u32[]{:S(2)}, u32[]{:S(2)}) collective-permute-start(bf16[4,40,256]{2,1,0:T(8,128)(2,1)S(1)} %get-tuple-element.20), channel_id=1, source_target_pairs={{0,16},{16,32},{32,48},{48,64},{64,80},{80,96},{96,112},{112,128},... | collective-permute-start | bytes 245768 | tf_op jit(solution)/shard_map/ppermute | solution.py:41
  45.9 0.0 copy-start.7
  45.9 5.6 %collective-permute-start.3 = (bf16[4,40,256]{2,1,0:T(8,128)(2,1)S(1)}, bf16[4,40,256]{2,1,0:T(8,128)(2,1)S(1)}, u32[]{:S(2)}, u32[]{:S(2)}) collective-permute-start(bf16[4,40,256]{2,1,0:T(8,128)(2,1)S(1)} %get-tuple-element.21), channel_id=1, source_target_pairs={{16,0},{32,16},{48,32},{64,48},{80,64},{96,80},{112,96},{128,112},... | collective-permute-start | bytes 245768 | tf_op jit(solution)/shard_map/ppermute | solution.py:41
  51.6 0.0 copy-done.5
  51.6 0.0 copy-done.7
  51.6 0.2 select_reduce_fusion.slots
  51.8 0.3 collective-permute-done.2.top
  52.1 1.5 %collective-permute-done.3.bottom = bf16[4,40,256]{2,1,0:T(8,128)(2,1)S(1)} collective-permute-done((bf16[4,40,256]{2,1,0:T(8,128)(2,1)S(1)}, bf16[4,40,256]{2,1,0:T(8,128)(2,1)S(1)}, u32[]{:S(2)}, u32[]{:S(2)}) %collective-permute-start.3) | collective-permute-done | bytes 81952 | tf_op jit(solution)/shard_map/ppermute | solution.py:41
  53.6 0.0 copy-done.1
  53.6 3.4 %shard_map.112.grown = bf16[32,32,256]{2,1,0:T(8,128)(2,1)S(1)} custom-call(bf16[32,32,256]{2,1,0:T(8,128)(2,1)S(1)} %copy-done, bf16[4,40,256]{2,1,0:T(8,128)(2,1)S(1)} %collective-permute-done.2.top, bf16[4,40,256]{2,1,0:T(8,128)(2,1)S(1)} %collective-permute-done.3.bottom, bf16[32,4,256]{2,1,0:T(4,128)(2,1)S(1)} %collective-permute-done.left, ...), custom_call_target="tpu_custom_call" | custom-call | flops 268435456 | bytes 16777216 | tf_op jit(solution)/shard_map/pallas_call | solution.py:442
  57.0 1.6 %all-to-all-done.1.parts = bf16[32,8,16,128]{3,2,1,0:T(8,128)(2,1)S(1)} async-done(((bf16[32,8,16,128]{3,2,1,0:T(8,128)(2,1)}), bf16[32,8,16,128]{3,2,1,0:T(8,128)(2,1)S(1)}, u32[]{:S(2)}, u32[]{:S(2)}) %all-to-all-start.1) | async-done | bytes 1048608 | tf_op jit(solution)/shard_map/all_to_all | solution.py:182
  58.6 1.9 %shard_map.114 = (bf16[32,32,256]{2,1,0:T(8,128)(2,1)S(1)}, bf16[8,256,256]{2,1,0:T(8,128)(2,1)S(1)}, bf16[2,4,32,256]{3,2,1,0:T(8,128)(2,1)}, bf16[4,32,256]{2,1,0:T(8,128)(2,1)S(1)}) custom-call(s32[4,4]{1,0:T(4,128)S(1)} %select_reduce_fusion.slots, bf16[32,32,256]{2,1,0:T(8,128)(2,1)S(1)} %shard_map.112.grown, ...), custom_call_target="tpu_custom_call" | custom-call | flops 268435456 | bytes 4194304 | tf_op jit(solution)/shard_map/pallas_call | solution.py:453
  60.5 4.4 %all-to-all-start.2 = ((bf16[2,4,32,256]{3,2,1,0:T(8,128)(2,1)}), bf16[2,4,32,256]{3,2,1,0:T(8,128)(2,1)S(1)}, u32[]{:S(2)}, u32[]{:S(2)}) async-start(bf16[2,4,32,256]{3,2,1,0:T(8,128)(2,1)} %get-tuple-element.25), calls=%async_computation.2 | async-start | bytes 262144 | tf_op jit(solution)/shard_map/all_to_all | solution.py:49
  64.9 7.0 %collective-permute-start.4 = (bf16[4,32,256]{2,1,0:T(8,128)(2,1)S(1)}, bf16[4,32,256]{2,1,0:T(8,128)(2,1)S(1)}, u32[]{:S(2)}, u32[]{:S(2)}) collective-permute-start(bf16[4,32,256]{2,1,0:T(8,128)(2,1)S(1)} %get-tuple-element.24), channel_id=1, source_target_pairs={{16,32},{48,64},{80,96},{112,128},{144,160},{176,192},{208,224},{2... | collective-permute-start | bytes 196616 | tf_op jit(solution)/shard_map/ppermute | solution.py:48
  71.9 0.1 fusion.8
  72.0 0.0 all-to-all-done.2
  72.0 1.9 %collective-permute-done.4 = bf16[4,32,256]{2,1,0:T(8,128)(2,1)S(1)} collective-permute-done((bf16[4,32,256]{2,1,0:T(8,128)(2,1)S(1)}, bf16[4,32,256]{2,1,0:T(8,128)(2,1)S(1)}, u32[]{:S(2)}, u32[]{:S(2)}) %collective-permute-start.4) | collective-permute-done | bytes 65568 | tf_op jit(solution)/shard_map/ppermute | solution.py:48
  73.9 0.1 pad_maximum_fusion
  74.0 4.0 %collective-permute-start.5 = (bf16[40,4,256]{2,1,0:T(4,128)(2,1)S(1)}, bf16[40,4,256]{2,1,0:T(4,128)(2,1)S(1)}, u32[]{:S(2)}, u32[]{:S(2)}) collective-permute-start(bf16[40,4,256]{2,1,0:T(4,128)(2,1)S(1)} %pad_maximum_fusion), channel_id=1, source_target_pairs={{0,1},{1,2},{2,3},{3,4},{4,5},{5,6},{6,7},{7,8},{8,9},{9,10},{10,1... | collective-permute-start | bytes 245768 | tf_op jit(solution)/shard_map/ppermute | solution.py:41
  78.0 0.1 pad_maximum_fusion.1
  78.0 3.4 %collective-permute-start.6 = (bf16[40,4,256]{2,1,0:T(4,128)(2,1)S(1)}, bf16[40,4,256]{2,1,0:T(4,128)(2,1)S(1)}, u32[]{:S(2)}, u32[]{:S(2)}) collective-permute-start(bf16[40,4,256]{2,1,0:T(4,128)(2,1)S(1)} %pad_maximum_fusion.1), channel_id=1, source_target_pairs={{1,0},{2,1},{3,2},{4,3},{5,4},{6,5},{7,6},{8,7},{9,8},{10,9},{11,1... | collective-permute-start | bytes 245768 | tf_op jit(solution)/shard_map/ppermute | solution.py:41
  81.4 4.4 %shard_map.115 = (bf16[32,16,256]{2,1,0:T(8,128)(2,1)S(1)}, f32[32,16,256]{2,1,0:T(8,128)S(1)}) custom-call(s32[4,4]{1,0:T(4,128)S(1)} %select_reduce_fusion.slots, bf16[32,32,256]{2,1,0:T(8,128)(2,1)S(1)} %get-tuple-element.23.cells, bf16[4,32,256]{2,1,0:T(8,128)(2,1)S(1)} %get-tuple-element.31.top, bf16[4,32,256]{2,1,0:T(8,128)(2,1)S(1)} %get-tuple-element.32.bottom, ...), custom_call_target="tpu_custom_call" | custom-call | flops 268435456 | bytes 16777216 | tf_op jit(solution)/shard_map/pallas_call | solution.py:464
  85.8 0.0 collective-permute-done.5.left
  85.8 1.0 %collective-permute-done.6.right = bf16[40,4,256]{2,1,0:T(4,128)(2,1)S(1)} collective-permute-done((bf16[40,4,256]{2,1,0:T(4,128)(2,1)S(1)}, bf16[40,4,256]{2,1,0:T(4,128)(2,1)S(1)}, u32[]{:S(2)}, u32[]{:S(2)}) %collective-permute-start.6) | collective-permute-done | bytes 81952 | tf_op jit(solution)/shard_map/ppermute | solution.py:41
  86.8 3.0 %shard_map.116 = bf16[32,32,256]{2,1,0:T(8,128)(2,1)} custom-call(s32[4,4]{1,0:T(4,128)S(1)} %select_reduce_fusion.slots, bf16[32,32,256]{2,1,0:T(8,128)(2,1)S(1)} %get-tuple-element.23.cells, bf16[40,4,256]{2,1,0:T(4,128)(2,1)S(1)} %collective-permute-done.5.left, bf16[40,4,256]{2,1,0:T(4,128)(2,1)S(1)} %collective-permute-done.6.right, ...), custom_call_target="tpu_custom_call" | custom-call | flops 268435456 | bytes 4194304 | tf_op jit(solution)/shard_map/pallas_call | solution.py:476
  (11 shorter events, 0.2 us)
Async XLA Ops:
  1.8 16.1 %copy-start = (bf16[32,32,256]{2,1,0:T(8,128)(2,1)S(1)}, bf16[32,32,256]{2,1,0:T(8,128)(2,1)}, u32[]{:S(2)}) copy-start(bf16[32,32,256]{2,1,0:T(8,128)(2,1)} %cells.5) | copy-start | bytes 1572868
  1.8 16.1 %copy-start.2 = (f32[8,128]{1,0:T(8,128)S(1)}, f32[8,128]{1,0:T(8,128)}, u32[]{:S(2)}) copy-start(f32[8,128]{1,0:T(8,128)} %get-tuple-element.17.token) | copy-start | bytes 12292
  1.8 32.8 %all-to-all-start = ((bf16[128,16,128]{2,1,0:T(8,128)(2,1)}), bf16[128,16,128]{2,1,0:T(8,128)(2,1)S(1)}, u32[]{:S(2)}, u32[]{:S(2)}) async-start(bf16[128,16,128]{2,1,0:T(8,128)(2,1)} %get-tuple-element.22), calls=%async_computation | async-start | bytes 1048576 | tf_op jit(solution)/shard_map/all_to_all | solution.py:149
  17.9 7.4 %copy-start.4 = (s32[32,32]{1,0:T(8,128)S(1)}, s32[32,32]{1,0:T(8,128)}, u32[]{:S(2)}) copy-start(s32[32,32]{1,0:T(8,128)} %param.17) | copy-start | bytes 12292
  18.0 16.8 %collective-permute-start = (bf16[32,4,256]{2,1,0:T(4,128)(2,1)S(1)}, bf16[32,4,256]{2,1,0:T(4,128)(2,1)S(1)}, u32[]{:S(2)}, u32[]{:S(2)}) collective-permute-start(bf16[32,4,256]{2,1,0:T(4,128)(2,1)S(1)} %get-tuple-element.18), channel_id=1, source_target_pairs={{0,1},{1,2},{2,3},{3,4},{4,5},{5,6},{6,7},{7,8},{8,9},{9,10},{10,1... | collective-permute-start | bytes 196616 | tf_op jit(solution)/shard_map/ppermute | solution.py:41
  22.2 12.5 %collective-permute-start.1 = (bf16[32,4,256]{2,1,0:T(4,128)(2,1)S(1)}, bf16[32,4,256]{2,1,0:T(4,128)(2,1)S(1)}, u32[]{:S(2)}, u32[]{:S(2)}) collective-permute-start(bf16[32,4,256]{2,1,0:T(4,128)(2,1)S(1)} %get-tuple-element.19), channel_id=1, source_target_pairs={{1,0},{2,1},{3,2},{4,3},{5,4},{6,5},{7,6},{8,7},{9,8},{10,9},{11,1... | collective-permute-start | bytes 196616 | tf_op jit(solution)/shard_map/ppermute | solution.py:41
  25.5 1.7 %copy-start.3 = (bf16[256,256]{1,0:T(8,128)(2,1)S(1)}, bf16[256,256]{1,0:T(8,128)(2,1)}, u32[]{:S(2)}) copy-start(bf16[256,256]{1,0:T(8,128)(2,1)} %param.16) | copy-start | bytes 393220
  25.6 0.7 copy-start.6
  26.3 0.7 copy-start.8
  26.3 0.7 copy-start.9
  26.3 0.7 copy-start.10
  37.1 21.5 %all-to-all-start.1 = ((bf16[32,8,16,128]{3,2,1,0:T(8,128)(2,1)}), bf16[32,8,16,128]{3,2,1,0:T(8,128)(2,1)S(1)}, u32[]{:S(2)}, u32[]{:S(2)}) async-start(bf16[32,8,16,128]{3,2,1,0:T(8,128)(2,1)} %shard_map.113), calls=%async_computation.1 | async-start | bytes 2097152 | tf_op jit(solution)/shard_map/all_to_all | solution.py:182
  43.8 9.8 %copy-start.1 = (bf16[256,256]{1,0:T(8,128)(2,1)S(1)}, bf16[256,256]{1,0:T(8,128)(2,1)}, u32[]{:S(2)}) copy-start(bf16[256,256]{1,0:T(8,128)(2,1)} %fecundity.5) | copy-start | bytes 393220
  43.8 7.7 %copy-start.5 = (s32[4,4]{1,0:T(4,128)S(1)}, s32[4,4]{1,0:T(4,128)}, u32[]{:S(2)}) copy-start(s32[4,4]{1,0:T(4,128)} %param.12) | copy-start | bytes 196
  43.9 8.3 %collective-permute-start.2 = (bf16[4,40,256]{2,1,0:T(8,128)(2,1)S(1)}, bf16[4,40,256]{2,1,0:T(8,128)(2,1)S(1)}, u32[]{:S(2)}, u32[]{:S(2)}) collective-permute-start(bf16[4,40,256]{2,1,0:T(8,128)(2,1)S(1)} %get-tuple-element.20), channel_id=1, source_target_pairs={{0,16},{16,32},{32,48},{48,64},{64,80},{80,96},{96,112},{112,128},... | collective-permute-start | bytes 245768 | tf_op jit(solution)/shard_map/ppermute | solution.py:41
  45.9 5.6 %copy-start.7 = (s32[1,1,16]{2,1,0:T(1,128)S(1)}, s32[1,1,16]{2,1,0:T(1,128)}, u32[]{:S(2)}) copy-start(s32[1,1,16]{2,1,0:T(1,128)} %param.13) | copy-start | bytes 196
  45.9 7.7 %collective-permute-start.3 = (bf16[4,40,256]{2,1,0:T(8,128)(2,1)S(1)}, bf16[4,40,256]{2,1,0:T(8,128)(2,1)S(1)}, u32[]{:S(2)}, u32[]{:S(2)}) collective-permute-start(bf16[4,40,256]{2,1,0:T(8,128)(2,1)S(1)} %get-tuple-element.21), channel_id=1, source_target_pairs={{16,0},{32,16},{48,32},{64,48},{80,64},{96,80},{112,96},{128,112},... | collective-permute-start | bytes 245768 | tf_op jit(solution)/shard_map/ppermute | solution.py:41
  60.5 11.5 %all-to-all-start.2 = ((bf16[2,4,32,256]{3,2,1,0:T(8,128)(2,1)}), bf16[2,4,32,256]{3,2,1,0:T(8,128)(2,1)S(1)}, u32[]{:S(2)}, u32[]{:S(2)}) async-start(bf16[2,4,32,256]{3,2,1,0:T(8,128)(2,1)} %get-tuple-element.25), calls=%async_computation.2 | async-start | bytes 262144 | tf_op jit(solution)/shard_map/all_to_all | solution.py:49
  64.9 8.9 %collective-permute-start.4 = (bf16[4,32,256]{2,1,0:T(8,128)(2,1)S(1)}, bf16[4,32,256]{2,1,0:T(8,128)(2,1)S(1)}, u32[]{:S(2)}, u32[]{:S(2)}) collective-permute-start(bf16[4,32,256]{2,1,0:T(8,128)(2,1)S(1)} %get-tuple-element.24), channel_id=1, source_target_pairs={{16,32},{48,64},{80,96},{112,128},{144,160},{176,192},{208,224},{2... | collective-permute-start | bytes 196616 | tf_op jit(solution)/shard_map/ppermute | solution.py:48
  74.0 11.8 %collective-permute-start.5 = (bf16[40,4,256]{2,1,0:T(4,128)(2,1)S(1)}, bf16[40,4,256]{2,1,0:T(4,128)(2,1)S(1)}, u32[]{:S(2)}, u32[]{:S(2)}) collective-permute-start(bf16[40,4,256]{2,1,0:T(4,128)(2,1)S(1)} %pad_maximum_fusion), channel_id=1, source_target_pairs={{0,1},{1,2},{2,3},{3,4},{4,5},{5,6},{6,7},{7,8},{8,9},{9,10},{10,1... | collective-permute-start | bytes 245768 | tf_op jit(solution)/shard_map/ppermute | solution.py:41
  78.0 8.7 %collective-permute-start.6 = (bf16[40,4,256]{2,1,0:T(4,128)(2,1)S(1)}, bf16[40,4,256]{2,1,0:T(4,128)(2,1)S(1)}, u32[]{:S(2)}, u32[]{:S(2)}) collective-permute-start(bf16[40,4,256]{2,1,0:T(4,128)(2,1)S(1)} %pad_maximum_fusion.1), channel_id=1, source_target_pairs={{1,0},{2,1},{3,2},{4,3},{5,4},{6,5},{7,6},{8,7},{9,8},{10,9},{11,1... | collective-permute-start | bytes 245768 | tf_op jit(solution)/shard_map/ppermute | solution.py:41

commit v9 on v7

--- a/solution.py
+++ b/solution.py
@@ -41,14 +41,8 @@
     return lax.ppermute(tail, axis, after), lax.ppermute(head, axis, before)
 
 
-def surround(near, far, head, tail):
-    even = lax.axis_index("co") == 0
-    count = math.prod(lax.axis_size(name) for name in ROW)
-    pairs = [(i, i + 1) for i in range(1, count - 1, 2)]
-    far = lax.ppermute(far, ROW, pairs + [(j, i) for i, j in pairs])
-    near = lax.all_to_all(near, "co", 0, 0, tiled=True)
-    near = jnp.where(even, near[1], near[0])
-    top, bottom = jnp.where(even, far, near), jnp.where(even, near, far)
+def surround(first, last, head, tail):
+    top, bottom = swap(first, last, ROW)
     head = jnp.concatenate([top[:, :RMAX], head, bottom[:, :RMAX]], axis=0)
     tail = jnp.concatenate([top[:, -RMAX:], tail, bottom[:, -RMAX:]], axis=0)
     return (top, bottom) + swap(head, tail, COL)
@@ -316,7 +310,7 @@
         grown[span] = result.reshape(BX, cols, cohorts)
 
 
-def harvest_kernel(slots, grown, parts, out, ops, near, far, head, tail):
+def harvest_kernel(slots, grown, parts, out, ops, first, last, head, tail):
     assemble(parts, ops)
     rows, cols, cohorts = grown.shape
     wide = 2 * BY
@@ -330,12 +324,10 @@
         out[span] = whole.astype(jnp.bfloat16)
         head[span] = whole[:, :RMAX].astype(jnp.bfloat16)
         tail[span] = whole[:, cols - RMAX :].astype(jnp.bfloat16)
-    even = lax.axis_index("co") == 0
-    at = jnp.where(even, rows - RMAX, 0)
-    for i in range(RMAX):
-        near[0, i] = out[at + i]
-        near[1, i] = out[at + i]
-        far[i] = out[rows - RMAX - at + i]
+        if i == 0:
+            first[...] = whole[:RMAX].astype(jnp.bfloat16)
+        if i == rows // BX - 1:
+            last[...] = whole[BX - RMAX :].astype(jnp.bfloat16)
 
 
 def middle_kernel(
@@ -451,17 +443,16 @@
         cost_estimate=pl.CostEstimate(flops=2**28, bytes_accessed=2**24, transcendentals=0),
     )(biomass, *around, weights, fecundity, moves)
     row_part = jax.ShapeDtypeStruct((RMAX, cols, cohorts), jnp.bfloat16)
-    row_pair = jax.ShapeDtypeStruct((2, RMAX, cols, cohorts), jnp.bfloat16)
     col_part = jax.ShapeDtypeStruct((rows, RMAX, cohorts), jnp.bfloat16)
-    cells, ops, near, far, head, tail = pl.pallas_call(
+    cells, ops, first, last, head, tail = pl.pallas_call(
         harvest_kernel,
-        out_shape=(state, operators, row_pair, row_part, col_part, col_part),
+        out_shape=(state, operators, row_part, row_part, col_part, col_part),
         in_specs=[SMEM, VMEM, VMEM],
         out_specs=(VMEM,) * 6,
         compiler_params=PARAMS,
         cost_estimate=pl.CostEstimate(flops=2**28, bytes_accessed=2**22, transcendentals=0),
     )(slots, grown, parts)
-    top, bottom, left, right = surround(near, far, head, tail)
+    top, bottom, left, right = surround(first, last, head, tail)
     high = rows + 2 * RMAX
     outer = 2 * BY
     inner, partial = pl.pallas_call(

time: 89.3 us -> 87.4 us (0.979)
  waiting for transfers between devices: 18.8 us -> 22.9 us
  blocking collectives: 3.5 us -> 0 us
  local copies, waits for them, and re-layouts: 4.38 us -> 1.64 us
  starting transfers between devices: 42.9 us -> 45 us
    ppermute x6 -> x8, starting transfers between devices: 17.6 us -> 22 us  [swap(): return (lax.ppermute(tail, axis, after), lax.ppermute(head, axis, before))]
    ppermute x6 -> x8, waiting for transfers between devices: 9.42 us -> 13.5 us  [swap(): return (lax.ppermute(tail, axis, after), lax.ppermute(head, axis, before))]
    all_to_all x1 -> x0, blocking collectives: 3.5 us -> none  [surround(): near = lax.all_to_all(near, 'co', 0, 0, tiled=True)]
    unnamed x34 -> x22, local copies, waits for them, and re-layouts: 4.12 us -> 1.38 us
    ppermute x1 -> x0, starting transfers between devices: 2.26 us -> none  [surround(): far = lax.ppermute(far, ROW, pairs + [(j, i) for i, j in pairs])]
  transfers between devices with their start and end apart: 9 -> 10, of which waited for: 4 -> 5; matrix products, arithmetic and copies ran while one was open for 2% -> 1% of each run, Pallas kernels for 9% -> 9%
where the time goes in v9:
time: 87.4 us; the launch traced here: 86.9 us
  starting transfers between devices  45 us (51%)
  waiting for transfers between devices  22.9 us (26%)
  Pallas kernels  16.2 us (19%)
  local copies, waits for them, and re-layouts  1.64 us (2%)
    ppermute x8, starting transfers between devices, swap(): return (lax.ppermute(tail, axis, after), lax.ppermute(head, axis, before))  22 us
    all_to_all x1, starting transfers between devices, fetch(): arrived = lax.all_to_all(spread, WIDE, 0, 0, tiled=True)  16.8 us
    ppermute x8, waiting for transfers between devices, swap(): return (lax.ppermute(tail, axis, after), lax.ppermute(head, axis, before))  13.5 us
    all_to_all x1, waiting for transfers between devices, fetch(): arrived = lax.all_to_all(spread, WIDE, 0, 0, tiled=True)  9.39 us
    all_to_all x1, starting transfers between devices, fetch(): parts = lax.all_to_all(wanted, NEAR, 0, 0, tiled=True)  6.24 us
    pallas_call x1, Pallas kernels, local(): pl.pallas_call(middle_kernel, out_shape=(jax.ShapeDtypeStruct((rows, cols...  4.39 us
    pallas_call x1, Pallas kernels, local(): pl.pallas_call(first_kernel, out_shape=state, in_specs=[VMEM] * 8, out_sp...  3.41 us
    pallas_call x1, Pallas kernels, local(): pl.pallas_call(last_kernel, out_shape=state, in_specs=[SMEM] + [VMEM] * 9...  3.03 us
  transfers between devices with their start and end apart: 10, of which 5 were waited for; matrix products, arithmetic and copies ran while one was open for 1% of the time, Pallas kernels for 9%

profile of v9, /device:TPU:1, one launch (start us, length us, event | category | flops | bytes accessed | tf_op | source)
XLA Modules:
  0.0 86.9 jit_solution(2618841807726999149)
XLA Ops:
  0.0 1.8 %shard_map.109 = (bf16[128,16,128]{2,1,0:T(8,128)(2,1)}, f32[8,128]{1,0:T(8,128)}) custom-call(s32[1,1,8]{2,1,0:T(1,128)} %tile_list.1, bf16[4,256,256]{2,1,0:T(8,128)(2,1)} %harvest_ops.1), custom_call_target="tpu_custom_call" | custom-call | bytes 1048576 | tf_op jit(solution)/shard_map/pallas_call | solution.py:127
  1.8 0.0 copy-start
  1.8 0.0 copy-start.2
  1.8 16.8 %all-to-all-start = ((bf16[128,16,128]{2,1,0:T(8,128)(2,1)}), bf16[128,16,128]{2,1,0:T(8,128)(2,1)S(1)}, u32[]{:S(2)}, u32[]{:S(2)}) async-start(bf16[128,16,128]{2,1,0:T(8,128)(2,1)} %get-tuple-element.24), calls=%async_computation | async-start | bytes 1048576 | tf_op jit(solution)/shard_map/all_to_all | solution.py:143
  18.6 0.0 copy-done
  18.6 0.0 copy-done.2
  18.6 0.0 copy-start.4
  18.6 0.1 shard_map.110
  18.7 4.8 %collective-permute-start = (bf16[32,4,256]{2,1,0:T(4,128)(2,1)S(1)}, bf16[32,4,256]{2,1,0:T(4,128)(2,1)S(1)}, u32[]{:S(2)}, u32[]{:S(2)}) collective-permute-start(bf16[32,4,256]{2,1,0:T(4,128)(2,1)S(1)} %get-tuple-element.20), channel_id=1, source_target_pairs={{0,1},{1,2},{2,3},{3,4},{4,5},{5,6},{6,7},{7,8},{8,9},{9,10},{10,1... | collective-permute-start | bytes 196616 | tf_op jit(solution)/shard_map/ppermute | solution.py:41
  23.5 1.3 %collective-permute-start.1 = (bf16[32,4,256]{2,1,0:T(4,128)(2,1)S(1)}, bf16[32,4,256]{2,1,0:T(4,128)(2,1)S(1)}, u32[]{:S(2)}, u32[]{:S(2)}) collective-permute-start(bf16[32,4,256]{2,1,0:T(4,128)(2,1)S(1)} %get-tuple-element.21), channel_id=1, source_target_pairs={{1,0},{2,1},{3,2},{4,3},{5,4},{6,5},{7,6},{8,7},{9,8},{10,9},{11,1... | collective-permute-start | bytes 196616 | tf_op jit(solution)/shard_map/ppermute | solution.py:41
  24.8 0.0 copy-done.4
  24.8 0.1 copy.18
  24.9 0.0 copy-start.3
  24.9 0.1 copy.19
  25.1 0.0 copy-start.6
  25.1 0.7 copy-done.6
  25.7 0.0 copy-start.8
  25.7 0.0 copy-start.9
  25.8 0.0 copy-start.10
  25.8 0.6 copy-done.8
  26.4 0.0 copy-done.9
  26.4 0.0 copy-done.10
  26.4 0.1 multiply_reduce_fusion
  26.5 0.1 fusion.5.weights
  26.6 0.0 copy-done.3
  26.7 9.4 %all-to-all-done.arrived = bf16[128,16,128]{2,1,0:T(8,128)(2,1)S(1)} async-done(((bf16[128,16,128]{2,1,0:T(8,128)(2,1)}), bf16[128,16,128]{2,1,0:T(8,128)(2,1)S(1)}, u32[]{:S(2)}, u32[]{:S(2)}) %all-to-all-start) | async-done | bytes 524320 | tf_op jit(solution)/shard_map/all_to_all | solution.py:143
  36.1 0.1 fusion.2
  36.2 0.0 collective-permute-done.left
  36.2 0.0 collective-permute-done.1.right
  36.2 2.3 %shard_map.113 = bf16[32,8,16,128]{3,2,1,0:T(8,128)(2,1)} custom-call(s32[32,8]{1,0:T(8,128)S(1)} %bitcast.13, bf16[128,16,128]{2,1,0:T(8,128)(2,1)S(1)} %all-to-all-done.arrived, bf16[32,4,256]{2,1,0:T(4,128)(2,1)S(1)} %collective-permute-done.left, bf16[32,4,256]{2,1,0:T(4,128)(2,1)S(1)} %collective-permute-done.1.right, f32[10,256]{1,0:T(8,128)S(1)} %fusion.5.weights, ...), custom_call_target="tpu_custom_call" | custom-call | bytes 1048576 | tf_op jit(solution)/shard_map/pallas_call | solution.py:168
  38.5 6.2 %all-to-all-start.1 = ((bf16[32,8,16,128]{3,2,1,0:T(8,128)(2,1)}), bf16[32,8,16,128]{3,2,1,0:T(8,128)(2,1)S(1)}, u32[]{:S(2)}, u32[]{:S(2)}) async-start(bf16[32,8,16,128]{3,2,1,0:T(8,128)(2,1)} %shard_map.113), calls=%async_computation.1 | async-start | bytes 2097152 | tf_op jit(solution)/shard_map/all_to_all | solution.py:176
  44.8 0.0 copy-start.1
  44.9 0.0 copy-start.5
  44.9 3.5 %collective-permute-start.2 = (bf16[4,40,256]{2,1,0:T(8,128)(2,1)S(1)}, bf16[4,40,256]{2,1,0:T(8,128)(2,1)S(1)}, u32[]{:S(2)}, u32[]{:S(2)}) collective-permute-start(bf16[4,40,256]{2,1,0:T(8,128)(2,1)S(1)} %get-tuple-element.22), channel_id=1, source_target_pairs={{0,16},{16,32},{32,48},{48,64},{64,80},{80,96},{96,112},{112,128},... | collective-permute-start | bytes 245768 | tf_op jit(solution)/shard_map/ppermute | solution.py:41
  48.4 0.0 copy-start.7
  48.4 1.9 %collective-permute-start.3 = (bf16[4,40,256]{2,1,0:T(8,128)(2,1)S(1)}, bf16[4,40,256]{2,1,0:T(8,128)(2,1)S(1)}, u32[]{:S(2)}, u32[]{:S(2)}) collective-permute-start(bf16[4,40,256]{2,1,0:T(8,128)(2,1)S(1)} %get-tuple-element.23), channel_id=1, source_target_pairs={{16,0},{32,16},{48,32},{64,48},{80,64},{96,80},{112,96},{128,112},... | collective-permute-start | bytes 245768 | tf_op jit(solution)/shard_map/ppermute | solution.py:41
  50.4 0.0 copy-done.5
  50.4 0.0 copy-done.7
  50.4 0.2 select_reduce_fusion.slots
  50.6 6.9 %collective-permute-done.2.top = bf16[4,40,256]{2,1,0:T(8,128)(2,1)S(1)} collective-permute-done((bf16[4,40,256]{2,1,0:T(8,128)(2,1)S(1)}, bf16[4,40,256]{2,1,0:T(8,128)(2,1)S(1)}, u32[]{:S(2)}, u32[]{:S(2)}) %collective-permute-start.2) | collective-permute-done | bytes 81952 | tf_op jit(solution)/shard_map/ppermute | solution.py:41
  57.5 2.1 %collective-permute-done.3.bottom = bf16[4,40,256]{2,1,0:T(8,128)(2,1)S(1)} collective-permute-done((bf16[4,40,256]{2,1,0:T(8,128)(2,1)S(1)}, bf16[4,40,256]{2,1,0:T(8,128)(2,1)S(1)}, u32[]{:S(2)}, u32[]{:S(2)}) %collective-permute-start.3) | collective-permute-done | bytes 81952 | tf_op jit(solution)/shard_map/ppermute | solution.py:41
  59.6 0.0 copy-done.1
  59.6 3.4 %shard_map.112.grown = bf16[32,32,256]{2,1,0:T(8,128)(2,1)S(1)} custom-call(bf16[32,32,256]{2,1,0:T(8,128)(2,1)S(1)} %copy-done, bf16[4,40,256]{2,1,0:T(8,128)(2,1)S(1)} %collective-permute-done.2.top, bf16[4,40,256]{2,1,0:T(8,128)(2,1)S(1)} %collective-permute-done.3.bottom, bf16[32,4,256]{2,1,0:T(4,128)(2,1)S(1)} %collective-permute-done.left, ...), custom_call_target="tpu_custom_call" | custom-call | flops 268435456 | bytes 16777216 | tf_op jit(solution)/shard_map/pallas_call | solution.py:436
  63.0 0.0 all-to-all-done.1.parts
  63.1 1.2 %shard_map.114 = (bf16[32,32,256]{2,1,0:T(8,128)(2,1)S(1)}, bf16[8,256,256]{2,1,0:T(8,128)(2,1)S(1)}, bf16[4,32,256]{2,1,0:T(8,128)(2,1)S(1)}, bf16[4,32,256]{2,...) custom-call(s32[4,4]{1,0:T(4,128)S(1)} %select_reduce_fusion.slots, ...), custom_call_target="tpu_custom_call" | custom-call | flops 268435456 | bytes 4194304 | tf_op jit(solution)/shard_map/pallas_call | solution.py:447
  64.3 2.3 %collective-permute-start.4 = (bf16[4,32,256]{2,1,0:T(8,128)(2,1)S(1)}, bf16[4,32,256]{2,1,0:T(8,128)(2,1)S(1)}, u32[]{:S(2)}, u32[]{:S(2)}) collective-permute-start(bf16[4,32,256]{2,1,0:T(8,128)(2,1)S(1)} %get-tuple-element.26), channel_id=1, source_target_pairs={{0,16},{16,32},{32,48},{48,64},{64,80},{80,96},{96,112},{112,128},... | collective-permute-start | bytes 196616 | tf_op jit(solution)/shard_map/ppermute | solution.py:41
  66.6 2.1 %collective-permute-start.5 = (bf16[4,32,256]{2,1,0:T(8,128)(2,1)S(1)}, bf16[4,32,256]{2,1,0:T(8,128)(2,1)S(1)}, u32[]{:S(2)}, u32[]{:S(2)}) collective-permute-start(bf16[4,32,256]{2,1,0:T(8,128)(2,1)S(1)} %get-tuple-element.28), channel_id=1, source_target_pairs={{16,0},{32,16},{48,32},{64,48},{80,64},{96,80},{112,96},{128,112},... | collective-permute-start | bytes 196616 | tf_op jit(solution)/shard_map/ppermute | solution.py:41
  68.6 0.0 collective-permute-done.4.top
  68.7 3.5 %collective-permute-done.5.bottom = bf16[4,32,256]{2,1,0:T(8,128)(2,1)S(1)} collective-permute-done((bf16[4,32,256]{2,1,0:T(8,128)(2,1)S(1)}, bf16[4,32,256]{2,1,0:T(8,128)(2,1)S(1)}, u32[]{:S(2)}, u32[]{:S(2)}) %collective-permute-start.5) | collective-permute-done | bytes 65568 | tf_op jit(solution)/shard_map/ppermute | solution.py:41
  72.2 0.1 pad_maximum_fusion
  72.3 4.8 %collective-permute-start.6 = (bf16[40,4,256]{2,1,0:T(4,128)(2,1)S(1)}, bf16[40,4,256]{2,1,0:T(4,128)(2,1)S(1)}, u32[]{:S(2)}, u32[]{:S(2)}) collective-permute-start(bf16[40,4,256]{2,1,0:T(4,128)(2,1)S(1)} %pad_maximum_fusion), channel_id=1, source_target_pairs={{0,1},{1,2},{2,3},{3,4},{4,5},{5,6},{6,7},{7,8},{8,9},{9,10},{10,1... | collective-permute-start | bytes 245768 | tf_op jit(solution)/shard_map/ppermute | solution.py:41
  77.1 0.1 pad_maximum_fusion.1
  77.1 1.3 %collective-permute-start.7 = (bf16[40,4,256]{2,1,0:T(4,128)(2,1)S(1)}, bf16[40,4,256]{2,1,0:T(4,128)(2,1)S(1)}, u32[]{:S(2)}, u32[]{:S(2)}) collective-permute-start(bf16[40,4,256]{2,1,0:T(4,128)(2,1)S(1)} %pad_maximum_fusion.1), channel_id=1, source_target_pairs={{1,0},{2,1},{3,2},{4,3},{5,4},{6,5},{7,6},{8,7},{9,8},{10,9},{11,1... | collective-permute-start | bytes 245768 | tf_op jit(solution)/shard_map/ppermute | solution.py:41
  78.4 4.4 %shard_map.115 = (bf16[32,16,256]{2,1,0:T(8,128)(2,1)S(1)}, f32[32,16,256]{2,1,0:T(8,128)S(1)}) custom-call(s32[4,4]{1,0:T(4,128)S(1)} %select_reduce_fusion.slots, bf16[32,32,256]{2,1,0:T(8,128)(2,1)S(1)} %get-tuple-element.25.cells, bf16[4,32,256]{2,1,0:T(8,128)(2,1)S(1)} %collective-permute-done.4.top, ...), custom_call_target="tpu_custom_call" | custom-call | flops 268435456 | bytes 16777216 | tf_op jit(solution)/shard_map/pallas_call | solution.py:458
  82.8 0.0 collective-permute-done.6.left
  82.8 1.0 %collective-permute-done.7.right = bf16[40,4,256]{2,1,0:T(4,128)(2,1)S(1)} collective-permute-done((bf16[40,4,256]{2,1,0:T(4,128)(2,1)S(1)}, bf16[40,4,256]{2,1,0:T(4,128)(2,1)S(1)}, u32[]{:S(2)}, u32[]{:S(2)}) %collective-permute-start.7) | collective-permute-done | bytes 81952 | tf_op jit(solution)/shard_map/ppermute | solution.py:41
  83.8 3.0 %shard_map.116 = bf16[32,32,256]{2,1,0:T(8,128)(2,1)} custom-call(s32[4,4]{1,0:T(4,128)S(1)} %select_reduce_fusion.slots, bf16[32,32,256]{2,1,0:T(8,128)(2,1)S(1)} %get-tuple-element.25.cells, bf16[40,4,256]{2,1,0:T(4,128)(2,1)S(1)} %collective-permute-done.6.left, bf16[40,4,256]{2,1,0:T(4,128)(2,1)S(1)} %collective-permute-done.7.right, ...), custom_call_target="tpu_custom_call" | custom-call | flops 268435456 | bytes 4194304 | tf_op jit(solution)/shard_map/pallas_call | solution.py:470
  (11 shorter events, 0.2 us)
Async XLA Ops:
  1.8 16.8 %copy-start = (bf16[32,32,256]{2,1,0:T(8,128)(2,1)S(1)}, bf16[32,32,256]{2,1,0:T(8,128)(2,1)}, u32[]{:S(2)}) copy-start(bf16[32,32,256]{2,1,0:T(8,128)(2,1)} %cells.5) | copy-start | bytes 1572868
  1.8 16.8 %copy-start.2 = (f32[8,128]{1,0:T(8,128)S(1)}, f32[8,128]{1,0:T(8,128)}, u32[]{:S(2)}) copy-start(f32[8,128]{1,0:T(8,128)} %get-tuple-element.19.token) | copy-start | bytes 12292
  1.8 34.3 %all-to-all-start = ((bf16[128,16,128]{2,1,0:T(8,128)(2,1)}), bf16[128,16,128]{2,1,0:T(8,128)(2,1)S(1)}, u32[]{:S(2)}, u32[]{:S(2)}) async-start(bf16[128,16,128]{2,1,0:T(8,128)(2,1)} %get-tuple-element.24), calls=%async_computation | async-start | bytes 1048576 | tf_op jit(solution)/shard_map/all_to_all | solution.py:143
  18.6 6.2 %copy-start.4 = (s32[32,32]{1,0:T(8,128)S(1)}, s32[32,32]{1,0:T(8,128)}, u32[]{:S(2)}) copy-start(s32[32,32]{1,0:T(8,128)} %param.17) | copy-start | bytes 12292
  18.7 17.5 %collective-permute-start = (bf16[32,4,256]{2,1,0:T(4,128)(2,1)S(1)}, bf16[32,4,256]{2,1,0:T(4,128)(2,1)S(1)}, u32[]{:S(2)}, u32[]{:S(2)}) collective-permute-start(bf16[32,4,256]{2,1,0:T(4,128)(2,1)S(1)} %get-tuple-element.20), channel_id=1, source_target_pairs={{0,1},{1,2},{2,3},{3,4},{4,5},{5,6},{6,7},{7,8},{8,9},{9,10},{10,1... | collective-permute-start | bytes 196616 | tf_op jit(solution)/shard_map/ppermute | solution.py:41
  23.5 12.8 %collective-permute-start.1 = (bf16[32,4,256]{2,1,0:T(4,128)(2,1)S(1)}, bf16[32,4,256]{2,1,0:T(4,128)(2,1)S(1)}, u32[]{:S(2)}, u32[]{:S(2)}) collective-permute-start(bf16[32,4,256]{2,1,0:T(4,128)(2,1)S(1)} %get-tuple-element.21), channel_id=1, source_target_pairs={{1,0},{2,1},{3,2},{4,3},{5,4},{6,5},{7,6},{8,7},{9,8},{10,9},{11,1... | collective-permute-start | bytes 196616 | tf_op jit(solution)/shard_map/ppermute | solution.py:41
  24.9 1.7 %copy-start.3 = (bf16[256,256]{1,0:T(8,128)(2,1)S(1)}, bf16[256,256]{1,0:T(8,128)(2,1)}, u32[]{:S(2)}) copy-start(bf16[256,256]{1,0:T(8,128)(2,1)} %param.16) | copy-start | bytes 393220
  25.1 0.7 copy-start.6
  25.7 0.7 copy-start.8
  25.7 0.7 copy-start.9
  25.8 0.7 copy-start.10
  38.5 24.5 %all-to-all-start.1 = ((bf16[32,8,16,128]{3,2,1,0:T(8,128)(2,1)}), bf16[32,8,16,128]{3,2,1,0:T(8,128)(2,1)S(1)}, u32[]{:S(2)}, u32[]{:S(2)}) async-start(bf16[32,8,16,128]{3,2,1,0:T(8,128)(2,1)} %shard_map.113), calls=%async_computation.1 | async-start | bytes 2097152 | tf_op jit(solution)/shard_map/all_to_all | solution.py:176
  44.8 14.8 %copy-start.1 = (bf16[256,256]{1,0:T(8,128)(2,1)S(1)}, bf16[256,256]{1,0:T(8,128)(2,1)}, u32[]{:S(2)}) copy-start(bf16[256,256]{1,0:T(8,128)(2,1)} %fecundity.5) | copy-start | bytes 393220
  44.9 5.5 %copy-start.5 = (s32[4,4]{1,0:T(4,128)S(1)}, s32[4,4]{1,0:T(4,128)}, u32[]{:S(2)}) copy-start(s32[4,4]{1,0:T(4,128)} %param.12) | copy-start | bytes 196
  44.9 12.6 %collective-permute-start.2 = (bf16[4,40,256]{2,1,0:T(8,128)(2,1)S(1)}, bf16[4,40,256]{2,1,0:T(8,128)(2,1)S(1)}, u32[]{:S(2)}, u32[]{:S(2)}) collective-permute-start(bf16[4,40,256]{2,1,0:T(8,128)(2,1)S(1)} %get-tuple-element.22), channel_id=1, source_target_pairs={{0,16},{16,32},{32,48},{48,64},{64,80},{80,96},{96,112},{112,128},... | collective-permute-start | bytes 245768 | tf_op jit(solution)/shard_map/ppermute | solution.py:41
  48.4 2.0 %copy-start.7 = (s32[1,1,16]{2,1,0:T(1,128)S(1)}, s32[1,1,16]{2,1,0:T(1,128)}, u32[]{:S(2)}) copy-start(s32[1,1,16]{2,1,0:T(1,128)} %param.13) | copy-start | bytes 196
  48.4 11.2 %collective-permute-start.3 = (bf16[4,40,256]{2,1,0:T(8,128)(2,1)S(1)}, bf16[4,40,256]{2,1,0:T(8,128)(2,1)S(1)}, u32[]{:S(2)}, u32[]{:S(2)}) collective-permute-start(bf16[4,40,256]{2,1,0:T(8,128)(2,1)S(1)} %get-tuple-element.23), channel_id=1, source_target_pairs={{16,0},{32,16},{48,32},{64,48},{80,64},{96,80},{112,96},{128,112},... | collective-permute-start | bytes 245768 | tf_op jit(solution)/shard_map/ppermute | solution.py:41
  64.3 4.3 %collective-permute-start.4 = (bf16[4,32,256]{2,1,0:T(8,128)(2,1)S(1)}, bf16[4,32,256]{2,1,0:T(8,128)(2,1)S(1)}, u32[]{:S(2)}, u32[]{:S(2)}) collective-permute-start(bf16[4,32,256]{2,1,0:T(8,128)(2,1)S(1)} %get-tuple-element.26), channel_id=1, source_target_pairs={{0,16},{16,32},{32,48},{48,64},{64,80},{80,96},{96,112},{112,128},... | collective-permute-start | bytes 196616 | tf_op jit(solution)/shard_map/ppermute | solution.py:41
  66.6 5.6 %collective-permute-start.5 = (bf16[4,32,256]{2,1,0:T(8,128)(2,1)S(1)}, bf16[4,32,256]{2,1,0:T(8,128)(2,1)S(1)}, u32[]{:S(2)}, u32[]{:S(2)}) collective-permute-start(bf16[4,32,256]{2,1,0:T(8,128)(2,1)S(1)} %get-tuple-element.28), channel_id=1, source_target_pairs={{16,0},{32,16},{48,32},{64,48},{80,64},{96,80},{112,96},{128,112},... | collective-permute-start | bytes 196616 | tf_op jit(solution)/shard_map/ppermute | solution.py:41
  72.3 10.6 %collective-permute-start.6 = (bf16[40,4,256]{2,1,0:T(4,128)(2,1)S(1)}, bf16[40,4,256]{2,1,0:T(4,128)(2,1)S(1)}, u32[]{:S(2)}, u32[]{:S(2)}) collective-permute-start(bf16[40,4,256]{2,1,0:T(4,128)(2,1)S(1)} %pad_maximum_fusion), channel_id=1, source_target_pairs={{0,1},{1,2},{2,3},{3,4},{4,5},{5,6},{6,7},{7,8},{8,9},{9,10},{10,1... | collective-permute-start | bytes 245768 | tf_op jit(solution)/shard_map/ppermute | solution.py:41
  77.1 6.7 %collective-permute-start.7 = (bf16[40,4,256]{2,1,0:T(4,128)(2,1)S(1)}, bf16[40,4,256]{2,1,0:T(4,128)(2,1)S(1)}, u32[]{:S(2)}, u32[]{:S(2)}) collective-permute-start(bf16[40,4,256]{2,1,0:T(4,128)(2,1)S(1)} %pad_maximum_fusion.1), channel_id=1, source_target_pairs={{1,0},{2,1},{3,2},{4,3},{5,4},{6,5},{7,6},{8,7},{9,8},{10,9},{11,1... | collective-permute-start | bytes 245768 | tf_op jit(solution)/shard_map/ppermute | solution.py:41

commit v10 on v9

--- a/solution.py
+++ b/solution.py
@@ -78,7 +78,7 @@
             out[i] = whole.astype(jnp.bfloat16)
 
 
-def spread_kernel(tile_list, harvest_ops, spread, token, listed, held, sems):
+def spread_kernel(tile_list, harvest_ops, spread, token, listed, held, stage, sems):
     mine = (lax.axis_index("xl") * 2 + lax.axis_index("yl")) * 2 + lax.axis_index("co")
     list_copy = pltpu.make_async_copy(tile_list, listed, sems.at[0])
     held_copy = pltpu.make_async_copy(harvest_ops.at[mine // 2], held, sems.at[1])
@@ -98,13 +98,19 @@
             piece = held[pl.ds(group * 32 + low * 16, 16), pl.ds(half * 128, 128)]
             message = jnp.where(sent, piece.astype(jnp.float32), names).astype(jnp.bfloat16)
             for far in range(4):
-                spread[(group * 4 + far) * 4 + near] = message
-
-
-def gather_kernel(places, arrived, left, right, weights, moves, wanted):
+                stage[(group * 4 + far) * 4 + near] = message
+        span = pl.ds(group * 16, 16)
+        pltpu.make_async_copy(stage.at[span], spread.at[span], sems.at[2 + group]).start()
+    for group in range(8):
+        span = pl.ds(group * 16, 16)
+        pltpu.make_async_copy(stage.at[span], spread.at[span], sems.at[2 + group]).wait()
+
+
+def gather_kernel(places, arrived, left, right, weights, moves, wanted, stage, sems):
     del left, right, weights, moves
     members, count = wanted.shape[:2]
     lower = lax.broadcasted_iota(jnp.int32, (16, 128), 1) < 64
+    size = members // 4
 
     def one(m, carry):
         found = []
@@ -112,10 +118,16 @@
             at = places[m, k]
             found.append(jnp.where(lower, arrived[at], arrived[at + 16]))
         for k in range(count):
-            wanted[m, k] = found[k]
-        return carry
-
-    lax.fori_loop(0, members, one, 0, unroll=2)
+            stage[m, k] = found[k]
+        return carry
+
+    for part in range(4):
+        lax.fori_loop(part * size, (part + 1) * size, one, 0, unroll=2)
+        span = pl.ds(part * size, size)
+        pltpu.make_async_copy(stage.at[span], wanted.at[span], sems.at[part]).start()
+    for part in range(4):
+        span = pl.ds(part * size, size)
+        pltpu.make_async_copy(stage.at[span], wanted.at[span], sems.at[part]).wait()
 
 
 def fetch(tile_list, harvest_ops, cells, weights, moves):
@@ -131,11 +143,12 @@
             jax.ShapeDtypeStruct((8, 128), jnp.float32),
         ),
         in_specs=[ANY, ANY],
-        out_specs=(VMEM, VMEM),
+        out_specs=(ANY, VMEM),
         scratch_shapes=[
             pltpu.SMEM(tile_list.shape, jnp.int32),
             pltpu.VMEM((cohorts, cohorts), jnp.bfloat16),
-            pltpu.SemaphoreType.DMA((2,)),
+            pltpu.VMEM((128, 16, 128), jnp.bfloat16),
+            pltpu.SemaphoreType.DMA((10,)),
         ],
         compiler_params=WHOLE,
         cost_estimate=small,
@@ -169,7 +182,10 @@
         gather_kernel,
         out_shape=jax.ShapeDtypeStruct((32, count, 16, 128), jnp.bfloat16),
         in_specs=[SMEM, VMEM] + [ANY] * 4,
-        out_specs=VMEM,
+        out_specs=ANY,
+        scratch_shapes=[
+            pltpu.VMEM((32, count, 16, 128), jnp.bfloat16), pltpu.SemaphoreType.DMA((4,))
+        ],
         compiler_params=PARAMS,
         cost_estimate=small,
     )(places, arrived, left, right, weights, moves)
@@ -310,8 +326,11 @@
         grown[span] = result.reshape(BX, cols, cohorts)
 
 
-def harvest_kernel(slots, grown, parts, out, ops, first, last, head, tail):
+def harvest_kernel(slot_table, grown, parts, out, ops, first, last, head, tail, slots, sem):
+    slot_copy = pltpu.make_async_copy(slot_table, slots, sem)
+    slot_copy.start()
     assemble(parts, ops)
+    slot_copy.wait()
     rows, cols, cohorts = grown.shape
     wide = 2 * BY
     for i in range(rows // BX):
@@ -331,8 +350,11 @@
 
 
 def middle_kernel(
-    slots, cells, top, bottom, weights, fecundity, moves, ops, inner, partial, padded, pairs, seeds
+    slot_table, cells, top, bottom, weights, fecundity, moves, ops,
+    inner, partial, padded, pairs, seeds, slots, sem,
 ):
+    slot_copy = pltpu.make_async_copy(slot_table, slots, sem)
+    slot_copy.start()
     rows, cols, cohorts = cells.shape
     fill_rows(cells, top, bottom, padded)
     clear_sides(padded)
@@ -348,6 +370,7 @@
         return carry
 
     lax.fori_loop(0, rows, one, 0, unroll=2)
+    slot_copy.wait()
     for i in range(0, rows // BX, 2):
         span = pl.ds(i * BX, 2 * BX)
         here = cells[span].astype(jnp.float32)[:, BY : cols - BY].reshape(-1, cohorts)
@@ -361,9 +384,11 @@
 
 
 def last_kernel(
-    slots, cells, left, right, weights, fecundity, moves, ops, inner, partial,
-    out, sides, pairs, seeds,
+    slot_table, cells, left, right, weights, fecundity, moves, ops, inner, partial,
+    out, sides, pairs, seeds, stage, slots, sem, sems,
 ):
+    slot_copy = pltpu.make_async_copy(slot_table, slots, sem)
+    slot_copy.start()
     rows, cols, cohorts = cells.shape
     near = lax.broadcasted_iota(jnp.int32, (BY, cohorts), 0) < RMAX
     gap = jnp.zeros((RMAX, cohorts), jnp.float32)
@@ -390,6 +415,7 @@
         return carry
 
     lax.fori_loop(0, rows, one, 0, unroll=4)
+    slot_copy.wait()
     for i in range(0, rows // BX, 2):
         span = pl.ds(i * BX, 2 * BX)
         here = cells[span].astype(jnp.float32)
@@ -404,7 +430,11 @@
             whole = jnp.concatenate(
                 [done[:, :BY], inner[at].astype(jnp.float32), done[:, BY:]], axis=1
             )
-            out[at] = whole.astype(jnp.bfloat16)
+            stage[at] = whole.astype(jnp.bfloat16)
+            pltpu.make_async_copy(stage.at[at], out.at[at], sems.at[i + k]).start()
+    for i in range(rows // BX):
+        at = pl.ds(i * BX, BX)
+        pltpu.make_async_copy(stage.at[at], out.at[at], sems.at[i]).wait()
 
 
 def scratch(rows, cols, cohorts, seeded=None):
@@ -442,13 +472,15 @@
         compiler_params=PARAMS,
         cost_estimate=pl.CostEstimate(flops=2**28, bytes_accessed=2**24, transcendentals=0),
     )(biomass, *around, weights, fecundity, moves)
+    slot_room = [pltpu.SMEM(slots.shape, jnp.int32), pltpu.SemaphoreType.DMA]
     row_part = jax.ShapeDtypeStruct((RMAX, cols, cohorts), jnp.bfloat16)
     col_part = jax.ShapeDtypeStruct((rows, RMAX, cohorts), jnp.bfloat16)
     cells, ops, first, last, head, tail = pl.pallas_call(
         harvest_kernel,
         out_shape=(state, operators, row_part, row_part, col_part, col_part),
-        in_specs=[SMEM, VMEM, VMEM],
+        in_specs=[ANY, VMEM, VMEM],
         out_specs=(VMEM,) * 6,
+        scratch_shapes=slot_room,
         compiler_params=PARAMS,
         cost_estimate=pl.CostEstimate(flops=2**28, bytes_accessed=2**22, transcendentals=0),
     )(slots, grown, parts)
@@ -461,22 +493,25 @@
             jax.ShapeDtypeStruct((rows, cols - outer, cohorts), jnp.bfloat16),
             jax.ShapeDtypeStruct((rows, outer, cohorts), jnp.float32),
         ),
-        in_specs=[SMEM] + [VMEM] * 7,
+        in_specs=[ANY] + [VMEM] * 7,
         out_specs=(VMEM, VMEM),
-        scratch_shapes=scratch(rows, cols, cohorts, cols - outer),
+        scratch_shapes=scratch(rows, cols, cohorts, cols - outer) + slot_room,
         compiler_params=PARAMS,
         cost_estimate=pl.CostEstimate(flops=2**28, bytes_accessed=2**24, transcendentals=0),
     )(slots, cells, top, bottom, weights, fecundity, moves, ops)
     return pl.pallas_call(
         last_kernel,
         out_shape=state,
-        in_specs=[SMEM] + [VMEM] * 9,
-        out_specs=VMEM,
+        in_specs=[ANY] + [VMEM] * 9,
+        out_specs=ANY,
         scratch_shapes=[
             pltpu.VMEM((high, outer, cohorts), jnp.float32),
             pltpu.VMEM((RMAX, high, BY, cohorts), jnp.float32),
             pltpu.VMEM((rows, outer, cohorts), jnp.bfloat16),
-        ],
+            pltpu.VMEM(shape, jnp.bfloat16),
+        ]
+        + slot_room
+        + [pltpu.SemaphoreType.DMA((rows // BX,))],
         compiler_params=PARAMS,
         cost_estimate=pl.CostEstimate(flops=2**28, bytes_accessed=2**22, transcendentals=0),
     )(slots, cells, left, right, weights, fecundity, moves, ops, inner, partial)

time: 87.4 us -> 86.9 us (level)
  Pallas kernels: 16.2 us -> 15.2 us
where the time goes in v10:
time: 86.9 us; the launch traced here: 86.4 us
  starting transfers between devices  45 us (52%)
  waiting for transfers between devices  23.5 us (27%)
  Pallas kernels  15.2 us (17%)
  local copies, waits for them, and re-layouts  1.64 us (2%)
    ppermute x8, starting transfers between devices, swap(): return (lax.ppermute(tail, axis, after), lax.ppermute(head, axis, before))  22 us
    all_to_all x1, starting transfers between devices, fetch(): arrived = lax.all_to_all(spread, WIDE, 0, 0, tiled=True)  16.8 us
    ppermute x8, waiting for transfers between devices, swap(): return (lax.ppermute(tail, axis, after), lax.ppermute(head, axis, before))  14.1 us
    all_to_all x1, waiting for transfers between devices, fetch(): arrived = lax.all_to_all(spread, WIDE, 0, 0, tiled=True)  9.39 us
    all_to_all x1, starting transfers between devices, fetch(): parts = lax.all_to_all(wanted, NEAR, 0, 0, tiled=True)  6.25 us
    pallas_call x1, Pallas kernels, local(): pl.pallas_call(middle_kernel, out_shape=(jax.ShapeDtypeStruct((rows, cols...  3.84 us
    pallas_call x1, Pallas kernels, local(): pl.pallas_call(first_kernel, out_shape=state, in_specs=[VMEM] * 8, out_sp...  3.4 us
    pallas_call x1, Pallas kernels, local(): pl.pallas_call(last_kernel, out_shape=state, in_specs=[ANY] + [VMEM] * 9,...  2.38 us
  transfers between devices with their start and end apart: 10, of which 5 were waited for; matrix products, arithmetic and copies ran while one was open for 1% of the time, Pallas kernels for 9%

profile of v10, /device:TPU:1, one launch (start us, length us, event | category | flops | bytes accessed | tf_op | source)
XLA Modules:
  0.0 86.4 jit_solution(15055283513342639581)
XLA Ops:
  0.0 2.4 %shard_map.109 = (bf16[128,16,128]{2,1,0:T(8,128)(2,1)}, f32[8,128]{1,0:T(8,128)}) custom-call(s32[1,1,8]{2,1,0:T(1,128)} %tile_list.1, bf16[4,256,256]{2,1,0:T(8,128)(2,1)} %harvest_ops.1), custom_call_target="tpu_custom_call" | custom-call | bytes 1048576 | tf_op jit(solution)/shard_map/pallas_call | solution.py:139
  2.4 0.0 copy-start
  2.4 0.0 copy-start.2
  2.4 16.8 %all-to-all-start = ((bf16[128,16,128]{2,1,0:T(8,128)(2,1)}), bf16[128,16,128]{2,1,0:T(8,128)(2,1)S(1)}, u32[]{:S(2)}, u32[]{:S(2)}) async-start(bf16[128,16,128]{2,1,0:T(8,128)(2,1)} %get-tuple-element.24), calls=%async_computation | async-start | bytes 1048576 | tf_op jit(solution)/shard_map/all_to_all | solution.py:156
  19.2 0.0 copy-done
  19.2 0.0 copy-done.2
  19.2 0.0 copy-start.4
  19.2 0.1 shard_map.110
  19.3 4.8 %collective-permute-start = (bf16[32,4,256]{2,1,0:T(4,128)(2,1)S(1)}, bf16[32,4,256]{2,1,0:T(4,128)(2,1)S(1)}, u32[]{:S(2)}, u32[]{:S(2)}) collective-permute-start(bf16[32,4,256]{2,1,0:T(4,128)(2,1)S(1)} %get-tuple-element.20), channel_id=1, source_target_pairs={{0,1},{1,2},{2,3},{3,4},{4,5},{5,6},{6,7},{7,8},{8,9},{9,10},{10,1... | collective-permute-start | bytes 196616 | tf_op jit(solution)/shard_map/ppermute | solution.py:41
  24.1 1.3 %collective-permute-start.1 = (bf16[32,4,256]{2,1,0:T(4,128)(2,1)S(1)}, bf16[32,4,256]{2,1,0:T(4,128)(2,1)S(1)}, u32[]{:S(2)}, u32[]{:S(2)}) collective-permute-start(bf16[32,4,256]{2,1,0:T(4,128)(2,1)S(1)} %get-tuple-element.21), channel_id=1, source_target_pairs={{1,0},{2,1},{3,2},{4,3},{5,4},{6,5},{7,6},{8,7},{9,8},{10,9},{11,1... | collective-permute-start | bytes 196616 | tf_op jit(solution)/shard_map/ppermute | solution.py:41
  25.4 0.0 copy-done.4
  25.4 0.1 copy.18
  25.5 0.0 copy-start.3
  25.5 0.1 copy.19
  25.7 0.0 copy-start.6
  25.7 0.7 copy-done.6
  26.4 0.0 copy-start.8
  26.4 0.0 copy-start.9
  26.4 0.0 copy-start.10
  26.4 0.6 copy-done.8
  27.0 0.0 copy-done.9
  27.0 0.0 copy-done.10
  27.0 0.1 multiply_reduce_fusion
  27.1 0.1 fusion.5.weights
  27.2 0.0 copy-done.3
  27.3 9.4 %all-to-all-done.arrived = bf16[128,16,128]{2,1,0:T(8,128)(2,1)S(1)} async-done(((bf16[128,16,128]{2,1,0:T(8,128)(2,1)}), bf16[128,16,128]{2,1,0:T(8,128)(2,1)S(1)}, u32[]{:S(2)}, u32[]{:S(2)}) %all-to-all-start) | async-done | bytes 524320 | tf_op jit(solution)/shard_map/all_to_all | solution.py:156
  36.7 0.1 fusion.2
  36.8 0.0 collective-permute-done.left
  36.8 0.0 collective-permute-done.1.right
  36.8 2.1 %shard_map.113 = bf16[32,8,16,128]{3,2,1,0:T(8,128)(2,1)} custom-call(s32[32,8]{1,0:T(8,128)S(1)} %bitcast.13, bf16[128,16,128]{2,1,0:T(8,128)(2,1)S(1)} %all-to-all-done.arrived, bf16[32,4,256]{2,1,0:T(4,128)(2,1)S(1)} %collective-permute-done.left, bf16[32,4,256]{2,1,0:T(4,128)(2,1)S(1)} %collective-permute-done.1.right, f32[10,256]{1,0:T(8,128)S(1)} %fusion.5.weights, ...), custom_call_target="tpu_custom_call" | custom-call | bytes 1048576 | tf_op jit(solution)/shard_map/pallas_call | solution.py:181
  38.9 6.2 %all-to-all-start.1 = ((bf16[32,8,16,128]{3,2,1,0:T(8,128)(2,1)}), bf16[32,8,16,128]{3,2,1,0:T(8,128)(2,1)S(1)}, u32[]{:S(2)}, u32[]{:S(2)}) async-start(bf16[32,8,16,128]{3,2,1,0:T(8,128)(2,1)} %shard_map.113), calls=%async_computation.1 | async-start | bytes 2097152 | tf_op jit(solution)/shard_map/all_to_all | solution.py:192
  45.2 0.0 copy-start.1
  45.2 0.0 copy-start.5
  45.2 3.5 %collective-permute-start.2 = (bf16[4,40,256]{2,1,0:T(8,128)(2,1)S(1)}, bf16[4,40,256]{2,1,0:T(8,128)(2,1)S(1)}, u32[]{:S(2)}, u32[]{:S(2)}) collective-permute-start(bf16[4,40,256]{2,1,0:T(8,128)(2,1)S(1)} %get-tuple-element.22), channel_id=1, source_target_pairs={{0,16},{16,32},{32,48},{48,64},{64,80},{80,96},{96,112},{112,128},... | collective-permute-start | bytes 245768 | tf_op jit(solution)/shard_map/ppermute | solution.py:41
  48.8 0.0 copy-start.7
  48.8 1.9 %collective-permute-start.3 = (bf16[4,40,256]{2,1,0:T(8,128)(2,1)S(1)}, bf16[4,40,256]{2,1,0:T(8,128)(2,1)S(1)}, u32[]{:S(2)}, u32[]{:S(2)}) collective-permute-start(bf16[4,40,256]{2,1,0:T(8,128)(2,1)S(1)} %get-tuple-element.23), channel_id=1, source_target_pairs={{16,0},{32,16},{48,32},{64,48},{80,64},{96,80},{112,96},{128,112},... | collective-permute-start | bytes 245768 | tf_op jit(solution)/shard_map/ppermute | solution.py:41
  50.7 0.0 copy-done.5
  50.7 0.0 copy-done.7
  50.7 0.2 select_reduce_fusion.slot_table
  51.0 6.9 %collective-permute-done.2.top = bf16[4,40,256]{2,1,0:T(8,128)(2,1)S(1)} collective-permute-done((bf16[4,40,256]{2,1,0:T(8,128)(2,1)S(1)}, bf16[4,40,256]{2,1,0:T(8,128)(2,1)S(1)}, u32[]{:S(2)}, u32[]{:S(2)}) %collective-permute-start.2) | collective-permute-done | bytes 81952 | tf_op jit(solution)/shard_map/ppermute | solution.py:41
  57.9 2.1 %collective-permute-done.3.bottom = bf16[4,40,256]{2,1,0:T(8,128)(2,1)S(1)} collective-permute-done((bf16[4,40,256]{2,1,0:T(8,128)(2,1)S(1)}, bf16[4,40,256]{2,1,0:T(8,128)(2,1)S(1)}, u32[]{:S(2)}, u32[]{:S(2)}) %collective-permute-start.3) | collective-permute-done | bytes 81952 | tf_op jit(solution)/shard_map/ppermute | solution.py:41
  60.0 0.0 copy-done.1
  60.0 3.4 %shard_map.112.grown = bf16[32,32,256]{2,1,0:T(8,128)(2,1)S(1)} custom-call(bf16[32,32,256]{2,1,0:T(8,128)(2,1)S(1)} %copy-done, bf16[4,40,256]{2,1,0:T(8,128)(2,1)S(1)} %collective-permute-done.2.top, bf16[4,40,256]{2,1,0:T(8,128)(2,1)S(1)} %collective-permute-done.3.bottom, bf16[32,4,256]{2,1,0:T(4,128)(2,1)S(1)} %collective-permute-done.left, ...), custom_call_target="tpu_custom_call" | custom-call | flops 268435456 | bytes 16777216 | tf_op jit(solution)/shard_map/pallas_call | solution.py:466
  63.4 0.0 all-to-all-done.1.parts
  63.4 1.0 %shard_map.114 = (bf16[32,32,256]{2,1,0:T(8,128)(2,1)S(1)}, bf16[8,256,256]{2,1,0:T(8,128)(2,1)S(1)}, bf16[4,32,256]{2,1,0:T(8,128)(2,1)S(1)}, bf16[4,32,256]{2,...) custom-call(s32[4,4]{1,0:T(4,128)S(1)} %select_reduce_fusion.slot_table, ...), custom_call_target="tpu_custom_call" | custom-call | flops 268435456 | bytes 4194304 | tf_op jit(solution)/shard_map/pallas_call | solution.py:478
  64.5 2.3 %collective-permute-start.4 = (bf16[4,32,256]{2,1,0:T(8,128)(2,1)S(1)}, bf16[4,32,256]{2,1,0:T(8,128)(2,1)S(1)}, u32[]{:S(2)}, u32[]{:S(2)}) collective-permute-start(bf16[4,32,256]{2,1,0:T(8,128)(2,1)S(1)} %get-tuple-element.26), channel_id=1, source_target_pairs={{0,16},{16,32},{32,48},{48,64},{64,80},{80,96},{96,112},{112,128},... | collective-permute-start | bytes 196616 | tf_op jit(solution)/shard_map/ppermute | solution.py:41
  66.8 2.1 %collective-permute-start.5 = (bf16[4,32,256]{2,1,0:T(8,128)(2,1)S(1)}, bf16[4,32,256]{2,1,0:T(8,128)(2,1)S(1)}, u32[]{:S(2)}, u32[]{:S(2)}) collective-permute-start(bf16[4,32,256]{2,1,0:T(8,128)(2,1)S(1)} %get-tuple-element.28), channel_id=1, source_target_pairs={{16,0},{32,16},{48,32},{64,48},{80,64},{96,80},{112,96},{128,112},... | collective-permute-start | bytes 196616 | tf_op jit(solution)/shard_map/ppermute | solution.py:41
  68.8 0.0 collective-permute-done.4.top
  68.9 3.5 %collective-permute-done.5.bottom = bf16[4,32,256]{2,1,0:T(8,128)(2,1)S(1)} collective-permute-done((bf16[4,32,256]{2,1,0:T(8,128)(2,1)S(1)}, bf16[4,32,256]{2,1,0:T(8,128)(2,1)S(1)}, u32[]{:S(2)}, u32[]{:S(2)}) %collective-permute-start.5) | collective-permute-done | bytes 65568 | tf_op jit(solution)/shard_map/ppermute | solution.py:41
  72.4 0.1 pad_maximum_fusion
  72.4 4.8 %collective-permute-start.6 = (bf16[40,4,256]{2,1,0:T(4,128)(2,1)S(1)}, bf16[40,4,256]{2,1,0:T(4,128)(2,1)S(1)}, u32[]{:S(2)}, u32[]{:S(2)}) collective-permute-start(bf16[40,4,256]{2,1,0:T(4,128)(2,1)S(1)} %pad_maximum_fusion), channel_id=1, source_target_pairs={{0,1},{1,2},{2,3},{3,4},{4,5},{5,6},{6,7},{7,8},{8,9},{9,10},{10,1... | collective-permute-start | bytes 245768 | tf_op jit(solution)/shard_map/ppermute | solution.py:41
  77.2 0.1 pad_maximum_fusion.1
  77.3 1.3 %collective-permute-start.7 = (bf16[40,4,256]{2,1,0:T(4,128)(2,1)S(1)}, bf16[40,4,256]{2,1,0:T(4,128)(2,1)S(1)}, u32[]{:S(2)}, u32[]{:S(2)}) collective-permute-start(bf16[40,4,256]{2,1,0:T(4,128)(2,1)S(1)} %pad_maximum_fusion.1), channel_id=1, source_target_pairs={{1,0},{2,1},{3,2},{4,3},{5,4},{6,5},{7,6},{8,7},{9,8},{10,9},{11,1... | collective-permute-start | bytes 245768 | tf_op jit(solution)/shard_map/ppermute | solution.py:41
  78.6 3.8 %shard_map.115 = (bf16[32,16,256]{2,1,0:T(8,128)(2,1)S(1)}, f32[32,16,256]{2,1,0:T(8,128)S(1)}) custom-call(s32[4,4]{1,0:T(4,128)S(1)} %select_reduce_fusion.slot_table, bf16[32,32,256]{2,1,0:T(8,128)(2,1)S(1)} %get-tuple-element.25.cells, bf16[4,32,256]{2,1,0:T(8,128)(2,1)S(1)} %collective-permute-done.4.top, ...), custom_call_target="tpu_custom_call" | custom-call | flops 268435456 | bytes 16777216 | tf_op jit(solution)/shard_map/pallas_call | solution.py:490
  82.5 0.0 collective-permute-done.6.left
  82.5 1.5 %collective-permute-done.7.right = bf16[40,4,256]{2,1,0:T(4,128)(2,1)S(1)} collective-permute-done((bf16[40,4,256]{2,1,0:T(4,128)(2,1)S(1)}, bf16[40,4,256]{2,1,0:T(4,128)(2,1)S(1)}, u32[]{:S(2)}, u32[]{:S(2)}) %collective-permute-start.7) | collective-permute-done | bytes 81952 | tf_op jit(solution)/shard_map/ppermute | solution.py:41
  84.0 2.4 %shard_map.116 = bf16[32,32,256]{2,1,0:T(8,128)(2,1)} custom-call(s32[4,4]{1,0:T(4,128)S(1)} %select_reduce_fusion.slot_table, bf16[32,32,256]{2,1,0:T(8,128)(2,1)S(1)} %get-tuple-element.25.cells, bf16[40,4,256]{2,1,0:T(4,128)(2,1)S(1)} %collective-permute-done.6.left, bf16[40,4,256]{2,1,0:T(4,128)(2,1)S(1)} %collective-permute-done.7.right, ...), custom_call_target="tpu_custom_call" | custom-call | flops 268435456 | bytes 4194304 | tf_op jit(solution)/shard_map/pallas_call | solution.py:502
  (11 shorter events, 0.2 us)
Async XLA Ops:
  2.4 16.8 %copy-start = (bf16[32,32,256]{2,1,0:T(8,128)(2,1)S(1)}, bf16[32,32,256]{2,1,0:T(8,128)(2,1)}, u32[]{:S(2)}) copy-start(bf16[32,32,256]{2,1,0:T(8,128)(2,1)} %cells.5) | copy-start | bytes 1572868
  2.4 16.8 %copy-start.2 = (f32[8,128]{1,0:T(8,128)S(1)}, f32[8,128]{1,0:T(8,128)}, u32[]{:S(2)}) copy-start(f32[8,128]{1,0:T(8,128)} %get-tuple-element.19.token) | copy-start | bytes 12292
  2.4 34.3 %all-to-all-start = ((bf16[128,16,128]{2,1,0:T(8,128)(2,1)}), bf16[128,16,128]{2,1,0:T(8,128)(2,1)S(1)}, u32[]{:S(2)}, u32[]{:S(2)}) async-start(bf16[128,16,128]{2,1,0:T(8,128)(2,1)} %get-tuple-element.24), calls=%async_computation | async-start | bytes 1048576 | tf_op jit(solution)/shard_map/all_to_all | solution.py:156
  19.2 6.2 %copy-start.4 = (s32[32,32]{1,0:T(8,128)S(1)}, s32[32,32]{1,0:T(8,128)}, u32[]{:S(2)}) copy-start(s32[32,32]{1,0:T(8,128)} %param.17) | copy-start | bytes 12292
  19.3 17.5 %collective-permute-start = (bf16[32,4,256]{2,1,0:T(4,128)(2,1)S(1)}, bf16[32,4,256]{2,1,0:T(4,128)(2,1)S(1)}, u32[]{:S(2)}, u32[]{:S(2)}) collective-permute-start(bf16[32,4,256]{2,1,0:T(4,128)(2,1)S(1)} %get-tuple-element.20), channel_id=1, source_target_pairs={{0,1},{1,2},{2,3},{3,4},{4,5},{5,6},{6,7},{7,8},{8,9},{9,10},{10,1... | collective-permute-start | bytes 196616 | tf_op jit(solution)/shard_map/ppermute | solution.py:41
  24.1 12.8 %collective-permute-start.1 = (bf16[32,4,256]{2,1,0:T(4,128)(2,1)S(1)}, bf16[32,4,256]{2,1,0:T(4,128)(2,1)S(1)}, u32[]{:S(2)}, u32[]{:S(2)}) collective-permute-start(bf16[32,4,256]{2,1,0:T(4,128)(2,1)S(1)} %get-tuple-element.21), channel_id=1, source_target_pairs={{1,0},{2,1},{3,2},{4,3},{5,4},{6,5},{7,6},{8,7},{9,8},{10,9},{11,1... | collective-permute-start | bytes 196616 | tf_op jit(solution)/shard_map/ppermute | solution.py:41
  25.5 1.7 %copy-start.3 = (bf16[256,256]{1,0:T(8,128)(2,1)S(1)}, bf16[256,256]{1,0:T(8,128)(2,1)}, u32[]{:S(2)}) copy-start(bf16[256,256]{1,0:T(8,128)(2,1)} %param.16) | copy-start | bytes 393220
  25.7 0.7 copy-start.6
  26.4 0.7 copy-start.8
  26.4 0.7 copy-start.9
  26.4 0.7 copy-start.10
  38.9 24.5 %all-to-all-start.1 = ((bf16[32,8,16,128]{3,2,1,0:T(8,128)(2,1)}), bf16[32,8,16,128]{3,2,1,0:T(8,128)(2,1)S(1)}, u32[]{:S(2)}, u32[]{:S(2)}) async-start(bf16[32,8,16,128]{3,2,1,0:T(8,128)(2,1)} %shard_map.113), calls=%async_computation.1 | async-start | bytes 2097152 | tf_op jit(solution)/shard_map/all_to_all | solution.py:192
  45.2 14.8 %copy-start.1 = (bf16[256,256]{1,0:T(8,128)(2,1)S(1)}, bf16[256,256]{1,0:T(8,128)(2,1)}, u32[]{:S(2)}) copy-start(bf16[256,256]{1,0:T(8,128)(2,1)} %fecundity.5) | copy-start | bytes 393220
  45.2 5.5 %copy-start.5 = (s32[4,4]{1,0:T(4,128)S(1)}, s32[4,4]{1,0:T(4,128)}, u32[]{:S(2)}) copy-start(s32[4,4]{1,0:T(4,128)} %param.12) | copy-start | bytes 196
  45.2 12.6 %collective-permute-start.2 = (bf16[4,40,256]{2,1,0:T(8,128)(2,1)S(1)}, bf16[4,40,256]{2,1,0:T(8,128)(2,1)S(1)}, u32[]{:S(2)}, u32[]{:S(2)}) collective-permute-start(bf16[4,40,256]{2,1,0:T(8,128)(2,1)S(1)} %get-tuple-element.22), channel_id=1, source_target_pairs={{0,16},{16,32},{32,48},{48,64},{64,80},{80,96},{96,112},{112,128},... | collective-permute-start | bytes 245768 | tf_op jit(solution)/shard_map/ppermute | solution.py:41
  48.8 2.0 %copy-start.7 = (s32[1,1,16]{2,1,0:T(1,128)S(1)}, s32[1,1,16]{2,1,0:T(1,128)}, u32[]{:S(2)}) copy-start(s32[1,1,16]{2,1,0:T(1,128)} %param.13) | copy-start | bytes 196
  48.8 11.2 %collective-permute-start.3 = (bf16[4,40,256]{2,1,0:T(8,128)(2,1)S(1)}, bf16[4,40,256]{2,1,0:T(8,128)(2,1)S(1)}, u32[]{:S(2)}, u32[]{:S(2)}) collective-permute-start(bf16[4,40,256]{2,1,0:T(8,128)(2,1)S(1)} %get-tuple-element.23), channel_id=1, source_target_pairs={{16,0},{32,16},{48,32},{64,48},{80,64},{96,80},{112,96},{128,112},... | collective-permute-start | bytes 245768 | tf_op jit(solution)/shard_map/ppermute | solution.py:41
  64.5 4.3 %collective-permute-start.4 = (bf16[4,32,256]{2,1,0:T(8,128)(2,1)S(1)}, bf16[4,32,256]{2,1,0:T(8,128)(2,1)S(1)}, u32[]{:S(2)}, u32[]{:S(2)}) collective-permute-start(bf16[4,32,256]{2,1,0:T(8,128)(2,1)S(1)} %get-tuple-element.26), channel_id=1, source_target_pairs={{0,16},{16,32},{32,48},{48,64},{64,80},{80,96},{96,112},{112,128},... | collective-permute-start | bytes 196616 | tf_op jit(solution)/shard_map/ppermute | solution.py:41
  66.8 5.6 %collective-permute-start.5 = (bf16[4,32,256]{2,1,0:T(8,128)(2,1)S(1)}, bf16[4,32,256]{2,1,0:T(8,128)(2,1)S(1)}, u32[]{:S(2)}, u32[]{:S(2)}) collective-permute-start(bf16[4,32,256]{2,1,0:T(8,128)(2,1)S(1)} %get-tuple-element.28), channel_id=1, source_target_pairs={{16,0},{32,16},{48,32},{64,48},{80,64},{96,80},{112,96},{128,112},... | collective-permute-start | bytes 196616 | tf_op jit(solution)/shard_map/ppermute | solution.py:41
  72.4 10.0 %collective-permute-start.6 = (bf16[40,4,256]{2,1,0:T(4,128)(2,1)S(1)}, bf16[40,4,256]{2,1,0:T(4,128)(2,1)S(1)}, u32[]{:S(2)}, u32[]{:S(2)}) collective-permute-start(bf16[40,4,256]{2,1,0:T(4,128)(2,1)S(1)} %pad_maximum_fusion), channel_id=1, source_target_pairs={{0,1},{1,2},{2,3},{3,4},{4,5},{5,6},{6,7},{7,8},{8,9},{9,10},{10,1... | collective-permute-start | bytes 245768 | tf_op jit(solution)/shard_map/ppermute | solution.py:41
  77.3 6.7 %collective-permute-start.7 = (bf16[40,4,256]{2,1,0:T(4,128)(2,1)S(1)}, bf16[40,4,256]{2,1,0:T(4,128)(2,1)S(1)}, u32[]{:S(2)}, u32[]{:S(2)}) collective-permute-start(bf16[40,4,256]{2,1,0:T(4,128)(2,1)S(1)} %pad_maximum_fusion.1), channel_id=1, source_target_pairs={{1,0},{2,1},{3,2},{4,3},{5,4},{6,5},{7,6},{8,7},{9,8},{10,9},{11,1... | collective-permute-start | bytes 245768 | tf_op jit(solution)/shard_map/ppermute | solution.py:41

commit v11 on v10

--- a/solution.py
+++ b/solution.py
@@ -78,7 +78,7 @@
             out[i] = whole.astype(jnp.bfloat16)
 
 
-def spread_kernel(tile_list, harvest_ops, spread, token, listed, held, stage, sems):
+def spread_kernel(tile_list, harvest_ops, spread, token, listed, held, sems):
     mine = (lax.axis_index("xl") * 2 + lax.axis_index("yl")) * 2 + lax.axis_index("co")
     list_copy = pltpu.make_async_copy(tile_list, listed, sems.at[0])
     held_copy = pltpu.make_async_copy(harvest_ops.at[mine // 2], held, sems.at[1])
@@ -98,12 +98,7 @@
             piece = held[pl.ds(group * 32 + low * 16, 16), pl.ds(half * 128, 128)]
             message = jnp.where(sent, piece.astype(jnp.float32), names).astype(jnp.bfloat16)
             for far in range(4):
-                stage[(group * 4 + far) * 4 + near] = message
-        span = pl.ds(group * 16, 16)
-        pltpu.make_async_copy(stage.at[span], spread.at[span], sems.at[2 + group]).start()
-    for group in range(8):
-        span = pl.ds(group * 16, 16)
-        pltpu.make_async_copy(stage.at[span], spread.at[span], sems.at[2 + group]).wait()
+                spread[(group * 4 + far) * 4 + near] = message
 
 
 def gather_kernel(places, arrived, left, right, weights, moves, wanted, stage, sems):
@@ -143,12 +138,11 @@
             jax.ShapeDtypeStruct((8, 128), jnp.float32),
         ),
         in_specs=[ANY, ANY],
-        out_specs=(ANY, VMEM),
+        out_specs=(VMEM, VMEM),
         scratch_shapes=[
             pltpu.SMEM(tile_list.shape, jnp.int32),
             pltpu.VMEM((cohorts, cohorts), jnp.bfloat16),
-            pltpu.VMEM((128, 16, 128), jnp.bfloat16),
-            pltpu.SemaphoreType.DMA((10,)),
+            pltpu.SemaphoreType.DMA((2,)),
         ],
         compiler_params=WHOLE,
         cost_estimate=small,
@@ -383,55 +377,78 @@
             inner[pl.ds((i + k) * BX, BX)] = done.astype(jnp.bfloat16)
 
 
-def last_kernel(
-    slot_table, cells, left, right, weights, fecundity, moves, ops, inner, partial,
-    out, sides, pairs, seeds, stage, slots, sem, sems,
+def finish_side(
+    lead, block, cells, side, weights, fecundity, moves, ops, partial, write, sides, pairs, seeds,
+    slots, slot_copy,
+):
+    rows, cols, cohorts = cells.shape
+    gap = jnp.zeros((BY, cohorts), jnp.float32)
+    at = BY - RMAX if lead < 0 else BY
+
+    def place(x, carry):
+        sides[x, pl.ds(BY if lead < 0 else 0, BY), :] = gap
+        sides[x, pl.ds(at, RMAX), :] = side[x].astype(jnp.float32)
+        for b in range(1, RMAX + 1):
+            pairs[b - 1, x] = sides[x, pl.ds(BY - b if lead < 0 else b, BY), :]
+        return carry
+
+    lax.fori_loop(0, rows + 2 * RMAX, place, 0, unroll=4)
+
+    def row_sum(x, b):
+        return None if b == 0 else pairs[b - 1, x]
+
+    first = 0 if lead < 0 else BY
+
+    def one(x, carry):
+        seeds[x] = partial[x, pl.ds(first, BY), :] + weigh(x, row_sum, weights)
+        return carry
+
+    lax.fori_loop(0, rows, one, 0, unroll=4)
+    start = block * BY
+    here = cells[...].astype(jnp.float32)[:, start : start + BY].reshape(-1, cohorts)
+    arrived = seeds[...].reshape(-1, cohorts).astype(jnp.bfloat16)
+    grown = establish(arrived, here, fecundity, moves)
+    slot_copy.wait()
+    size = BX * BY
+    for i in range(rows // BX):
+        done = remove(grown[i * size : (i + 1) * size], slots[i, block], ops)
+        write(i, done.reshape(BX, BY, cohorts))
+
+
+def left_kernel(
+    slot_table, cells, left, weights, fecundity, moves, ops, partial,
+    result, sides, pairs, seeds, slots, sem,
 ):
     slot_copy = pltpu.make_async_copy(slot_table, slots, sem)
     slot_copy.start()
-    rows, cols, cohorts = cells.shape
-    near = lax.broadcasted_iota(jnp.int32, (BY, cohorts), 0) < RMAX
-    gap = jnp.zeros((RMAX, cohorts), jnp.float32)
-
-    def place(x, carry):
-        sides[x, pl.ds(BY - RMAX, RMAX), :] = left[x].astype(jnp.float32)
-        sides[x, pl.ds(BY, RMAX), :] = gap
-        sides[x, pl.ds(BY + RMAX, RMAX), :] = right[x].astype(jnp.float32)
-        for b in range(1, RMAX + 1):
-            pairs[b - 1, x] = jnp.where(
-                near, sides[x, pl.ds(BY - b, BY), :], sides[x, pl.ds(RMAX + b, BY), :]
-            )
-        return carry
-
-    lax.fori_loop(0, rows + 2 * RMAX, place, 0, unroll=4)
-
-    def row_sum(x, b):
-        return None if b == 0 else pairs[b - 1, x]
-
-    def one(x, carry):
-        extra = weigh(x, row_sum, weights)
-        both = jnp.concatenate([jnp.where(near, extra, 0.0), jnp.where(near, 0.0, extra)], axis=0)
-        seeds[x] = (partial[x] + both).astype(jnp.bfloat16)
-        return carry
-
-    lax.fori_loop(0, rows, one, 0, unroll=4)
-    slot_copy.wait()
-    for i in range(0, rows // BX, 2):
-        span = pl.ds(i * BX, 2 * BX)
-        here = cells[span].astype(jnp.float32)
-        here = jnp.concatenate([here[:, :BY], here[:, cols - BY :]], axis=1).reshape(-1, cohorts)
-        grown = establish(seeds[span].reshape(-1, cohorts), here, fecundity, moves)
-        half = grown.shape[0] // 2
-        for k in range(2):
-            done = remove_pair(
-                grown[k * half : (k + 1) * half], (slots[i + k, 0], slots[i + k, 3]), ops
-            )
-            at = pl.ds((i + k) * BX, BX)
-            whole = jnp.concatenate(
-                [done[:, :BY], inner[at].astype(jnp.float32), done[:, BY:]], axis=1
-            )
-            stage[at] = whole.astype(jnp.bfloat16)
-            pltpu.make_async_copy(stage.at[at], out.at[at], sems.at[i + k]).start()
+
+    def write(i, done):
+        result[pl.ds(i * BX, BX)] = done
+
+    finish_side(
+        -1, 0, cells, left, weights, fecundity, moves, ops, partial, write, sides, pairs, seeds,
+        slots, slot_copy,
+    )
+
+
+def last_kernel(
+    slot_table, cells, right, weights, fecundity, moves, ops, partial, before, inner,
+    out, sides, pairs, seeds, slots, sem, stage, sems,
+):
+    rows, cols, _ = cells.shape
+    slot_copy = pltpu.make_async_copy(slot_table, slots, sem)
+    slot_copy.start()
+
+    def write(i, done):
+        at = pl.ds(i * BX, BX)
+        whole = jnp.concatenate([before[at], inner[at].astype(jnp.float32), done], axis=1)
+        stage[at] = whole.astype(jnp.bfloat16)
+        pltpu.make_async_copy(stage.at[at], out.at[at], sems.at[i]).start()
+
+    finish_side(
+        1, cols // BY - 1, cells, right, weights, fecundity, moves, ops, partial, write, sides,
+        pairs, seeds, slots, slot_copy,
+    )
     for i in range(rows // BX):
         at = pl.ds(i * BX, BX)
         pltpu.make_async_copy(stage.at[at], out.at[at], sems.at[i]).wait()
@@ -499,22 +516,30 @@
         compiler_params=PARAMS,
         cost_estimate=pl.CostEstimate(flops=2**28, bytes_accessed=2**24, transcendentals=0),
     )(slots, cells, top, bottom, weights, fecundity, moves, ops)
+    side_room = [
+        pltpu.VMEM((high, outer, cohorts), jnp.float32),
+        pltpu.VMEM((RMAX, high, BY, cohorts), jnp.float32),
+        pltpu.VMEM((rows, BY, cohorts), jnp.float32),
+    ] + slot_room
+    before = pl.pallas_call(
+        left_kernel,
+        out_shape=jax.ShapeDtypeStruct((rows, BY, cohorts), jnp.float32),
+        in_specs=[ANY] + [VMEM] * 7,
+        out_specs=VMEM,
+        scratch_shapes=side_room,
+        compiler_params=PARAMS,
+        cost_estimate=pl.CostEstimate(flops=2**27, bytes_accessed=2**22, transcendentals=0),
+    )(slots, cells, left, weights, fecundity, moves, ops, partial)
     return pl.pallas_call(
         last_kernel,
         out_shape=state,
         in_specs=[ANY] + [VMEM] * 9,
         out_specs=ANY,
-        scratch_shapes=[
-            pltpu.VMEM((high, outer, cohorts), jnp.float32),
-            pltpu.VMEM((RMAX, high, BY, cohorts), jnp.float32),
-            pltpu.VMEM((rows, outer, cohorts), jnp.bfloat16),
-            pltpu.VMEM(shape, jnp.bfloat16),
-        ]
-        + slot_room
-        + [pltpu.SemaphoreType.DMA((rows // BX,))],
+        scratch_shapes=side_room
+        + [pltpu.VMEM(shape, jnp.bfloat16), pltpu.SemaphoreType.DMA((rows // BX,))],
         compiler_params=PARAMS,
         cost_estimate=pl.CostEstimate(flops=2**28, bytes_accessed=2**22, transcendentals=0),
-    )(slots, cells, left, right, weights, fecundity, moves, ops, inner, partial)
+    )(slots, cells, right, weights, fecundity, moves, ops, partial, before, inner)
 
 
 def solution(mesh):

time: 86.9 us -> 86 us (0.990)
  waiting for transfers between devices: 23.5 us -> 22.2 us
    ppermute x8, waiting for transfers between devices: 14.1 us -> 12.8 us  [swap(): return (lax.ppermute(tail, axis, after), lax.ppermute(head, axis, before))]
    pallas_call x0 -> x1, Pallas kernels: none -> 1.26 us  [local(): pl.pallas_call(left_kernel, out_shape=jax.ShapeDtypeStruct((rows, BY, coh...]
  transfers between devices with their start and end apart: 10 -> 10, of which waited for: 5 -> 5; matrix products, arithmetic and copies ran while one was open for 1% -> 1% of each run, Pallas kernels for 9% -> 10%
where the time goes in v11:
time: 86 us; the launch traced here: 85.4 us
  starting transfers between devices  45 us (52%)
  waiting for transfers between devices  22.2 us (26%)
  Pallas kernels  15.5 us (18%)
  local copies, waits for them, and re-layouts  1.64 us (2%)
    ppermute x8, starting transfers between devices, swap(): return (lax.ppermute(tail, axis, after), lax.ppermute(head, axis, before))  22 us
    all_to_all x1, starting transfers between devices, fetch(): arrived = lax.all_to_all(spread, WIDE, 0, 0, tiled=True)  16.8 us
    ppermute x8, waiting for transfers between devices, swap(): return (lax.ppermute(tail, axis, after), lax.ppermute(head, axis, before))  12.8 us
    all_to_all x1, waiting for transfers between devices, fetch(): arrived = lax.all_to_all(spread, WIDE, 0, 0, tiled=True)  9.39 us
    all_to_all x1, starting transfers between devices, fetch(): parts = lax.all_to_all(wanted, NEAR, 0, 0, tiled=True)  6.25 us
    pallas_call x1, Pallas kernels, local(): pl.pallas_call(middle_kernel, out_shape=(jax.ShapeDtypeStruct((rows, cols...  3.84 us
    pallas_call x1, Pallas kernels, local(): pl.pallas_call(first_kernel, out_shape=state, in_specs=[VMEM] * 8, out_sp...  3.4 us
    pallas_call x1, Pallas kernels, fetch(): pl.pallas_call(gather_kernel, out_shape=jax.ShapeDtypeStruct((32, count,...  2.05 us
  transfers between devices with their start and end apart: 10, of which 5 were waited for; matrix products, arithmetic and copies ran while one was open for 1% of the time, Pallas kernels for 10%

profile of v11, /device:TPU:1, one launch (start us, length us, event | category | flops | bytes accessed | tf_op | source)
XLA Modules:
  0.0 85.4 jit_solution(107151431803502247)
XLA Ops:
  0.0 1.8 %shard_map.109 = (bf16[128,16,128]{2,1,0:T(8,128)(2,1)}, f32[8,128]{1,0:T(8,128)}) custom-call(s32[1,1,8]{2,1,0:T(1,128)} %tile_list.1, bf16[4,256,256]{2,1,0:T(8,128)(2,1)} %harvest_ops.1), custom_call_target="tpu_custom_call" | custom-call | bytes 1048576 | tf_op jit(solution)/shard_map/pallas_call | solution.py:134
  1.8 0.0 copy-start
  1.8 0.0 copy-start.2
  1.8 16.8 %all-to-all-start = ((bf16[128,16,128]{2,1,0:T(8,128)(2,1)}), bf16[128,16,128]{2,1,0:T(8,128)(2,1)S(1)}, u32[]{:S(2)}, u32[]{:S(2)}) async-start(bf16[128,16,128]{2,1,0:T(8,128)(2,1)} %get-tuple-element.24), calls=%async_computation | async-start | bytes 1048576 | tf_op jit(solution)/shard_map/all_to_all | solution.py:150
  18.6 0.0 copy-done
  18.6 0.0 copy-done.2
  18.6 0.0 copy-start.4
  18.6 0.1 shard_map.110
  18.7 4.8 %collective-permute-start = (bf16[32,4,256]{2,1,0:T(4,128)(2,1)S(1)}, bf16[32,4,256]{2,1,0:T(4,128)(2,1)S(1)}, u32[]{:S(2)}, u32[]{:S(2)}) collective-permute-start(bf16[32,4,256]{2,1,0:T(4,128)(2,1)S(1)} %get-tuple-element.20), channel_id=1, source_target_pairs={{0,1},{1,2},{2,3},{3,4},{4,5},{5,6},{6,7},{7,8},{8,9},{9,10},{10,1... | collective-permute-start | bytes 196616 | tf_op jit(solution)/shard_map/ppermute | solution.py:41
  23.5 1.3 %collective-permute-start.1 = (bf16[32,4,256]{2,1,0:T(4,128)(2,1)S(1)}, bf16[32,4,256]{2,1,0:T(4,128)(2,1)S(1)}, u32[]{:S(2)}, u32[]{:S(2)}) collective-permute-start(bf16[32,4,256]{2,1,0:T(4,128)(2,1)S(1)} %get-tuple-element.21), channel_id=1, source_target_pairs={{1,0},{2,1},{3,2},{4,3},{5,4},{6,5},{7,6},{8,7},{9,8},{10,9},{11,1... | collective-permute-start | bytes 196616 | tf_op jit(solution)/shard_map/ppermute | solution.py:41
  24.8 0.0 copy-done.4
  24.8 0.1 copy.18
  24.9 0.0 copy-start.3
  24.9 0.1 copy.19
  25.1 0.0 copy-start.6
  25.1 0.7 copy-done.6
  25.7 0.0 copy-start.8
  25.7 0.0 copy-start.9
  25.8 0.0 copy-start.10
  25.8 0.6 copy-done.8
  26.4 0.0 copy-done.9
  26.4 0.0 copy-done.10
  26.4 0.1 multiply_reduce_fusion
  26.5 0.1 fusion.5.weights
  26.6 0.0 copy-done.3
  26.7 9.4 %all-to-all-done.arrived = bf16[128,16,128]{2,1,0:T(8,128)(2,1)S(1)} async-done(((bf16[128,16,128]{2,1,0:T(8,128)(2,1)}), bf16[128,16,128]{2,1,0:T(8,128)(2,1)S(1)}, u32[]{:S(2)}, u32[]{:S(2)}) %all-to-all-start) | async-done | bytes 524320 | tf_op jit(solution)/shard_map/all_to_all | solution.py:150
  36.1 0.1 fusion.2
  36.2 0.0 collective-permute-done.left
  36.2 0.0 collective-permute-done.1.right
  36.2 2.1 %shard_map.113 = bf16[32,8,16,128]{3,2,1,0:T(8,128)(2,1)} custom-call(s32[32,8]{1,0:T(8,128)S(1)} %bitcast.13, bf16[128,16,128]{2,1,0:T(8,128)(2,1)S(1)} %all-to-all-done.arrived, bf16[32,4,256]{2,1,0:T(4,128)(2,1)S(1)} %collective-permute-done.left, bf16[32,4,256]{2,1,0:T(4,128)(2,1)S(1)} %collective-permute-done.1.right, f32[10,256]{1,0:T(8,128)S(1)} %fusion.5.weights, ...), custom_call_target="tpu_custom_call" | custom-call | bytes 1048576 | tf_op jit(solution)/shard_map/pallas_call | solution.py:175
  38.3 6.2 %all-to-all-start.1 = ((bf16[32,8,16,128]{3,2,1,0:T(8,128)(2,1)}), bf16[32,8,16,128]{3,2,1,0:T(8,128)(2,1)S(1)}, u32[]{:S(2)}, u32[]{:S(2)}) async-start(bf16[32,8,16,128]{3,2,1,0:T(8,128)(2,1)} %shard_map.113), calls=%async_computation.1 | async-start | bytes 2097152 | tf_op jit(solution)/shard_map/all_to_all | solution.py:186
  44.6 0.0 copy-start.1
  44.6 0.0 copy-start.5
  44.6 3.5 %collective-permute-start.2 = (bf16[4,40,256]{2,1,0:T(8,128)(2,1)S(1)}, bf16[4,40,256]{2,1,0:T(8,128)(2,1)S(1)}, u32[]{:S(2)}, u32[]{:S(2)}) collective-permute-start(bf16[4,40,256]{2,1,0:T(8,128)(2,1)S(1)} %get-tuple-element.22), channel_id=1, source_target_pairs={{0,16},{16,32},{32,48},{48,64},{64,80},{80,96},{96,112},{112,128},... | collective-permute-start | bytes 245768 | tf_op jit(solution)/shard_map/ppermute | solution.py:41
  48.2 0.0 copy-start.7
  48.2 1.9 %collective-permute-start.3 = (bf16[4,40,256]{2,1,0:T(8,128)(2,1)S(1)}, bf16[4,40,256]{2,1,0:T(8,128)(2,1)S(1)}, u32[]{:S(2)}, u32[]{:S(2)}) collective-permute-start(bf16[4,40,256]{2,1,0:T(8,128)(2,1)S(1)} %get-tuple-element.23), channel_id=1, source_target_pairs={{16,0},{32,16},{48,32},{64,48},{80,64},{96,80},{112,96},{128,112},... | collective-permute-start | bytes 245768 | tf_op jit(solution)/shard_map/ppermute | solution.py:41
  50.1 0.0 copy-done.5
  50.1 0.0 copy-done.7
  50.1 0.2 select_reduce_fusion.slot_table
  50.3 6.9 %collective-permute-done.2.top = bf16[4,40,256]{2,1,0:T(8,128)(2,1)S(1)} collective-permute-done((bf16[4,40,256]{2,1,0:T(8,128)(2,1)S(1)}, bf16[4,40,256]{2,1,0:T(8,128)(2,1)S(1)}, u32[]{:S(2)}, u32[]{:S(2)}) %collective-permute-start.2) | collective-permute-done | bytes 81952 | tf_op jit(solution)/shard_map/ppermute | solution.py:41
  57.3 2.1 %collective-permute-done.3.bottom = bf16[4,40,256]{2,1,0:T(8,128)(2,1)S(1)} collective-permute-done((bf16[4,40,256]{2,1,0:T(8,128)(2,1)S(1)}, bf16[4,40,256]{2,1,0:T(8,128)(2,1)S(1)}, u32[]{:S(2)}, u32[]{:S(2)}) %collective-permute-start.3) | collective-permute-done | bytes 81952 | tf_op jit(solution)/shard_map/ppermute | solution.py:41
  59.4 0.0 copy-done.1
  59.4 3.4 %shard_map.112.grown = bf16[32,32,256]{2,1,0:T(8,128)(2,1)S(1)} custom-call(bf16[32,32,256]{2,1,0:T(8,128)(2,1)S(1)} %copy-done, bf16[4,40,256]{2,1,0:T(8,128)(2,1)S(1)} %collective-permute-done.2.top, bf16[4,40,256]{2,1,0:T(8,128)(2,1)S(1)} %collective-permute-done.3.bottom, bf16[32,4,256]{2,1,0:T(4,128)(2,1)S(1)} %collective-permute-done.left, ...), custom_call_target="tpu_custom_call" | custom-call | flops 268435456 | bytes 16777216 | tf_op jit(solution)/shard_map/pallas_call | solution.py:483
  62.8 0.0 all-to-all-done.1.parts
  62.8 1.0 %shard_map.114 = (bf16[32,32,256]{2,1,0:T(8,128)(2,1)S(1)}, bf16[8,256,256]{2,1,0:T(8,128)(2,1)S(1)}, bf16[4,32,256]{2,1,0:T(8,128)(2,1)S(1)}, bf16[4,32,256]{2,...) custom-call(s32[4,4]{1,0:T(4,128)S(1)} %select_reduce_fusion.slot_table, ...), custom_call_target="tpu_custom_call" | custom-call | flops 268435456 | bytes 4194304 | tf_op jit(solution)/shard_map/pallas_call | solution.py:495
  63.9 2.3 %collective-permute-start.4 = (bf16[4,32,256]{2,1,0:T(8,128)(2,1)S(1)}, bf16[4,32,256]{2,1,0:T(8,128)(2,1)S(1)}, u32[]{:S(2)}, u32[]{:S(2)}) collective-permute-start(bf16[4,32,256]{2,1,0:T(8,128)(2,1)S(1)} %get-tuple-element.26), channel_id=1, source_target_pairs={{0,16},{16,32},{32,48},{48,64},{64,80},{80,96},{96,112},{112,128},... | collective-permute-start | bytes 196616 | tf_op jit(solution)/shard_map/ppermute | solution.py:41
  66.1 2.1 %collective-permute-start.5 = (bf16[4,32,256]{2,1,0:T(8,128)(2,1)S(1)}, bf16[4,32,256]{2,1,0:T(8,128)(2,1)S(1)}, u32[]{:S(2)}, u32[]{:S(2)}) collective-permute-start(bf16[4,32,256]{2,1,0:T(8,128)(2,1)S(1)} %get-tuple-element.28), channel_id=1, source_target_pairs={{16,0},{32,16},{48,32},{64,48},{80,64},{96,80},{112,96},{128,112},... | collective-permute-start | bytes 196616 | tf_op jit(solution)/shard_map/ppermute | solution.py:41
  68.2 0.0 collective-permute-done.4.top
  68.2 3.5 %collective-permute-done.5.bottom = bf16[4,32,256]{2,1,0:T(8,128)(2,1)S(1)} collective-permute-done((bf16[4,32,256]{2,1,0:T(8,128)(2,1)S(1)}, bf16[4,32,256]{2,1,0:T(8,128)(2,1)S(1)}, u32[]{:S(2)}, u32[]{:S(2)}) %collective-permute-start.5) | collective-permute-done | bytes 65568 | tf_op jit(solution)/shard_map/ppermute | solution.py:41
  71.7 0.1 pad_maximum_fusion.1
  71.8 4.8 %collective-permute-start.7 = (bf16[40,4,256]{2,1,0:T(4,128)(2,1)S(1)}, bf16[40,4,256]{2,1,0:T(4,128)(2,1)S(1)}, u32[]{:S(2)}, u32[]{:S(2)}) collective-permute-start(bf16[40,4,256]{2,1,0:T(4,128)(2,1)S(1)} %pad_maximum_fusion.1), channel_id=1, source_target_pairs={{0,1},{1,2},{2,3},{3,4},{4,5},{5,6},{6,7},{7,8},{8,9},{9,10},{10,1... | collective-permute-start | bytes 245768 | tf_op jit(solution)/shard_map/ppermute | solution.py:41
  76.6 0.1 pad_maximum_fusion
  76.7 1.3 %collective-permute-start.6 = (bf16[40,4,256]{2,1,0:T(4,128)(2,1)S(1)}, bf16[40,4,256]{2,1,0:T(4,128)(2,1)S(1)}, u32[]{:S(2)}, u32[]{:S(2)}) collective-permute-start(bf16[40,4,256]{2,1,0:T(4,128)(2,1)S(1)} %pad_maximum_fusion), channel_id=1, source_target_pairs={{1,0},{2,1},{3,2},{4,3},{5,4},{6,5},{7,6},{8,7},{9,8},{10,9},{11,1... | collective-permute-start | bytes 245768 | tf_op jit(solution)/shard_map/ppermute | solution.py:41
  78.0 3.8 %shard_map.115 = (bf16[32,16,256]{2,1,0:T(8,128)(2,1)S(1)}, f32[32,16,256]{2,1,0:T(8,128)S(1)}) custom-call(s32[4,4]{1,0:T(4,128)S(1)} %select_reduce_fusion.slot_table, bf16[32,32,256]{2,1,0:T(8,128)(2,1)S(1)} %get-tuple-element.25.cells, bf16[4,32,256]{2,1,0:T(8,128)(2,1)S(1)} %collective-permute-done.4.top, ...), custom_call_target="tpu_custom_call" | custom-call | flops 268435456 | bytes 16777216 | tf_op jit(solution)/shard_map/pallas_call | solution.py:507
  81.8 0.0 collective-permute-done.7.left
  81.9 1.3 %shard_map.116.before = f32[32,8,256]{2,1,0:T(8,128)S(1)} custom-call(s32[4,4]{1,0:T(4,128)S(1)} %select_reduce_fusion.slot_table, bf16[32,32,256]{2,1,0:T(8,128)(2,1)S(1)} %get-tuple-element.25.cells, bf16[40,4,256]{2,1,0:T(4,128)(2,1)S(1)} %collective-permute-done.7.left, f32[10,256]{1,0:T(8,128)S(1)} %fusion.5.weights, bf16[256,256]{1,0:T(8,128)(2,1)S(1)} %copy-done.1, ...), custom_call_target="tpu_custom_call" | custom-call | flops 134217728 | bytes 4194304 | tf_op jit(solution)/shard_map/pallas_call | solution.py:524
  83.1 0.3 collective-permute-done.6.right
  83.4 2.0 %shard_map.117 = bf16[32,32,256]{2,1,0:T(8,128)(2,1)} custom-call(s32[4,4]{1,0:T(4,128)S(1)} %select_reduce_fusion.slot_table, bf16[32,32,256]{2,1,0:T(8,128)(2,1)S(1)} %get-tuple-element.25.cells, bf16[40,4,256]{2,1,0:T(4,128)(2,1)S(1)} %collective-permute-done.6.right, f32[10,256]{1,0:T(8,128)S(1)} %fusion.5.weights, bf16[256,256]{1,0:T(8,128)(2,1)S(1)} %copy-done.1, ...), custom_call_target="tpu_custom_call" | custom-call | flops 268435456 | bytes 4194304 | tf_op jit(solution)/shard_map/pallas_call | solution.py:533
  (11 shorter events, 0.2 us)
Async XLA Ops:
  1.8 16.8 %copy-start = (bf16[32,32,256]{2,1,0:T(8,128)(2,1)S(1)}, bf16[32,32,256]{2,1,0:T(8,128)(2,1)}, u32[]{:S(2)}) copy-start(bf16[32,32,256]{2,1,0:T(8,128)(2,1)} %cells.5) | copy-start | bytes 1572868
  1.8 16.8 %copy-start.2 = (f32[8,128]{1,0:T(8,128)S(1)}, f32[8,128]{1,0:T(8,128)}, u32[]{:S(2)}) copy-start(f32[8,128]{1,0:T(8,128)} %get-tuple-element.19.token) | copy-start | bytes 12292
  1.8 34.3 %all-to-all-start = ((bf16[128,16,128]{2,1,0:T(8,128)(2,1)}), bf16[128,16,128]{2,1,0:T(8,128)(2,1)S(1)}, u32[]{:S(2)}, u32[]{:S(2)}) async-start(bf16[128,16,128]{2,1,0:T(8,128)(2,1)} %get-tuple-element.24), calls=%async_computation | async-start | bytes 1048576 | tf_op jit(solution)/shard_map/all_to_all | solution.py:150
  18.6 6.2 %copy-start.4 = (s32[32,32]{1,0:T(8,128)S(1)}, s32[32,32]{1,0:T(8,128)}, u32[]{:S(2)}) copy-start(s32[32,32]{1,0:T(8,128)} %param.17) | copy-start | bytes 12292
  18.7 17.5 %collective-permute-start = (bf16[32,4,256]{2,1,0:T(4,128)(2,1)S(1)}, bf16[32,4,256]{2,1,0:T(4,128)(2,1)S(1)}, u32[]{:S(2)}, u32[]{:S(2)}) collective-permute-start(bf16[32,4,256]{2,1,0:T(4,128)(2,1)S(1)} %get-tuple-element.20), channel_id=1, source_target_pairs={{0,1},{1,2},{2,3},{3,4},{4,5},{5,6},{6,7},{7,8},{8,9},{9,10},{10,1... | collective-permute-start | bytes 196616 | tf_op jit(solution)/shard_map/ppermute | solution.py:41
  23.5 12.8 %collective-permute-start.1 = (bf16[32,4,256]{2,1,0:T(4,128)(2,1)S(1)}, bf16[32,4,256]{2,1,0:T(4,128)(2,1)S(1)}, u32[]{:S(2)}, u32[]{:S(2)}) collective-permute-start(bf16[32,4,256]{2,1,0:T(4,128)(2,1)S(1)} %get-tuple-element.21), channel_id=1, source_target_pairs={{1,0},{2,1},{3,2},{4,3},{5,4},{6,5},{7,6},{8,7},{9,8},{10,9},{11,1... | collective-permute-start | bytes 196616 | tf_op jit(solution)/shard_map/ppermute | solution.py:41
  24.9 1.7 %copy-start.3 = (bf16[256,256]{1,0:T(8,128)(2,1)S(1)}, bf16[256,256]{1,0:T(8,128)(2,1)}, u32[]{:S(2)}) copy-start(bf16[256,256]{1,0:T(8,128)(2,1)} %param.16) | copy-start | bytes 393220
  25.1 0.7 copy-start.6
  25.7 0.7 copy-start.8
  25.7 0.7 copy-start.9
  25.8 0.7 copy-start.10
  38.3 24.5 %all-to-all-start.1 = ((bf16[32,8,16,128]{3,2,1,0:T(8,128)(2,1)}), bf16[32,8,16,128]{3,2,1,0:T(8,128)(2,1)S(1)}, u32[]{:S(2)}, u32[]{:S(2)}) async-start(bf16[32,8,16,128]{3,2,1,0:T(8,128)(2,1)} %shard_map.113), calls=%async_computation.1 | async-start | bytes 2097152 | tf_op jit(solution)/shard_map/all_to_all | solution.py:186
  44.6 14.8 %copy-start.1 = (bf16[256,256]{1,0:T(8,128)(2,1)S(1)}, bf16[256,256]{1,0:T(8,128)(2,1)}, u32[]{:S(2)}) copy-start(bf16[256,256]{1,0:T(8,128)(2,1)} %fecundity.7) | copy-start | bytes 393220
  44.6 5.5 %copy-start.5 = (s32[4,4]{1,0:T(4,128)S(1)}, s32[4,4]{1,0:T(4,128)}, u32[]{:S(2)}) copy-start(s32[4,4]{1,0:T(4,128)} %param.12) | copy-start | bytes 196
  44.6 12.6 %collective-permute-start.2 = (bf16[4,40,256]{2,1,0:T(8,128)(2,1)S(1)}, bf16[4,40,256]{2,1,0:T(8,128)(2,1)S(1)}, u32[]{:S(2)}, u32[]{:S(2)}) collective-permute-start(bf16[4,40,256]{2,1,0:T(8,128)(2,1)S(1)} %get-tuple-element.22), channel_id=1, source_target_pairs={{0,16},{16,32},{32,48},{48,64},{64,80},{80,96},{96,112},{112,128},... | collective-permute-start | bytes 245768 | tf_op jit(solution)/shard_map/ppermute | solution.py:41
  48.2 2.0 %copy-start.7 = (s32[1,1,16]{2,1,0:T(1,128)S(1)}, s32[1,1,16]{2,1,0:T(1,128)}, u32[]{:S(2)}) copy-start(s32[1,1,16]{2,1,0:T(1,128)} %param.13) | copy-start | bytes 196
  48.2 11.2 %collective-permute-start.3 = (bf16[4,40,256]{2,1,0:T(8,128)(2,1)S(1)}, bf16[4,40,256]{2,1,0:T(8,128)(2,1)S(1)}, u32[]{:S(2)}, u32[]{:S(2)}) collective-permute-start(bf16[4,40,256]{2,1,0:T(8,128)(2,1)S(1)} %get-tuple-element.23), channel_id=1, source_target_pairs={{16,0},{32,16},{48,32},{64,48},{80,64},{96,80},{112,96},{128,112},... | collective-permute-start | bytes 245768 | tf_op jit(solution)/shard_map/ppermute | solution.py:41
  63.9 4.3 %collective-permute-start.4 = (bf16[4,32,256]{2,1,0:T(8,128)(2,1)S(1)}, bf16[4,32,256]{2,1,0:T(8,128)(2,1)S(1)}, u32[]{:S(2)}, u32[]{:S(2)}) collective-permute-start(bf16[4,32,256]{2,1,0:T(8,128)(2,1)S(1)} %get-tuple-element.26), channel_id=1, source_target_pairs={{0,16},{16,32},{32,48},{48,64},{64,80},{80,96},{96,112},{112,128},... | collective-permute-start | bytes 196616 | tf_op jit(solution)/shard_map/ppermute | solution.py:41
  66.1 5.6 %collective-permute-start.5 = (bf16[4,32,256]{2,1,0:T(8,128)(2,1)S(1)}, bf16[4,32,256]{2,1,0:T(8,128)(2,1)S(1)}, u32[]{:S(2)}, u32[]{:S(2)}) collective-permute-start(bf16[4,32,256]{2,1,0:T(8,128)(2,1)S(1)} %get-tuple-element.28), channel_id=1, source_target_pairs={{16,0},{32,16},{48,32},{64,48},{80,64},{96,80},{112,96},{128,112},... | collective-permute-start | bytes 196616 | tf_op jit(solution)/shard_map/ppermute | solution.py:41
  71.8 10.0 %collective-permute-start.7 = (bf16[40,4,256]{2,1,0:T(4,128)(2,1)S(1)}, bf16[40,4,256]{2,1,0:T(4,128)(2,1)S(1)}, u32[]{:S(2)}, u32[]{:S(2)}) collective-permute-start(bf16[40,4,256]{2,1,0:T(4,128)(2,1)S(1)} %pad_maximum_fusion.1), channel_id=1, source_target_pairs={{0,1},{1,2},{2,3},{3,4},{4,5},{5,6},{6,7},{7,8},{8,9},{9,10},{10,1... | collective-permute-start | bytes 245768 | tf_op jit(solution)/shard_map/ppermute | solution.py:41
  76.7 6.7 %collective-permute-start.6 = (bf16[40,4,256]{2,1,0:T(4,128)(2,1)S(1)}, bf16[40,4,256]{2,1,0:T(4,128)(2,1)S(1)}, u32[]{:S(2)}, u32[]{:S(2)}) collective-permute-start(bf16[40,4,256]{2,1,0:T(4,128)(2,1)S(1)} %pad_maximum_fusion), channel_id=1, source_target_pairs={{1,0},{2,1},{3,2},{4,3},{5,4},{6,5},{7,6},{8,7},{9,8},{10,9},{11,1... | collective-permute-start | bytes 245768 | tf_op jit(solution)/shard_map/ppermute | solution.py:41

commit v12 on v11

--- a/solution.py
+++ b/solution.py
@@ -415,43 +415,55 @@
         write(i, done.reshape(BX, BY, cohorts))
 
 
+def write_half(low, out, inner, stage, sems):
+    wide = 2 * BY
+
+    def copy(i):
+        at = pl.ds(i * BX, BX)
+        half = out.at[at, pl.ds(0 if low else wide, wide), :]
+        return pltpu.make_async_copy(stage.at[at], half, sems.at[i])
+
+    def write(i, done):
+        at = pl.ds(i * BX, BX)
+        kept = inner[at].astype(jnp.float32)
+        parts = [done, kept[:, :BY]] if low else [kept[:, BY:], done]
+        stage[at] = jnp.concatenate(parts, axis=1).astype(jnp.bfloat16)
+        copy(i).start()
+
+    def wait():
+        for i in range(stage.shape[0] // BX):
+            copy(i).wait()
+
+    return write, wait
+
+
 def left_kernel(
-    slot_table, cells, left, weights, fecundity, moves, ops, partial,
-    result, sides, pairs, seeds, slots, sem,
+    slot_table, cells, left, weights, fecundity, moves, ops, partial, inner,
+    out, sides, pairs, seeds, slots, sem, stage, sems,
 ):
     slot_copy = pltpu.make_async_copy(slot_table, slots, sem)
     slot_copy.start()
-
-    def write(i, done):
-        result[pl.ds(i * BX, BX)] = done
-
+    write, wait = write_half(True, out, inner, stage, sems)
     finish_side(
         -1, 0, cells, left, weights, fecundity, moves, ops, partial, write, sides, pairs, seeds,
         slots, slot_copy,
     )
+    wait()
 
 
 def last_kernel(
-    slot_table, cells, right, weights, fecundity, moves, ops, partial, before, inner,
+    slot_table, cells, right, weights, fecundity, moves, ops, partial, inner, begun,
     out, sides, pairs, seeds, slots, sem, stage, sems,
 ):
-    rows, cols, _ = cells.shape
+    del begun
     slot_copy = pltpu.make_async_copy(slot_table, slots, sem)
     slot_copy.start()
-
-    def write(i, done):
-        at = pl.ds(i * BX, BX)
-        whole = jnp.concatenate([before[at], inner[at].astype(jnp.float32), done], axis=1)
-        stage[at] = whole.astype(jnp.bfloat16)
-        pltpu.make_async_copy(stage.at[at], out.at[at], sems.at[i]).start()
-
+    write, wait = write_half(False, out, inner, stage, sems)
     finish_side(
-        1, cols // BY - 1, cells, right, weights, fecundity, moves, ops, partial, write, sides,
-        pairs, seeds, slots, slot_copy,
+        1, cells.shape[1] // BY - 1, cells, right, weights, fecundity, moves, ops, partial, write,
+        sides, pairs, seeds, slots, slot_copy,
     )
-    for i in range(rows // BX):
-        at = pl.ds(i * BX, BX)
-        pltpu.make_async_copy(stage.at[at], out.at[at], sems.at[i]).wait()
+    wait()
 
 
 def scratch(rows, cols, cohorts, seeded=None):
@@ -521,25 +533,29 @@
         pltpu.VMEM((RMAX, high, BY, cohorts), jnp.float32),
         pltpu.VMEM((rows, BY, cohorts), jnp.float32),
     ] + slot_room
-    before = pl.pallas_call(
+    half_room = [
+        pltpu.VMEM((rows, outer, cohorts), jnp.bfloat16),
+        pltpu.SemaphoreType.DMA((rows // BX,)),
+    ]
+    begun = pl.pallas_call(
         left_kernel,
-        out_shape=jax.ShapeDtypeStruct((rows, BY, cohorts), jnp.float32),
-        in_specs=[ANY] + [VMEM] * 7,
-        out_specs=VMEM,
-        scratch_shapes=side_room,
+        out_shape=state,
+        in_specs=[ANY] + [VMEM] * 8,
+        out_specs=ANY,
+        scratch_shapes=side_room + half_room,
         compiler_params=PARAMS,
         cost_estimate=pl.CostEstimate(flops=2**27, bytes_accessed=2**22, transcendentals=0),
-    )(slots, cells, left, weights, fecundity, moves, ops, partial)
+    )(slots, cells, left, weights, fecundity, moves, ops, partial, inner)
     return pl.pallas_call(
         last_kernel,
         out_shape=state,
-        in_specs=[ANY] + [VMEM] * 9,
+        in_specs=[ANY] + [VMEM] * 8 + [ANY],
         out_specs=ANY,
-        scratch_shapes=side_room
-        + [pltpu.VMEM(shape, jnp.bfloat16), pltpu.SemaphoreType.DMA((rows // BX,))],
+        scratch_shapes=side_room + half_room,
+        input_output_aliases={9: 0},
         compiler_params=PARAMS,
         cost_estimate=pl.CostEstimate(flops=2**28, bytes_accessed=2**22, transcendentals=0),
-    )(slots, cells, right, weights, fecundity, moves, ops, partial, before, inner)
+    )(slots, cells, right, weights, fecundity, moves, ops, partial, inner, begun)
 
 
 def solution(mesh):

time: 86 us -> 86.6 us (level)
  transfers between devices with their start and end apart: 10 -> 10, of which waited for: 5 -> 4; matrix products, arithmetic and copies ran while one was open for 1% -> 1% of each run, Pallas kernels for 10% -> 11%
where the time goes in v12:
time: 86.6 us; the launch traced here: 85.8 us
  starting transfers between devices  45 us (52%)
  waiting for transfers between devices  21.9 us (25%)
  Pallas kernels  16.1 us (19%)
  local copies, waits for them, and re-layouts  1.64 us (2%)
    ppermute x8, starting transfers between devices, swap(): return (lax.ppermute(tail, axis, after), lax.ppermute(head, axis, before))  22 us
    all_to_all x1, starting transfers between devices, fetch(): arrived = lax.all_to_all(spread, WIDE, 0, 0, tiled=True)  16.8 us
    ppermute x8, waiting for transfers between devices, swap(): return (lax.ppermute(tail, axis, after), lax.ppermute(head, axis, before))  12.5 us
    all_to_all x1, waiting for transfers between devices, fetch(): arrived = lax.all_to_all(spread, WIDE, 0, 0, tiled=True)  9.39 us
    all_to_all x1, starting transfers between devices, fetch(): parts = lax.all_to_all(wanted, NEAR, 0, 0, tiled=True)  6.25 us
    pallas_call x1, Pallas kernels, local(): pl.pallas_call(middle_kernel, out_shape=(jax.ShapeDtypeStruct((rows, cols...  3.84 us
    pallas_call x1, Pallas kernels, local(): pl.pallas_call(first_kernel, out_shape=state, in_specs=[VMEM] * 8, out_sp...  3.4 us
    pallas_call x1, Pallas kernels, fetch(): pl.pallas_call(gather_kernel, out_shape=jax.ShapeDtypeStruct((32, count,...  2.05 us
  transfers between devices with their start and end apart: 10, of which 4 were waited for; matrix products, arithmetic and copies ran while one was open for 1% of the time, Pallas kernels for 11%

profile of v12, /device:TPU:1, one launch (start us, length us, event | category | flops | bytes accessed | tf_op | source)
XLA Modules:
  0.0 85.8 jit_solution(15014871881199951713)
XLA Ops:
  0.0 1.8 %shard_map.109 = (bf16[128,16,128]{2,1,0:T(8,128)(2,1)}, f32[8,128]{1,0:T(8,128)}) custom-call(s32[1,1,8]{2,1,0:T(1,128)} %tile_list.1, bf16[4,256,256]{2,1,0:T(8,128)(2,1)} %harvest_ops.1), custom_call_target="tpu_custom_call" | custom-call | bytes 1048576 | tf_op jit(solution)/shard_map/pallas_call | solution.py:134
  1.8 0.0 copy-start
  1.8 0.0 copy-start.2
  1.8 16.8 %all-to-all-start = ((bf16[128,16,128]{2,1,0:T(8,128)(2,1)}), bf16[128,16,128]{2,1,0:T(8,128)(2,1)S(1)}, u32[]{:S(2)}, u32[]{:S(2)}) async-start(bf16[128,16,128]{2,1,0:T(8,128)(2,1)} %get-tuple-element.24), calls=%async_computation | async-start | bytes 1048576 | tf_op jit(solution)/shard_map/all_to_all | solution.py:150
  18.6 0.0 copy-done
  18.6 0.0 copy-done.2
  18.6 0.0 copy-start.4
  18.6 0.1 shard_map.110
  18.7 4.8 %collective-permute-start = (bf16[32,4,256]{2,1,0:T(4,128)(2,1)S(1)}, bf16[32,4,256]{2,1,0:T(4,128)(2,1)S(1)}, u32[]{:S(2)}, u32[]{:S(2)}) collective-permute-start(bf16[32,4,256]{2,1,0:T(4,128)(2,1)S(1)} %get-tuple-element.20), channel_id=1, source_target_pairs={{0,1},{1,2},{2,3},{3,4},{4,5},{5,6},{6,7},{7,8},{8,9},{9,10},{10,1... | collective-permute-start | bytes 196616 | tf_op jit(solution)/shard_map/ppermute | solution.py:41
  23.5 1.3 %collective-permute-start.1 = (bf16[32,4,256]{2,1,0:T(4,128)(2,1)S(1)}, bf16[32,4,256]{2,1,0:T(4,128)(2,1)S(1)}, u32[]{:S(2)}, u32[]{:S(2)}) collective-permute-start(bf16[32,4,256]{2,1,0:T(4,128)(2,1)S(1)} %get-tuple-element.21), channel_id=1, source_target_pairs={{1,0},{2,1},{3,2},{4,3},{5,4},{6,5},{7,6},{8,7},{9,8},{10,9},{11,1... | collective-permute-start | bytes 196616 | tf_op jit(solution)/shard_map/ppermute | solution.py:41
  24.8 0.0 copy-done.4
  24.8 0.1 copy.19
  24.9 0.0 copy-start.3
  24.9 0.1 copy.20
  25.1 0.0 copy-start.6
  25.1 0.7 copy-done.6
  25.7 0.0 copy-start.8
  25.7 0.0 copy-start.9
  25.8 0.0 copy-start.10
  25.8 0.6 copy-done.8
  26.4 0.0 copy-done.9
  26.4 0.0 copy-done.10
  26.4 0.1 multiply_reduce_fusion
  26.5 0.1 fusion.5.weights
  26.6 0.0 copy-done.3
  26.7 9.4 %all-to-all-done.arrived = bf16[128,16,128]{2,1,0:T(8,128)(2,1)S(1)} async-done(((bf16[128,16,128]{2,1,0:T(8,128)(2,1)}), bf16[128,16,128]{2,1,0:T(8,128)(2,1)S(1)}, u32[]{:S(2)}, u32[]{:S(2)}) %all-to-all-start) | async-done | bytes 524320 | tf_op jit(solution)/shard_map/all_to_all | solution.py:150
  36.1 0.1 fusion.2
  36.2 0.0 collective-permute-done.left
  36.2 0.0 collective-permute-done.1.right
  36.2 2.1 %shard_map.113 = bf16[32,8,16,128]{3,2,1,0:T(8,128)(2,1)} custom-call(s32[32,8]{1,0:T(8,128)S(1)} %bitcast.13, bf16[128,16,128]{2,1,0:T(8,128)(2,1)S(1)} %all-to-all-done.arrived, bf16[32,4,256]{2,1,0:T(4,128)(2,1)S(1)} %collective-permute-done.left, bf16[32,4,256]{2,1,0:T(4,128)(2,1)S(1)} %collective-permute-done.1.right, f32[10,256]{1,0:T(8,128)S(1)} %fusion.5.weights, ...), custom_call_target="tpu_custom_call" | custom-call | bytes 1048576 | tf_op jit(solution)/shard_map/pallas_call | solution.py:175
  38.3 6.2 %all-to-all-start.1 = ((bf16[32,8,16,128]{3,2,1,0:T(8,128)(2,1)}), bf16[32,8,16,128]{3,2,1,0:T(8,128)(2,1)S(1)}, u32[]{:S(2)}, u32[]{:S(2)}) async-start(bf16[32,8,16,128]{3,2,1,0:T(8,128)(2,1)} %shard_map.113), calls=%async_computation.1 | async-start | bytes 2097152 | tf_op jit(solution)/shard_map/all_to_all | solution.py:186
  44.6 0.0 copy-start.1
  44.6 0.0 copy-start.5
  44.6 3.5 %collective-permute-start.2 = (bf16[4,40,256]{2,1,0:T(8,128)(2,1)S(1)}, bf16[4,40,256]{2,1,0:T(8,128)(2,1)S(1)}, u32[]{:S(2)}, u32[]{:S(2)}) collective-permute-start(bf16[4,40,256]{2,1,0:T(8,128)(2,1)S(1)} %get-tuple-element.22), channel_id=1, source_target_pairs={{0,16},{16,32},{32,48},{48,64},{64,80},{80,96},{96,112},{112,128},... | collective-permute-start | bytes 245768 | tf_op jit(solution)/shard_map/ppermute | solution.py:41
  48.2 0.0 copy-start.7
  48.2 1.9 %collective-permute-start.3 = (bf16[4,40,256]{2,1,0:T(8,128)(2,1)S(1)}, bf16[4,40,256]{2,1,0:T(8,128)(2,1)S(1)}, u32[]{:S(2)}, u32[]{:S(2)}) collective-permute-start(bf16[4,40,256]{2,1,0:T(8,128)(2,1)S(1)} %get-tuple-element.23), channel_id=1, source_target_pairs={{16,0},{32,16},{48,32},{64,48},{80,64},{96,80},{112,96},{128,112},... | collective-permute-start | bytes 245768 | tf_op jit(solution)/shard_map/ppermute | solution.py:41
  50.1 0.0 copy-done.5
  50.1 0.0 copy-done.7
  50.1 0.2 select_reduce_fusion.slot_table
  50.3 6.9 %collective-permute-done.2.top = bf16[4,40,256]{2,1,0:T(8,128)(2,1)S(1)} collective-permute-done((bf16[4,40,256]{2,1,0:T(8,128)(2,1)S(1)}, bf16[4,40,256]{2,1,0:T(8,128)(2,1)S(1)}, u32[]{:S(2)}, u32[]{:S(2)}) %collective-permute-start.2) | collective-permute-done | bytes 81952 | tf_op jit(solution)/shard_map/ppermute | solution.py:41
  57.3 2.1 %collective-permute-done.3.bottom = bf16[4,40,256]{2,1,0:T(8,128)(2,1)S(1)} collective-permute-done((bf16[4,40,256]{2,1,0:T(8,128)(2,1)S(1)}, bf16[4,40,256]{2,1,0:T(8,128)(2,1)S(1)}, u32[]{:S(2)}, u32[]{:S(2)}) %collective-permute-start.3) | collective-permute-done | bytes 81952 | tf_op jit(solution)/shard_map/ppermute | solution.py:41
  59.4 0.0 copy-done.1
  59.4 3.4 %shard_map.112.grown = bf16[32,32,256]{2,1,0:T(8,128)(2,1)S(1)} custom-call(bf16[32,32,256]{2,1,0:T(8,128)(2,1)S(1)} %copy-done, bf16[4,40,256]{2,1,0:T(8,128)(2,1)S(1)} %collective-permute-done.2.top, bf16[4,40,256]{2,1,0:T(8,128)(2,1)S(1)} %collective-permute-done.3.bottom, bf16[32,4,256]{2,1,0:T(4,128)(2,1)S(1)} %collective-permute-done.left, ...), custom_call_target="tpu_custom_call" | custom-call | flops 268435456 | bytes 16777216 | tf_op jit(solution)/shard_map/pallas_call | solution.py:495
  62.8 0.0 all-to-all-done.1.parts
  62.8 1.0 %shard_map.114 = (bf16[32,32,256]{2,1,0:T(8,128)(2,1)S(1)}, bf16[8,256,256]{2,1,0:T(8,128)(2,1)S(1)}, bf16[4,32,256]{2,1,0:T(8,128)(2,1)S(1)}, bf16[4,32,256]{2,...) custom-call(s32[4,4]{1,0:T(4,128)S(1)} %select_reduce_fusion.slot_table, ...), custom_call_target="tpu_custom_call" | custom-call | flops 268435456 | bytes 4194304 | tf_op jit(solution)/shard_map/pallas_call | solution.py:507
  63.9 2.3 %collective-permute-start.4 = (bf16[4,32,256]{2,1,0:T(8,128)(2,1)S(1)}, bf16[4,32,256]{2,1,0:T(8,128)(2,1)S(1)}, u32[]{:S(2)}, u32[]{:S(2)}) collective-permute-start(bf16[4,32,256]{2,1,0:T(8,128)(2,1)S(1)} %get-tuple-element.26), channel_id=1, source_target_pairs={{0,16},{16,32},{32,48},{48,64},{64,80},{80,96},{96,112},{112,128},... | collective-permute-start | bytes 196616 | tf_op jit(solution)/shard_map/ppermute | solution.py:41
  66.1 2.1 %collective-permute-start.5 = (bf16[4,32,256]{2,1,0:T(8,128)(2,1)S(1)}, bf16[4,32,256]{2,1,0:T(8,128)(2,1)S(1)}, u32[]{:S(2)}, u32[]{:S(2)}) collective-permute-start(bf16[4,32,256]{2,1,0:T(8,128)(2,1)S(1)} %get-tuple-element.28), channel_id=1, source_target_pairs={{16,0},{32,16},{48,32},{64,48},{80,64},{96,80},{112,96},{128,112},... | collective-permute-start | bytes 196616 | tf_op jit(solution)/shard_map/ppermute | solution.py:41
  68.2 0.0 collective-permute-done.4.top
  68.2 3.5 %collective-permute-done.5.bottom = bf16[4,32,256]{2,1,0:T(8,128)(2,1)S(1)} collective-permute-done((bf16[4,32,256]{2,1,0:T(8,128)(2,1)S(1)}, bf16[4,32,256]{2,1,0:T(8,128)(2,1)S(1)}, u32[]{:S(2)}, u32[]{:S(2)}) %collective-permute-start.5) | collective-permute-done | bytes 65568 | tf_op jit(solution)/shard_map/ppermute | solution.py:41
  71.7 0.1 pad_maximum_fusion.1
  71.8 4.8 %collective-permute-start.7 = (bf16[40,4,256]{2,1,0:T(4,128)(2,1)S(1)}, bf16[40,4,256]{2,1,0:T(4,128)(2,1)S(1)}, u32[]{:S(2)}, u32[]{:S(2)}) collective-permute-start(bf16[40,4,256]{2,1,0:T(4,128)(2,1)S(1)} %pad_maximum_fusion.1), channel_id=1, source_target_pairs={{0,1},{1,2},{2,3},{3,4},{4,5},{5,6},{6,7},{7,8},{8,9},{9,10},{10,1... | collective-permute-start | bytes 245768 | tf_op jit(solution)/shard_map/ppermute | solution.py:41
  76.6 0.1 pad_maximum_fusion
  76.7 1.3 %collective-permute-start.6 = (bf16[40,4,256]{2,1,0:T(4,128)(2,1)S(1)}, bf16[40,4,256]{2,1,0:T(4,128)(2,1)S(1)}, u32[]{:S(2)}, u32[]{:S(2)}) collective-permute-start(bf16[40,4,256]{2,1,0:T(4,128)(2,1)S(1)} %pad_maximum_fusion), channel_id=1, source_target_pairs={{1,0},{2,1},{3,2},{4,3},{5,4},{6,5},{7,6},{8,7},{9,8},{10,9},{11,1... | collective-permute-start | bytes 245768 | tf_op jit(solution)/shard_map/ppermute | solution.py:41
  78.0 3.8 %shard_map.115 = (bf16[32,16,256]{2,1,0:T(8,128)(2,1)S(1)}, f32[32,16,256]{2,1,0:T(8,128)S(1)}) custom-call(s32[4,4]{1,0:T(4,128)S(1)} %select_reduce_fusion.slot_table, bf16[32,32,256]{2,1,0:T(8,128)(2,1)S(1)} %get-tuple-element.25.cells, bf16[4,32,256]{2,1,0:T(8,128)(2,1)S(1)} %collective-permute-done.4.top, ...), custom_call_target="tpu_custom_call" | custom-call | flops 268435456 | bytes 16777216 | tf_op jit(solution)/shard_map/pallas_call | solution.py:519
  81.8 0.0 collective-permute-done.7.left
  81.9 2.0 %shard_map.116.begun = bf16[32,32,256]{2,1,0:T(8,128)(2,1)} custom-call(s32[4,4]{1,0:T(4,128)S(1)} %select_reduce_fusion.slot_table, bf16[32,32,256]{2,1,0:T(8,128)(2,1)S(1)} %get-tuple-element.25.cells, bf16[40,4,256]{2,1,0:T(4,128)(2,1)S(1)} %collective-permute-done.7.left, f32[10,256]{1,0:T(8,128)S(1)} %fusion.5.weights, bf16[256,256]{1,0:T(8,128)(2,1)S(1)} %copy-done.1, ...), custom_call_target="tpu_custom_call" | custom-call | flops 134217728 | bytes 4194304 | tf_op jit(solution)/shard_map/pallas_call | solution.py:540
  83.8 0.0 collective-permute-done.6.right
  83.8 2.0 %shard_map.117 = bf16[32,32,256]{2,1,0:T(8,128)(2,1)} custom-call(s32[4,4]{1,0:T(4,128)S(1)} %select_reduce_fusion.slot_table, bf16[32,32,256]{2,1,0:T(8,128)(2,1)S(1)} %get-tuple-element.25.cells, bf16[40,4,256]{2,1,0:T(4,128)(2,1)S(1)} %collective-permute-done.6.right, f32[10,256]{1,0:T(8,128)S(1)} %fusion.5.weights, ...), custom_call_target="tpu_custom_call", output_to_operand_aliasing={{}: (9, {})} | custom-call | flops 268435456 | bytes 4194304 | tf_op jit(solution)/shard_map/pallas_call | solution.py:549
  (11 shorter events, 0.2 us)
Async XLA Ops:
  1.8 16.8 %copy-start = (bf16[32,32,256]{2,1,0:T(8,128)(2,1)S(1)}, bf16[32,32,256]{2,1,0:T(8,128)(2,1)}, u32[]{:S(2)}) copy-start(bf16[32,32,256]{2,1,0:T(8,128)(2,1)} %cells.5) | copy-start | bytes 1572868
  1.8 16.8 %copy-start.2 = (f32[8,128]{1,0:T(8,128)S(1)}, f32[8,128]{1,0:T(8,128)}, u32[]{:S(2)}) copy-start(f32[8,128]{1,0:T(8,128)} %get-tuple-element.19.token) | copy-start | bytes 12292
  1.8 34.3 %all-to-all-start = ((bf16[128,16,128]{2,1,0:T(8,128)(2,1)}), bf16[128,16,128]{2,1,0:T(8,128)(2,1)S(1)}, u32[]{:S(2)}, u32[]{:S(2)}) async-start(bf16[128,16,128]{2,1,0:T(8,128)(2,1)} %get-tuple-element.24), calls=%async_computation | async-start | bytes 1048576 | tf_op jit(solution)/shard_map/all_to_all | solution.py:150
  18.6 6.2 %copy-start.4 = (s32[32,32]{1,0:T(8,128)S(1)}, s32[32,32]{1,0:T(8,128)}, u32[]{:S(2)}) copy-start(s32[32,32]{1,0:T(8,128)} %param.17) | copy-start | bytes 12292
  18.7 17.5 %collective-permute-start = (bf16[32,4,256]{2,1,0:T(4,128)(2,1)S(1)}, bf16[32,4,256]{2,1,0:T(4,128)(2,1)S(1)}, u32[]{:S(2)}, u32[]{:S(2)}) collective-permute-start(bf16[32,4,256]{2,1,0:T(4,128)(2,1)S(1)} %get-tuple-element.20), channel_id=1, source_target_pairs={{0,1},{1,2},{2,3},{3,4},{4,5},{5,6},{6,7},{7,8},{8,9},{9,10},{10,1... | collective-permute-start | bytes 196616 | tf_op jit(solution)/shard_map/ppermute | solution.py:41
  23.5 12.8 %collective-permute-start.1 = (bf16[32,4,256]{2,1,0:T(4,128)(2,1)S(1)}, bf16[32,4,256]{2,1,0:T(4,128)(2,1)S(1)}, u32[]{:S(2)}, u32[]{:S(2)}) collective-permute-start(bf16[32,4,256]{2,1,0:T(4,128)(2,1)S(1)} %get-tuple-element.21), channel_id=1, source_target_pairs={{1,0},{2,1},{3,2},{4,3},{5,4},{6,5},{7,6},{8,7},{9,8},{10,9},{11,1... | collective-permute-start | bytes 196616 | tf_op jit(solution)/shard_map/ppermute | solution.py:41
  24.9 1.7 %copy-start.3 = (bf16[256,256]{1,0:T(8,128)(2,1)S(1)}, bf16[256,256]{1,0:T(8,128)(2,1)}, u32[]{:S(2)}) copy-start(bf16[256,256]{1,0:T(8,128)(2,1)} %param.16) | copy-start | bytes 393220
  25.1 0.7 copy-start.6
  25.7 0.7 copy-start.8
  25.7 0.7 copy-start.9
  25.8 0.7 copy-start.10
  38.3 24.5 %all-to-all-start.1 = ((bf16[32,8,16,128]{3,2,1,0:T(8,128)(2,1)}), bf16[32,8,16,128]{3,2,1,0:T(8,128)(2,1)S(1)}, u32[]{:S(2)}, u32[]{:S(2)}) async-start(bf16[32,8,16,128]{3,2,1,0:T(8,128)(2,1)} %shard_map.113), calls=%async_computation.1 | async-start | bytes 2097152 | tf_op jit(solution)/shard_map/all_to_all | solution.py:186
  44.6 14.8 %copy-start.1 = (bf16[256,256]{1,0:T(8,128)(2,1)S(1)}, bf16[256,256]{1,0:T(8,128)(2,1)}, u32[]{:S(2)}) copy-start(bf16[256,256]{1,0:T(8,128)(2,1)} %fecundity.7) | copy-start | bytes 393220
  44.6 5.5 %copy-start.5 = (s32[4,4]{1,0:T(4,128)S(1)}, s32[4,4]{1,0:T(4,128)}, u32[]{:S(2)}) copy-start(s32[4,4]{1,0:T(4,128)} %param.12) | copy-start | bytes 196
  44.6 12.6 %collective-permute-start.2 = (bf16[4,40,256]{2,1,0:T(8,128)(2,1)S(1)}, bf16[4,40,256]{2,1,0:T(8,128)(2,1)S(1)}, u32[]{:S(2)}, u32[]{:S(2)}) collective-permute-start(bf16[4,40,256]{2,1,0:T(8,128)(2,1)S(1)} %get-tuple-element.22), channel_id=1, source_target_pairs={{0,16},{16,32},{32,48},{48,64},{64,80},{80,96},{96,112},{112,128},... | collective-permute-start | bytes 245768 | tf_op jit(solution)/shard_map/ppermute | solution.py:41
  48.2 2.0 %copy-start.7 = (s32[1,1,16]{2,1,0:T(1,128)S(1)}, s32[1,1,16]{2,1,0:T(1,128)}, u32[]{:S(2)}) copy-start(s32[1,1,16]{2,1,0:T(1,128)} %param.13) | copy-start | bytes 196
  48.2 11.2 %collective-permute-start.3 = (bf16[4,40,256]{2,1,0:T(8,128)(2,1)S(1)}, bf16[4,40,256]{2,1,0:T(8,128)(2,1)S(1)}, u32[]{:S(2)}, u32[]{:S(2)}) collective-permute-start(bf16[4,40,256]{2,1,0:T(8,128)(2,1)S(1)} %get-tuple-element.23), channel_id=1, source_target_pairs={{16,0},{32,16},{48,32},{64,48},{80,64},{96,80},{112,96},{128,112},... | collective-permute-start | bytes 245768 | tf_op jit(solution)/shard_map/ppermute | solution.py:41
  63.9 4.3 %collective-permute-start.4 = (bf16[4,32,256]{2,1,0:T(8,128)(2,1)S(1)}, bf16[4,32,256]{2,1,0:T(8,128)(2,1)S(1)}, u32[]{:S(2)}, u32[]{:S(2)}) collective-permute-start(bf16[4,32,256]{2,1,0:T(8,128)(2,1)S(1)} %get-tuple-element.26), channel_id=1, source_target_pairs={{0,16},{16,32},{32,48},{48,64},{64,80},{80,96},{96,112},{112,128},... | collective-permute-start | bytes 196616 | tf_op jit(solution)/shard_map/ppermute | solution.py:41
  66.1 5.6 %collective-permute-start.5 = (bf16[4,32,256]{2,1,0:T(8,128)(2,1)S(1)}, bf16[4,32,256]{2,1,0:T(8,128)(2,1)S(1)}, u32[]{:S(2)}, u32[]{:S(2)}) collective-permute-start(bf16[4,32,256]{2,1,0:T(8,128)(2,1)S(1)} %get-tuple-element.28), channel_id=1, source_target_pairs={{16,0},{32,16},{48,32},{64,48},{80,64},{96,80},{112,96},{128,112},... | collective-permute-start | bytes 196616 | tf_op jit(solution)/shard_map/ppermute | solution.py:41
  71.8 10.0 %collective-permute-start.7 = (bf16[40,4,256]{2,1,0:T(4,128)(2,1)S(1)}, bf16[40,4,256]{2,1,0:T(4,128)(2,1)S(1)}, u32[]{:S(2)}, u32[]{:S(2)}) collective-permute-start(bf16[40,4,256]{2,1,0:T(4,128)(2,1)S(1)} %pad_maximum_fusion.1), channel_id=1, source_target_pairs={{0,1},{1,2},{2,3},{3,4},{4,5},{5,6},{6,7},{7,8},{8,9},{9,10},{10,1... | collective-permute-start | bytes 245768 | tf_op jit(solution)/shard_map/ppermute | solution.py:41
  76.7 7.1 %collective-permute-start.6 = (bf16[40,4,256]{2,1,0:T(4,128)(2,1)S(1)}, bf16[40,4,256]{2,1,0:T(4,128)(2,1)S(1)}, u32[]{:S(2)}, u32[]{:S(2)}) collective-permute-start(bf16[40,4,256]{2,1,0:T(4,128)(2,1)S(1)} %pad_maximum_fusion), channel_id=1, source_target_pairs={{1,0},{2,1},{3,2},{4,3},{5,4},{6,5},{7,6},{8,7},{9,8},{10,9},{11,1... | collective-permute-start | bytes 245768 | tf_op jit(solution)/shard_map/ppermute | solution.py:41

commit v13 on v11

--- a/solution.py
+++ b/solution.py
@@ -78,7 +78,7 @@
             out[i] = whole.astype(jnp.bfloat16)
 
 
-def spread_kernel(tile_list, harvest_ops, spread, token, listed, held, sems):
+def spread_kernel(tile_list, harvest_ops, spread, token, listed, held, stage, sems):
     mine = (lax.axis_index("xl") * 2 + lax.axis_index("yl")) * 2 + lax.axis_index("co")
     list_copy = pltpu.make_async_copy(tile_list, listed, sems.at[0])
     held_copy = pltpu.make_async_copy(harvest_ops.at[mine // 2], held, sems.at[1])
@@ -98,7 +98,13 @@
             piece = held[pl.ds(group * 32 + low * 16, 16), pl.ds(half * 128, 128)]
             message = jnp.where(sent, piece.astype(jnp.float32), names).astype(jnp.bfloat16)
             for far in range(4):
-                spread[(group * 4 + far) * 4 + near] = message
+                stage[(group * 4 + far) * 4 + near] = message
+        if group % 4 == 3:
+            span = pl.ds((group - 3) * 16, 64)
+            pltpu.make_async_copy(stage.at[span], spread.at[span], sems.at[2 + group // 4]).start()
+    for part in range(2):
+        span = pl.ds(part * 64, 64)
+        pltpu.make_async_copy(stage.at[span], spread.at[span], sems.at[2 + part]).wait()
 
 
 def gather_kernel(places, arrived, left, right, weights, moves, wanted, stage, sems):
@@ -138,11 +144,12 @@
             jax.ShapeDtypeStruct((8, 128), jnp.float32),
         ),
         in_specs=[ANY, ANY],
-        out_specs=(VMEM, VMEM),
+        out_specs=(ANY, VMEM),
         scratch_shapes=[
             pltpu.SMEM(tile_list.shape, jnp.int32),
             pltpu.VMEM((cohorts, cohorts), jnp.bfloat16),
-            pltpu.SemaphoreType.DMA((2,)),
+            pltpu.VMEM((128, 16, 128), jnp.bfloat16),
+            pltpu.SemaphoreType.DMA((4,)),
         ],
         compiler_params=WHOLE,
         cost_estimate=small,

time: 86 us -> 86.6 us (level)
  no operation moved by 1% of the time
where the time goes in v13:
time: 86.6 us; the launch traced here: 86 us
  starting transfers between devices  45 us (52%)
  waiting for transfers between devices  22.2 us (26%)
  Pallas kernels  16.1 us (19%)
  local copies, waits for them, and re-layouts  1.64 us (2%)
    ppermute x8, starting transfers between devices, swap(): return (lax.ppermute(tail, axis, after), lax.ppermute(head, axis, before))  22 us
    all_to_all x1, starting transfers between devices, fetch(): arrived = lax.all_to_all(spread, WIDE, 0, 0, tiled=True)  16.8 us
    ppermute x8, waiting for transfers between devices, swap(): return (lax.ppermute(tail, axis, after), lax.ppermute(head, axis, before))  12.8 us
    all_to_all x1, waiting for transfers between devices, fetch(): arrived = lax.all_to_all(spread, WIDE, 0, 0, tiled=True)  9.39 us
    all_to_all x1, starting transfers between devices, fetch(): parts = lax.all_to_all(wanted, NEAR, 0, 0, tiled=True)  6.25 us
    pallas_call x1, Pallas kernels, local(): pl.pallas_call(middle_kernel, out_shape=(jax.ShapeDtypeStruct((rows, cols...  3.85 us
    pallas_call x1, Pallas kernels, local(): pl.pallas_call(first_kernel, out_shape=state, in_specs=[VMEM] * 8, out_sp...  3.41 us
    pallas_call x1, Pallas kernels, fetch(): pl.pallas_call(spread_kernel, out_shape=(jax.ShapeDtypeStruct((128, 16, 1...  2.34 us
  transfers between devices with their start and end apart: 10, of which 5 were waited for; matrix products, arithmetic and copies ran while one was open for 1% of the time, Pallas kernels for 10%

profile of v13, /device:TPU:1, one launch (start us, length us, event | category | flops | bytes accessed | tf_op | source)
XLA Modules:
  0.0 86.0 jit_solution(7689698626972706595)
XLA Ops:
  0.0 2.3 %shard_map.109 = (bf16[128,16,128]{2,1,0:T(8,128)(2,1)}, f32[8,128]{1,0:T(8,128)}) custom-call(s32[1,1,8]{2,1,0:T(1,128)} %tile_list.1, bf16[4,256,256]{2,1,0:T(8,128)(2,1)} %harvest_ops.1), custom_call_target="tpu_custom_call" | custom-call | bytes 1048576 | tf_op jit(solution)/shard_map/pallas_call | solution.py:140
  2.3 0.0 copy-start
  2.4 0.0 copy-start.2
  2.4 16.8 %all-to-all-start = ((bf16[128,16,128]{2,1,0:T(8,128)(2,1)}), bf16[128,16,128]{2,1,0:T(8,128)(2,1)S(1)}, u32[]{:S(2)}, u32[]{:S(2)}) async-start(bf16[128,16,128]{2,1,0:T(8,128)(2,1)} %get-tuple-element.24), calls=%async_computation | async-start | bytes 1048576 | tf_op jit(solution)/shard_map/all_to_all | solution.py:157
  19.2 0.0 copy-done
  19.2 0.0 copy-done.2
  19.2 0.0 copy-start.4
  19.2 0.1 shard_map.110
  19.3 4.8 %collective-permute-start = (bf16[32,4,256]{2,1,0:T(4,128)(2,1)S(1)}, bf16[32,4,256]{2,1,0:T(4,128)(2,1)S(1)}, u32[]{:S(2)}, u32[]{:S(2)}) collective-permute-start(bf16[32,4,256]{2,1,0:T(4,128)(2,1)S(1)} %get-tuple-element.20), channel_id=1, source_target_pairs={{0,1},{1,2},{2,3},{3,4},{4,5},{5,6},{6,7},{7,8},{8,9},{9,10},{10,1... | collective-permute-start | bytes 196616 | tf_op jit(solution)/shard_map/ppermute | solution.py:41
  24.1 1.3 %collective-permute-start.1 = (bf16[32,4,256]{2,1,0:T(4,128)(2,1)S(1)}, bf16[32,4,256]{2,1,0:T(4,128)(2,1)S(1)}, u32[]{:S(2)}, u32[]{:S(2)}) collective-permute-start(bf16[32,4,256]{2,1,0:T(4,128)(2,1)S(1)} %get-tuple-element.21), channel_id=1, source_target_pairs={{1,0},{2,1},{3,2},{4,3},{5,4},{6,5},{7,6},{8,7},{9,8},{10,9},{11,1... | collective-permute-start | bytes 196616 | tf_op jit(solution)/shard_map/ppermute | solution.py:41
  25.4 0.0 copy-done.4
  25.4 0.1 copy.18
  25.5 0.0 copy-start.3
  25.5 0.1 copy.19
  25.6 0.0 copy-start.6
  25.7 0.7 copy-done.6
  26.3 0.0 copy-start.8
  26.3 0.0 copy-start.9
  26.3 0.0 copy-start.10
  26.3 0.6 copy-done.8
  27.0 0.0 copy-done.9
  27.0 0.0 copy-done.10
  27.0 0.1 multiply_reduce_fusion
  27.1 0.1 fusion.5.weights
  27.2 0.0 copy-done.3
  27.2 9.4 %all-to-all-done.arrived = bf16[128,16,128]{2,1,0:T(8,128)(2,1)S(1)} async-done(((bf16[128,16,128]{2,1,0:T(8,128)(2,1)}), bf16[128,16,128]{2,1,0:T(8,128)(2,1)S(1)}, u32[]{:S(2)}, u32[]{:S(2)}) %all-to-all-start) | async-done | bytes 524320 | tf_op jit(solution)/shard_map/all_to_all | solution.py:157
  36.7 0.1 fusion.2
  36.8 0.0 collective-permute-done.left
  36.8 0.0 collective-permute-done.1.right
  36.8 2.1 %shard_map.113 = bf16[32,8,16,128]{3,2,1,0:T(8,128)(2,1)} custom-call(s32[32,8]{1,0:T(8,128)S(1)} %bitcast.13, bf16[128,16,128]{2,1,0:T(8,128)(2,1)S(1)} %all-to-all-done.arrived, bf16[32,4,256]{2,1,0:T(4,128)(2,1)S(1)} %collective-permute-done.left, bf16[32,4,256]{2,1,0:T(4,128)(2,1)S(1)} %collective-permute-done.1.right, f32[10,256]{1,0:T(8,128)S(1)} %fusion.5.weights, ...), custom_call_target="tpu_custom_call" | custom-call | bytes 1048576 | tf_op jit(solution)/shard_map/pallas_call | solution.py:182
  38.9 6.2 %all-to-all-start.1 = ((bf16[32,8,16,128]{3,2,1,0:T(8,128)(2,1)}), bf16[32,8,16,128]{3,2,1,0:T(8,128)(2,1)S(1)}, u32[]{:S(2)}, u32[]{:S(2)}) async-start(bf16[32,8,16,128]{3,2,1,0:T(8,128)(2,1)} %shard_map.113), calls=%async_computation.1 | async-start | bytes 2097152 | tf_op jit(solution)/shard_map/all_to_all | solution.py:193
  45.1 0.0 copy-start.1
  45.2 0.0 copy-start.5
  45.2 3.5 %collective-permute-start.2 = (bf16[4,40,256]{2,1,0:T(8,128)(2,1)S(1)}, bf16[4,40,256]{2,1,0:T(8,128)(2,1)S(1)}, u32[]{:S(2)}, u32[]{:S(2)}) collective-permute-start(bf16[4,40,256]{2,1,0:T(8,128)(2,1)S(1)} %get-tuple-element.22), channel_id=1, source_target_pairs={{0,16},{16,32},{32,48},{48,64},{64,80},{80,96},{96,112},{112,128},... | collective-permute-start | bytes 245768 | tf_op jit(solution)/shard_map/ppermute | solution.py:41
  48.8 0.0 copy-start.7
  48.8 1.9 %collective-permute-start.3 = (bf16[4,40,256]{2,1,0:T(8,128)(2,1)S(1)}, bf16[4,40,256]{2,1,0:T(8,128)(2,1)S(1)}, u32[]{:S(2)}, u32[]{:S(2)}) collective-permute-start(bf16[4,40,256]{2,1,0:T(8,128)(2,1)S(1)} %get-tuple-element.23), channel_id=1, source_target_pairs={{16,0},{32,16},{48,32},{64,48},{80,64},{96,80},{112,96},{128,112},... | collective-permute-start | bytes 245768 | tf_op jit(solution)/shard_map/ppermute | solution.py:41
  50.7 0.0 copy-done.5
  50.7 0.0 copy-done.7
  50.7 0.2 select_reduce_fusion.slot_table
  50.9 6.9 %collective-permute-done.2.top = bf16[4,40,256]{2,1,0:T(8,128)(2,1)S(1)} collective-permute-done((bf16[4,40,256]{2,1,0:T(8,128)(2,1)S(1)}, bf16[4,40,256]{2,1,0:T(8,128)(2,1)S(1)}, u32[]{:S(2)}, u32[]{:S(2)}) %collective-permute-start.2) | collective-permute-done | bytes 81952 | tf_op jit(solution)/shard_map/ppermute | solution.py:41
  57.9 2.1 %collective-permute-done.3.bottom = bf16[4,40,256]{2,1,0:T(8,128)(2,1)S(1)} collective-permute-done((bf16[4,40,256]{2,1,0:T(8,128)(2,1)S(1)}, bf16[4,40,256]{2,1,0:T(8,128)(2,1)S(1)}, u32[]{:S(2)}, u32[]{:S(2)}) %collective-permute-start.3) | collective-permute-done | bytes 81952 | tf_op jit(solution)/shard_map/ppermute | solution.py:41
  60.0 0.0 copy-done.1
  60.0 3.4 %shard_map.112.grown = bf16[32,32,256]{2,1,0:T(8,128)(2,1)S(1)} custom-call(bf16[32,32,256]{2,1,0:T(8,128)(2,1)S(1)} %copy-done, bf16[4,40,256]{2,1,0:T(8,128)(2,1)S(1)} %collective-permute-done.2.top, bf16[4,40,256]{2,1,0:T(8,128)(2,1)S(1)} %collective-permute-done.3.bottom, bf16[32,4,256]{2,1,0:T(4,128)(2,1)S(1)} %collective-permute-done.left, ...), custom_call_target="tpu_custom_call" | custom-call | flops 268435456 | bytes 16777216 | tf_op jit(solution)/shard_map/pallas_call | solution.py:490
  63.4 0.0 all-to-all-done.1.parts
  63.4 1.0 %shard_map.114 = (bf16[32,32,256]{2,1,0:T(8,128)(2,1)S(1)}, bf16[8,256,256]{2,1,0:T(8,128)(2,1)S(1)}, bf16[4,32,256]{2,1,0:T(8,128)(2,1)S(1)}, bf16[4,32,256]{2,...) custom-call(s32[4,4]{1,0:T(4,128)S(1)} %select_reduce_fusion.slot_table, ...), custom_call_target="tpu_custom_call" | custom-call | flops 268435456 | bytes 4194304 | tf_op jit(solution)/shard_map/pallas_call | solution.py:502
  64.5 2.3 %collective-permute-start.4 = (bf16[4,32,256]{2,1,0:T(8,128)(2,1)S(1)}, bf16[4,32,256]{2,1,0:T(8,128)(2,1)S(1)}, u32[]{:S(2)}, u32[]{:S(2)}) collective-permute-start(bf16[4,32,256]{2,1,0:T(8,128)(2,1)S(1)} %get-tuple-element.26), channel_id=1, source_target_pairs={{0,16},{16,32},{32,48},{48,64},{64,80},{80,96},{96,112},{112,128},... | collective-permute-start | bytes 196616 | tf_op jit(solution)/shard_map/ppermute | solution.py:41
  66.7 2.1 %collective-permute-start.5 = (bf16[4,32,256]{2,1,0:T(8,128)(2,1)S(1)}, bf16[4,32,256]{2,1,0:T(8,128)(2,1)S(1)}, u32[]{:S(2)}, u32[]{:S(2)}) collective-permute-start(bf16[4,32,256]{2,1,0:T(8,128)(2,1)S(1)} %get-tuple-element.28), channel_id=1, source_target_pairs={{16,0},{32,16},{48,32},{64,48},{80,64},{96,80},{112,96},{128,112},... | collective-permute-start | bytes 196616 | tf_op jit(solution)/shard_map/ppermute | solution.py:41
  68.8 0.0 collective-permute-done.4.top
  68.8 3.5 %collective-permute-done.5.bottom = bf16[4,32,256]{2,1,0:T(8,128)(2,1)S(1)} collective-permute-done((bf16[4,32,256]{2,1,0:T(8,128)(2,1)S(1)}, bf16[4,32,256]{2,1,0:T(8,128)(2,1)S(1)}, u32[]{:S(2)}, u32[]{:S(2)}) %collective-permute-start.5) | collective-permute-done | bytes 65568 | tf_op jit(solution)/shard_map/ppermute | solution.py:41
  72.3 0.1 pad_maximum_fusion.1
  72.4 4.8 %collective-permute-start.7 = (bf16[40,4,256]{2,1,0:T(4,128)(2,1)S(1)}, bf16[40,4,256]{2,1,0:T(4,128)(2,1)S(1)}, u32[]{:S(2)}, u32[]{:S(2)}) collective-permute-start(bf16[40,4,256]{2,1,0:T(4,128)(2,1)S(1)} %pad_maximum_fusion.1), channel_id=1, source_target_pairs={{0,1},{1,2},{2,3},{3,4},{4,5},{5,6},{6,7},{7,8},{8,9},{9,10},{10,1... | collective-permute-start | bytes 245768 | tf_op jit(solution)/shard_map/ppermute | solution.py:41
  77.2 0.1 pad_maximum_fusion
  77.3 1.3 %collective-permute-start.6 = (bf16[40,4,256]{2,1,0:T(4,128)(2,1)S(1)}, bf16[40,4,256]{2,1,0:T(4,128)(2,1)S(1)}, u32[]{:S(2)}, u32[]{:S(2)}) collective-permute-start(bf16[40,4,256]{2,1,0:T(4,128)(2,1)S(1)} %pad_maximum_fusion), channel_id=1, source_target_pairs={{1,0},{2,1},{3,2},{4,3},{5,4},{6,5},{7,6},{8,7},{9,8},{10,9},{11,1... | collective-permute-start | bytes 245768 | tf_op jit(solution)/shard_map/ppermute | solution.py:41
  78.6 3.8 %shard_map.115 = (bf16[32,16,256]{2,1,0:T(8,128)(2,1)S(1)}, f32[32,16,256]{2,1,0:T(8,128)S(1)}) custom-call(s32[4,4]{1,0:T(4,128)S(1)} %select_reduce_fusion.slot_table, bf16[32,32,256]{2,1,0:T(8,128)(2,1)S(1)} %get-tuple-element.25.cells, bf16[4,32,256]{2,1,0:T(8,128)(2,1)S(1)} %collective-permute-done.4.top, ...), custom_call_target="tpu_custom_call" | custom-call | flops 268435456 | bytes 16777216 | tf_op jit(solution)/shard_map/pallas_call | solution.py:514
  82.4 0.0 collective-permute-done.7.left
  82.4 1.3 %shard_map.116.before = f32[32,8,256]{2,1,0:T(8,128)S(1)} custom-call(s32[4,4]{1,0:T(4,128)S(1)} %select_reduce_fusion.slot_table, bf16[32,32,256]{2,1,0:T(8,128)(2,1)S(1)} %get-tuple-element.25.cells, bf16[40,4,256]{2,1,0:T(4,128)(2,1)S(1)} %collective-permute-done.7.left, f32[10,256]{1,0:T(8,128)S(1)} %fusion.5.weights, bf16[256,256]{1,0:T(8,128)(2,1)S(1)} %copy-done.1, ...), custom_call_target="tpu_custom_call" | custom-call | flops 134217728 | bytes 4194304 | tf_op jit(solution)/shard_map/pallas_call | solution.py:531
  83.7 0.3 collective-permute-done.6.right
  84.0 2.0 %shard_map.117 = bf16[32,32,256]{2,1,0:T(8,128)(2,1)} custom-call(s32[4,4]{1,0:T(4,128)S(1)} %select_reduce_fusion.slot_table, bf16[32,32,256]{2,1,0:T(8,128)(2,1)S(1)} %get-tuple-element.25.cells, bf16[40,4,256]{2,1,0:T(4,128)(2,1)S(1)} %collective-permute-done.6.right, f32[10,256]{1,0:T(8,128)S(1)} %fusion.5.weights, bf16[256,256]{1,0:T(8,128)(2,1)S(1)} %copy-done.1, ...), custom_call_target="tpu_custom_call" | custom-call | flops 268435456 | bytes 4194304 | tf_op jit(solution)/shard_map/pallas_call | solution.py:540
  (11 shorter events, 0.2 us)
Async XLA Ops:
  2.3 16.8 %copy-start = (bf16[32,32,256]{2,1,0:T(8,128)(2,1)S(1)}, bf16[32,32,256]{2,1,0:T(8,128)(2,1)}, u32[]{:S(2)}) copy-start(bf16[32,32,256]{2,1,0:T(8,128)(2,1)} %cells.5) | copy-start | bytes 1572868
  2.4 16.8 %copy-start.2 = (f32[8,128]{1,0:T(8,128)S(1)}, f32[8,128]{1,0:T(8,128)}, u32[]{:S(2)}) copy-start(f32[8,128]{1,0:T(8,128)} %get-tuple-element.19.token) | copy-start | bytes 12292
  2.4 34.3 %all-to-all-start = ((bf16[128,16,128]{2,1,0:T(8,128)(2,1)}), bf16[128,16,128]{2,1,0:T(8,128)(2,1)S(1)}, u32[]{:S(2)}, u32[]{:S(2)}) async-start(bf16[128,16,128]{2,1,0:T(8,128)(2,1)} %get-tuple-element.24), calls=%async_computation | async-start | bytes 1048576 | tf_op jit(solution)/shard_map/all_to_all | solution.py:157
  19.2 6.2 %copy-start.4 = (s32[32,32]{1,0:T(8,128)S(1)}, s32[32,32]{1,0:T(8,128)}, u32[]{:S(2)}) copy-start(s32[32,32]{1,0:T(8,128)} %param.17) | copy-start | bytes 12292
  19.3 17.5 %collective-permute-start = (bf16[32,4,256]{2,1,0:T(4,128)(2,1)S(1)}, bf16[32,4,256]{2,1,0:T(4,128)(2,1)S(1)}, u32[]{:S(2)}, u32[]{:S(2)}) collective-permute-start(bf16[32,4,256]{2,1,0:T(4,128)(2,1)S(1)} %get-tuple-element.20), channel_id=1, source_target_pairs={{0,1},{1,2},{2,3},{3,4},{4,5},{5,6},{6,7},{7,8},{8,9},{9,10},{10,1... | collective-permute-start | bytes 196616 | tf_op jit(solution)/shard_map/ppermute | solution.py:41
  24.1 12.8 %collective-permute-start.1 = (bf16[32,4,256]{2,1,0:T(4,128)(2,1)S(1)}, bf16[32,4,256]{2,1,0:T(4,128)(2,1)S(1)}, u32[]{:S(2)}, u32[]{:S(2)}) collective-permute-start(bf16[32,4,256]{2,1,0:T(4,128)(2,1)S(1)} %get-tuple-element.21), channel_id=1, source_target_pairs={{1,0},{2,1},{3,2},{4,3},{5,4},{6,5},{7,6},{8,7},{9,8},{10,9},{11,1... | collective-permute-start | bytes 196616 | tf_op jit(solution)/shard_map/ppermute | solution.py:41
  25.5 1.7 %copy-start.3 = (bf16[256,256]{1,0:T(8,128)(2,1)S(1)}, bf16[256,256]{1,0:T(8,128)(2,1)}, u32[]{:S(2)}) copy-start(bf16[256,256]{1,0:T(8,128)(2,1)} %param.16) | copy-start | bytes 393220
  25.6 0.7 copy-start.6
  26.3 0.7 copy-start.8
  26.3 0.7 copy-start.9
  26.3 0.7 copy-start.10
  38.9 24.5 %all-to-all-start.1 = ((bf16[32,8,16,128]{3,2,1,0:T(8,128)(2,1)}), bf16[32,8,16,128]{3,2,1,0:T(8,128)(2,1)S(1)}, u32[]{:S(2)}, u32[]{:S(2)}) async-start(bf16[32,8,16,128]{3,2,1,0:T(8,128)(2,1)} %shard_map.113), calls=%async_computation.1 | async-start | bytes 2097152 | tf_op jit(solution)/shard_map/all_to_all | solution.py:193
  45.1 14.8 %copy-start.1 = (bf16[256,256]{1,0:T(8,128)(2,1)S(1)}, bf16[256,256]{1,0:T(8,128)(2,1)}, u32[]{:S(2)}) copy-start(bf16[256,256]{1,0:T(8,128)(2,1)} %fecundity.7) | copy-start | bytes 393220
  45.2 5.5 %copy-start.5 = (s32[4,4]{1,0:T(4,128)S(1)}, s32[4,4]{1,0:T(4,128)}, u32[]{:S(2)}) copy-start(s32[4,4]{1,0:T(4,128)} %param.12) | copy-start | bytes 196
  45.2 12.6 %collective-permute-start.2 = (bf16[4,40,256]{2,1,0:T(8,128)(2,1)S(1)}, bf16[4,40,256]{2,1,0:T(8,128)(2,1)S(1)}, u32[]{:S(2)}, u32[]{:S(2)}) collective-permute-start(bf16[4,40,256]{2,1,0:T(8,128)(2,1)S(1)} %get-tuple-element.22), channel_id=1, source_target_pairs={{0,16},{16,32},{32,48},{48,64},{64,80},{80,96},{96,112},{112,128},... | collective-permute-start | bytes 245768 | tf_op jit(solution)/shard_map/ppermute | solution.py:41
  48.8 2.0 %copy-start.7 = (s32[1,1,16]{2,1,0:T(1,128)S(1)}, s32[1,1,16]{2,1,0:T(1,128)}, u32[]{:S(2)}) copy-start(s32[1,1,16]{2,1,0:T(1,128)} %param.13) | copy-start | bytes 196
  48.8 11.2 %collective-permute-start.3 = (bf16[4,40,256]{2,1,0:T(8,128)(2,1)S(1)}, bf16[4,40,256]{2,1,0:T(8,128)(2,1)S(1)}, u32[]{:S(2)}, u32[]{:S(2)}) collective-permute-start(bf16[4,40,256]{2,1,0:T(8,128)(2,1)S(1)} %get-tuple-element.23), channel_id=1, source_target_pairs={{16,0},{32,16},{48,32},{64,48},{80,64},{96,80},{112,96},{128,112},... | collective-permute-start | bytes 245768 | tf_op jit(solution)/shard_map/ppermute | solution.py:41
  64.5 4.3 %collective-permute-start.4 = (bf16[4,32,256]{2,1,0:T(8,128)(2,1)S(1)}, bf16[4,32,256]{2,1,0:T(8,128)(2,1)S(1)}, u32[]{:S(2)}, u32[]{:S(2)}) collective-permute-start(bf16[4,32,256]{2,1,0:T(8,128)(2,1)S(1)} %get-tuple-element.26), channel_id=1, source_target_pairs={{0,16},{16,32},{32,48},{48,64},{64,80},{80,96},{96,112},{112,128},... | collective-permute-start | bytes 196616 | tf_op jit(solution)/shard_map/ppermute | solution.py:41
  66.7 5.6 %collective-permute-start.5 = (bf16[4,32,256]{2,1,0:T(8,128)(2,1)S(1)}, bf16[4,32,256]{2,1,0:T(8,128)(2,1)S(1)}, u32[]{:S(2)}, u32[]{:S(2)}) collective-permute-start(bf16[4,32,256]{2,1,0:T(8,128)(2,1)S(1)} %get-tuple-element.28), channel_id=1, source_target_pairs={{16,0},{32,16},{48,32},{64,48},{80,64},{96,80},{112,96},{128,112},... | collective-permute-start | bytes 196616 | tf_op jit(solution)/shard_map/ppermute | solution.py:41
  72.4 10.0 %collective-permute-start.7 = (bf16[40,4,256]{2,1,0:T(4,128)(2,1)S(1)}, bf16[40,4,256]{2,1,0:T(4,128)(2,1)S(1)}, u32[]{:S(2)}, u32[]{:S(2)}) collective-permute-start(bf16[40,4,256]{2,1,0:T(4,128)(2,1)S(1)} %pad_maximum_fusion.1), channel_id=1, source_target_pairs={{0,1},{1,2},{2,3},{3,4},{4,5},{5,6},{6,7},{7,8},{8,9},{9,10},{10,1... | collective-permute-start | bytes 245768 | tf_op jit(solution)/shard_map/ppermute | solution.py:41
  77.3 6.7 %collective-permute-start.6 = (bf16[40,4,256]{2,1,0:T(4,128)(2,1)S(1)}, bf16[40,4,256]{2,1,0:T(4,128)(2,1)S(1)}, u32[]{:S(2)}, u32[]{:S(2)}) collective-permute-start(bf16[40,4,256]{2,1,0:T(4,128)(2,1)S(1)} %pad_maximum_fusion), channel_id=1, source_target_pairs={{1,0},{2,1},{3,2},{4,3},{5,4},{6,5},{7,6},{8,7},{9,8},{10,9},{11,1... | collective-permute-start | bytes 245768 | tf_op jit(solution)/shard_map/ppermute | solution.py:41
